TPU v7x, 512 devices: a whole 4x4x16 slice. The times are simulated.
512 devices in a mesh: tm: 128 (over y_hi, z, x), rows: 4 (over y_lo, core).
Axes of the slice: x: 4, y: 4 (y_hi: 2, y_lo: 2; y = y_hi * 2 + y_lo), z: 16, core: 2. Of those that a mesh axis runs over, the one named last changes fastest.
Arguments:
- latents: bfloat16 [128, 16, 32, 640], P('tm', 'rows'), may hold values from -20 to 20
- gn_gain: float32 [640], replicated, may hold values from 0.5 to 2
- conv_weight: bfloat16 [9, 640, 640], P(None, 'rows'), may hold values from -0.078125 to 0.078125
- conv_bias: float32 [640], replicated, may hold values from -3 to 3
- ln_gain: float32 [640], replicated, may hold values from 0.5 to 2
- qkv_weight: bfloat16 [640, 1920], P('rows'), may hold values from -1.5 to 1.5
Outputs:
- restyled: bfloat16 [128, 16, 32, 640], P('tm', 'rows')
All inputs are finite; a program needn't handle non-finite values.
Results may differ from a plain program's by a relative error of at most 0.023.
Values may be sent and summed in bfloat16 or wider, within the bound.
No kernel may reach another device: no remote copies, remote signals or barrier semaphores. Data moves between devices by JAX's collectives and lax.ppermute only.
A program may use at most 64 MiB of HBM per device.

v0:
```python
import jax
import jax.numpy as jnp
from jax import lax
from jax.sharding import PartitionSpec as P

HEADS = 8
GROUPS = 32


EPS = 1e-05


def extended(x, sides, width):
    for axis, dim in sides:
        devices, length = (lax.axis_size(axis), x.shape[dim])
        up = [(i, (i + 1) % devices) for i in range(devices - 1)]
        down = [(j, i) for i, j in up]
        last = lax.slice_in_dim(x, length - width, length, axis=dim)
        leading = lax.slice_in_dim(x, 0, width, axis=dim)
        before = lax.ppermute(last, axis, up)
        after = lax.ppermute(leading, axis, down)
        x = jnp.concatenate([before, x, after], axis=dim)
    return x


def broadcast(value, axis, source):
    kept = jnp.where(lax.axis_index(axis) == source, value, 0).astype(value.dtype)
    return lax.psum(kept, axis)


def shifted(block, axis, distance):
    devices = range(lax.axis_size(axis))
    route = [(i - distance, i) for i in devices if i - distance in devices]
    return lax.ppermute(block, axis, route)


def conv_taps(padded, weights):
    height = padded.shape[1] - 2
    width = padded.shape[2] - 2
    count = weights.shape[1]
    total = jnp.zeros((padded.shape[0] * height * width, weights.shape[2]), jnp.float32)
    for row_tap in range(3):
        for col_tap in range(3):
            window = padded[:, row_tap : row_tap + height, col_tap : col_tap + width, :].reshape(
                -1, count
            )
            total = total + jnp.dot(
                window, weights[3 * row_tap + col_tap], preferred_element_type=jnp.float32
            )
    return total


def on_device(latents, gn_gain, conv_weight, conv_bias, ln_gain, qkv_weight):
    frames, rows_dev, width, chans = latents.shape
    group_size = chans // GROUPS
    row_devices = lax.axis_size("rows")
    height = rows_dev * row_devices
    count = height * width * group_size
    cells = rows_dev * width
    values = latents.astype(jnp.float32).reshape(frames, cells, GROUPS, group_size)
    total = lax.psum(jnp.sum(values, axis=(1, 3)), "rows")
    mean = total / count
    centred = values - mean[:, None, :, None]
    spread = lax.psum(jnp.sum(centred * centred, axis=(1, 3)), "rows") / count
    normed = (centred * lax.rsqrt(spread + EPS)[:, None, :, None]).reshape(
        frames, rows_dev, width, chans
    ) * gn_gain
    act = jax.nn.silu(normed).astype(jnp.bfloat16)
    padded = extended(act, (("rows", 1),), 1)
    padded = jnp.pad(padded, ((0, 0), (0, 0), (1, 1), (0, 0)))
    conv = conv_taps(padded, lax.all_gather(conv_weight, "rows", axis=1, tiled=True))
    residual = (
        latents.astype(jnp.float32).reshape(frames * cells, chans) + conv + conv_bias
    ).astype(jnp.bfloat16)
    rfloat = residual.astype(jnp.float32)
    centre = jnp.mean(rfloat, axis=1, keepdims=True)
    deviation = rfloat - centre
    variance = jnp.mean(deviation * deviation, axis=1, keepdims=True)
    feats = (deviation * lax.rsqrt(variance + EPS) * ln_gain).astype(jnp.bfloat16)
    proj = jnp.dot(
        feats,
        lax.all_gather(qkv_weight, "rows", axis=0, tiled=True),
        preferred_element_type=jnp.float32,
    )
    query = proj[:, :chans].astype(jnp.bfloat16).reshape(frames, cells, chans)
    keys = proj[:, chans : 2 * chans].astype(jnp.bfloat16).reshape(frames, cells, chans)
    vals = proj[:, 2 * chans :].astype(jnp.bfloat16).reshape(frames, cells, chans)
    anchor_keys, anchor_vals = (broadcast(keys[0], "tm", 0), broadcast(vals[0], "tm", 0))
    moved_keys, moved_vals = shifted((keys[frames - 1], vals[frames - 1]), "tm", 1)
    leading = lax.axis_index("tm") == 0
    moved_keys = jnp.where(leading, keys[0], moved_keys)
    moved_vals = jnp.where(leading, vals[0], moved_vals)
    prev_keys = jnp.concatenate([moved_keys[None], keys[: frames - 1]], 0)
    prev_vals = jnp.concatenate([moved_vals[None], vals[: frames - 1]], 0)
    head_dim = chans // HEADS
    scale = head_dim ** (-0.5)
    query_heads = query.reshape(frames, cells, HEADS, head_dim).transpose(2, 0, 1, 3)
    start_state = (
        jnp.full((HEADS, frames, cells), -jnp.inf, jnp.float32),
        jnp.zeros((HEADS, frames, cells), jnp.float32),
        jnp.zeros((HEADS, frames, cells, head_dim), jnp.float32),
    )
    piece_ak = lax.all_gather(anchor_keys[None], "rows", axis=1, tiled=True)
    piece_av = lax.all_gather(anchor_vals[None], "rows", axis=1, tiled=True)
    piece_pk = lax.all_gather(prev_keys, "rows", axis=1, tiled=True)
    piece_pv = lax.all_gather(prev_vals, "rows", axis=1, tiled=True)
    span = piece_pk.shape[1]
    key_all = jnp.concatenate([piece_ak, piece_pk], 1)
    val_all = jnp.concatenate([piece_av, piece_pv], 1)
    key_heads = key_all.reshape(frames, 2 * span, HEADS, head_dim).transpose(2, 0, 1, 3)
    val_heads = val_all.reshape(frames, 2 * span, HEADS, head_dim).transpose(2, 0, 1, 3)

    def one_head(item):
        q_head, k_head, v_head, top_old, den_old, acc_old = item
        scores = (
            jnp.einsum("fpd,fkd->fpk", q_head, k_head, preferred_element_type=jnp.float32) * scale
        )
        top_new = jnp.maximum(top_old, jnp.max(scores, axis=-1))
        weights = jnp.exp(scores - top_new[..., None])
        factor = jnp.exp(top_old - top_new)
        den_new = den_old * factor + jnp.sum(weights, axis=-1)
        acc_new = acc_old * factor[..., None] + jnp.einsum(
            "fpk,fkd->fpd", weights.astype(jnp.bfloat16), v_head, preferred_element_type=jnp.float32
        )
        return (top_new, den_new, acc_new)

    final_top, final_den, final_acc = lax.map(
        one_head, (query_heads, key_heads, val_heads) + tuple(start_state)
    )
    mixed = final_acc / final_den[..., None]
    attn = mixed.transpose(1, 2, 0, 3).reshape(frames * cells, chans)
    restyled = (residual.astype(jnp.float32) + attn).astype(jnp.bfloat16)
    return restyled.reshape(frames, rows_dev, width, chans)


def solution(mesh):
    return jax.shard_map(
        on_device,
        mesh=mesh,
        in_specs=(
            P("tm", "rows", None, None),
            P(),
            P(None, "rows", None),
            P(),
            P(),
            P("rows", None),
        ),
        out_specs=P("tm", "rows", None, None),
        check_vma=False,
    )
```

profile of v0, /device:TPU:1, one launch (start us, length us, event | category | flops | bytes accessed | tf_op | source)
XLA Modules:
  0.0 1431.6 jit_solution(12072458116486620923)
XLA Ops:
  6.5 0.7 all-gather.5.cloned.1.call-update
  7.3 0.7 all-gather.7.cloned.1.call-update
  8.1 1.0 convert_reduce_fusion
  9.1 0.1 reduce_sum.65
  9.2 11.9 psum.28
  21.6 5.8 psum.29
  27.6 0.1 multiply_convert_fusion.1
  27.7 3.5 collective-permute-start
  31.3 1.9 collective-permute-start.1
  33.2 4.1 collective-permute-done.1
  37.5 58.6 %all-gather.5.cloned.1.call-done = bf16[9,640,640]{2,1,0:T(8,128)(2,1)} async-done(((bf16[9,160,640]{2,1,0:T(8,128)(2,1)}), bf16[9,640,640]{2,1,0:T(8,128)(2,1)}) %all-gather.5.cloned.1.call-update) | async-done | bytes 7372816 | tf_op jit(solution)/shard_map/all_gather | solution.py:71
  96.2 1.4 fusion.20
  97.6 1.5 fusion.19
  99.1 1.5 convolution_add_fusion.7
  100.5 1.5 convolution_add_fusion.6
  102.0 1.5 convolution_add_fusion.5
  103.5 1.5 convolution_add_fusion.4
  105.0 1.5 convolution_add_fusion.3
  106.4 1.5 convolution_add_fusion.2
  107.9 1.6 fusion.33
  109.5 0.2 multiply_reduce_fusion
  109.7 29.0 %all-gather.7.cloned.1.call-done = bf16[640,1920]{1,0:T(8,128)(2,1)} async-done(((bf16[160,1920]{1,0:T(8,128)(2,1)}), bf16[640,1920]{1,0:T(8,128)(2,1)}) %all-gather.7.cloned.1.call-update) | async-done | bytes 2457616 | tf_op jit(solution)/shard_map/all_gather | solution.py:82
  138.7 2.3 convolution_convert_fusion
  141.1 3.1 collective-permute-start.3
  144.2 3.6 collective-permute-done.3
  147.8 0.8 broadcast_select_fusion
  148.6 4.1 collective-permute-start.2
  152.7 0.2 copy.11
  152.9 8.0 all-gather.1
  160.9 12.0 all-gather
  172.9 1174.0 %all-reduce.4.cloned.1.call-done = (bf16[1,128,640]{2,1,0:T(8,128)(2,1)}, bf16[1,128,640]{2,1,0:T(8,128)(2,1)}) async-done(((bf16[1,128,640]{2,1,0:T(8,128)(2,1)}, bf16[1,128,640]{2,1,0:T(8,128)(2,1)}), (bf16[1,128,640]{2,1,0:T(8,128)(2,1)}, bf16[1,128,640]{2,1,0:T(8,128)(2,1)})) %all-reduce.4.cloned.1.call-update) | async-done | bytes 327696 | tf_op jit(solution)/shard_map/psum | solution.py:28
  1346.9 50.8 %all_gather.22 = bf16[1,512,640]{2,1,0:T(8,128)(2,1)S(1)} all-gather(bf16[1,128,640]{2,1,0:T(8,128)(2,1)} %get-tuple-element.59), channel_id=1, replica_groups=mesh['tm'=128,'rows'=4] {'rows'}, dimensions={1}, use_global_device_ids=true | all-gather | bytes 819200 | tf_op jit(solution)/shard_map/all_gather | solution.py:104
  1397.7 0.1 pad_maximum_fusion.1
  1397.8 0.7 copy.13
  1398.5 8.2 all_gather.20
  1406.7 1.2 pad_maximum_fusion
  1407.9 1.6 copy.12
  1409.5 14.7 %while.12 = (s32[]{:T(128)}, f32[8,1,128]{2,1,0:T(1,128)S(1)}, f32[8,1,128,80]{2,3,1,0:T(8,128)S(1)}, bf16[8,1,128,80]{2,3,0,1:T(8,128)(2,1)S(1)}, bf16[8,1,1024...) while((s32[]{:T(128)}, f32[8,1,128]{2,1,0:T(1,128)S(1)}, ...), condition=%wide.region_13.14_spmd, body=%wide.region_10.13_spmd.sunk | while | flops 42740096 | bytes 1969233 | solution.py:127
  1409.5 1.2 fusion.51
  1410.7 0.3 fusion.53
  1411.0 0.2 fusion.52
  1411.3 1.2 fusion.51
  1412.6 0.3 fusion.53
  1412.9 0.2 fusion.52
  1413.1 1.2 fusion.51
  1414.4 0.3 fusion.53
  1414.7 0.2 fusion.52
  1415.0 1.2 fusion.51
  1416.2 0.3 fusion.53
  1416.5 0.2 fusion.52
  1416.8 1.2 fusion.51
  1418.1 0.3 fusion.53
  1418.4 0.2 fusion.52
  1418.6 1.2 fusion.51
  1419.9 0.3 fusion.53
  1420.2 0.2 fusion.52
  1420.5 1.2 fusion.51
  1421.7 0.3 fusion.53
  1422.1 0.2 fusion.52
  1422.3 1.2 fusion.51
  1423.6 0.3 fusion.53
  1423.9 0.2 fusion.52
  1424.2 0.2 copy.18
  1424.3 0.7 add_convert_fusion
  (51 shorter events, 1.4 us)
Async XLA Ops:
  6.5 14.8 %copy-start = (bf16[1,4,32,640]{3,2,1,0:T(8,128)(2,1)S(1)}, bf16[1,4,32,640]{3,2,1,0:T(8,128)(2,1)}, u32[]{:S(2)}) copy-start(bf16[1,4,32,640]{3,2,1,0:T(8,128)(2,1)} %param.8) | copy-start | bytes 491524
  6.5 21.0 %copy-start.1 = (f32[640]{0:T(1024)S(1)}, f32[640]{0:T(1024)}, u32[]{:S(2)}) copy-start(f32[640]{0:T(1024)} %param.9) | copy-start | bytes 7684
  6.5 89.6 %all-gather.5.cloned.1.call-start = ((), (), s32[]{:S(2)}) async-start(), calls=%async_computation | async-start | bytes 9216000 | tf_op jit(solution)/shard_map/all_gather | solution.py:71
  7.3 131.5 %all-gather.7.cloned.1.call-start = ((), (), s32[]{:S(2)}) async-start(), calls=%async_computation.1 | async-start | bytes 3072000 | tf_op jit(solution)/shard_map/all_gather | solution.py:82
  8.0 1338.9 %all-reduce.4.cloned.1.call-start = ((), (), s32[]{:S(2)}) async-start(), calls=%async_computation.2 | async-start | bytes 655360 | tf_op jit(solution)/shard_map/psum | solution.py:28
  27.7 5.5 collective-permute-start
  31.3 6.0 collective-permute-start.1
  103.5 4.4 copy-start.2
  104.9 33.8 %copy-start.3 = (f32[640]{0:T(1024)S(1)}, f32[640]{0:T(1024)}, u32[]{:S(2)}) copy-start(f32[640]{0:T(1024)} %param.12) | copy-start | bytes 7684
  141.1 6.7 collective-permute-start.3
  148.6 12.3 collective-permute-start.2
Sparse Core Ops, SparseCore 0:
  9.5 86.6 all-gather.4
  98.3 40.4 all-gather.6
  153.0 1193.8 all-reduce.3
where the time goes:
time: 1430 us
  waiting for transfers between devices  1270 us (89%)
  blocking collectives  96.6 us (7%)
  matrix products  27.9 us (2%)
    psum x1, waiting for transfers between devices, broadcast(): return lax.psum(kept, axis)  1170 us
    all_gather x1, waiting for transfers between devices, on_device(): lax.all_gather(conv_weight, 'rows', axis=1, tiled=True)  58.6 us
    all_gather x1, blocking collectives, on_device(): piece_av = lax.all_gather(anchor_vals[None], 'rows', axis=1, tiled=True)  50.8 us
    all_gather x1, waiting for transfers between devices, on_device(): lax.all_gather(qkv_weight, 'rows', axis=0, tiled=True)  29 us
  transfers between devices with their start and end apart: 7, of which 5 were waited for; matrix products, arithmetic and copies ran while one was open for 1% of the time, Pallas kernels for 0%

commit v1 on v0

--- a/solution.py
+++ b/solution.py
@@ -23,9 +23,16 @@
     return x
 
 
-def broadcast(value, axis, source):
-    kept = jnp.where(lax.axis_index(axis) == source, value, 0).astype(value.dtype)
-    return lax.psum(kept, axis)
+def broadcast(value, axis):
+    devices = lax.axis_size(axis)
+    me = lax.axis_index(axis)
+    step = devices // 2
+    while step:
+        route = [(i, i + step) for i in range(0, devices, 2 * step)]
+        came = lax.ppermute(value, axis, route)
+        value = jnp.where(me % (2 * step) == step, came, value)
+        step //= 2
+    return value
 
 
 def shifted(block, axis, distance):
@@ -85,7 +92,8 @@
     query = proj[:, :chans].astype(jnp.bfloat16).reshape(frames, cells, chans)
     keys = proj[:, chans : 2 * chans].astype(jnp.bfloat16).reshape(frames, cells, chans)
     vals = proj[:, 2 * chans :].astype(jnp.bfloat16).reshape(frames, cells, chans)
-    anchor_keys, anchor_vals = (broadcast(keys[0], "tm", 0), broadcast(vals[0], "tm", 0))
+    anchor = broadcast(jnp.concatenate([keys[0], vals[0]], axis=1), "tm")
+    anchor_keys, anchor_vals = (anchor[:, :chans], anchor[:, chans:])
     moved_keys, moved_vals = shifted((keys[frames - 1], vals[frames - 1]), "tm", 1)
     leading = lax.axis_index("tm") == 0
     moved_keys = jnp.where(leading, keys[0], moved_keys)

time: 1430 us -> 262 us (0.18)
  the two profiles are of different devices: /device:TPU:1 before, /device:TPU:423 now
where the time goes in v1:
time: 262 us; the launch traced here: 261 us
  waiting for transfers between devices  96.3 us (37%)
  starting transfers between devices  59.7 us (23%)
  blocking collectives  48 us (18%)
  matrix products  32.9 us (13%)
  between operations  14 us (5%)
  other arithmetic  7.06 us (3%)
  local copies, waits for them, and re-layouts  3.27 us (1%)
    all_gather x1, waiting for transfers between devices, on_device(): lax.all_gather(conv_weight, 'rows', axis=1, tiled=True)  59.4 us
    ppermute x2, starting transfers between devices, shifted(): return lax.ppermute(block, axis, route)  49.7 us
    all_gather x1, waiting for transfers between devices, on_device(): lax.all_gather(qkv_weight, 'rows', axis=0, tiled=True)  29.4 us
    dot_general x9, matrix products, conv_taps(): jnp.dot(window, weights[3 * row_tap + col_tap], preferred_element_type=jn...  13.2 us
    all_gather x1, blocking collectives, on_device(): piece_pv = lax.all_gather(prev_vals, 'rows', axis=1, tiled=True)  10.2 us
    dot_general x8, matrix products, one_head(): jnp.einsum('fpd,fkd->fpk', q_head, k_head, preferred_element_type=jnp.flo...  10 us
    all_gather x1, blocking collectives, on_device(): piece_av = lax.all_gather(anchor_vals[None], 'rows', axis=1, tiled=True)  8.68 us
    all_gather x1, blocking collectives, on_device(): piece_pk = lax.all_gather(prev_keys, 'rows', axis=1, tiled=True)  8.46 us
  transfers between devices with their start and end apart: 13, of which 5 were waited for; matrix products, arithmetic and copies ran while one was open for 6% of the time, Pallas kernels for 0%

profile of v1, /device:TPU:423, one launch (start us, length us, event | category | flops | bytes accessed | tf_op | source)
XLA Modules:
  0.0 261.3 jit_solution(2959333323817746763)
XLA Ops:
  6.5 0.7 all-gather.7.cloned.1.call-update
  7.3 0.7 all-gather.9.cloned.1.call-update
  8.0 1.0 convert_reduce_fusion
  9.2 5.7 %psum.14 = f32[1,32]{1,0:T(1,128)S(1)} all-reduce(f32[1,32]{1,0:T(1,128)S(1)} %bitcast.128), channel_id=1, replica_groups=mesh['tm'=128,'rows'=4] {'rows'}, use_global_device_ids=true, to_apply=%region_2.0 | all-reduce | flops 32 | bytes 256 | tf_op jit(solution)/shard_map/psum | solution.py:68
  15.3 7.0 %psum.15 = f32[1,32]{1,0:T(1,128)S(1)} all-reduce(f32[1,32]{1,0:T(1,128)S(1)} %bitcast.127), channel_id=1, replica_groups=mesh['tm'=128,'rows'=4] {'rows'}, use_global_device_ids=true, to_apply=%region_5.6 | all-reduce | flops 32 | bytes 256 | tf_op jit(solution)/shard_map/psum | solution.py:71
  22.7 2.6 collective-permute-start
  25.3 1.9 collective-permute-start.1
  27.2 3.4 %collective-permute-done.1 = bf16[1,1,32,640]{3,2,1,0:T(8,128)(2,1)S(1)} collective-permute-done((bf16[1,1,32,640]{3,2,1,0:T(8,128)(2,1)S(1)}, bf16[1,1,32,640]{3,2,1,0:T(8,128)(2,1)S(1)}, u32[]{:S(2)}, u32[]{:S(2)}) %collective-permute-start.1) | collective-permute-done | bytes 40992 | tf_op jit(solution)/shard_map/ppermute | solution.py:21
  30.8 59.4 %all-gather.7.cloned.1.call-done = bf16[9,640,640]{2,1,0:T(8,128)(2,1)} async-done(((bf16[9,160,640]{2,1,0:T(8,128)(2,1)}), bf16[9,640,640]{2,1,0:T(8,128)(2,1)}) %all-gather.7.cloned.1.call-update) | async-done | bytes 7372816 | tf_op jit(solution)/shard_map/all_gather | solution.py:78
  90.2 1.4 fusion.20
  91.7 1.5 fusion.19
  93.2 1.5 convolution_add_fusion.7
  94.6 1.5 convolution_add_fusion.6
  96.1 1.5 convolution_add_fusion.5
  97.5 1.5 convolution_add_fusion.4
  99.0 1.5 convolution_add_fusion.3
  100.5 1.5 convolution_add_fusion.2
  102.0 1.6 fusion.34
  103.7 29.4 %all-gather.9.cloned.1.call-done = bf16[640,1920]{1,0:T(8,128)(2,1)} async-done(((bf16[160,1920]{1,0:T(8,128)(2,1)}), bf16[640,1920]{1,0:T(8,128)(2,1)}) %all-gather.9.cloned.1.call-update) | async-done | bytes 2457616 | tf_op jit(solution)/shard_map/all_gather | solution.py:89
  133.1 2.3 convolution_convert_fusion
  135.5 0.7 collective-permute-start.2
  136.2 0.7 collective-permute-start.3
  137.0 0.7 collective-permute-start.4
  137.7 0.7 collective-permute-start.5
  138.5 0.7 collective-permute-start.6
  139.3 43.8 %collective-permute-start.10 = (bf16[128,640]{1,0:T(8,128)(2,1)S(1)}, bf16[128,640]{1,0:T(8,128)(2,1)S(1)}, u32[]{:S(2)}, u32[]{:S(2)}) collective-permute-start(bf16[128,640]{1,0:T(8,128)(2,1)S(1)} %slice.128), channel_id=1, source_target_pairs={{0,4},{4,8},{8,12},{12,16},{16,20},{20,24},{24,28},{28,32},{32,36}... | collective-permute-start | bytes 491528 | tf_op jit(solution)/shard_map/ppermute | solution.py:41
  183.1 0.7 collective-permute-start.7
  183.8 1.5 collective-permute-done.10
  185.4 5.9 %collective-permute-start.9 = (bf16[128,640]{1,0:T(8,128)(2,1)S(1)}, bf16[128,640]{1,0:T(8,128)(2,1)S(1)}, u32[]{:S(2)}, u32[]{:S(2)}) collective-permute-start(bf16[128,640]{1,0:T(8,128)(2,1)S(1)} %get-tuple-element.61), channel_id=1, source_target_pairs={{0,4},{4,8},{8,12},{12,16},{16,20},{20,24},{24,28},{28,32},{32,36}... | collective-permute-start | bytes 491528 | tf_op jit(solution)/shard_map/ppermute | solution.py:41
  191.5 10.2 %all-gather.3 = bf16[512,640]{1,0:T(8,128)(2,1)S(1)} all-gather(bf16[128,640]{1,0:T(8,128)(2,1)S(1)} %get-tuple-element.60), channel_id=5, replica_groups=mesh['tm'=128,'rows'=4] {'rows'}, dimensions={0}, use_global_device_ids=true | all-gather | bytes 819200 | tf_op jit(solution)/shard_map/all_gather | solution.py:114
  201.7 1.3 collective-permute-start.8
  203.1 8.5 %all-gather.1 = bf16[512,640]{1,0:T(8,128)(2,1)} all-gather(bf16[128,640]{1,0:T(8,128)(2,1)S(1)} %broadcast_select_fusion.8), channel_id=3, replica_groups=mesh['tm'=128,'rows'=4] {'rows'}, dimensions={0}, use_global_device_ids=true | all-gather | bytes 819200 | tf_op jit(solution)/shard_map/all_gather | solution.py:113
  211.5 1.3 collective-permute-done.8
  212.9 8.7 %all-gather.2 = bf16[512,640]{1,0:T(8,128)(2,1)S(1)} all-gather(bf16[128,640]{1,0:T(8,128)(2,1)S(1)} %get-tuple-element.63), channel_id=4, replica_groups=mesh['tm'=128,'rows'=4] {'rows'}, dimensions={0}, use_global_device_ids=true | all-gather | bytes 819200 | tf_op jit(solution)/shard_map/all_gather | solution.py:112
  221.7 0.7 copy.13
  222.3 8.0 %all-gather = bf16[512,640]{1,0:T(8,128)(2,1)S(1)} all-gather(bf16[128,640]{1,0:T(8,128)(2,1)S(1)} %get-tuple-element.64), channel_id=2, replica_groups=mesh['tm'=128,'rows'=4] {'rows'}, dimensions={0}, use_global_device_ids=true | all-gather | bytes 819200 | tf_op jit(solution)/shard_map/all_gather | solution.py:111
  230.3 1.2 pad_maximum_fusion
  231.5 1.6 copy.12
  233.1 19.5 %while.12 = (s32[]{:T(128)}, f32[8,1,128]{2,1,0:T(1,128)S(1)}, f32[8,1,128,80]{2,3,1,0:T(8,128)}, bf16[8,1,128,80]{2,3,0,1:T(8,128)(2,1)S(1)}, bf16[8,1,1024,80]...) while((s32[]{:T(128)}, f32[8,1,128]{2,1,0:T(1,128)S(1)}, ...), condition=%wide.region_11.12_spmd, body=%wide.region_8.11_spmd.sunk | while | flops 42740096 | bytes 1969233 | solution.py:135
  233.1 1.2 fusion.52
  234.3 0.9 fusion.54
  235.3 0.2 fusion.53
  235.5 1.3 fusion.52
  236.8 0.9 fusion.54
  237.7 0.2 fusion.53
  238.0 1.3 fusion.52
  239.2 0.9 fusion.54
  240.2 0.2 fusion.53
  240.4 1.3 fusion.52
  241.7 0.9 fusion.54
  242.6 0.2 fusion.53
  242.9 1.2 fusion.52
  244.1 0.9 fusion.54
  245.0 0.2 fusion.53
  245.3 1.3 fusion.52
  246.6 0.9 fusion.54
  247.5 0.2 fusion.53
  247.7 1.2 fusion.52
  249.0 0.9 fusion.54
  249.9 0.2 fusion.53
  250.2 1.3 fusion.52
  251.4 0.9 fusion.54
  252.6 1.0 bitcast_divide_fusion
  253.8 0.7 add_convert_fusion
  (71 shorter events, 2.7 us)
Async XLA Ops:
  6.5 8.5 %copy-start = (bf16[1,4,32,640]{3,2,1,0:T(8,128)(2,1)S(1)}, bf16[1,4,32,640]{3,2,1,0:T(8,128)(2,1)}, u32[]{:S(2)}) copy-start(bf16[1,4,32,640]{3,2,1,0:T(8,128)(2,1)} %param.8) | copy-start | bytes 491524
  6.5 16.0 %copy-start.1 = (f32[640]{0:T(1024)S(1)}, f32[640]{0:T(1024)}, u32[]{:S(2)}) copy-start(f32[640]{0:T(1024)} %param.9) | copy-start | bytes 7684
  6.5 83.7 %all-gather.7.cloned.1.call-start = ((), (), s32[]{:S(2)}) async-start(), calls=%async_computation | async-start | bytes 9216000 | tf_op jit(solution)/shard_map/all_gather | solution.py:78
  7.3 125.8 %all-gather.9.cloned.1.call-start = ((), (), s32[]{:S(2)}) async-start(), calls=%async_computation.1 | async-start | bytes 3072000 | tf_op jit(solution)/shard_map/all_gather | solution.py:89
  22.7 4.5 %collective-permute-start = (bf16[1,1,32,640]{3,2,1,0:T(8,128)(2,1)S(1)}, bf16[1,1,32,640]{3,2,1,0:T(8,128)(2,1)S(1)}, u32[]{:S(2)}, u32[]{:S(2)}) collective-permute-start(bf16[1,1,32,640]{3,2,1,0:T(8,128)(2,1)S(1)} %get-tuple-element.73), channel_id=1, source_target_pairs={{0,1},{1,2},{2,3},{4,5},{5,6},{6,7},{8,9},{9,10},{10,11},{12,13},{... | collective-permute-start | bytes 122888 | tf_op jit(solution)/shard_map/ppermute | solution.py:20
  25.3 5.3 %collective-permute-start.1 = (bf16[1,1,32,640]{3,2,1,0:T(8,128)(2,1)S(1)}, bf16[1,1,32,640]{3,2,1,0:T(8,128)(2,1)S(1)}, u32[]{:S(2)}, u32[]{:S(2)}) collective-permute-start(bf16[1,1,32,640]{3,2,1,0:T(8,128)(2,1)S(1)} %get-tuple-element.74), channel_id=1, source_target_pairs={{1,0},{2,1},{3,2},{5,4},{6,5},{7,6},{9,8},{10,9},{11,10},{13,12},{... | collective-permute-start | bytes 122888 | tf_op jit(solution)/shard_map/ppermute | solution.py:21
  97.5 4.4 %copy-start.2 = (f32[640]{0:T(1024)S(1)}, f32[640]{0:T(1024)}, u32[]{:S(2)}) copy-start(f32[640]{0:T(1024)} %param.11) | copy-start | bytes 7684
  99.0 34.1 %copy-start.3 = (f32[640]{0:T(1024)S(1)}, f32[640]{0:T(1024)}, u32[]{:S(2)}) copy-start(f32[640]{0:T(1024)} %param.12) | copy-start | bytes 7684
  135.5 0.7 collective-permute-start.2
  136.2 0.7 collective-permute-start.3
  137.0 0.7 collective-permute-start.4
  137.7 0.7 collective-permute-start.5
  138.5 44.6 %collective-permute-start.6 = (bf16[128,1280]{1,0:T(8,128)(2,1)S(1)}, bf16[128,1280]{1,0:T(8,128)(2,1)S(1)}, u32[]{:S(2)}, u32[]{:S(2)}) collective-permute-start(bf16[128,1280]{1,0:T(8,128)(2,1)S(1)} %broadcast_select_fusion.3), channel_id=1, source_target_pairs={{0,16},{32,48},{64,80},{96,112},{128,144},{160,176},{192,208},{224... | collective-permute-start | bytes 983048 | tf_op jit(solution)/shard_map/ppermute | solution.py:32
  139.3 46.1 %collective-permute-start.10 = (bf16[128,640]{1,0:T(8,128)(2,1)S(1)}, bf16[128,640]{1,0:T(8,128)(2,1)S(1)}, u32[]{:S(2)}, u32[]{:S(2)}) collective-permute-start(bf16[128,640]{1,0:T(8,128)(2,1)S(1)} %slice.128), channel_id=1, source_target_pairs={{0,4},{4,8},{8,12},{12,16},{16,20},{20,24},{24,28},{28,32},{32,36}... | collective-permute-start | bytes 491528 | tf_op jit(solution)/shard_map/ppermute | solution.py:41
  183.1 18.5 %collective-permute-start.7 = (bf16[128,1280]{1,0:T(8,128)(2,1)S(1)}, bf16[128,1280]{1,0:T(8,128)(2,1)S(1)}, u32[]{:S(2)}, u32[]{:S(2)}) collective-permute-start(bf16[128,1280]{1,0:T(8,128)(2,1)S(1)} %broadcast_select_fusion.4), channel_id=1, source_target_pairs={{0,8},{16,24},{32,40},{48,56},{64,72},{80,88},{96,104},{112,120},{... | collective-permute-start | bytes 983048 | tf_op jit(solution)/shard_map/ppermute | solution.py:32
  185.4 17.7 %collective-permute-start.9 = (bf16[128,640]{1,0:T(8,128)(2,1)S(1)}, bf16[128,640]{1,0:T(8,128)(2,1)S(1)}, u32[]{:S(2)}, u32[]{:S(2)}) collective-permute-start(bf16[128,640]{1,0:T(8,128)(2,1)S(1)} %get-tuple-element.61), channel_id=1, source_target_pairs={{0,4},{4,8},{8,12},{12,16},{16,20},{20,24},{24,28},{28,32},{32,36}... | collective-permute-start | bytes 491528 | tf_op jit(solution)/shard_map/ppermute | solution.py:41
  201.7 11.1 %collective-permute-start.8 = (bf16[128,1280]{1,0:T(8,128)(2,1)S(1)}, bf16[128,1280]{1,0:T(8,128)(2,1)S(1)}, u32[]{:S(2)}, u32[]{:S(2)}) collective-permute-start(bf16[128,1280]{1,0:T(8,128)(2,1)S(1)} %broadcast_select_fusion.5), channel_id=1, source_target_pairs={{0,4},{8,12},{16,20},{24,28},{32,36},{40,44},{48,52},{56,60},{64,6... | collective-permute-start | bytes 983048 | tf_op jit(solution)/shard_map/ppermute | solution.py:32
Sparse Core Ops, SparseCore 0:
  9.5 80.7 all-gather.6
  92.3 40.7 all-gather.8

commit v2 on v0

v2 whole, which is shorter than its diff:
```python
import functools
import jax
import jax.numpy as jnp
from jax import lax
from jax.experimental import pallas as pl
from jax.experimental.pallas import tpu as pltpu
from jax.sharding import PartitionSpec as P

HEADS = 8
GROUPS = 32
EPS = 1e-05
BOTH = ("tm", "rows")
VMEM = pl.BlockSpec(memory_space=pltpu.VMEM)
SMEM = pl.BlockSpec(memory_space=pltpu.SMEM)


def tree_levels(devices):
    if devices == 128:
        z = [("z", s) for s in (8, 4, 2, 1)]
        x = [("x", s) for s in (2, 1)]
        y = [("y", 1)]
        size = {"y": 2, "z": 16, "x": 4}
        orders = (z + x + y, x + y + z)

        def index(at, sign):
            return (at["y"] * 16 + (sign * at["z"]) % 16) * 4 + at["x"]

    else:
        steps = []
        while 2 ** len(steps) < devices:
            steps.insert(0, ("z", 2 ** len(steps)))
        size = {"z": devices}
        orders = (steps, steps)

        def index(at, sign):
            return at["z"]

    levels = [[] for _ in orders[0]]
    for core, order in enumerate(orders):
        sign = 1 - 2 * core
        known = [{axis: 0 for axis in size}]
        for level, (axis, step) in enumerate(order):
            fresh = []
            for at in known:
                to = dict(at)
                to[axis] = at[axis] + step
                fresh.append(to)
                for chip in range(2):
                    row = chip * 2 + core
                    levels[level].append((index(at, sign) * 4 + row, index(to, sign) * 4 + row))
            known = known + fresh
    return levels


def to_rows(x, flip):
    return lax.ppermute(x, "rows", [(i, i ^ flip) for i in range(4)])


def gathered(x):
    core = to_rows(x, 1)
    chip = to_rows(x, 2)
    return x, core, chip, to_rows(chip, 1)


def conv_kernel(width, me_ref, b0, b1, b2, b3, gain, weight, pool, keep, send, x_ref, taps, acc):
    me = me_ref[0]
    blocks = (b0, b1, b2, b3)
    cells, chans = x_ref.shape
    part = cells // 4
    for flip, block in enumerate(blocks):
        at = pl.multiple_of((me ^ flip) * part, part)
        x_ref[pl.ds(at, part), :] = block[...].astype(jnp.float32)
    values = x_ref[...]

    def group_mean(column):
        wide = jnp.broadcast_to(column, (8, chans))
        out = jnp.dot(
            wide, pool[...], precision=lax.Precision.HIGHEST, preferred_element_type=jnp.float32
        )
        return out[:1]

    scale = 1.0 / (cells * (640 // GROUPS))
    mean = group_mean(jnp.sum(values, axis=0, keepdims=True)) * scale
    centred = values - mean
    spread = group_mean(jnp.sum(centred * centred, axis=0, keepdims=True)) * scale
    normed = centred * (lax.rsqrt(spread + EPS) * gain[...])
    act = normed / (1.0 + jnp.exp(-normed))
    act = act.astype(jnp.bfloat16).astype(jnp.float32)
    column = lax.broadcasted_iota(jnp.int32, (cells, 1), 0) & (width - 1)
    before = jnp.where(column == 0, 0.0, pltpu.roll(act, 1, 0))
    after = jnp.where(column == width - 1, 0.0, pltpu.roll(act, cells - 1, 0))
    taps[:width, :] = jnp.zeros((width, taps.shape[1]), jnp.bfloat16)
    taps[width + cells :, :] = jnp.zeros((width, taps.shape[1]), jnp.bfloat16)
    taps[width : width + cells, :] = jnp.concatenate([before, act, after], axis=1).astype(
        jnp.bfloat16
    )
    acc[...] = sum(
        jnp.dot(
            taps[row * width : row * width + cells, :],
            weight[row],
            preferred_element_type=jnp.float32,
        )
        for row in range(3)
    )
    for flip in range(4):
        at = pl.multiple_of((me ^ flip) * part, part)
        out = acc[pl.ds(at, part), :]
        if flip % 2 == 0:
            keep[flip // 2] = out
        else:
            send[flip // 2] = out.astype(jnp.bfloat16)


def norm_kernel(lat, kept, core, chip, bias, gain, residual, feats):
    conv = kept[0] + core[0].astype(jnp.float32) + chip[...].astype(jnp.float32)
    res = (lat[...].astype(jnp.float32) + conv + bias[...]).astype(jnp.bfloat16)
    residual[...] = res
    rfloat = res.astype(jnp.float32)
    dev = rfloat - jnp.mean(rfloat, axis=1, keepdims=True)
    var = jnp.mean(dev * dev, axis=1, keepdims=True)
    feats[...] = (dev * lax.rsqrt(var + EPS) * gain[...]).astype(jnp.bfloat16)


def head_window(head, head_dim, chans):
    low = head * head_dim // 128 * 128
    high = min(-(-(head + 1) * head_dim // 128) * 128, chans)
    lane = low + lax.broadcasted_iota(jnp.int32, (1, high - low), 1)
    inside = (lane >= head * head_dim) & (lane < (head + 1) * head_dim)
    return slice(low, high), inside


def project(blocks, weight, joined, keys, vals):
    part, chans = blocks[0].shape
    for at, block in enumerate(blocks):
        joined[at * part : (at + 1) * part, :] = block[...]
    for out, first in ((keys, chans), (vals, 2 * chans)):
        out[...] = jnp.dot(
            joined[...], weight[:, first : first + chans], preferred_element_type=jnp.float32
        ).astype(jnp.bfloat16)


def scores_of(query, keys, head, window, inside):
    q_head = jnp.where(inside, query[:, window], 0)
    return lax.dot_general(
        q_head,
        keys[:, window],
        (((1,), (1,)), ((), ())),
        preferred_element_type=jnp.float32,
    )


def prev_kernel(own, p0, p1, p2, p3, weight, query, top, den, acc, joined, keys, vals):
    part, chans = own.shape
    head_dim = chans // HEADS
    scale = head_dim ** (-0.5)
    query[...] = jnp.dot(
        own[...], weight[:, :chans], preferred_element_type=jnp.float32
    ).astype(jnp.bfloat16)
    project((p0, p1, p2, p3), weight, joined, keys, vals)
    acc[...] = jnp.zeros_like(acc)
    for head in range(HEADS):
        window, inside = head_window(head, head_dim, chans)
        s = scores_of(query, keys, head, window, inside)
        peak = jnp.max(s, axis=1, keepdims=True)
        w = jnp.exp((s - peak) * scale)
        top[:, head : head + 1] = peak
        den[:, head : head + 1] = jnp.sum(w, axis=1, keepdims=True)
        out = jnp.dot(
            w.astype(jnp.bfloat16), vals[:, window], preferred_element_type=jnp.float32
        )
        acc[:, window] = jnp.where(inside, out, acc[:, window])


def anchor_kernel(
    query, a0, a1, a2, a3, weight, top, den, acc, residual, restyled, joined, keys, vals, mixed
):
    part, chans = query.shape
    head_dim = chans // HEADS
    scale = head_dim ** (-0.5)
    project((a0, a1, a2, a3), weight, joined, keys, vals)
    for head in range(HEADS):
        window, inside = head_window(head, head_dim, chans)
        s = scores_of(query, keys, head, window, inside)
        old = top[:, head : head + 1]
        peak = jnp.maximum(old, jnp.max(s, axis=1, keepdims=True))
        factor = jnp.exp((old - peak) * scale)
        w = jnp.exp((s - peak) * scale)
        total = den[:, head : head + 1] * factor + jnp.sum(w, axis=1, keepdims=True)
        out = jnp.dot(
            w.astype(jnp.bfloat16), vals[:, window], preferred_element_type=jnp.float32
        )
        out = (acc[:, window] * factor + out) / total
        mixed[:, window] = jnp.where(inside, out, mixed[:, window])
    restyled[...] = (residual[...].astype(jnp.float32) + mixed[...]).astype(jnp.bfloat16)


def call(kernel, outs, ins, scratch=(), flops=0, limit=24):
    moved = sum(a.size * a.dtype.itemsize for a in ins) + sum(
        o.size * o.dtype.itemsize for o in outs
    )
    specs = [SMEM if a.dtype == jnp.int32 else VMEM for a in ins]
    return pl.pallas_call(
        kernel,
        out_shape=list(outs),
        in_specs=specs,
        out_specs=[VMEM] * len(outs),
        scratch_shapes=list(scratch),
        compiler_params=pltpu.CompilerParams(vmem_limit_bytes=limit * 2**20),
        cost_estimate=pl.CostEstimate(flops=flops, bytes_accessed=moved, transcendentals=0),
    )(*ins)


def on_device(latents, gn_gain, conv_weight, conv_bias, ln_gain, qkv_weight):
    _, rows_dev, width, chans = latents.shape
    part = rows_dev * width
    cells = 4 * part
    share = chans // 4
    me = lax.axis_index("rows")
    first = lax.axis_index("tm") == 0
    shape = jax.ShapeDtypeStruct
    bf16, f32 = jnp.bfloat16, jnp.float32
    lat = latents.reshape(part, chans)

    qkv = lax.all_gather(qkv_weight, "rows", axis=0, tiled=True)

    split = lat.reshape(part, 4, share).transpose(1, 0, 2)
    pieces = [lax.dynamic_index_in_dim(split, me ^ flip, 0, keepdims=False) for flip in range(4)]
    blocks = [pieces[0]] + [to_rows(pieces[flip], flip) for flip in (1, 2, 3)]
    gain = lax.dynamic_slice_in_dim(gn_gain, me * share, share).reshape(1, share)
    group = jnp.arange(share) // (chans // GROUPS)
    pool = (group[:, None] == group[None, :]).astype(f32)
    keep, send = call(
        functools.partial(conv_kernel, width),
        [shape((2, part, chans), f32), shape((2, part, chans), bf16)],
        [me.reshape(1), *blocks, gain, conv_weight.reshape(3, 3 * share, chans), pool],
        [
            pltpu.VMEM((cells, share), f32),
            pltpu.VMEM((cells + 2 * width, 3 * share), bf16),
            pltpu.VMEM((cells, chans), f32),
        ],
        flops=2 * cells * 9 * share * chans,
    )
    core = to_rows(send, 1)
    chip = to_rows((keep[1] + core[1].astype(f32)).astype(bf16), 2)
    residual, feats = call(
        norm_kernel,
        [shape((part, chans), bf16)] * 2,
        [lat, keep, core, chip, conv_bias.reshape(1, chans), ln_gain.reshape(1, chans)],
    )

    devices = lax.axis_size("tm")
    prev = lax.ppermute(feats, "tm", [(i, i + 1) for i in range(devices - 1)])
    prev = gathered(jnp.where(first, feats, prev))
    anchor = jnp.where(first, feats, jnp.zeros_like(feats))
    for route in tree_levels(devices):
        anchor = anchor + lax.ppermute(anchor, BOTH, route)
    anchor = gathered(anchor)

    scratch = [
        pltpu.VMEM((cells, chans), bf16),
        pltpu.VMEM((cells, chans), bf16),
        pltpu.VMEM((cells, chans), bf16),
    ]
    flops = 2 * cells * chans * 2 * chans + 4 * part * cells * chans
    query, top, den, acc = call(
        prev_kernel,
        [
            shape((part, chans), bf16),
            shape((part, HEADS), f32),
            shape((part, HEADS), f32),
            shape((part, chans), f32),
        ],
        [feats, *prev, qkv],
        scratch,
        flops=flops,
    )
    (restyled,) = call(
        anchor_kernel,
        [shape((part, chans), bf16)],
        [query, *anchor, qkv, top, den, acc, residual],
        scratch + [pltpu.VMEM((part, chans), f32)],
        flops=flops,
    )
    return restyled.reshape(1, rows_dev, width, chans)


def solution(mesh):
    return jax.shard_map(
        on_device,
        mesh=mesh,
        in_specs=(
            P("tm", "rows", None, None),
            P(),
            P(None, "rows", None),
            P(),
            P(),
            P("rows", None),
        ),
        out_specs=P("tm", "rows", None, None),
        check_vma=False,
    )
```

time: 1430 us -> 131 us (0.09)
  the two profiles are of different devices: /device:TPU:1 before, /device:TPU:511 now
where the time goes in v2:
time: 131 us
  starting transfers between devices  67.9 us (52%)
  waiting for transfers between devices  33.3 us (25%)
  between operations  13.9 us (11%)
  Pallas kernels  11 us (8%)
  local copies, waits for them, and re-layouts  4.19 us (3%)
    ppermute x11, starting transfers between devices, to_rows(): return lax.ppermute(x, 'rows', [(i, i ^ flip) for i in range(4)])  61.3 us
    ppermute x7, waiting for transfers between devices, on_device(): anchor = anchor + lax.ppermute(anchor, BOTH, route)  15.7 us
    ppermute x11, waiting for transfers between devices, to_rows(): return lax.ppermute(x, 'rows', [(i, i ^ flip) for i in range(4)])  11.6 us
    pallas_call x4, Pallas kernels, call(): pl.pallas_call(kernel, out_shape=list(outs), in_specs=specs, out_specs=[V...  11 us
    ppermute x7, starting transfers between devices, on_device(): anchor = anchor + lax.ppermute(anchor, BOTH, route)  5.32 us
    ppermute x1, waiting for transfers between devices, on_device(): prev = lax.ppermute(feats, 'tm', [(i, i + 1) for i in range(devices - 1)])  5.27 us
  transfers between devices with their start and end apart: 20, of which 5 were waited for; matrix products, arithmetic and copies ran while one was open for 2% of the time, Pallas kernels for 5%

profile of v2, /device:TPU:511, one launch (start us, length us, event | category | flops | bytes accessed | tf_op | source)
XLA Modules:
  0.0 130.8 jit_solution(2453256118390055066)
XLA Ops:
  6.5 0.0 copy-start.3
  6.5 0.0 all-gather.2.cloned.1.call-start
  6.5 0.7 all-gather.2.cloned.1.call-update
  7.3 1.1 reshape_reshape.3
  8.4 0.5 constant_dynamic-slice_fusion
  9.0 2.6 %collective-permute-start = (bf16[128,160]{1,0:T(8,128)(2,1)S(1)}, bf16[128,160]{1,0:T(8,128)(2,1)S(1)}, u32[]{:S(2)}, u32[]{:S(2)}) collective-permute-start(bf16[128,160]{1,0:T(8,128)(2,1)S(1)} %bitcast.29), channel_id=1, source_target_pairs={{0,1},{1,0},{2,3},{3,2},{4,5},{5,4},{6,7},{7,6},{8,9},{9,8},{10,11... | collective-permute-start | bytes 122888 | tf_op jit(solution)/shard_map/ppermute | solution.py:56
  11.6 0.0 copy-start.4
  11.6 0.0 copy-start.5
  11.6 0.0 copy-start.2
  11.6 2.5 %collective-permute-start.1 = (bf16[128,160]{1,0:T(8,128)(2,1)S(1)}, bf16[128,160]{1,0:T(8,128)(2,1)S(1)}, u32[]{:S(2)}, u32[]{:S(2)}) collective-permute-start(bf16[128,160]{1,0:T(8,128)(2,1)S(1)} %bitcast.30), channel_id=1, source_target_pairs={{0,2},{1,3},{2,0},{3,1},{4,6},{5,7},{6,4},{7,5},{8,10},{9,11},{10,... | collective-permute-start | bytes 122888 | tf_op jit(solution)/shard_map/ppermute | solution.py:56
  14.2 3.1 %collective-permute-start.2 = (bf16[128,160]{1,0:T(8,128)(2,1)S(1)}, bf16[128,160]{1,0:T(8,128)(2,1)S(1)}, u32[]{:S(2)}, u32[]{:S(2)}) collective-permute-start(bf16[128,160]{1,0:T(8,128)(2,1)S(1)} %bitcast.31), channel_id=1, source_target_pairs={{0,3},{1,2},{2,1},{3,0},{4,7},{5,6},{6,5},{7,4},{8,11},{9,10},{10,... | collective-permute-start | bytes 122888 | tf_op jit(solution)/shard_map/ppermute | solution.py:56
  17.3 0.1 compare_convert_fusion.pool
  17.4 0.8 dynamic_slice.8
  18.2 0.0 collective-permute-done.b1
  18.2 0.0 collective-permute-done.1.b2
  18.2 1.9 %collective-permute-done.2.b3 = bf16[128,160]{1,0:T(8,128)(2,1)S(1)} collective-permute-done((bf16[128,160]{1,0:T(8,128)(2,1)S(1)}, bf16[128,160]{1,0:T(8,128)(2,1)S(1)}, u32[]{:S(2)}, u32[]{:S(2)}) %collective-permute-start.2) | collective-permute-done | bytes 40992 | tf_op jit(solution)/shard_map/ppermute | solution.py:56
  20.1 0.0 copy-done.3
  20.1 2.4 %shard_map.64 = (f32[2,128,640]{2,1,0:T(8,128)S(1)}, bf16[2,128,640]{2,1,0:T(8,128)(2,1)S(1)}) custom-call(s32[1]{0:T(128)} %bitcast.1.me_ref, bf16[128,160]{1,0:T(8,128)(2,1)S(1)} %bitcast.26, bf16[128,160]{1,0:T(8,128)(2,1)S(1)} %collective-permute-done.b1, bf16[128,160]{1,0:T(8,128)(2,1)S(1)} %collective-permute-done.1.b2, ...), custom_call_target="tpu_custom_call" | custom-call | flops 943718400 | bytes 3093124 | tf_op jit(solution)/shard_map/pallas_call | solution.py:202
  22.4 2.3 %collective-permute-start.3 = (bf16[2,128,640]{2,1,0:T(8,128)(2,1)S(1)}, bf16[2,128,640]{2,1,0:T(8,128)(2,1)S(1)}, u32[]{:S(2)}, u32[]{:S(2)}) collective-permute-start(bf16[2,128,640]{2,1,0:T(8,128)(2,1)S(1)} %get-tuple-element.14), channel_id=1, source_target_pairs={{0,1},{1,0},{2,3},{3,2},{4,5},{5,4},{6,7},{7,6},{8,9},{9,8},{10,11... | collective-permute-start | bytes 983048 | tf_op jit(solution)/shard_map/ppermute | solution.py:56
  24.7 1.2 collective-permute-done.3.core
  26.0 2.9 %collective-permute-start.4 = (bf16[128,640]{1,0:T(8,128)(2,1)S(1)}, bf16[128,640]{1,0:T(8,128)(2,1)S(1)}, u32[]{:S(2)}, u32[]{:S(2)}) collective-permute-start(bf16[128,640]{1,0:T(8,128)(2,1)S(1)} %fusion), channel_id=1, source_target_pairs={{0,2},{1,3},{2,0},{3,1},{4,6},{5,7},{6,4},{7,5},{8,10},{9,11},{10,... | collective-permute-start | bytes 491528 | tf_op jit(solution)/shard_map/ppermute | solution.py:56
  28.9 0.0 copy-done.4
  28.9 0.0 copy-done.5
  29.0 8.5 %collective-permute-done.4.chip = bf16[128,640]{1,0:T(8,128)(2,1)S(1)} collective-permute-done((bf16[128,640]{1,0:T(8,128)(2,1)S(1)}, bf16[128,640]{1,0:T(8,128)(2,1)S(1)}, u32[]{:S(2)}, u32[]{:S(2)}) %collective-permute-start.4) | collective-permute-done | bytes 163872 | tf_op jit(solution)/shard_map/ppermute | solution.py:56
  37.4 0.0 copy-done.2
  37.4 0.3 shard_map.65
  37.7 1.3 collective-permute-start.5
  39.0 5.3 %collective-permute-done.5 = bf16[128,640]{1,0:T(8,128)(2,1)S(1)} collective-permute-done((bf16[128,640]{1,0:T(8,128)(2,1)S(1)}, bf16[128,640]{1,0:T(8,128)(2,1)S(1)}, u32[]{:S(2)}, u32[]{:S(2)}) %collective-permute-start.5) | collective-permute-done | bytes 163872 | tf_op jit(solution)/shard_map/ppermute | solution.py:252
  44.3 0.7 collective-permute-start.9
  45.0 0.0 collective-permute-done.9
  45.1 0.7 collective-permute-start.10
  45.7 0.0 collective-permute-done.10
  45.8 0.7 collective-permute-start.11
  46.5 0.0 collective-permute-done.11
  46.5 0.7 collective-permute-start.12
  47.2 0.0 collective-permute-done.12
  47.3 0.7 collective-permute-start.13
  48.0 0.0 collective-permute-done.13
  48.0 0.7 collective-permute-start.14
  48.7 0.0 collective-permute-done.14
  48.8 1.3 collective-permute-start.15
  50.1 2.9 %collective-permute-start.7 = (bf16[128,640]{1,0:T(8,128)(2,1)S(1)}, bf16[128,640]{1,0:T(8,128)(2,1)S(1)}, u32[]{:S(2)}, u32[]{:S(2)}) collective-permute-start(bf16[128,640]{1,0:T(8,128)(2,1)S(1)} %get-tuple-element.26.p0), channel_id=1, source_target_pairs={{0,2},{1,3},{2,0},{3,1},{4,6},{5,7},{6,4},{7,5},{8,10},{9,11},{10,... | collective-permute-start | bytes 491528 | tf_op jit(solution)/shard_map/ppermute | solution.py:56
  53.0 15.7 %collective-permute-done.15 = bf16[128,640]{1,0:T(8,128)(2,1)S(1)} collective-permute-done((bf16[128,640]{1,0:T(8,128)(2,1)S(1)}, bf16[128,640]{1,0:T(8,128)(2,1)S(1)}, u32[]{:S(2)}, u32[]{:S(2)}) %collective-permute-start.15) | collective-permute-done | bytes 163872 | tf_op jit(solution)/shard_map/ppermute | solution.py:256
  68.7 2.9 %collective-permute-start.17 = (bf16[128,640]{1,0:T(8,128)(2,1)S(1)}, bf16[128,640]{1,0:T(8,128)(2,1)S(1)}, u32[]{:S(2)}, u32[]{:S(2)}) collective-permute-start(bf16[128,640]{1,0:T(8,128)(2,1)S(1)} %add.62.a0), channel_id=1, source_target_pairs={{0,2},{1,3},{2,0},{3,1},{4,6},{5,7},{6,4},{7,5},{8,10},{9,11},{10,... | collective-permute-start | bytes 491528 | tf_op jit(solution)/shard_map/ppermute | solution.py:56
  71.6 35.9 %collective-permute-start.6 = (bf16[128,640]{1,0:T(8,128)(2,1)S(1)}, bf16[128,640]{1,0:T(8,128)(2,1)S(1)}, u32[]{:S(2)}, u32[]{:S(2)}) collective-permute-start(bf16[128,640]{1,0:T(8,128)(2,1)S(1)} %get-tuple-element.26.p0), channel_id=1, source_target_pairs={{0,1},{1,0},{2,3},{3,2},{4,5},{5,4},{6,7},{7,6},{8,9},{9,8},{10,11... | collective-permute-start | bytes 491528 | tf_op jit(solution)/shard_map/ppermute | solution.py:56
  107.5 0.0 collective-permute-done.7.p2
  107.5 1.9 %collective-permute-start.8 = (bf16[128,640]{1,0:T(8,128)(2,1)S(1)}, bf16[128,640]{1,0:T(8,128)(2,1)S(1)}, u32[]{:S(2)}, u32[]{:S(2)}) collective-permute-start(bf16[128,640]{1,0:T(8,128)(2,1)S(1)} %collective-permute-done.7.p2), channel_id=1, source_target_pairs={{0,1},{1,0},{2,3},{3,2},{4,5},{5,4},{6,7},{7,6},{8,9},{9,8},{10,11... | collective-permute-start | bytes 491528 | tf_op jit(solution)/shard_map/ppermute | solution.py:56
  109.4 2.4 %collective-permute-start.16 = (bf16[128,640]{1,0:T(8,128)(2,1)S(1)}, bf16[128,640]{1,0:T(8,128)(2,1)S(1)}, u32[]{:S(2)}, u32[]{:S(2)}) collective-permute-start(bf16[128,640]{1,0:T(8,128)(2,1)S(1)} %add.62.a0), channel_id=1, source_target_pairs={{0,1},{1,0},{2,3},{3,2},{4,5},{5,4},{6,7},{7,6},{8,9},{9,8},{10,11... | collective-permute-start | bytes 491528 | tf_op jit(solution)/shard_map/ppermute | solution.py:56
  111.9 0.0 collective-permute-done.17.a2
  111.9 1.9 %collective-permute-start.18 = (bf16[128,640]{1,0:T(8,128)(2,1)S(1)}, bf16[128,640]{1,0:T(8,128)(2,1)S(1)}, u32[]{:S(2)}, u32[]{:S(2)}) collective-permute-start(bf16[128,640]{1,0:T(8,128)(2,1)S(1)} %collective-permute-done.17.a2), channel_id=1, source_target_pairs={{0,1},{1,0},{2,3},{3,2},{4,5},{5,4},{6,7},{7,6},{8,9},{9,8},{10,11... | collective-permute-start | bytes 491528 | tf_op jit(solution)/shard_map/ppermute | solution.py:56
  113.8 0.0 collective-permute-done.6.p1
  113.8 0.0 collective-permute-done.8.p3
  113.8 0.0 all-gather.2.cloned.1.call-done.weight
  113.9 0.0 copy-start
  113.9 1.7 %copy-done = bf16[640,1920]{1,0:T(8,128)(2,1)S(1)} copy-done((bf16[640,1920]{1,0:T(8,128)(2,1)S(1)}, bf16[640,1920]{1,0:T(8,128)(2,1)}, u32[]{:S(2)}) %copy-start) | copy-done | bytes 2457624
  115.5 0.0 copy-start.1
  115.5 3.4 %shard_map.66 = (bf16[128,640]{1,0:T(8,128)(2,1)S(1)}, f32[128,8]{1,0:T(8,128)S(1)}, f32[128,8]{1,0:T(8,128)S(1)}, f32[128,640]{1,0:T(8,128)S(1)}) custom-call(bf16[128,640]{1,0:T(8,128)(2,1)S(1)} %get-tuple-element.15.own, bf16[128,640]{1,0:T(8,128)(2,1)S(1)} %get-tuple-element.26.p0, bf16[128,640]{1,0:T(8,128)(2,1)S(1)} %collective-permute-done.6.p1, ...), custom_call_target="tpu_custom_call" | custom-call | flops 1006632960 | bytes 3776512 | tf_op jit(solution)/shard_map/pallas_call | solution.py:202
  118.9 0.0 collective-permute-done.16.a1
  118.9 0.0 collective-permute-done.18.a3
  119.0 0.0 copy-done.1
  119.0 5.0 %shard_map.67 = bf16[128,640]{1,0:T(8,128)(2,1)} custom-call(bf16[128,640]{1,0:T(8,128)(2,1)S(1)} %get-tuple-element.16.query, bf16[128,640]{1,0:T(8,128)(2,1)S(1)} %add.62.a0, bf16[128,640]{1,0:T(8,128)(2,1)S(1)} %collective-permute-done.16.a1, bf16[128,640]{1,0:T(8,128)(2,1)S(1)} %collective-permute-done.17.a2, ...), custom_call_target="tpu_custom_call" | custom-call | flops 1006632960 | bytes 3940352 | tf_op jit(solution)/shard_map/pallas_call | solution.py:202
  (16 shorter events, 0.4 us)
Async XLA Ops:
  6.5 13.5 %copy-start.3 = (bf16[9,160,640]{2,1,0:T(8,128)(2,1)S(1)}, bf16[9,160,640]{2,1,0:T(8,128)(2,1)}, u32[]{:S(2)}) copy-start(bf16[9,160,640]{2,1,0:T(8,128)(2,1)} %param.8) | copy-start | bytes 5529604
  6.5 107.3 %all-gather.2.cloned.1.call-start = ((), (), s32[]{:S(2)}) async-start(), calls=%async_computation | async-start | bytes 3072000 | tf_op jit(solution)/shard_map/all_gather | solution.py:224
  9.0 9.2 %collective-permute-start = (bf16[128,160]{1,0:T(8,128)(2,1)S(1)}, bf16[128,160]{1,0:T(8,128)(2,1)S(1)}, u32[]{:S(2)}, u32[]{:S(2)}) collective-permute-start(bf16[128,160]{1,0:T(8,128)(2,1)S(1)} %bitcast.29), channel_id=1, source_target_pairs={{0,1},{1,0},{2,3},{3,2},{4,5},{5,4},{6,7},{7,6},{8,9},{9,8},{10,11... | collective-permute-start | bytes 122888 | tf_op jit(solution)/shard_map/ppermute | solution.py:56
  11.6 17.3 %copy-start.4 = (f32[640]{0:T(1024)S(1)}, f32[640]{0:T(1024)}, u32[]{:S(2)}) copy-start(f32[640]{0:T(1024)} %param.9) | copy-start | bytes 7684
  11.6 17.4 %copy-start.5 = (f32[640]{0:T(1024)S(1)}, f32[640]{0:T(1024)}, u32[]{:S(2)}) copy-start(f32[640]{0:T(1024)} %param.10) | copy-start | bytes 7684
  11.6 25.8 %copy-start.2 = (bf16[1,4,32,640]{3,2,1,0:T(8,128)(2,1)S(1)}, bf16[1,4,32,640]{3,2,1,0:T(8,128)(2,1)}, u32[]{:S(2)}) copy-start(bf16[1,4,32,640]{3,2,1,0:T(8,128)(2,1)} %param.6) | copy-start | bytes 491524
  11.6 6.5 %collective-permute-start.1 = (bf16[128,160]{1,0:T(8,128)(2,1)S(1)}, bf16[128,160]{1,0:T(8,128)(2,1)S(1)}, u32[]{:S(2)}, u32[]{:S(2)}) collective-permute-start(bf16[128,160]{1,0:T(8,128)(2,1)S(1)} %bitcast.30), channel_id=1, source_target_pairs={{0,2},{1,3},{2,0},{3,1},{4,6},{5,7},{6,4},{7,5},{8,10},{9,11},{10,... | collective-permute-start | bytes 122888 | tf_op jit(solution)/shard_map/ppermute | solution.py:56
  14.2 5.9 %collective-permute-start.2 = (bf16[128,160]{1,0:T(8,128)(2,1)S(1)}, bf16[128,160]{1,0:T(8,128)(2,1)S(1)}, u32[]{:S(2)}, u32[]{:S(2)}) collective-permute-start(bf16[128,160]{1,0:T(8,128)(2,1)S(1)} %bitcast.31), channel_id=1, source_target_pairs={{0,3},{1,2},{2,1},{3,0},{4,7},{5,6},{6,5},{7,4},{8,11},{9,10},{10,... | collective-permute-start | bytes 122888 | tf_op jit(solution)/shard_map/ppermute | solution.py:56
  22.4 3.5 %collective-permute-start.3 = (bf16[2,128,640]{2,1,0:T(8,128)(2,1)S(1)}, bf16[2,128,640]{2,1,0:T(8,128)(2,1)S(1)}, u32[]{:S(2)}, u32[]{:S(2)}) collective-permute-start(bf16[2,128,640]{2,1,0:T(8,128)(2,1)S(1)} %get-tuple-element.14), channel_id=1, source_target_pairs={{0,1},{1,0},{2,3},{3,2},{4,5},{5,4},{6,7},{7,6},{8,9},{9,8},{10,11... | collective-permute-start | bytes 983048 | tf_op jit(solution)/shard_map/ppermute | solution.py:56
  26.0 11.4 %collective-permute-start.4 = (bf16[128,640]{1,0:T(8,128)(2,1)S(1)}, bf16[128,640]{1,0:T(8,128)(2,1)S(1)}, u32[]{:S(2)}, u32[]{:S(2)}) collective-permute-start(bf16[128,640]{1,0:T(8,128)(2,1)S(1)} %fusion), channel_id=1, source_target_pairs={{0,2},{1,3},{2,0},{3,1},{4,6},{5,7},{6,4},{7,5},{8,10},{9,11},{10,... | collective-permute-start | bytes 491528 | tf_op jit(solution)/shard_map/ppermute | solution.py:56
  37.7 6.6 %collective-permute-start.5 = (bf16[128,640]{1,0:T(8,128)(2,1)S(1)}, bf16[128,640]{1,0:T(8,128)(2,1)S(1)}, u32[]{:S(2)}, u32[]{:S(2)}) collective-permute-start(bf16[128,640]{1,0:T(8,128)(2,1)S(1)} %get-tuple-element.15.own), channel_id=1, source_target_pairs={{0,4},{4,8},{8,12},{12,16},{16,20},{20,24},{24,28},{28,32},{32,36}... | collective-permute-start | bytes 491528 | tf_op jit(solution)/shard_map/ppermute | solution.py:252
  44.3 0.7 collective-permute-start.9
  45.1 0.7 collective-permute-start.10
  45.8 0.7 collective-permute-start.11
  46.5 0.7 collective-permute-start.12
  47.3 0.7 collective-permute-start.13
  48.0 0.7 collective-permute-start.14
  48.8 19.9 %collective-permute-start.15 = (bf16[128,640]{1,0:T(8,128)(2,1)S(1)}, bf16[128,640]{1,0:T(8,128)(2,1)S(1)}, u32[]{:S(2)}, u32[]{:S(2)}) collective-permute-start(bf16[128,640]{1,0:T(8,128)(2,1)S(1)} %add.61), channel_id=1, source_target_pairs={{0,256},{2,258},{128,384},{130,386},{64,320},{66,322},{192,448},{1... | collective-permute-start | bytes 491528 | tf_op jit(solution)/shard_map/ppermute | solution.py:256
  50.1 57.4 %collective-permute-start.7 = (bf16[128,640]{1,0:T(8,128)(2,1)S(1)}, bf16[128,640]{1,0:T(8,128)(2,1)S(1)}, u32[]{:S(2)}, u32[]{:S(2)}) collective-permute-start(bf16[128,640]{1,0:T(8,128)(2,1)S(1)} %get-tuple-element.26.p0), channel_id=1, source_target_pairs={{0,2},{1,3},{2,0},{3,1},{4,6},{5,7},{6,4},{7,5},{8,10},{9,11},{10,... | collective-permute-start | bytes 491528 | tf_op jit(solution)/shard_map/ppermute | solution.py:56
  68.7 43.2 %collective-permute-start.17 = (bf16[128,640]{1,0:T(8,128)(2,1)S(1)}, bf16[128,640]{1,0:T(8,128)(2,1)S(1)}, u32[]{:S(2)}, u32[]{:S(2)}) collective-permute-start(bf16[128,640]{1,0:T(8,128)(2,1)S(1)} %add.62.a0), channel_id=1, source_target_pairs={{0,2},{1,3},{2,0},{3,1},{4,6},{5,7},{6,4},{7,5},{8,10},{9,11},{10,... | collective-permute-start | bytes 491528 | tf_op jit(solution)/shard_map/ppermute | solution.py:56
  71.6 42.2 %collective-permute-start.6 = (bf16[128,640]{1,0:T(8,128)(2,1)S(1)}, bf16[128,640]{1,0:T(8,128)(2,1)S(1)}, u32[]{:S(2)}, u32[]{:S(2)}) collective-permute-start(bf16[128,640]{1,0:T(8,128)(2,1)S(1)} %get-tuple-element.26.p0), channel_id=1, source_target_pairs={{0,1},{1,0},{2,3},{3,2},{4,5},{5,4},{6,7},{7,6},{8,9},{9,8},{10,11... | collective-permute-start | bytes 491528 | tf_op jit(solution)/shard_map/ppermute | solution.py:56
  107.5 6.3 %collective-permute-start.8 = (bf16[128,640]{1,0:T(8,128)(2,1)S(1)}, bf16[128,640]{1,0:T(8,128)(2,1)S(1)}, u32[]{:S(2)}, u32[]{:S(2)}) collective-permute-start(bf16[128,640]{1,0:T(8,128)(2,1)S(1)} %collective-permute-done.7.p2), channel_id=1, source_target_pairs={{0,1},{1,0},{2,3},{3,2},{4,5},{5,4},{6,7},{7,6},{8,9},{9,8},{10,11... | collective-permute-start | bytes 491528 | tf_op jit(solution)/shard_map/ppermute | solution.py:56
  109.4 9.5 %collective-permute-start.16 = (bf16[128,640]{1,0:T(8,128)(2,1)S(1)}, bf16[128,640]{1,0:T(8,128)(2,1)S(1)}, u32[]{:S(2)}, u32[]{:S(2)}) collective-permute-start(bf16[128,640]{1,0:T(8,128)(2,1)S(1)} %add.62.a0), channel_id=1, source_target_pairs={{0,1},{1,0},{2,3},{3,2},{4,5},{5,4},{6,7},{7,6},{8,9},{9,8},{10,11... | collective-permute-start | bytes 491528 | tf_op jit(solution)/shard_map/ppermute | solution.py:56
  111.9 7.1 %collective-permute-start.18 = (bf16[128,640]{1,0:T(8,128)(2,1)S(1)}, bf16[128,640]{1,0:T(8,128)(2,1)S(1)}, u32[]{:S(2)}, u32[]{:S(2)}) collective-permute-start(bf16[128,640]{1,0:T(8,128)(2,1)S(1)} %collective-permute-done.17.a2), channel_id=1, source_target_pairs={{0,1},{1,0},{2,3},{3,2},{4,5},{5,4},{6,7},{7,6},{8,9},{9,8},{10,11... | collective-permute-start | bytes 491528 | tf_op jit(solution)/shard_map/ppermute | solution.py:56
  113.9 1.7 %copy-start = (bf16[640,1920]{1,0:T(8,128)(2,1)S(1)}, bf16[640,1920]{1,0:T(8,128)(2,1)}, u32[]{:S(2)}) copy-start(bf16[640,1920]{1,0:T(8,128)(2,1)} %all-gather.2.cloned.1.call-done.weight) | copy-start | bytes 7372804
  115.5 3.4 %copy-start.1 = (bf16[640,1920]{1,0:T(8,128)(2,1)S(1)}, bf16[640,1920]{1,0:T(8,128)(2,1)}, u32[]{:S(2)}) copy-start(bf16[640,1920]{1,0:T(8,128)(2,1)} %all-gather.2.cloned.1.call-done.weight) | copy-start | bytes 7372804
Sparse Core Ops, SparseCore 0:
  9.5 41.7 all-gather.1

commit v3 on v2

--- a/solution.py
+++ b/solution.py
@@ -56,20 +56,34 @@
     return lax.ppermute(x, "rows", [(i, i ^ flip) for i in range(4)])
 
 
+def after(x, *done):
+    return lax.optimization_barrier((x, *done))[0]
+
+
 def gathered(x):
     core = to_rows(x, 1)
     chip = to_rows(x, 2)
     return x, core, chip, to_rows(chip, 1)
 
 
-def conv_kernel(width, me_ref, b0, b1, b2, b3, gain, weight, pool, keep, send, x_ref, taps, acc):
+def split_kernel(share, me_ref, own, core, mine, away):
+    for out, want in ((mine, me_ref[0]), (away, me_ref[0] ^ 2)):
+        for block in range(4):
+
+            @pl.when(want == block)
+            def _():
+                for at, source in enumerate((own, core)):
+                    out[at] = source[:, block * share : (block + 1) * share]
+
+
+def conv_kernel(width, me_ref, mine, came, gain, weight, pool, keep, send, x_ref, taps, acc):
     me = me_ref[0]
-    blocks = (b0, b1, b2, b3)
+    blocks = (mine[0], mine[1], came[0], came[1])
     cells, chans = x_ref.shape
     part = cells // 4
     for flip, block in enumerate(blocks):
         at = pl.multiple_of((me ^ flip) * part, part)
-        x_ref[pl.ds(at, part), :] = block[...].astype(jnp.float32)
+        x_ref[pl.ds(at, part), :] = block.astype(jnp.float32)
     values = x_ref[...]
 
     def group_mean(column):
@@ -83,7 +97,7 @@
     mean = group_mean(jnp.sum(values, axis=0, keepdims=True)) * scale
     centred = values - mean
     spread = group_mean(jnp.sum(centred * centred, axis=0, keepdims=True)) * scale
-    normed = centred * (lax.rsqrt(spread + EPS) * gain[...])
+    normed = centred * (lax.rsqrt(spread + EPS) * gain[pl.ds(me, 1), :])
     act = normed / (1.0 + jnp.exp(-normed))
     act = act.astype(jnp.bfloat16).astype(jnp.float32)
     column = lax.broadcasted_iota(jnp.int32, (cells, 1), 0) & (width - 1)
@@ -149,8 +163,15 @@
     )
 
 
-def prev_kernel(own, p0, p1, p2, p3, weight, query, top, den, acc, joined, keys, vals):
+def prev_kernel(
+    me_ref, own, p0, p1, p2, p3, w0, w1, w2, w3, query, top, den, acc, weight, joined, keys, vals
+):
+    me = me_ref[0]
     part, chans = own.shape
+    share = w0.shape[0]
+    for flip, shard in enumerate((w0, w1, w2, w3)):
+        at = pl.multiple_of((me ^ flip) * share, share)
+        weight[pl.ds(at, share), :] = shard[...]
     head_dim = chans // HEADS
     scale = head_dim ** (-0.5)
     query[...] = jnp.dot(
@@ -221,18 +242,18 @@
     bf16, f32 = jnp.bfloat16, jnp.float32
     lat = latents.reshape(part, chans)
 
-    qkv = lax.all_gather(qkv_weight, "rows", axis=0, tiled=True)
-
-    split = lat.reshape(part, 4, share).transpose(1, 0, 2)
-    pieces = [lax.dynamic_index_in_dim(split, me ^ flip, 0, keepdims=False) for flip in range(4)]
-    blocks = [pieces[0]] + [to_rows(pieces[flip], flip) for flip in (1, 2, 3)]
-    gain = lax.dynamic_slice_in_dim(gn_gain, me * share, share).reshape(1, share)
+    mine, away = call(
+        functools.partial(split_kernel, share),
+        [shape((2, part, share), bf16)] * 2,
+        [me.reshape(1), lat, to_rows(lat, 1)],
+    )
+    came = to_rows(away, 2)
     group = jnp.arange(share) // (chans // GROUPS)
     pool = (group[:, None] == group[None, :]).astype(f32)
     keep, send = call(
         functools.partial(conv_kernel, width),
         [shape((2, part, chans), f32), shape((2, part, chans), bf16)],
-        [me.reshape(1), *blocks, gain, conv_weight.reshape(3, 3 * share, chans), pool],
+        [me.reshape(1), mine, came, gn_gain.reshape(4, share), conv_weight.reshape(3, 3 * share, chans), pool],
         [
             pltpu.VMEM((cells, share), f32),
             pltpu.VMEM((cells + 2 * width, 3 * share), bf16),
@@ -241,20 +262,40 @@
         flops=2 * cells * 9 * share * chans,
     )
     core = to_rows(send, 1)
-    chip = to_rows((keep[1] + core[1].astype(f32)).astype(bf16), 2)
+    half = (keep[1] + core[1].astype(f32)).astype(bf16)
+    chip = to_rows(half, 2)
+    devices = lax.axis_size("tm")
+    far = [
+        (tm * 4 + row, (tm + devices // 2) % devices * 4 + (row ^ 2))
+        for tm in range(devices)
+        for row in range(4)
+    ]
+    weight_chip = lax.ppermute(after(qkv_weight, half), BOTH, far)
     residual, feats = call(
         norm_kernel,
         [shape((part, chans), bf16)] * 2,
         [lat, keep, core, chip, conv_bias.reshape(1, chans), ln_gain.reshape(1, chans)],
     )
 
-    devices = lax.axis_size("tm")
-    prev = lax.ppermute(feats, "tm", [(i, i + 1) for i in range(devices - 1)])
-    prev = gathered(jnp.where(first, feats, prev))
-    anchor = jnp.where(first, feats, jnp.zeros_like(feats))
-    for route in tree_levels(devices):
-        anchor = anchor + lax.ppermute(anchor, BOTH, route)
-    anchor = gathered(anchor)
+    routes = tree_levels(devices)
+    tree = lambda level, x: x + lax.ppermute(x, BOTH, routes[level])
+    routes = routes + [[]] * (7 - len(routes))
+    anchor = tree(0, jnp.where(first, feats, jnp.zeros_like(feats)))
+    prev = lax.ppermute(after(feats, anchor), "tm", [(i, i + 1) for i in range(devices - 1)])
+    anchor = tree(1, anchor)
+    prev = jnp.where(first, feats, prev)
+    anchor = after(anchor, prev)
+    prev_core = to_rows(prev, 1)
+    prev_chip = to_rows(prev, 2)
+    anchor = after(tree(2, anchor), prev_core)
+    weight_core = to_rows(after(qkv_weight, anchor), 1)
+    anchor = after(tree(3, anchor), prev_chip, weight_core)
+    prev_last = to_rows(after(prev_chip, anchor), 1)
+    weight_last = to_rows(after(weight_chip, anchor), 1)
+    anchor = after(tree(4, anchor), prev_last)
+    anchor = after(tree(5, anchor), weight_last)
+    prev = (prev, prev_core, prev_chip, prev_last)
+    qkv = [qkv_weight, weight_core, weight_chip, weight_last]
 
     scratch = [
         pltpu.VMEM((cells, chans), bf16),
@@ -262,22 +303,24 @@
         pltpu.VMEM((cells, chans), bf16),
     ]
     flops = 2 * cells * chans * 2 * chans + 4 * part * cells * chans
-    query, top, den, acc = call(
+    query, top, den, acc, weight = call(
         prev_kernel,
         [
             shape((part, chans), bf16),
             shape((part, HEADS), f32),
             shape((part, HEADS), f32),
             shape((part, chans), f32),
+            shape((chans, 3 * chans), bf16),
         ],
-        [feats, *prev, qkv],
+        [me.reshape(1), after(feats, anchor), *prev, *qkv],
         scratch,
         flops=flops,
     )
+    anchor = gathered(after(tree(6, anchor), acc))
     (restyled,) = call(
         anchor_kernel,
         [shape((part, chans), bf16)],
-        [query, *anchor, qkv, top, den, acc, residual],
+        [query, *anchor, weight, top, den, acc, residual],
         scratch + [pltpu.VMEM((part, chans), f32)],
         flops=flops,
     )

time: 131 us -> 125 us (0.954)
  the two profiles are of different devices: /device:TPU:511 before, /device:TPU:1 now
where the time goes in v3:
time: 125 us
  starting transfers between devices  82.1 us (66%)
  waiting for transfers between devices  27 us (22%)
  Pallas kernels  11.5 us (9%)
  local copies, waits for them, and re-layouts  3.21 us (3%)
    ppermute x7, starting transfers between devices, on_device(): tree = lambda level, x: x + lax.ppermute(x, BOTH, routes[level])  39.4 us
    ppermute x12, starting transfers between devices, to_rows(): return lax.ppermute(x, 'rows', [(i, i ^ flip) for i in range(4)])  39.4 us
    ppermute x12, waiting for transfers between devices, to_rows(): return lax.ppermute(x, 'rows', [(i, i ^ flip) for i in range(4)])  20 us
    pallas_call x5, Pallas kernels, call(): pl.pallas_call(kernel, out_shape=list(outs), in_specs=specs, out_specs=[V...  11.5 us
    ppermute x7, waiting for transfers between devices, on_device(): tree = lambda level, x: x + lax.ppermute(x, BOTH, routes[level])  7.03 us
  transfers between devices with their start and end apart: 21, of which 13 were waited for; matrix products, arithmetic and copies ran while one was open for 1% of the time, Pallas kernels for 3%

profile of v3, /device:TPU:1, one launch (start us, length us, event | category | flops | bytes accessed | tf_op | source)
XLA Modules:
  0.0 124.6 jit_solution(2160241592974305778)
XLA Ops:
  0.0 0.0 copy-start.4
  0.0 0.0 copy-start.5
  0.0 8.9 %collective-permute-start = (bf16[128,640]{1,0:T(8,128)(2,1)}, bf16[128,640]{1,0:T(8,128)(2,1)S(1)}, u32[]{:S(2)}, u32[]{:S(2)}) collective-permute-start(bf16[128,640]{1,0:T(8,128)(2,1)} %bitcast.6), channel_id=1, source_target_pairs={{0,1},{1,0},{2,3},{3,2},{4,5},{5,4},{6,7},{7,6},{8,9},{9,8},{10,11... | collective-permute-start | bytes 491528 | tf_op jit(solution)/shard_map/ppermute | solution.py:56
  8.9 1.2 collective-permute-done.core
  10.1 0.0 copy-start
  10.1 0.9 copy-done
  11.1 0.0 copy-start.1
  11.1 0.2 shard_map.64
  11.3 1.9 %collective-permute-start.1 = (bf16[2,128,160]{2,1,0:T(8,128)(2,1)S(1)}, bf16[2,128,160]{2,1,0:T(8,128)(2,1)S(1)}, u32[]{:S(2)}, u32[]{:S(2)}) collective-permute-start(bf16[2,128,160]{2,1,0:T(8,128)(2,1)S(1)} %get-tuple-element.29), channel_id=1, source_target_pairs={{0,2},{1,3},{2,0},{3,1},{4,6},{5,7},{6,4},{7,5},{8,10},{9,11},{10,... | collective-permute-start | bytes 245768 | tf_op jit(solution)/shard_map/ppermute | solution.py:56
  13.2 0.1 compare_convert_fusion.pool
  13.3 0.8 reshape.54.gain
  14.1 3.9 %collective-permute-done.1.came = bf16[2,128,160]{2,1,0:T(8,128)(2,1)S(1)} collective-permute-done((bf16[2,128,160]{2,1,0:T(8,128)(2,1)S(1)}, bf16[2,128,160]{2,1,0:T(8,128)(2,1)S(1)}, u32[]{:S(2)}, u32[]{:S(2)}) %collective-permute-start.1) | collective-permute-done | bytes 81952 | tf_op jit(solution)/shard_map/ppermute | solution.py:56
  18.0 0.0 copy-start.2
  18.0 1.5 %copy-done.2 = bf16[9,160,640]{2,1,0:T(8,128)(2,1)S(1)} copy-done((bf16[9,160,640]{2,1,0:T(8,128)(2,1)S(1)}, bf16[9,160,640]{2,1,0:T(8,128)(2,1)}, u32[]{:S(2)}) %copy-start.2) | copy-done | bytes 1843224
  19.5 2.4 %shard_map.65 = (f32[2,128,640]{2,1,0:T(8,128)S(1)}, bf16[2,128,640]{2,1,0:T(8,128)(2,1)S(1)}) custom-call(s32[1]{0:T(128)} %bitcast.me_ref, bf16[2,128,160]{2,1,0:T(8,128)(2,1)S(1)} %get-tuple-element.28.mine, bf16[2,128,160]{2,1,0:T(8,128)(2,1)S(1)} %collective-permute-done.1.came, f32[4,160]{1,0:T(4,128)S(1)} %reshape.54.gain, ...), custom_call_target="tpu_custom_call" | custom-call | flops 943718400 | bytes 3095044 | tf_op jit(solution)/shard_map/pallas_call | solution.py:223
  21.9 0.0 copy-start.3
  21.9 3.1 %collective-permute-start.2 = (bf16[2,128,640]{2,1,0:T(8,128)(2,1)S(1)}, bf16[2,128,640]{2,1,0:T(8,128)(2,1)S(1)}, u32[]{:S(2)}, u32[]{:S(2)}) collective-permute-start(bf16[2,128,640]{2,1,0:T(8,128)(2,1)S(1)} %get-tuple-element.31), channel_id=1, source_target_pairs={{0,1},{1,0},{2,3},{3,2},{4,5},{5,4},{6,7},{7,6},{8,9},{9,8},{10,11... | collective-permute-start | bytes 983048 | tf_op jit(solution)/shard_map/ppermute | solution.py:56
  25.1 1.2 collective-permute-done.2.core
  26.3 1.9 %collective-permute-start.3 = (bf16[128,640]{1,0:T(8,128)(2,1)S(1)}, bf16[128,640]{1,0:T(8,128)(2,1)S(1)}, u32[]{:S(2)}, u32[]{:S(2)}) collective-permute-start(bf16[128,640]{1,0:T(8,128)(2,1)S(1)} %fusion), channel_id=1, source_target_pairs={{0,2},{1,3},{2,0},{3,1},{4,6},{5,7},{6,4},{7,5},{8,10},{9,11},{10,... | collective-permute-start | bytes 491528 | tf_op jit(solution)/shard_map/ppermute | solution.py:56
  28.3 0.0 copy-done.4
  28.3 0.0 copy-done.5
  28.3 5.3 %collective-permute-done.3.chip = bf16[128,640]{1,0:T(8,128)(2,1)S(1)} collective-permute-done((bf16[128,640]{1,0:T(8,128)(2,1)S(1)}, bf16[128,640]{1,0:T(8,128)(2,1)S(1)}, u32[]{:S(2)}, u32[]{:S(2)}) %collective-permute-start.3) | collective-permute-done | bytes 163872 | tf_op jit(solution)/shard_map/ppermute | solution.py:56
  33.6 0.0 copy-done.1
  33.6 0.3 shard_map.66
  33.9 1.3 %collective-permute-start.4 = (bf16[128,640]{1,0:T(8,128)(2,1)S(1)}, bf16[128,640]{1,0:T(8,128)(2,1)S(1)}, u32[]{:S(2)}, u32[]{:S(2)}) collective-permute-start(bf16[128,640]{1,0:T(8,128)(2,1)S(1)} %broadcast_select_fusion.1), channel_id=1, source_target_pairs={{0,128},{2,130},{1,9},{3,11}} | collective-permute-start | bytes 491528 | tf_op jit(solution)/shard_map/ppermute | solution.py:281
  35.2 2.3 %collective-permute-done.4 = bf16[128,640]{1,0:T(8,128)(2,1)S(1)} collective-permute-done((bf16[128,640]{1,0:T(8,128)(2,1)S(1)}, bf16[128,640]{1,0:T(8,128)(2,1)S(1)}, u32[]{:S(2)}, u32[]{:S(2)}) %collective-permute-start.4) | collective-permute-done | bytes 163872 | tf_op jit(solution)/shard_map/ppermute | solution.py:281
  37.6 1.3 %collective-permute-start.6 = (bf16[128,640]{1,0:T(8,128)(2,1)S(1)}, bf16[128,640]{1,0:T(8,128)(2,1)S(1)}, u32[]{:S(2)}, u32[]{:S(2)}) collective-permute-start(bf16[128,640]{1,0:T(8,128)(2,1)S(1)} %get-tuple-element.43.own), channel_id=1, source_target_pairs={{0,4},{4,8},{8,12},{12,16},{16,20},{20,24},{24,28},{28,32},{32,36}... | collective-permute-start | bytes 491528 | tf_op jit(solution)/shard_map/ppermute | solution.py:284
  38.9 5.7 %collective-permute-start.5 = (bf16[128,640]{1,0:T(8,128)(2,1)S(1)}, bf16[128,640]{1,0:T(8,128)(2,1)S(1)}, u32[]{:S(2)}, u32[]{:S(2)}) collective-permute-start(bf16[128,640]{1,0:T(8,128)(2,1)S(1)} %fusion.1), channel_id=1, source_target_pairs={{0,64},{2,66},{128,192},{130,194},{1,5},{3,7},{9,13},{11,15}} | collective-permute-start | bytes 491528 | tf_op jit(solution)/shard_map/ppermute | solution.py:281
  44.5 0.0 collective-permute-done.6
  44.6 2.2 %collective-permute-done.5 = bf16[128,640]{1,0:T(8,128)(2,1)S(1)} collective-permute-done((bf16[128,640]{1,0:T(8,128)(2,1)S(1)}, bf16[128,640]{1,0:T(8,128)(2,1)S(1)}, u32[]{:S(2)}, u32[]{:S(2)}) %collective-permute-start.5) | collective-permute-done | bytes 163872 | tf_op jit(solution)/shard_map/ppermute | solution.py:281
  46.8 3.8 %collective-permute-start.7 = (bf16[128,640]{1,0:T(8,128)(2,1)S(1)}, bf16[128,640]{1,0:T(8,128)(2,1)S(1)}, u32[]{:S(2)}, u32[]{:S(2)}) collective-permute-start(bf16[128,640]{1,0:T(8,128)(2,1)S(1)} %add.36), channel_id=1, source_target_pairs={{0,32},{2,34},{128,160},{130,162},{64,96},{66,98},{192,224},{194,2... | collective-permute-start | bytes 491528 | tf_op jit(solution)/shard_map/ppermute | solution.py:281
  50.6 6.4 %collective-permute-start.8 = (bf16[128,640]{1,0:T(8,128)(2,1)S(1)}, bf16[128,640]{1,0:T(8,128)(2,1)S(1)}, u32[]{:S(2)}, u32[]{:S(2)}) collective-permute-start(bf16[128,640]{1,0:T(8,128)(2,1)S(1)} %broadcast_select_fusion.p0), channel_id=1, source_target_pairs={{0,1},{1,0},{2,3},{3,2},{4,5},{5,4},{6,7},{7,6},{8,9},{9,8},{10,11... | collective-permute-start | bytes 491528 | tf_op jit(solution)/shard_map/ppermute | solution.py:56
  57.0 0.0 collective-permute-done.7
  57.1 0.9 collective-permute-done.8.p1
  58.0 0.0 copy-done.3
  58.0 2.3 %collective-permute-start.11 = (bf16[160,1920]{1,0:T(8,128)(2,1)S(1)}, bf16[160,1920]{1,0:T(8,128)(2,1)S(1)}, u32[]{:S(2)}, u32[]{:S(2)}) collective-permute-start(bf16[160,1920]{1,0:T(8,128)(2,1)S(1)} %copy-done.3), channel_id=1, source_target_pairs={{0,1},{1,0},{2,3},{3,2},{4,5},{5,4},{6,7},{7,6},{8,9},{9,8},{10,11... | collective-permute-start | bytes 1843208 | tf_op jit(solution)/shard_map/ppermute | solution.py:56
  60.3 1.9 %collective-permute-start.15 = (bf16[160,1920]{1,0:T(8,128)(2,1)S(1)}, bf16[160,1920]{1,0:T(8,128)(2,1)S(1)}, u32[]{:S(2)}, u32[]{:S(2)}) collective-permute-start(bf16[160,1920]{1,0:T(8,128)(2,1)S(1)} %copy-done.3), channel_id=1, source_target_pairs={{0,258},{1,259},{2,256},{3,257},{4,262},{5,263},{6,260},{7,261},{8... | collective-permute-start | bytes 1843208 | tf_op jit(solution)/shard_map/ppermute | solution.py:273
  62.2 18.0 %collective-permute-start.9 = (bf16[128,640]{1,0:T(8,128)(2,1)S(1)}, bf16[128,640]{1,0:T(8,128)(2,1)S(1)}, u32[]{:S(2)}, u32[]{:S(2)}) collective-permute-start(bf16[128,640]{1,0:T(8,128)(2,1)S(1)} %add.37), channel_id=1, source_target_pairs={{0,16},{2,18},{128,144},{130,146},{64,80},{66,82},{192,208},{194,2... | collective-permute-start | bytes 491528 | tf_op jit(solution)/shard_map/ppermute | solution.py:281
  80.2 3.2 %collective-permute-start.10 = (bf16[128,640]{1,0:T(8,128)(2,1)S(1)}, bf16[128,640]{1,0:T(8,128)(2,1)S(1)}, u32[]{:S(2)}, u32[]{:S(2)}) collective-permute-start(bf16[128,640]{1,0:T(8,128)(2,1)S(1)} %broadcast_select_fusion.p0), channel_id=1, source_target_pairs={{0,2},{1,3},{2,0},{3,1},{4,6},{5,7},{6,4},{7,5},{8,10},{9,11},{10,... | collective-permute-start | bytes 491528 | tf_op jit(solution)/shard_map/ppermute | solution.py:56
  83.4 0.0 collective-permute-done.9
  83.5 2.8 %collective-permute-done.10.p2 = bf16[128,640]{1,0:T(8,128)(2,1)S(1)} collective-permute-done((bf16[128,640]{1,0:T(8,128)(2,1)S(1)}, bf16[128,640]{1,0:T(8,128)(2,1)S(1)}, u32[]{:S(2)}, u32[]{:S(2)}) %collective-permute-start.10) | collective-permute-done | bytes 163872 | tf_op jit(solution)/shard_map/ppermute | solution.py:56
  86.3 0.0 collective-permute-done.11.w1
  86.3 0.0 collective-permute-done.15.w2
  86.3 1.9 %collective-permute-start.16 = (bf16[160,1920]{1,0:T(8,128)(2,1)S(1)}, bf16[160,1920]{1,0:T(8,128)(2,1)S(1)}, u32[]{:S(2)}, u32[]{:S(2)}) collective-permute-start(bf16[160,1920]{1,0:T(8,128)(2,1)S(1)} %collective-permute-done.15.w2), channel_id=1, source_target_pairs={{0,1},{1,0},{2,3},{3,2},{4,5},{5,4},{6,7},{7,6},{8,9},{9,8},{10,11... | collective-permute-start | bytes 1843208 | tf_op jit(solution)/shard_map/ppermute | solution.py:56
  88.2 7.8 %collective-permute-start.12 = (bf16[128,640]{1,0:T(8,128)(2,1)S(1)}, bf16[128,640]{1,0:T(8,128)(2,1)S(1)}, u32[]{:S(2)}, u32[]{:S(2)}) collective-permute-start(bf16[128,640]{1,0:T(8,128)(2,1)S(1)} %add.38), channel_id=1, source_target_pairs={{0,8},{2,10},{128,136},{130,138},{64,72},{66,74},{192,200},{194,20... | collective-permute-start | bytes 491528 | tf_op jit(solution)/shard_map/ppermute | solution.py:281
  96.1 1.9 %collective-permute-start.13 = (bf16[128,640]{1,0:T(8,128)(2,1)S(1)}, bf16[128,640]{1,0:T(8,128)(2,1)S(1)}, u32[]{:S(2)}, u32[]{:S(2)}) collective-permute-start(bf16[128,640]{1,0:T(8,128)(2,1)S(1)} %collective-permute-done.10.p2), channel_id=1, source_target_pairs={{0,1},{1,0},{2,3},{3,2},{4,5},{5,4},{6,7},{7,6},{8,9},{9,8},{10,11... | collective-permute-start | bytes 491528 | tf_op jit(solution)/shard_map/ppermute | solution.py:56
  98.0 0.3 collective-permute-done.12
  98.4 1.0 collective-permute-done.13.p3
  99.4 1.5 %collective-permute-start.14 = (bf16[128,640]{1,0:T(8,128)(2,1)S(1)}, bf16[128,640]{1,0:T(8,128)(2,1)S(1)}, u32[]{:S(2)}, u32[]{:S(2)}) collective-permute-start(bf16[128,640]{1,0:T(8,128)(2,1)S(1)} %add.39), channel_id=1, source_target_pairs={{0,4},{2,6},{128,132},{130,134},{64,68},{66,70},{192,196},{194,198... | collective-permute-start | bytes 491528 | tf_op jit(solution)/shard_map/ppermute | solution.py:281
  100.9 2.2 %collective-permute-done.14 = bf16[128,640]{1,0:T(8,128)(2,1)S(1)} collective-permute-done((bf16[128,640]{1,0:T(8,128)(2,1)S(1)}, bf16[128,640]{1,0:T(8,128)(2,1)S(1)}, u32[]{:S(2)}, u32[]{:S(2)}) %collective-permute-start.14) | collective-permute-done | bytes 163872 | tf_op jit(solution)/shard_map/ppermute | solution.py:281
  103.2 0.0 collective-permute-done.16.w3
  103.2 1.3 %collective-permute-start.17 = (bf16[128,640]{1,0:T(8,128)(2,1)S(1)}, bf16[128,640]{1,0:T(8,128)(2,1)S(1)}, u32[]{:S(2)}, u32[]{:S(2)}) collective-permute-start(bf16[128,640]{1,0:T(8,128)(2,1)S(1)} %add.40), channel_id=1, source_target_pairs={{0,256},{2,258},{128,384},{130,386},{64,320},{66,322},{192,448},{1... | collective-permute-start | bytes 491528 | tf_op jit(solution)/shard_map/ppermute | solution.py:281
  104.5 3.6 %shard_map.67 = (bf16[128,640]{1,0:T(8,128)(2,1)S(1)}, f32[128,8]{1,0:T(8,128)S(1)}, f32[128,8]{1,0:T(8,128)S(1)}, f32[128,640]{1,0:T(8,128)S(1)}, bf16[640,1920]{1,0:T(8,128)(2,1)S(1)}) custom-call(s32[1]{0:T(128)} %bitcast.me_ref, bf16[128,640]{1,0:T(8,128)(2,1)S(1)} %get-tuple-element.43.own, bf16[128,640]{1,0:T(8,128)(2,1)S(1)} %broadcast_select_fusion.p0, ...), custom_call_target="tpu_custom_call" | custom-call | flops 1006632960 | bytes 6234116 | tf_op jit(solution)/shard_map/pallas_call | solution.py:223
  108.1 0.0 collective-permute-done.17
  108.2 2.0 %collective-permute-start.19 = (bf16[128,640]{1,0:T(8,128)(2,1)S(1)}, bf16[128,640]{1,0:T(8,128)(2,1)S(1)}, u32[]{:S(2)}, u32[]{:S(2)}) collective-permute-start(bf16[128,640]{1,0:T(8,128)(2,1)S(1)} %add.41.a0), channel_id=1, source_target_pairs={{0,2},{1,3},{2,0},{3,1},{4,6},{5,7},{6,4},{7,5},{8,10},{9,11},{10,... | collective-permute-start | bytes 491528 | tf_op jit(solution)/shard_map/ppermute | solution.py:56
  110.2 2.7 %collective-permute-start.18 = (bf16[128,640]{1,0:T(8,128)(2,1)S(1)}, bf16[128,640]{1,0:T(8,128)(2,1)S(1)}, u32[]{:S(2)}, u32[]{:S(2)}) collective-permute-start(bf16[128,640]{1,0:T(8,128)(2,1)S(1)} %add.41.a0), channel_id=1, source_target_pairs={{0,1},{1,0},{2,3},{3,2},{4,5},{5,4},{6,7},{7,6},{8,9},{9,8},{10,11... | collective-permute-start | bytes 491528 | tf_op jit(solution)/shard_map/ppermute | solution.py:56
  112.8 2.6 %collective-permute-done.19.a2 = bf16[128,640]{1,0:T(8,128)(2,1)S(1)} collective-permute-done((bf16[128,640]{1,0:T(8,128)(2,1)S(1)}, bf16[128,640]{1,0:T(8,128)(2,1)S(1)}, u32[]{:S(2)}, u32[]{:S(2)}) %collective-permute-start.19) | collective-permute-done | bytes 163872 | tf_op jit(solution)/shard_map/ppermute | solution.py:56
  115.4 3.2 %collective-permute-start.20 = (bf16[128,640]{1,0:T(8,128)(2,1)S(1)}, bf16[128,640]{1,0:T(8,128)(2,1)S(1)}, u32[]{:S(2)}, u32[]{:S(2)}) collective-permute-start(bf16[128,640]{1,0:T(8,128)(2,1)S(1)} %collective-permute-done.19.a2), channel_id=1, source_target_pairs={{0,1},{1,0},{2,3},{3,2},{4,5},{5,4},{6,7},{7,6},{8,9},{9,8},{10,11... | collective-permute-start | bytes 491528 | tf_op jit(solution)/shard_map/ppermute | solution.py:56
  118.6 0.0 collective-permute-done.18.a1
  118.6 1.0 collective-permute-done.20.a3
  119.6 5.0 %shard_map.68 = bf16[128,640]{1,0:T(8,128)(2,1)} custom-call(bf16[128,640]{1,0:T(8,128)(2,1)S(1)} %get-tuple-element.44.query, bf16[128,640]{1,0:T(8,128)(2,1)S(1)} %add.41.a0, bf16[128,640]{1,0:T(8,128)(2,1)S(1)} %collective-permute-done.18.a1, bf16[128,640]{1,0:T(8,128)(2,1)S(1)} %collective-permute-done.19.a2, ...), custom_call_target="tpu_custom_call" | custom-call | flops 1006632960 | bytes 3940352 | tf_op jit(solution)/shard_map/pallas_call | solution.py:223
  (13 shorter events, 0.4 us)
Async XLA Ops:
  0.0 28.3 %copy-start.4 = (f32[640]{0:T(1024)S(1)}, f32[640]{0:T(1024)}, u32[]{:S(2)}) copy-start(f32[640]{0:T(1024)} %param.9) | copy-start | bytes 7684
  0.0 28.3 %copy-start.5 = (f32[640]{0:T(1024)S(1)}, f32[640]{0:T(1024)}, u32[]{:S(2)}) copy-start(f32[640]{0:T(1024)} %param.10) | copy-start | bytes 7684
  0.0 10.1 %collective-permute-start = (bf16[128,640]{1,0:T(8,128)(2,1)}, bf16[128,640]{1,0:T(8,128)(2,1)S(1)}, u32[]{:S(2)}, u32[]{:S(2)}) collective-permute-start(bf16[128,640]{1,0:T(8,128)(2,1)} %bitcast.6), channel_id=1, source_target_pairs={{0,1},{1,0},{2,3},{3,2},{4,5},{5,4},{6,7},{7,6},{8,9},{9,8},{10,11... | collective-permute-start | bytes 491528 | tf_op jit(solution)/shard_map/ppermute | solution.py:56
  10.1 0.9 copy-start
  11.1 22.6 %copy-start.1 = (bf16[1,4,32,640]{3,2,1,0:T(8,128)(2,1)S(1)}, bf16[1,4,32,640]{3,2,1,0:T(8,128)(2,1)}, u32[]{:S(2)}) copy-start(bf16[1,4,32,640]{3,2,1,0:T(8,128)(2,1)} %param.6) | copy-start | bytes 491524
  11.3 6.7 %collective-permute-start.1 = (bf16[2,128,160]{2,1,0:T(8,128)(2,1)S(1)}, bf16[2,128,160]{2,1,0:T(8,128)(2,1)S(1)}, u32[]{:S(2)}, u32[]{:S(2)}) collective-permute-start(bf16[2,128,160]{2,1,0:T(8,128)(2,1)S(1)} %get-tuple-element.29), channel_id=1, source_target_pairs={{0,2},{1,3},{2,0},{3,1},{4,6},{5,7},{6,4},{7,5},{8,10},{9,11},{10,... | collective-permute-start | bytes 245768 | tf_op jit(solution)/shard_map/ppermute | solution.py:56
  18.0 1.5 %copy-start.2 = (bf16[9,160,640]{2,1,0:T(8,128)(2,1)S(1)}, bf16[9,160,640]{2,1,0:T(8,128)(2,1)}, u32[]{:S(2)}) copy-start(bf16[9,160,640]{2,1,0:T(8,128)(2,1)} %param.8) | copy-start | bytes 5529604
  21.9 36.2 %copy-start.3 = (bf16[160,1920]{1,0:T(8,128)(2,1)S(1)}, bf16[160,1920]{1,0:T(8,128)(2,1)}, u32[]{:S(2)}) copy-start(bf16[160,1920]{1,0:T(8,128)(2,1)} %w0.1) | copy-start | bytes 1843204
  21.9 4.4 %collective-permute-start.2 = (bf16[2,128,640]{2,1,0:T(8,128)(2,1)S(1)}, bf16[2,128,640]{2,1,0:T(8,128)(2,1)S(1)}, u32[]{:S(2)}, u32[]{:S(2)}) collective-permute-start(bf16[2,128,640]{2,1,0:T(8,128)(2,1)S(1)} %get-tuple-element.31), channel_id=1, source_target_pairs={{0,1},{1,0},{2,3},{3,2},{4,5},{5,4},{6,7},{7,6},{8,9},{9,8},{10,11... | collective-permute-start | bytes 983048 | tf_op jit(solution)/shard_map/ppermute | solution.py:56
  26.3 7.3 %collective-permute-start.3 = (bf16[128,640]{1,0:T(8,128)(2,1)S(1)}, bf16[128,640]{1,0:T(8,128)(2,1)S(1)}, u32[]{:S(2)}, u32[]{:S(2)}) collective-permute-start(bf16[128,640]{1,0:T(8,128)(2,1)S(1)} %fusion), channel_id=1, source_target_pairs={{0,2},{1,3},{2,0},{3,1},{4,6},{5,7},{6,4},{7,5},{8,10},{9,11},{10,... | collective-permute-start | bytes 491528 | tf_op jit(solution)/shard_map/ppermute | solution.py:56
  33.9 3.6 %collective-permute-start.4 = (bf16[128,640]{1,0:T(8,128)(2,1)S(1)}, bf16[128,640]{1,0:T(8,128)(2,1)S(1)}, u32[]{:S(2)}, u32[]{:S(2)}) collective-permute-start(bf16[128,640]{1,0:T(8,128)(2,1)S(1)} %broadcast_select_fusion.1), channel_id=1, source_target_pairs={{0,128},{2,130},{1,9},{3,11}} | collective-permute-start | bytes 491528 | tf_op jit(solution)/shard_map/ppermute | solution.py:281
  37.6 7.0 %collective-permute-start.6 = (bf16[128,640]{1,0:T(8,128)(2,1)S(1)}, bf16[128,640]{1,0:T(8,128)(2,1)S(1)}, u32[]{:S(2)}, u32[]{:S(2)}) collective-permute-start(bf16[128,640]{1,0:T(8,128)(2,1)S(1)} %get-tuple-element.43.own), channel_id=1, source_target_pairs={{0,4},{4,8},{8,12},{12,16},{16,20},{20,24},{24,28},{28,32},{32,36}... | collective-permute-start | bytes 491528 | tf_op jit(solution)/shard_map/ppermute | solution.py:284
  38.9 7.9 %collective-permute-start.5 = (bf16[128,640]{1,0:T(8,128)(2,1)S(1)}, bf16[128,640]{1,0:T(8,128)(2,1)S(1)}, u32[]{:S(2)}, u32[]{:S(2)}) collective-permute-start(bf16[128,640]{1,0:T(8,128)(2,1)S(1)} %fusion.1), channel_id=1, source_target_pairs={{0,64},{2,66},{128,192},{130,194},{1,5},{3,7},{9,13},{11,15}} | collective-permute-start | bytes 491528 | tf_op jit(solution)/shard_map/ppermute | solution.py:281
  46.8 10.2 %collective-permute-start.7 = (bf16[128,640]{1,0:T(8,128)(2,1)S(1)}, bf16[128,640]{1,0:T(8,128)(2,1)S(1)}, u32[]{:S(2)}, u32[]{:S(2)}) collective-permute-start(bf16[128,640]{1,0:T(8,128)(2,1)S(1)} %add.36), channel_id=1, source_target_pairs={{0,32},{2,34},{128,160},{130,162},{64,96},{66,98},{192,224},{194,2... | collective-permute-start | bytes 491528 | tf_op jit(solution)/shard_map/ppermute | solution.py:281
  50.6 7.4 %collective-permute-start.8 = (bf16[128,640]{1,0:T(8,128)(2,1)S(1)}, bf16[128,640]{1,0:T(8,128)(2,1)S(1)}, u32[]{:S(2)}, u32[]{:S(2)}) collective-permute-start(bf16[128,640]{1,0:T(8,128)(2,1)S(1)} %broadcast_select_fusion.p0), channel_id=1, source_target_pairs={{0,1},{1,0},{2,3},{3,2},{4,5},{5,4},{6,7},{7,6},{8,9},{9,8},{10,11... | collective-permute-start | bytes 491528 | tf_op jit(solution)/shard_map/ppermute | solution.py:56
  58.0 28.3 %collective-permute-start.11 = (bf16[160,1920]{1,0:T(8,128)(2,1)S(1)}, bf16[160,1920]{1,0:T(8,128)(2,1)S(1)}, u32[]{:S(2)}, u32[]{:S(2)}) collective-permute-start(bf16[160,1920]{1,0:T(8,128)(2,1)S(1)} %copy-done.3), channel_id=1, source_target_pairs={{0,1},{1,0},{2,3},{3,2},{4,5},{5,4},{6,7},{7,6},{8,9},{9,8},{10,11... | collective-permute-start | bytes 1843208 | tf_op jit(solution)/shard_map/ppermute | solution.py:56
  60.3 26.0 %collective-permute-start.15 = (bf16[160,1920]{1,0:T(8,128)(2,1)S(1)}, bf16[160,1920]{1,0:T(8,128)(2,1)S(1)}, u32[]{:S(2)}, u32[]{:S(2)}) collective-permute-start(bf16[160,1920]{1,0:T(8,128)(2,1)S(1)} %copy-done.3), channel_id=1, source_target_pairs={{0,258},{1,259},{2,256},{3,257},{4,262},{5,263},{6,260},{7,261},{8... | collective-permute-start | bytes 1843208 | tf_op jit(solution)/shard_map/ppermute | solution.py:273
  62.2 21.2 %collective-permute-start.9 = (bf16[128,640]{1,0:T(8,128)(2,1)S(1)}, bf16[128,640]{1,0:T(8,128)(2,1)S(1)}, u32[]{:S(2)}, u32[]{:S(2)}) collective-permute-start(bf16[128,640]{1,0:T(8,128)(2,1)S(1)} %add.37), channel_id=1, source_target_pairs={{0,16},{2,18},{128,144},{130,146},{64,80},{66,82},{192,208},{194,2... | collective-permute-start | bytes 491528 | tf_op jit(solution)/shard_map/ppermute | solution.py:281
  80.2 6.1 %collective-permute-start.10 = (bf16[128,640]{1,0:T(8,128)(2,1)S(1)}, bf16[128,640]{1,0:T(8,128)(2,1)S(1)}, u32[]{:S(2)}, u32[]{:S(2)}) collective-permute-start(bf16[128,640]{1,0:T(8,128)(2,1)S(1)} %broadcast_select_fusion.p0), channel_id=1, source_target_pairs={{0,2},{1,3},{2,0},{3,1},{4,6},{5,7},{6,4},{7,5},{8,10},{9,11},{10,... | collective-permute-start | bytes 491528 | tf_op jit(solution)/shard_map/ppermute | solution.py:56
  86.3 16.9 %collective-permute-start.16 = (bf16[160,1920]{1,0:T(8,128)(2,1)S(1)}, bf16[160,1920]{1,0:T(8,128)(2,1)S(1)}, u32[]{:S(2)}, u32[]{:S(2)}) collective-permute-start(bf16[160,1920]{1,0:T(8,128)(2,1)S(1)} %collective-permute-done.15.w2), channel_id=1, source_target_pairs={{0,1},{1,0},{2,3},{3,2},{4,5},{5,4},{6,7},{7,6},{8,9},{9,8},{10,11... | collective-permute-start | bytes 1843208 | tf_op jit(solution)/shard_map/ppermute | solution.py:56
  88.2 10.1 %collective-permute-start.12 = (bf16[128,640]{1,0:T(8,128)(2,1)S(1)}, bf16[128,640]{1,0:T(8,128)(2,1)S(1)}, u32[]{:S(2)}, u32[]{:S(2)}) collective-permute-start(bf16[128,640]{1,0:T(8,128)(2,1)S(1)} %add.38), channel_id=1, source_target_pairs={{0,8},{2,10},{128,136},{130,138},{64,72},{66,74},{192,200},{194,20... | collective-permute-start | bytes 491528 | tf_op jit(solution)/shard_map/ppermute | solution.py:281
  96.1 3.3 %collective-permute-start.13 = (bf16[128,640]{1,0:T(8,128)(2,1)S(1)}, bf16[128,640]{1,0:T(8,128)(2,1)S(1)}, u32[]{:S(2)}, u32[]{:S(2)}) collective-permute-start(bf16[128,640]{1,0:T(8,128)(2,1)S(1)} %collective-permute-done.10.p2), channel_id=1, source_target_pairs={{0,1},{1,0},{2,3},{3,2},{4,5},{5,4},{6,7},{7,6},{8,9},{9,8},{10,11... | collective-permute-start | bytes 491528 | tf_op jit(solution)/shard_map/ppermute | solution.py:56
  99.4 3.8 %collective-permute-start.14 = (bf16[128,640]{1,0:T(8,128)(2,1)S(1)}, bf16[128,640]{1,0:T(8,128)(2,1)S(1)}, u32[]{:S(2)}, u32[]{:S(2)}) collective-permute-start(bf16[128,640]{1,0:T(8,128)(2,1)S(1)} %add.39), channel_id=1, source_target_pairs={{0,4},{2,6},{128,132},{130,134},{64,68},{66,70},{192,196},{194,198... | collective-permute-start | bytes 491528 | tf_op jit(solution)/shard_map/ppermute | solution.py:281
  103.2 4.9 %collective-permute-start.17 = (bf16[128,640]{1,0:T(8,128)(2,1)S(1)}, bf16[128,640]{1,0:T(8,128)(2,1)S(1)}, u32[]{:S(2)}, u32[]{:S(2)}) collective-permute-start(bf16[128,640]{1,0:T(8,128)(2,1)S(1)} %add.40), channel_id=1, source_target_pairs={{0,256},{2,258},{128,384},{130,386},{64,320},{66,322},{192,448},{1... | collective-permute-start | bytes 491528 | tf_op jit(solution)/shard_map/ppermute | solution.py:281
  108.2 7.2 %collective-permute-start.19 = (bf16[128,640]{1,0:T(8,128)(2,1)S(1)}, bf16[128,640]{1,0:T(8,128)(2,1)S(1)}, u32[]{:S(2)}, u32[]{:S(2)}) collective-permute-start(bf16[128,640]{1,0:T(8,128)(2,1)S(1)} %add.41.a0), channel_id=1, source_target_pairs={{0,2},{1,3},{2,0},{3,1},{4,6},{5,7},{6,4},{7,5},{8,10},{9,11},{10,... | collective-permute-start | bytes 491528 | tf_op jit(solution)/shard_map/ppermute | solution.py:56
  110.2 8.4 %collective-permute-start.18 = (bf16[128,640]{1,0:T(8,128)(2,1)S(1)}, bf16[128,640]{1,0:T(8,128)(2,1)S(1)}, u32[]{:S(2)}, u32[]{:S(2)}) collective-permute-start(bf16[128,640]{1,0:T(8,128)(2,1)S(1)} %add.41.a0), channel_id=1, source_target_pairs={{0,1},{1,0},{2,3},{3,2},{4,5},{5,4},{6,7},{7,6},{8,9},{9,8},{10,11... | collective-permute-start | bytes 491528 | tf_op jit(solution)/shard_map/ppermute | solution.py:56
  115.4 4.2 %collective-permute-start.20 = (bf16[128,640]{1,0:T(8,128)(2,1)S(1)}, bf16[128,640]{1,0:T(8,128)(2,1)S(1)}, u32[]{:S(2)}, u32[]{:S(2)}) collective-permute-start(bf16[128,640]{1,0:T(8,128)(2,1)S(1)} %collective-permute-done.19.a2), channel_id=1, source_target_pairs={{0,1},{1,0},{2,3},{3,2},{4,5},{5,4},{6,7},{7,6},{8,9},{9,8},{10,11... | collective-permute-start | bytes 491528 | tf_op jit(solution)/shard_map/ppermute | solution.py:56

commit v4 on v3

--- a/solution.py
+++ b/solution.py
@@ -192,15 +192,12 @@
         acc[:, window] = jnp.where(inside, out, acc[:, window])
 
 
-def anchor_kernel(
-    query, a0, a1, a2, a3, weight, top, den, acc, residual, restyled, joined, keys, vals, mixed
-):
-    part, chans = query.shape
-    head_dim = chans // HEADS
+def attend(blocks, query, weight, top, den, acc, joined, keys, vals):
+    head_dim = query.shape[1] // HEADS
     scale = head_dim ** (-0.5)
-    project((a0, a1, a2, a3), weight, joined, keys, vals)
+    project(blocks, weight, joined, keys, vals)
     for head in range(HEADS):
-        window, inside = head_window(head, head_dim, chans)
+        window, inside = head_window(head, head_dim, query.shape[1])
         s = scores_of(query, keys, head, window, inside)
         old = top[:, head : head + 1]
         peak = jnp.maximum(old, jnp.max(s, axis=1, keepdims=True))
@@ -210,8 +207,27 @@
         out = jnp.dot(
             w.astype(jnp.bfloat16), vals[:, window], preferred_element_type=jnp.float32
         )
-        out = (acc[:, window] * factor + out) / total
-        mixed[:, window] = jnp.where(inside, out, mixed[:, window])
+        yield head, window, inside, peak, total, acc[:, window] * factor + out
+
+
+def more_kernel(
+    query, a0, a1, weight, top, den, acc, new_top, new_den, new_acc, joined, keys, vals
+):
+    for head, window, inside, peak, total, out in attend(
+        (a0, a1), query, weight, top, den, acc, joined, keys, vals
+    ):
+        new_top[:, head : head + 1] = peak
+        new_den[:, head : head + 1] = total
+        new_acc[:, window] = jnp.where(inside, out, new_acc[:, window])
+
+
+def last_kernel(
+    query, a0, a1, weight, top, den, acc, residual, restyled, joined, keys, vals, mixed
+):
+    for head, window, inside, _, total, out in attend(
+        (a0, a1), query, weight, top, den, acc, joined, keys, vals
+    ):
+        mixed[:, window] = jnp.where(inside, out / total, mixed[:, window])
     restyled[...] = (residual[...].astype(jnp.float32) + mixed[...]).astype(jnp.bfloat16)
 
 
@@ -247,7 +263,19 @@
         [shape((2, part, share), bf16)] * 2,
         [me.reshape(1), lat, to_rows(lat, 1)],
     )
-    came = to_rows(away, 2)
+    devices = lax.axis_size("tm")
+    far = [
+        (tm * 4 + row, (tm + devices // 2) % devices * 4 + (row ^ 2))
+        for tm in range(devices)
+        for row in range(4)
+    ]
+    cut = share // 3 // 16 * 16
+    chunk = lambda low, high, *done: lax.ppermute(
+        after(qkv_weight[low:high], *done), BOTH, far
+    )
+    chunk0 = chunk(0, cut, away)
+    came = after(to_rows(away, 2), chunk0)
+    chunk1 = chunk(cut, 2 * cut, came)
     group = jnp.arange(share) // (chans // GROUPS)
     pool = (group[:, None] == group[None, :]).astype(f32)
     keep, send = call(
@@ -262,15 +290,10 @@
         flops=2 * cells * 9 * share * chans,
     )
     core = to_rows(send, 1)
-    half = (keep[1] + core[1].astype(f32)).astype(bf16)
+    half = after((keep[1] + core[1].astype(f32)).astype(bf16), chunk1)
     chip = to_rows(half, 2)
-    devices = lax.axis_size("tm")
-    far = [
-        (tm * 4 + row, (tm + devices // 2) % devices * 4 + (row ^ 2))
-        for tm in range(devices)
-        for row in range(4)
-    ]
-    weight_chip = lax.ppermute(after(qkv_weight, half), BOTH, far)
+    chunk2 = chunk(2 * cut, share, half)
+    chip = after(chip, chunk2)
     residual, feats = call(
         norm_kernel,
         [shape((part, chans), bf16)] * 2,
@@ -280,6 +303,7 @@
     routes = tree_levels(devices)
     tree = lambda level, x: x + lax.ppermute(x, BOTH, routes[level])
     routes = routes + [[]] * (7 - len(routes))
+    weight_chip = jnp.concatenate([chunk0, chunk1, chunk2], axis=0)
     anchor = tree(0, jnp.where(first, feats, jnp.zeros_like(feats)))
     prev = lax.ppermute(after(feats, anchor), "tm", [(i, i + 1) for i in range(devices - 1)])
     anchor = tree(1, anchor)
@@ -291,38 +315,40 @@
     weight_core = to_rows(after(qkv_weight, anchor), 1)
     anchor = after(tree(3, anchor), prev_chip, weight_core)
     prev_last = to_rows(after(prev_chip, anchor), 1)
+    anchor = after(tree(4, anchor), prev_last)
     weight_last = to_rows(after(weight_chip, anchor), 1)
-    anchor = after(tree(4, anchor), prev_last)
     anchor = after(tree(5, anchor), weight_last)
     prev = (prev, prev_core, prev_chip, prev_last)
     qkv = [qkv_weight, weight_core, weight_chip, weight_last]
 
-    scratch = [
-        pltpu.VMEM((cells, chans), bf16),
-        pltpu.VMEM((cells, chans), bf16),
-        pltpu.VMEM((cells, chans), bf16),
+    scratch = lambda keys: [pltpu.VMEM((keys, chans), bf16)] * 3
+    flops = lambda keys: 2 * keys * chans * 2 * chans + 4 * part * keys * chans
+    state = [
+        shape((part, HEADS), f32),
+        shape((part, HEADS), f32),
+        shape((part, chans), f32),
     ]
-    flops = 2 * cells * chans * 2 * chans + 4 * part * cells * chans
-    query, top, den, acc, weight = call(
+    query, *prior, weight = call(
         prev_kernel,
-        [
-            shape((part, chans), bf16),
-            shape((part, HEADS), f32),
-            shape((part, HEADS), f32),
-            shape((part, chans), f32),
-            shape((chans, 3 * chans), bf16),
-        ],
+        [shape((part, chans), bf16), *state, shape((chans, 3 * chans), bf16)],
         [me.reshape(1), after(feats, anchor), *prev, *qkv],
-        scratch,
-        flops=flops,
-    )
-    anchor = gathered(after(tree(6, anchor), acc))
+        scratch(cells),
+        flops=flops(cells),
+    )
+    anchor, anchor_core, anchor_chip, anchor_last = gathered(after(tree(6, anchor), prior[2]))
+    prior = call(
+        more_kernel,
+        state,
+        [query, anchor, anchor_core, weight, *prior],
+        scratch(2 * part),
+        flops=flops(2 * part),
+    )
     (restyled,) = call(
-        anchor_kernel,
+        last_kernel,
         [shape((part, chans), bf16)],
-        [query, *anchor, weight, top, den, acc, residual],
-        scratch + [pltpu.VMEM((part, chans), f32)],
-        flops=flops,
+        [query, anchor_chip, anchor_last, weight, *prior, residual],
+        scratch(2 * part) + [pltpu.VMEM((part, chans), f32)],
+        flops=flops(2 * part),
     )
     return restyled.reshape(1, rows_dev, width, chans)
 

time: 125 us -> 139 us (1.11)
  the two profiles are of different devices: /device:TPU:1 before, /device:TPU:41 now
where the time goes in v4:
time: 139 us; the launch traced here: 138 us
  starting transfers between devices  69.2 us (50%)
  waiting for transfers between devices  50.6 us (36%)
  Pallas kernels  13.5 us (10%)
  local copies, waits for them, and re-layouts  4.34 us (3%)
    ppermute x12, starting transfers between devices, to_rows(): return lax.ppermute(x, 'rows', [(i, i ^ flip) for i in range(4)])  50 us
    ppermute x7, waiting for transfers between devices, on_device(): tree = lambda level, x: x + lax.ppermute(x, BOTH, routes[level])  25.9 us
    pallas_call x6, Pallas kernels, call(): pl.pallas_call(kernel, out_shape=list(outs), in_specs=specs, out_specs=[V...  13.5 us
    ppermute x12, waiting for transfers between devices, to_rows(): return lax.ppermute(x, 'rows', [(i, i ^ flip) for i in range(4)])  12 us
    ppermute x3, starting transfers between devices, on_device(): lax.ppermute(after(qkv_weight[low:high], *done), BOTH, far)  10.7 us
    ppermute x3, waiting for transfers between devices, on_device(): lax.ppermute(after(qkv_weight[low:high], *done), BOTH, far)  8.34 us
    ppermute x7, starting transfers between devices, on_device(): tree = lambda level, x: x + lax.ppermute(x, BOTH, routes[level])  5.3 us
    ppermute x1, waiting for transfers between devices, on_device(): lax.ppermute(after(feats, anchor), 'tm', [(i, i + 1) for i in range(devic...  4.37 us
  transfers between devices with their start and end apart: 23, of which 11 were waited for; matrix products, arithmetic and copies ran while one was open for 2% of the time, Pallas kernels for 5%

profile of v4, /device:TPU:41, one launch (start us, length us, event | category | flops | bytes accessed | tf_op | source)
XLA Modules:
  0.0 138.5 jit_solution(6950276378538250103)
XLA Ops:
  0.0 2.7 %collective-permute-start = (bf16[128,640]{1,0:T(8,128)(2,1)}, bf16[128,640]{1,0:T(8,128)(2,1)S(1)}, u32[]{:S(2)}, u32[]{:S(2)}) collective-permute-start(bf16[128,640]{1,0:T(8,128)(2,1)} %bitcast.6), channel_id=1, source_target_pairs={{0,1},{1,0},{2,3},{3,2},{4,5},{5,4},{6,7},{7,6},{8,9},{9,8},{10,11... | collective-permute-start | bytes 491528 | tf_op jit(solution)/shard_map/ppermute | solution.py:56
  2.7 1.0 fusion.1
  3.8 0.2 collective-permute-done.core
  3.9 0.9 copy-done
  4.8 0.2 shard_map.64
  5.1 0.0 copy-start.4
  5.1 0.0 copy-start.5
  5.1 0.0 copy-start.1
  5.1 2.2 %collective-permute-start.1 = (bf16[2,128,160]{2,1,0:T(8,128)(2,1)S(1)}, bf16[2,128,160]{2,1,0:T(8,128)(2,1)S(1)}, u32[]{:S(2)}, u32[]{:S(2)}) collective-permute-start(bf16[2,128,160]{2,1,0:T(8,128)(2,1)S(1)} %get-tuple-element.37), channel_id=1, source_target_pairs={{0,2},{1,3},{2,0},{3,1},{4,6},{5,7},{6,4},{7,5},{8,10},{9,11},{10,... | collective-permute-start | bytes 245768 | tf_op jit(solution)/shard_map/ppermute | solution.py:56
  7.3 4.0 %collective-permute-start.2 = (bf16[48,1920]{1,0:T(8,128)(2,1)S(1)}, bf16[48,1920]{1,0:T(8,128)(2,1)S(1)}, u32[]{:S(2)}, u32[]{:S(2)}) collective-permute-start(bf16[48,1920]{1,0:T(8,128)(2,1)S(1)} %get-tuple-element.38), channel_id=1, source_target_pairs={{0,258},{1,259},{2,256},{3,257},{4,262},{5,263},{6,260},{7,261},{8... | collective-permute-start | bytes 552968 | tf_op jit(solution)/shard_map/ppermute | solution.py:273
  11.4 0.1 compare_convert_fusion.pool
  11.5 0.8 reshape.54.gain
  12.2 0.0 collective-permute-done.1.came
  12.2 3.6 %collective-permute-done.2 = bf16[48,1920]{1,0:T(8,128)(2,1)S(1)} collective-permute-done((bf16[48,1920]{1,0:T(8,128)(2,1)S(1)}, bf16[48,1920]{1,0:T(8,128)(2,1)S(1)}, u32[]{:S(2)}, u32[]{:S(2)}) %collective-permute-start.2) | collective-permute-done | bytes 184352 | tf_op jit(solution)/shard_map/ppermute | solution.py:273
  15.8 1.5 %copy-done.3 = bf16[9,160,640]{2,1,0:T(8,128)(2,1)S(1)} copy-done((bf16[9,160,640]{2,1,0:T(8,128)(2,1)S(1)}, bf16[9,160,640]{2,1,0:T(8,128)(2,1)}, u32[]{:S(2)}) %copy-start.3) | copy-done | bytes 1843224
  17.3 2.4 %shard_map.65 = (f32[2,128,640]{2,1,0:T(8,128)S(1)}, bf16[2,128,640]{2,1,0:T(8,128)(2,1)S(1)}) custom-call(s32[1]{0:T(128)} %bitcast.me_ref, bf16[2,128,160]{2,1,0:T(8,128)(2,1)S(1)} %get-tuple-element.36.mine, bf16[2,128,160]{2,1,0:T(8,128)(2,1)S(1)} %collective-permute-done.1.came, f32[4,160]{1,0:T(4,128)S(1)} %reshape.54.gain, ...), custom_call_target="tpu_custom_call" | custom-call | flops 943718400 | bytes 3095044 | tf_op jit(solution)/shard_map/pallas_call | solution.py:239
  19.7 3.0 %collective-permute-start.3 = (bf16[2,128,640]{2,1,0:T(8,128)(2,1)S(1)}, bf16[2,128,640]{2,1,0:T(8,128)(2,1)S(1)}, u32[]{:S(2)}, u32[]{:S(2)}) collective-permute-start(bf16[2,128,640]{2,1,0:T(8,128)(2,1)S(1)} %get-tuple-element.41), channel_id=1, source_target_pairs={{0,1},{1,0},{2,3},{3,2},{4,5},{5,4},{6,7},{7,6},{8,9},{9,8},{10,11... | collective-permute-start | bytes 983048 | tf_op jit(solution)/shard_map/ppermute | solution.py:56
  22.8 0.0 copy-done.2
  22.8 3.4 %collective-permute-start.4 = (bf16[48,1920]{1,0:T(8,128)(2,1)S(1)}, bf16[48,1920]{1,0:T(8,128)(2,1)S(1)}, u32[]{:S(2)}, u32[]{:S(2)}) collective-permute-start(bf16[48,1920]{1,0:T(8,128)(2,1)S(1)} %get-tuple-element.42), channel_id=1, source_target_pairs={{0,258},{1,259},{2,256},{3,257},{4,262},{5,263},{6,260},{7,261},{8... | collective-permute-start | bytes 552968 | tf_op jit(solution)/shard_map/ppermute | solution.py:273
  26.2 0.0 collective-permute-done.3.core
  26.2 4.7 %collective-permute-done.4 = bf16[48,1920]{1,0:T(8,128)(2,1)S(1)} collective-permute-done((bf16[48,1920]{1,0:T(8,128)(2,1)S(1)}, bf16[48,1920]{1,0:T(8,128)(2,1)S(1)}, u32[]{:S(2)}, u32[]{:S(2)}) %collective-permute-start.4) | collective-permute-done | bytes 184352 | tf_op jit(solution)/shard_map/ppermute | solution.py:273
  31.0 3.4 %collective-permute-start.6 = (bf16[64,1920]{1,0:T(8,128)(2,1)S(1)}, bf16[64,1920]{1,0:T(8,128)(2,1)S(1)}, u32[]{:S(2)}, u32[]{:S(2)}) collective-permute-start(bf16[64,1920]{1,0:T(8,128)(2,1)S(1)} %slice.19), channel_id=1, source_target_pairs={{0,258},{1,259},{2,256},{3,257},{4,262},{5,263},{6,260},{7,261},{8... | collective-permute-start | bytes 737288 | tf_op jit(solution)/shard_map/ppermute | solution.py:273
  34.3 5.4 %collective-permute-start.5 = (bf16[128,640]{1,0:T(8,128)(2,1)S(1)}, bf16[128,640]{1,0:T(8,128)(2,1)S(1)}, u32[]{:S(2)}, u32[]{:S(2)}) collective-permute-start(bf16[128,640]{1,0:T(8,128)(2,1)S(1)} %fusion), channel_id=1, source_target_pairs={{0,2},{1,3},{2,0},{3,1},{4,6},{5,7},{6,4},{7,5},{8,10},{9,11},{10,... | collective-permute-start | bytes 491528 | tf_op jit(solution)/shard_map/ppermute | solution.py:56
  39.7 0.0 copy-done.4
  39.8 0.0 copy-done.5
  39.8 3.4 %collective-permute-done.5.chip = bf16[128,640]{1,0:T(8,128)(2,1)S(1)} collective-permute-done((bf16[128,640]{1,0:T(8,128)(2,1)S(1)}, bf16[128,640]{1,0:T(8,128)(2,1)S(1)}, u32[]{:S(2)}, u32[]{:S(2)}) %collective-permute-start.5) | collective-permute-done | bytes 163872 | tf_op jit(solution)/shard_map/ppermute | solution.py:56
  43.2 0.0 collective-permute-done.6
  43.2 0.0 copy-done.1
  43.2 0.3 shard_map.66
  43.5 0.7 collective-permute-start.7
  44.2 0.0 collective-permute-done.7
  44.2 3.1 %collective-permute-start.9 = (bf16[128,640]{1,0:T(8,128)(2,1)S(1)}, bf16[128,640]{1,0:T(8,128)(2,1)S(1)}, u32[]{:S(2)}, u32[]{:S(2)}) collective-permute-start(bf16[128,640]{1,0:T(8,128)(2,1)S(1)} %get-tuple-element.56.own), channel_id=1, source_target_pairs={{0,4},{4,8},{8,12},{12,16},{16,20},{20,24},{24,28},{28,32},{32,36}... | collective-permute-start | bytes 491528 | tf_op jit(solution)/shard_map/ppermute | solution.py:308
  47.4 0.7 collective-permute-start.8
  48.0 4.4 %collective-permute-done.9 = bf16[128,640]{1,0:T(8,128)(2,1)S(1)} collective-permute-done((bf16[128,640]{1,0:T(8,128)(2,1)S(1)}, bf16[128,640]{1,0:T(8,128)(2,1)S(1)}, u32[]{:S(2)}, u32[]{:S(2)}) %collective-permute-start.9) | collective-permute-done | bytes 163872 | tf_op jit(solution)/shard_map/ppermute | solution.py:308
  52.4 0.0 collective-permute-done.8
  52.5 0.7 collective-permute-start.10
  53.2 4.7 %collective-permute-start.11 = (bf16[128,640]{1,0:T(8,128)(2,1)S(1)}, bf16[128,640]{1,0:T(8,128)(2,1)S(1)}, u32[]{:S(2)}, u32[]{:S(2)}) collective-permute-start(bf16[128,640]{1,0:T(8,128)(2,1)S(1)} %broadcast_select_fusion.p0), channel_id=1, source_target_pairs={{0,1},{1,0},{2,3},{3,2},{4,5},{5,4},{6,7},{7,6},{8,9},{9,8},{10,11... | collective-permute-start | bytes 491528 | tf_op jit(solution)/shard_map/ppermute | solution.py:56
  57.9 0.0 collective-permute-done.10
  58.0 0.9 collective-permute-done.11.p1
  58.9 2.3 %collective-permute-start.14 = (bf16[160,1920]{1,0:T(8,128)(2,1)S(1)}, bf16[160,1920]{1,0:T(8,128)(2,1)S(1)}, u32[]{:S(2)}, u32[]{:S(2)}) collective-permute-start(bf16[160,1920]{1,0:T(8,128)(2,1)S(1)} %copy-done.2), channel_id=1, source_target_pairs={{0,1},{1,0},{2,3},{3,2},{4,5},{5,4},{6,7},{7,6},{8,9},{9,8},{10,11... | collective-permute-start | bytes 1843208 | tf_op jit(solution)/shard_map/ppermute | solution.py:56
  61.2 3.4 %collective-permute-start.13 = (bf16[128,640]{1,0:T(8,128)(2,1)S(1)}, bf16[128,640]{1,0:T(8,128)(2,1)S(1)}, u32[]{:S(2)}, u32[]{:S(2)}) collective-permute-start(bf16[128,640]{1,0:T(8,128)(2,1)S(1)} %broadcast_select_fusion.p0), channel_id=1, source_target_pairs={{0,2},{1,3},{2,0},{3,1},{4,6},{5,7},{6,4},{7,5},{8,10},{9,11},{10,... | collective-permute-start | bytes 491528 | tf_op jit(solution)/shard_map/ppermute | solution.py:56
  64.6 0.7 collective-permute-start.12
  65.3 0.0 collective-permute-done.12
  65.4 3.4 %collective-permute-done.13.p2 = bf16[128,640]{1,0:T(8,128)(2,1)S(1)} collective-permute-done((bf16[128,640]{1,0:T(8,128)(2,1)S(1)}, bf16[128,640]{1,0:T(8,128)(2,1)S(1)}, u32[]{:S(2)}, u32[]{:S(2)}) %collective-permute-start.13) | collective-permute-done | bytes 163872 | tf_op jit(solution)/shard_map/ppermute | solution.py:56
  68.8 0.0 collective-permute-done.14.w1
  68.8 0.7 collective-permute-start.15
  69.4 18.1 %collective-permute-start.16 = (bf16[128,640]{1,0:T(8,128)(2,1)S(1)}, bf16[128,640]{1,0:T(8,128)(2,1)S(1)}, u32[]{:S(2)}, u32[]{:S(2)}) collective-permute-start(bf16[128,640]{1,0:T(8,128)(2,1)S(1)} %collective-permute-done.13.p2), channel_id=1, source_target_pairs={{0,1},{1,0},{2,3},{3,2},{4,5},{5,4},{6,7},{7,6},{8,9},{9,8},{10,11... | collective-permute-start | bytes 491528 | tf_op jit(solution)/shard_map/ppermute | solution.py:56
  87.6 0.0 collective-permute-done.15
  87.6 0.9 collective-permute-done.16.p3
  88.5 2.3 %collective-permute-start.18 = (bf16[160,1920]{1,0:T(8,128)(2,1)S(1)}, bf16[160,1920]{1,0:T(8,128)(2,1)S(1)}, u32[]{:S(2)}, u32[]{:S(2)}) collective-permute-start(bf16[160,1920]{1,0:T(8,128)(2,1)S(1)} %constant_dynamic-update-slice_fusion.w2), channel_id=1, source_target_pairs={{0,1},{1,0},{2,3},{3,2},{4,5},{5,4},{6,7},{7,6},{8,9},{9,8},{10,11... | collective-permute-start | bytes 1843208 | tf_op jit(solution)/shard_map/ppermute | solution.py:56
  90.8 0.7 collective-permute-start.17
  91.5 0.0 collective-permute-done.17
  91.6 0.9 collective-permute-done.18.w3
  92.5 1.3 collective-permute-start.19
  93.8 3.6 %shard_map.67 = (bf16[128,640]{1,0:T(8,128)(2,1)S(1)}, f32[128,8]{1,0:T(8,128)S(1)}, f32[128,8]{1,0:T(8,128)S(1)}, f32[128,640]{1,0:T(8,128)S(1)}, bf16[640,1920]{1,0:T(8,128)(2,1)S(1)}) custom-call(s32[1]{0:T(128)} %bitcast.me_ref, bf16[128,640]{1,0:T(8,128)(2,1)S(1)} %get-tuple-element.56.own, bf16[128,640]{1,0:T(8,128)(2,1)S(1)} %broadcast_select_fusion.p0, ...), custom_call_target="tpu_custom_call" | custom-call | flops 1006632960 | bytes 6234116 | tf_op jit(solution)/shard_map/pallas_call | solution.py:239
  97.3 25.9 %collective-permute-done.19 = bf16[128,640]{1,0:T(8,128)(2,1)S(1)} collective-permute-done((bf16[128,640]{1,0:T(8,128)(2,1)S(1)}, bf16[128,640]{1,0:T(8,128)(2,1)S(1)}, u32[]{:S(2)}, u32[]{:S(2)}) %collective-permute-start.19) | collective-permute-done | bytes 163872 | tf_op jit(solution)/shard_map/ppermute | solution.py:304
  123.3 1.9 %collective-permute-start.20 = (bf16[128,640]{1,0:T(8,128)(2,1)S(1)}, bf16[128,640]{1,0:T(8,128)(2,1)S(1)}, u32[]{:S(2)}, u32[]{:S(2)}) collective-permute-start(bf16[128,640]{1,0:T(8,128)(2,1)S(1)} %add.41.a0), channel_id=1, source_target_pairs={{0,2},{1,3},{2,0},{3,1},{4,6},{5,7},{6,4},{7,5},{8,10},{9,11},{10,... | collective-permute-start | bytes 491528 | tf_op jit(solution)/shard_map/ppermute | solution.py:56
  125.2 1.9 %collective-permute-start.22 = (bf16[128,640]{1,0:T(8,128)(2,1)S(1)}, bf16[128,640]{1,0:T(8,128)(2,1)S(1)}, u32[]{:S(2)}, u32[]{:S(2)}) collective-permute-start(bf16[128,640]{1,0:T(8,128)(2,1)S(1)} %add.41.a0), channel_id=1, source_target_pairs={{0,1},{1,0},{2,3},{3,2},{4,5},{5,4},{6,7},{7,6},{8,9},{9,8},{10,11... | collective-permute-start | bytes 491528 | tf_op jit(solution)/shard_map/ppermute | solution.py:56
  127.2 2.2 %collective-permute-done.20.a0 = bf16[128,640]{1,0:T(8,128)(2,1)S(1)} collective-permute-done((bf16[128,640]{1,0:T(8,128)(2,1)S(1)}, bf16[128,640]{1,0:T(8,128)(2,1)S(1)}, u32[]{:S(2)}, u32[]{:S(2)}) %collective-permute-start.20) | collective-permute-done | bytes 163872 | tf_op jit(solution)/shard_map/ppermute | solution.py:56
  129.4 2.1 %collective-permute-start.21 = (bf16[128,640]{1,0:T(8,128)(2,1)S(1)}, bf16[128,640]{1,0:T(8,128)(2,1)S(1)}, u32[]{:S(2)}, u32[]{:S(2)}) collective-permute-start(bf16[128,640]{1,0:T(8,128)(2,1)S(1)} %collective-permute-done.20.a0), channel_id=1, source_target_pairs={{0,1},{1,0},{2,3},{3,2},{4,5},{5,4},{6,7},{7,6},{8,9},{9,8},{10,11... | collective-permute-start | bytes 491528 | tf_op jit(solution)/shard_map/ppermute | solution.py:56
  131.5 0.0 collective-permute-done.22.a1
  131.5 2.9 %shard_map.68 = (f32[128,8]{1,0:T(8,128)S(1)}, f32[128,8]{1,0:T(8,128)S(1)}, f32[128,640]{1,0:T(8,128)S(1)}) custom-call(bf16[128,640]{1,0:T(8,128)(2,1)S(1)} %get-tuple-element.57.query, bf16[128,640]{1,0:T(8,128)(2,1)S(1)} %add.41.a0, bf16[128,640]{1,0:T(8,128)(2,1)S(1)} %collective-permute-done.22.a1, bf16[640,1920]{1,0:T(8,128)(2,1)S(1)} %get-tuple-element.60.weight, ...), custom_call_target="tpu_custom_call" | custom-call | flops 503316480 | bytes 3620864 | tf_op jit(solution)/shard_map/pallas_call | solution.py:239
  134.4 0.0 collective-permute-done.21.a1
  134.4 4.1 %shard_map.69 = bf16[128,640]{1,0:T(8,128)(2,1)} custom-call(bf16[128,640]{1,0:T(8,128)(2,1)S(1)} %get-tuple-element.57.query, bf16[128,640]{1,0:T(8,128)(2,1)S(1)} %collective-permute-done.20.a0, bf16[128,640]{1,0:T(8,128)(2,1)S(1)} %collective-permute-done.21.a1, bf16[640,1920]{1,0:T(8,128)(2,1)S(1)} %get-tuple-element.60.weight, ...), custom_call_target="tpu_custom_call" | custom-call | flops 503316480 | bytes 3612672 | tf_op jit(solution)/shard_map/pallas_call | solution.py:239
  (20 shorter events, 0.5 us)
Async XLA Ops:
  0.0 22.8 %copy-start.2 = (bf16[160,1920]{1,0:T(8,128)(2,1)S(1)}, bf16[160,1920]{1,0:T(8,128)(2,1)}, u32[]{:S(2)}) copy-start(bf16[160,1920]{1,0:T(8,128)(2,1)} %w0.1) | copy-start | bytes 1843204
  0.0 3.9 %collective-permute-start = (bf16[128,640]{1,0:T(8,128)(2,1)}, bf16[128,640]{1,0:T(8,128)(2,1)S(1)}, u32[]{:S(2)}, u32[]{:S(2)}) collective-permute-start(bf16[128,640]{1,0:T(8,128)(2,1)} %bitcast.6), channel_id=1, source_target_pairs={{0,1},{1,0},{2,3},{3,2},{4,5},{5,4},{6,7},{7,6},{8,9},{9,8},{10,11... | collective-permute-start | bytes 491528 | tf_op jit(solution)/shard_map/ppermute | solution.py:56
  3.9 0.9 copy-start
  5.1 34.7 %copy-start.4 = (f32[640]{0:T(1024)S(1)}, f32[640]{0:T(1024)}, u32[]{:S(2)}) copy-start(f32[640]{0:T(1024)} %param.9) | copy-start | bytes 7684
  5.1 34.7 %copy-start.5 = (f32[640]{0:T(1024)S(1)}, f32[640]{0:T(1024)}, u32[]{:S(2)}) copy-start(f32[640]{0:T(1024)} %param.10) | copy-start | bytes 7684
  5.1 38.1 %copy-start.1 = (bf16[1,4,32,640]{3,2,1,0:T(8,128)(2,1)S(1)}, bf16[1,4,32,640]{3,2,1,0:T(8,128)(2,1)}, u32[]{:S(2)}) copy-start(bf16[1,4,32,640]{3,2,1,0:T(8,128)(2,1)} %param.6) | copy-start | bytes 491524
  5.1 7.1 %collective-permute-start.1 = (bf16[2,128,160]{2,1,0:T(8,128)(2,1)S(1)}, bf16[2,128,160]{2,1,0:T(8,128)(2,1)S(1)}, u32[]{:S(2)}, u32[]{:S(2)}) collective-permute-start(bf16[2,128,160]{2,1,0:T(8,128)(2,1)S(1)} %get-tuple-element.37), channel_id=1, source_target_pairs={{0,2},{1,3},{2,0},{3,1},{4,6},{5,7},{6,4},{7,5},{8,10},{9,11},{10,... | collective-permute-start | bytes 245768 | tf_op jit(solution)/shard_map/ppermute | solution.py:56
  7.3 8.5 %collective-permute-start.2 = (bf16[48,1920]{1,0:T(8,128)(2,1)S(1)}, bf16[48,1920]{1,0:T(8,128)(2,1)S(1)}, u32[]{:S(2)}, u32[]{:S(2)}) collective-permute-start(bf16[48,1920]{1,0:T(8,128)(2,1)S(1)} %get-tuple-element.38), channel_id=1, source_target_pairs={{0,258},{1,259},{2,256},{3,257},{4,262},{5,263},{6,260},{7,261},{8... | collective-permute-start | bytes 552968 | tf_op jit(solution)/shard_map/ppermute | solution.py:273
  15.8 1.5 %copy-start.3 = (bf16[9,160,640]{2,1,0:T(8,128)(2,1)S(1)}, bf16[9,160,640]{2,1,0:T(8,128)(2,1)}, u32[]{:S(2)}) copy-start(bf16[9,160,640]{2,1,0:T(8,128)(2,1)} %param.8) | copy-start | bytes 5529604
  19.7 6.4 %collective-permute-start.3 = (bf16[2,128,640]{2,1,0:T(8,128)(2,1)S(1)}, bf16[2,128,640]{2,1,0:T(8,128)(2,1)S(1)}, u32[]{:S(2)}, u32[]{:S(2)}) collective-permute-start(bf16[2,128,640]{2,1,0:T(8,128)(2,1)S(1)} %get-tuple-element.41), channel_id=1, source_target_pairs={{0,1},{1,0},{2,3},{3,2},{4,5},{5,4},{6,7},{7,6},{8,9},{9,8},{10,11... | collective-permute-start | bytes 983048 | tf_op jit(solution)/shard_map/ppermute | solution.py:56
  22.8 8.2 %collective-permute-start.4 = (bf16[48,1920]{1,0:T(8,128)(2,1)S(1)}, bf16[48,1920]{1,0:T(8,128)(2,1)S(1)}, u32[]{:S(2)}, u32[]{:S(2)}) collective-permute-start(bf16[48,1920]{1,0:T(8,128)(2,1)S(1)} %get-tuple-element.42), channel_id=1, source_target_pairs={{0,258},{1,259},{2,256},{3,257},{4,262},{5,263},{6,260},{7,261},{8... | collective-permute-start | bytes 552968 | tf_op jit(solution)/shard_map/ppermute | solution.py:273
  31.0 12.2 %collective-permute-start.6 = (bf16[64,1920]{1,0:T(8,128)(2,1)S(1)}, bf16[64,1920]{1,0:T(8,128)(2,1)S(1)}, u32[]{:S(2)}, u32[]{:S(2)}) collective-permute-start(bf16[64,1920]{1,0:T(8,128)(2,1)S(1)} %slice.19), channel_id=1, source_target_pairs={{0,258},{1,259},{2,256},{3,257},{4,262},{5,263},{6,260},{7,261},{8... | collective-permute-start | bytes 737288 | tf_op jit(solution)/shard_map/ppermute | solution.py:273
  34.3 8.9 %collective-permute-start.5 = (bf16[128,640]{1,0:T(8,128)(2,1)S(1)}, bf16[128,640]{1,0:T(8,128)(2,1)S(1)}, u32[]{:S(2)}, u32[]{:S(2)}) collective-permute-start(bf16[128,640]{1,0:T(8,128)(2,1)S(1)} %fusion), channel_id=1, source_target_pairs={{0,2},{1,3},{2,0},{3,1},{4,6},{5,7},{6,4},{7,5},{8,10},{9,11},{10,... | collective-permute-start | bytes 491528 | tf_op jit(solution)/shard_map/ppermute | solution.py:56
  43.5 0.7 collective-permute-start.7
  44.2 8.2 %collective-permute-start.9 = (bf16[128,640]{1,0:T(8,128)(2,1)S(1)}, bf16[128,640]{1,0:T(8,128)(2,1)S(1)}, u32[]{:S(2)}, u32[]{:S(2)}) collective-permute-start(bf16[128,640]{1,0:T(8,128)(2,1)S(1)} %get-tuple-element.56.own), channel_id=1, source_target_pairs={{0,4},{4,8},{8,12},{12,16},{16,20},{20,24},{24,28},{28,32},{32,36}... | collective-permute-start | bytes 491528 | tf_op jit(solution)/shard_map/ppermute | solution.py:308
  47.4 5.1 %collective-permute-start.8 = (bf16[128,640]{1,0:T(8,128)(2,1)S(1)}, bf16[128,640]{1,0:T(8,128)(2,1)S(1)}, u32[]{:S(2)}, u32[]{:S(2)}) collective-permute-start(bf16[128,640]{1,0:T(8,128)(2,1)S(1)} %fusion.2), channel_id=1, source_target_pairs={{0,64},{2,66},{128,192},{130,194},{1,5},{3,7},{9,13},{11,15}} | collective-permute-start | bytes 491528 | tf_op jit(solution)/shard_map/ppermute | solution.py:304
  52.5 5.4 %collective-permute-start.10 = (bf16[128,640]{1,0:T(8,128)(2,1)S(1)}, bf16[128,640]{1,0:T(8,128)(2,1)S(1)}, u32[]{:S(2)}, u32[]{:S(2)}) collective-permute-start(bf16[128,640]{1,0:T(8,128)(2,1)S(1)} %add.36), channel_id=1, source_target_pairs={{0,32},{2,34},{128,160},{130,162},{64,96},{66,98},{192,224},{194,2... | collective-permute-start | bytes 491528 | tf_op jit(solution)/shard_map/ppermute | solution.py:304
  53.2 5.8 %collective-permute-start.11 = (bf16[128,640]{1,0:T(8,128)(2,1)S(1)}, bf16[128,640]{1,0:T(8,128)(2,1)S(1)}, u32[]{:S(2)}, u32[]{:S(2)}) collective-permute-start(bf16[128,640]{1,0:T(8,128)(2,1)S(1)} %broadcast_select_fusion.p0), channel_id=1, source_target_pairs={{0,1},{1,0},{2,3},{3,2},{4,5},{5,4},{6,7},{7,6},{8,9},{9,8},{10,11... | collective-permute-start | bytes 491528 | tf_op jit(solution)/shard_map/ppermute | solution.py:56
  58.9 9.8 %collective-permute-start.14 = (bf16[160,1920]{1,0:T(8,128)(2,1)S(1)}, bf16[160,1920]{1,0:T(8,128)(2,1)S(1)}, u32[]{:S(2)}, u32[]{:S(2)}) collective-permute-start(bf16[160,1920]{1,0:T(8,128)(2,1)S(1)} %copy-done.2), channel_id=1, source_target_pairs={{0,1},{1,0},{2,3},{3,2},{4,5},{5,4},{6,7},{7,6},{8,9},{9,8},{10,11... | collective-permute-start | bytes 1843208 | tf_op jit(solution)/shard_map/ppermute | solution.py:56
  61.2 7.5 %collective-permute-start.13 = (bf16[128,640]{1,0:T(8,128)(2,1)S(1)}, bf16[128,640]{1,0:T(8,128)(2,1)S(1)}, u32[]{:S(2)}, u32[]{:S(2)}) collective-permute-start(bf16[128,640]{1,0:T(8,128)(2,1)S(1)} %broadcast_select_fusion.p0), channel_id=1, source_target_pairs={{0,2},{1,3},{2,0},{3,1},{4,6},{5,7},{6,4},{7,5},{8,10},{9,11},{10,... | collective-permute-start | bytes 491528 | tf_op jit(solution)/shard_map/ppermute | solution.py:56
  64.6 0.7 collective-permute-start.12
  68.8 18.8 %collective-permute-start.15 = (bf16[128,640]{1,0:T(8,128)(2,1)S(1)}, bf16[128,640]{1,0:T(8,128)(2,1)S(1)}, u32[]{:S(2)}, u32[]{:S(2)}) collective-permute-start(bf16[128,640]{1,0:T(8,128)(2,1)S(1)} %add.38), channel_id=1, source_target_pairs={{0,8},{2,10},{128,136},{130,138},{64,72},{66,74},{192,200},{194,20... | collective-permute-start | bytes 491528 | tf_op jit(solution)/shard_map/ppermute | solution.py:304
  69.4 19.1 %collective-permute-start.16 = (bf16[128,640]{1,0:T(8,128)(2,1)S(1)}, bf16[128,640]{1,0:T(8,128)(2,1)S(1)}, u32[]{:S(2)}, u32[]{:S(2)}) collective-permute-start(bf16[128,640]{1,0:T(8,128)(2,1)S(1)} %collective-permute-done.13.p2), channel_id=1, source_target_pairs={{0,1},{1,0},{2,3},{3,2},{4,5},{5,4},{6,7},{7,6},{8,9},{9,8},{10,11... | collective-permute-start | bytes 491528 | tf_op jit(solution)/shard_map/ppermute | solution.py:56
  88.5 3.9 %collective-permute-start.18 = (bf16[160,1920]{1,0:T(8,128)(2,1)S(1)}, bf16[160,1920]{1,0:T(8,128)(2,1)S(1)}, u32[]{:S(2)}, u32[]{:S(2)}) collective-permute-start(bf16[160,1920]{1,0:T(8,128)(2,1)S(1)} %constant_dynamic-update-slice_fusion.w2), channel_id=1, source_target_pairs={{0,1},{1,0},{2,3},{3,2},{4,5},{5,4},{6,7},{7,6},{8,9},{9,8},{10,11... | collective-permute-start | bytes 1843208 | tf_op jit(solution)/shard_map/ppermute | solution.py:56
  90.8 0.7 collective-permute-start.17
  92.5 30.8 %collective-permute-start.19 = (bf16[128,640]{1,0:T(8,128)(2,1)S(1)}, bf16[128,640]{1,0:T(8,128)(2,1)S(1)}, u32[]{:S(2)}, u32[]{:S(2)}) collective-permute-start(bf16[128,640]{1,0:T(8,128)(2,1)S(1)} %add.40), channel_id=1, source_target_pairs={{0,256},{2,258},{128,384},{130,386},{64,320},{66,322},{192,448},{1... | collective-permute-start | bytes 491528 | tf_op jit(solution)/shard_map/ppermute | solution.py:304
  123.3 6.1 %collective-permute-start.20 = (bf16[128,640]{1,0:T(8,128)(2,1)S(1)}, bf16[128,640]{1,0:T(8,128)(2,1)S(1)}, u32[]{:S(2)}, u32[]{:S(2)}) collective-permute-start(bf16[128,640]{1,0:T(8,128)(2,1)S(1)} %add.41.a0), channel_id=1, source_target_pairs={{0,2},{1,3},{2,0},{3,1},{4,6},{5,7},{6,4},{7,5},{8,10},{9,11},{10,... | collective-permute-start | bytes 491528 | tf_op jit(solution)/shard_map/ppermute | solution.py:56
  125.2 6.2 %collective-permute-start.22 = (bf16[128,640]{1,0:T(8,128)(2,1)S(1)}, bf16[128,640]{1,0:T(8,128)(2,1)S(1)}, u32[]{:S(2)}, u32[]{:S(2)}) collective-permute-start(bf16[128,640]{1,0:T(8,128)(2,1)S(1)} %add.41.a0), channel_id=1, source_target_pairs={{0,1},{1,0},{2,3},{3,2},{4,5},{5,4},{6,7},{7,6},{8,9},{9,8},{10,11... | collective-permute-start | bytes 491528 | tf_op jit(solution)/shard_map/ppermute | solution.py:56
  129.4 5.0 %collective-permute-start.21 = (bf16[128,640]{1,0:T(8,128)(2,1)S(1)}, bf16[128,640]{1,0:T(8,128)(2,1)S(1)}, u32[]{:S(2)}, u32[]{:S(2)}) collective-permute-start(bf16[128,640]{1,0:T(8,128)(2,1)S(1)} %collective-permute-done.20.a0), channel_id=1, source_target_pairs={{0,1},{1,0},{2,3},{3,2},{4,5},{5,4},{6,7},{7,6},{8,9},{9,8},{10,11... | collective-permute-start | bytes 491528 | tf_op jit(solution)/shard_map/ppermute | solution.py:56

commit v5 on v4

--- a/solution.py
+++ b/solution.py
@@ -10,45 +10,16 @@
 GROUPS = 32
 EPS = 1e-05
 BOTH = ("tm", "rows")
+HBM = pl.BlockSpec(memory_space=pltpu.HBM)
 VMEM = pl.BlockSpec(memory_space=pltpu.VMEM)
 SMEM = pl.BlockSpec(memory_space=pltpu.SMEM)
 
 
 def tree_levels(devices):
-    if devices == 128:
-        z = [("z", s) for s in (8, 4, 2, 1)]
-        x = [("x", s) for s in (2, 1)]
-        y = [("y", 1)]
-        size = {"y": 2, "z": 16, "x": 4}
-        orders = (z + x + y, x + y + z)
-
-        def index(at, sign):
-            return (at["y"] * 16 + (sign * at["z"]) % 16) * 4 + at["x"]
-
-    else:
-        steps = []
-        while 2 ** len(steps) < devices:
-            steps.insert(0, ("z", 2 ** len(steps)))
-        size = {"z": devices}
-        orders = (steps, steps)
-
-        def index(at, sign):
-            return at["z"]
-
-    levels = [[] for _ in orders[0]]
-    for core, order in enumerate(orders):
-        sign = 1 - 2 * core
-        known = [{axis: 0 for axis in size}]
-        for level, (axis, step) in enumerate(order):
-            fresh = []
-            for at in known:
-                to = dict(at)
-                to[axis] = at[axis] + step
-                fresh.append(to)
-                for chip in range(2):
-                    row = chip * 2 + core
-                    levels[level].append((index(at, sign) * 4 + row, index(to, sign) * 4 + row))
-            known = known + fresh
+    levels, step = [], devices // 2
+    while step:
+        levels.append([(tm, tm + step) for tm in range(0, devices, 2 * step)])
+        step //= 2
     return levels
 
 
@@ -76,7 +47,11 @@
                     out[at] = source[:, block * share : (block + 1) * share]
 
 
-def conv_kernel(width, me_ref, mine, came, gain, weight, pool, keep, send, x_ref, taps, acc):
+def conv_kernel(
+    width, me_ref, mine, came, gain, weight_hbm, pool, keep, send, x_ref, taps, acc, weight, landed
+):
+    load = pltpu.make_async_copy(weight_hbm, weight, landed)
+    load.start()
     me = me_ref[0]
     blocks = (mine[0], mine[1], came[0], came[1])
     cells, chans = x_ref.shape
@@ -108,6 +83,7 @@
     taps[width : width + cells, :] = jnp.concatenate([before, act, after], axis=1).astype(
         jnp.bfloat16
     )
+    load.wait()
     acc[...] = sum(
         jnp.dot(
             taps[row * width : row * width + cells, :],
@@ -231,11 +207,13 @@
     restyled[...] = (residual[...].astype(jnp.float32) + mixed[...]).astype(jnp.bfloat16)
 
 
-def call(kernel, outs, ins, scratch=(), flops=0, limit=24):
+def call(kernel, outs, ins, scratch=(), flops=0, limit=24, hbm=()):
     moved = sum(a.size * a.dtype.itemsize for a in ins) + sum(
         o.size * o.dtype.itemsize for o in outs
     )
-    specs = [SMEM if a.dtype == jnp.int32 else VMEM for a in ins]
+    specs = [
+        HBM if i in hbm else SMEM if a.dtype == jnp.int32 else VMEM for i, a in enumerate(ins)
+    ]
     return pl.pallas_call(
         kernel,
         out_shape=list(outs),
@@ -263,19 +241,7 @@
         [shape((2, part, share), bf16)] * 2,
         [me.reshape(1), lat, to_rows(lat, 1)],
     )
-    devices = lax.axis_size("tm")
-    far = [
-        (tm * 4 + row, (tm + devices // 2) % devices * 4 + (row ^ 2))
-        for tm in range(devices)
-        for row in range(4)
-    ]
-    cut = share // 3 // 16 * 16
-    chunk = lambda low, high, *done: lax.ppermute(
-        after(qkv_weight[low:high], *done), BOTH, far
-    )
-    chunk0 = chunk(0, cut, away)
-    came = after(to_rows(away, 2), chunk0)
-    chunk1 = chunk(cut, 2 * cut, came)
+    came = to_rows(away, 2)
     group = jnp.arange(share) // (chans // GROUPS)
     pool = (group[:, None] == group[None, :]).astype(f32)
     keep, send = call(
@@ -286,38 +252,50 @@
             pltpu.VMEM((cells, share), f32),
             pltpu.VMEM((cells + 2 * width, 3 * share), bf16),
             pltpu.VMEM((cells, chans), f32),
+            pltpu.VMEM((3, 3 * share, chans), bf16),
+            pltpu.SemaphoreType.DMA,
         ],
+        hbm=(4,),
         flops=2 * cells * 9 * share * chans,
     )
     core = to_rows(send, 1)
-    half = after((keep[1] + core[1].astype(f32)).astype(bf16), chunk1)
+    half = (keep[1] + core[1].astype(f32)).astype(bf16)
     chip = to_rows(half, 2)
-    chunk2 = chunk(2 * cut, share, half)
-    chip = after(chip, chunk2)
     residual, feats = call(
         norm_kernel,
         [shape((part, chans), bf16)] * 2,
         [lat, keep, core, chip, conv_bias.reshape(1, chans), ln_gain.reshape(1, chans)],
     )
 
+    devices = lax.axis_size("tm")
+    far = [
+        (tm * 4 + row, (tm + devices // 2) % devices * 4 + (row ^ 2))
+        for tm in range(devices)
+        for row in range(4)
+    ]
+    cut = share // 3 // 16 * 16
+    chunk = lambda low, high, done: lax.ppermute(after(qkv_weight[low:high], done), BOTH, far)
     routes = tree_levels(devices)
-    tree = lambda level, x: x + lax.ppermute(x, BOTH, routes[level])
     routes = routes + [[]] * (7 - len(routes))
-    weight_chip = jnp.concatenate([chunk0, chunk1, chunk2], axis=0)
+    tree = lambda level, x: x + lax.ppermute(x, "tm", routes[level])
     anchor = tree(0, jnp.where(first, feats, jnp.zeros_like(feats)))
     prev = lax.ppermute(after(feats, anchor), "tm", [(i, i + 1) for i in range(devices - 1)])
+    chunk0 = chunk(0, cut, anchor)
     anchor = tree(1, anchor)
     prev = jnp.where(first, feats, prev)
-    anchor = after(anchor, prev)
-    prev_core = to_rows(prev, 1)
-    prev_chip = to_rows(prev, 2)
-    anchor = after(tree(2, anchor), prev_core)
+    anchor = after(anchor, prev, chunk0)
+    chunk1 = chunk(cut, 2 * cut, anchor)
+    prev_core = to_rows(after(prev, anchor), 1)
+    anchor = after(tree(2, anchor), prev_core, chunk1)
+    chunk2 = chunk(2 * cut, share, anchor)
     weight_core = to_rows(after(qkv_weight, anchor), 1)
-    anchor = after(tree(3, anchor), prev_chip, weight_core)
+    anchor = after(tree(3, anchor), weight_core, chunk2)
+    prev_chip = to_rows(after(prev, anchor), 2)
+    weight_chip = jnp.concatenate([chunk0, chunk1, chunk2], axis=0)
+    weight_last = to_rows(after(weight_chip, anchor), 1)
+    anchor = after(tree(4, anchor), prev_chip, weight_last)
     prev_last = to_rows(after(prev_chip, anchor), 1)
-    anchor = after(tree(4, anchor), prev_last)
-    weight_last = to_rows(after(weight_chip, anchor), 1)
-    anchor = after(tree(5, anchor), weight_last)
+    anchor = after(tree(5, anchor), prev_last)
     prev = (prev, prev_core, prev_chip, prev_last)
     qkv = [qkv_weight, weight_core, weight_chip, weight_last]
 

time: 139 us -> 121 us (0.87)
  the two profiles are of different devices: /device:TPU:41 before, /device:TPU:1 now
where the time goes in v5:
time: 121 us; the launch traced here: 120 us
  starting transfers between devices  71.6 us (59%)
  waiting for transfers between devices  30.7 us (25%)
  Pallas kernels  13.7 us (11%)
  local copies, waits for them, and re-layouts  3.32 us (3%)
    ppermute x12, starting transfers between devices, to_rows(): return lax.ppermute(x, 'rows', [(i, i ^ flip) for i in range(4)])  42 us
    ppermute x12, waiting for transfers between devices, to_rows(): return lax.ppermute(x, 'rows', [(i, i ^ flip) for i in range(4)])  18.9 us
    ppermute x7, starting transfers between devices, on_device(): tree = lambda level, x: x + lax.ppermute(x, 'tm', routes[level])  14.7 us
    pallas_call x6, Pallas kernels, call(): pl.pallas_call(kernel, out_shape=list(outs), in_specs=specs, out_specs=[V...  13.7 us
    ppermute x3, starting transfers between devices, on_device(): lax.ppermute(after(qkv_weight[low:high], done), BOTH, far)  13.7 us
    ppermute x7, waiting for transfers between devices, on_device(): tree = lambda level, x: x + lax.ppermute(x, 'tm', routes[level])  8.51 us
    ppermute x3, waiting for transfers between devices, on_device(): lax.ppermute(after(qkv_weight[low:high], done), BOTH, far)  3.36 us
    unnamed x14, local copies, waits for them, and re-layouts  2.47 us
  transfers between devices with their start and end apart: 23, of which 13 were waited for; matrix products, arithmetic and copies ran while one was open for 1% of the time, Pallas kernels for 5%

profile of v5, /device:TPU:1, one launch (start us, length us, event | category | flops | bytes accessed | tf_op | source)
XLA Modules:
  0.0 120.3 jit_solution(14716834502310523383)
XLA Ops:
  0.0 0.0 copy-start.4
  0.0 0.0 copy-start.5
  0.0 8.9 %collective-permute-start = (bf16[128,640]{1,0:T(8,128)(2,1)}, bf16[128,640]{1,0:T(8,128)(2,1)S(1)}, u32[]{:S(2)}, u32[]{:S(2)}) collective-permute-start(bf16[128,640]{1,0:T(8,128)(2,1)} %bitcast.6), channel_id=1, source_target_pairs={{0,1},{1,0},{2,3},{3,2},{4,5},{5,4},{6,7},{7,6},{8,9},{9,8},{10,11... | collective-permute-start | bytes 491528 | tf_op jit(solution)/shard_map/ppermute | solution.py:27
  8.9 1.2 collective-permute-done.core
  10.1 0.0 copy-start
  10.1 0.9 copy-done
  11.1 0.0 copy-start.1
  11.1 0.2 shard_map.64
  11.3 1.9 %collective-permute-start.1 = (bf16[2,128,160]{2,1,0:T(8,128)(2,1)S(1)}, bf16[2,128,160]{2,1,0:T(8,128)(2,1)S(1)}, u32[]{:S(2)}, u32[]{:S(2)}) collective-permute-start(bf16[2,128,160]{2,1,0:T(8,128)(2,1)S(1)} %get-tuple-element.36), channel_id=1, source_target_pairs={{0,2},{1,3},{2,0},{3,1},{4,6},{5,7},{6,4},{7,5},{8,10},{9,11},{10,... | collective-permute-start | bytes 245768 | tf_op jit(solution)/shard_map/ppermute | solution.py:27
  13.2 0.1 compare_convert_fusion.pool
  13.3 0.8 reshape.54.gain
  14.1 3.9 %collective-permute-done.1.came = bf16[2,128,160]{2,1,0:T(8,128)(2,1)S(1)} collective-permute-done((bf16[2,128,160]{2,1,0:T(8,128)(2,1)S(1)}, bf16[2,128,160]{2,1,0:T(8,128)(2,1)S(1)}, u32[]{:S(2)}, u32[]{:S(2)}) %collective-permute-start.1) | collective-permute-done | bytes 81952 | tf_op jit(solution)/shard_map/ppermute | solution.py:27
  18.0 1.5 %copy-done.3 = bf16[9,160,640]{2,1,0:T(8,128)(2,1)S(1)} copy-done((bf16[9,160,640]{2,1,0:T(8,128)(2,1)S(1)}, bf16[9,160,640]{2,1,0:T(8,128)(2,1)}, u32[]{:S(2)}) %copy-start.3) | copy-done | bytes 1843224
  19.5 2.7 %shard_map.65 = (f32[2,128,640]{2,1,0:T(8,128)S(1)}, bf16[2,128,640]{2,1,0:T(8,128)(2,1)S(1)}) custom-call(s32[1]{0:T(128)} %bitcast.me_ref, bf16[2,128,160]{2,1,0:T(8,128)(2,1)S(1)} %get-tuple-element.35.mine, bf16[2,128,160]{2,1,0:T(8,128)(2,1)S(1)} %collective-permute-done.1.came, f32[4,160]{1,0:T(4,128)S(1)} %reshape.54.gain, ...), custom_call_target="tpu_custom_call" | custom-call | flops 943718400 | bytes 3095044 | tf_op jit(solution)/shard_map/pallas_call | solution.py:217
  22.2 3.0 %collective-permute-start.2 = (bf16[2,128,640]{2,1,0:T(8,128)(2,1)S(1)}, bf16[2,128,640]{2,1,0:T(8,128)(2,1)S(1)}, u32[]{:S(2)}, u32[]{:S(2)}) collective-permute-start(bf16[2,128,640]{2,1,0:T(8,128)(2,1)S(1)} %get-tuple-element.38), channel_id=1, source_target_pairs={{0,1},{1,0},{2,3},{3,2},{4,5},{5,4},{6,7},{7,6},{8,9},{9,8},{10,11... | collective-permute-start | bytes 983048 | tf_op jit(solution)/shard_map/ppermute | solution.py:27
  25.2 1.2 %collective-permute-done.2.core = bf16[2,128,640]{2,1,0:T(8,128)(2,1)S(1)} collective-permute-done((bf16[2,128,640]{2,1,0:T(8,128)(2,1)S(1)}, bf16[2,128,640]{2,1,0:T(8,128)(2,1)S(1)}, u32[]{:S(2)}, u32[]{:S(2)}) %collective-permute-start.2) | collective-permute-done | bytes 327712 | tf_op jit(solution)/shard_map/ppermute | solution.py:27
  26.5 1.9 %collective-permute-start.3 = (bf16[128,640]{1,0:T(8,128)(2,1)S(1)}, bf16[128,640]{1,0:T(8,128)(2,1)S(1)}, u32[]{:S(2)}, u32[]{:S(2)}) collective-permute-start(bf16[128,640]{1,0:T(8,128)(2,1)S(1)} %fusion), channel_id=1, source_target_pairs={{0,2},{1,3},{2,0},{3,1},{4,6},{5,7},{6,4},{7,5},{8,10},{9,11},{10,... | collective-permute-start | bytes 491528 | tf_op jit(solution)/shard_map/ppermute | solution.py:27
  28.4 0.0 copy-done.4
  28.4 0.0 copy-done.5
  28.4 5.3 %collective-permute-done.3.chip = bf16[128,640]{1,0:T(8,128)(2,1)S(1)} collective-permute-done((bf16[128,640]{1,0:T(8,128)(2,1)S(1)}, bf16[128,640]{1,0:T(8,128)(2,1)S(1)}, u32[]{:S(2)}, u32[]{:S(2)}) %collective-permute-start.3) | collective-permute-done | bytes 163872 | tf_op jit(solution)/shard_map/ppermute | solution.py:27
  33.8 0.0 copy-done.1
  33.8 0.3 shard_map.66
  34.1 1.3 %collective-permute-start.4 = (bf16[128,640]{1,0:T(8,128)(2,1)S(1)}, bf16[128,640]{1,0:T(8,128)(2,1)S(1)}, u32[]{:S(2)}, u32[]{:S(2)}) collective-permute-start(bf16[128,640]{1,0:T(8,128)(2,1)S(1)} %broadcast_select_fusion.1), channel_id=1, source_target_pairs={{0,256},{1,257},{2,258},{3,259}} | collective-permute-start | bytes 491528 | tf_op jit(solution)/shard_map/ppermute | solution.py:280
  35.4 2.6 %collective-permute-done.4 = bf16[128,640]{1,0:T(8,128)(2,1)S(1)} collective-permute-done((bf16[128,640]{1,0:T(8,128)(2,1)S(1)}, bf16[128,640]{1,0:T(8,128)(2,1)S(1)}, u32[]{:S(2)}, u32[]{:S(2)}) %collective-permute-start.4) | collective-permute-done | bytes 163872 | tf_op jit(solution)/shard_map/ppermute | solution.py:280
  38.0 6.9 %collective-permute-start.5 = (bf16[128,640]{1,0:T(8,128)(2,1)S(1)}, bf16[128,640]{1,0:T(8,128)(2,1)S(1)}, u32[]{:S(2)}, u32[]{:S(2)}) collective-permute-start(bf16[128,640]{1,0:T(8,128)(2,1)S(1)} %fusion.2), channel_id=1, source_target_pairs={{0,128},{256,384},{1,129},{257,385},{2,130},{258,386},{3,131},{259... | collective-permute-start | bytes 491528 | tf_op jit(solution)/shard_map/ppermute | solution.py:280
  44.9 1.3 %collective-permute-start.6 = (bf16[128,640]{1,0:T(8,128)(2,1)S(1)}, bf16[128,640]{1,0:T(8,128)(2,1)S(1)}, u32[]{:S(2)}, u32[]{:S(2)}) collective-permute-start(bf16[128,640]{1,0:T(8,128)(2,1)S(1)} %get-tuple-element.54.own), channel_id=1, source_target_pairs={{0,4},{4,8},{8,12},{12,16},{16,20},{20,24},{24,28},{28,32},{32,36}... | collective-permute-start | bytes 491528 | tf_op jit(solution)/shard_map/ppermute | solution.py:282
  46.2 0.0 copy-done.2
  46.2 5.3 %collective-permute-start.7 = (bf16[48,1920]{1,0:T(8,128)(2,1)S(1)}, bf16[48,1920]{1,0:T(8,128)(2,1)S(1)}, u32[]{:S(2)}, u32[]{:S(2)}) collective-permute-start(bf16[48,1920]{1,0:T(8,128)(2,1)S(1)} %get-tuple-element.41), channel_id=1, source_target_pairs={{0,258},{1,259},{2,256},{3,257},{4,262},{5,263},{6,260},{7,261},{8... | collective-permute-start | bytes 552968 | tf_op jit(solution)/shard_map/ppermute | solution.py:277
  51.5 0.0 collective-permute-done.5
  51.6 0.0 collective-permute-done.6
  51.6 3.4 %collective-permute-done.7 = bf16[48,1920]{1,0:T(8,128)(2,1)S(1)} collective-permute-done((bf16[48,1920]{1,0:T(8,128)(2,1)S(1)}, bf16[48,1920]{1,0:T(8,128)(2,1)S(1)}, u32[]{:S(2)}, u32[]{:S(2)}) %collective-permute-start.7) | collective-permute-done | bytes 184352 | tf_op jit(solution)/shard_map/ppermute | solution.py:277
  55.0 6.5 %collective-permute-start.10 = (bf16[48,1920]{1,0:T(8,128)(2,1)S(1)}, bf16[48,1920]{1,0:T(8,128)(2,1)S(1)}, u32[]{:S(2)}, u32[]{:S(2)}) collective-permute-start(bf16[48,1920]{1,0:T(8,128)(2,1)S(1)} %get-tuple-element.44), channel_id=1, source_target_pairs={{0,258},{1,259},{2,256},{3,257},{4,262},{5,263},{6,260},{7,261},{8... | collective-permute-start | bytes 552968 | tf_op jit(solution)/shard_map/ppermute | solution.py:277
  61.5 1.3 %collective-permute-start.8 = (bf16[128,640]{1,0:T(8,128)(2,1)S(1)}, bf16[128,640]{1,0:T(8,128)(2,1)S(1)}, u32[]{:S(2)}, u32[]{:S(2)}) collective-permute-start(bf16[128,640]{1,0:T(8,128)(2,1)S(1)} %add.36), channel_id=1, source_target_pairs={{0,64},{128,192},{256,320},{384,448},{1,65},{129,193},{257,321},{3... | collective-permute-start | bytes 491528 | tf_op jit(solution)/shard_map/ppermute | solution.py:280
  62.8 5.9 %collective-permute-start.9 = (bf16[128,640]{1,0:T(8,128)(2,1)S(1)}, bf16[128,640]{1,0:T(8,128)(2,1)S(1)}, u32[]{:S(2)}, u32[]{:S(2)}) collective-permute-start(bf16[128,640]{1,0:T(8,128)(2,1)S(1)} %broadcast_select_fusion.p0), channel_id=1, source_target_pairs={{0,1},{1,0},{2,3},{3,2},{4,5},{5,4},{6,7},{7,6},{8,9},{9,8},{10,11... | collective-permute-start | bytes 491528 | tf_op jit(solution)/shard_map/ppermute | solution.py:27
  68.7 0.0 collective-permute-done.8
  68.8 0.9 collective-permute-done.9.p1
  69.7 0.0 collective-permute-done.10
  69.7 1.9 %collective-permute-start.13 = (bf16[64,1920]{1,0:T(8,128)(2,1)S(1)}, bf16[64,1920]{1,0:T(8,128)(2,1)S(1)}, u32[]{:S(2)}, u32[]{:S(2)}) collective-permute-start(bf16[64,1920]{1,0:T(8,128)(2,1)S(1)} %slice.19), channel_id=1, source_target_pairs={{0,258},{1,259},{2,256},{3,257},{4,262},{5,263},{6,260},{7,261},{8... | collective-permute-start | bytes 737288 | tf_op jit(solution)/shard_map/ppermute | solution.py:277
  71.6 4.4 %collective-permute-start.12 = (bf16[160,1920]{1,0:T(8,128)(2,1)S(1)}, bf16[160,1920]{1,0:T(8,128)(2,1)S(1)}, u32[]{:S(2)}, u32[]{:S(2)}) collective-permute-start(bf16[160,1920]{1,0:T(8,128)(2,1)S(1)} %copy-done.2), channel_id=1, source_target_pairs={{0,1},{1,0},{2,3},{3,2},{4,5},{5,4},{6,7},{7,6},{8,9},{9,8},{10,11... | collective-permute-start | bytes 1843208 | tf_op jit(solution)/shard_map/ppermute | solution.py:27
  76.0 1.3 %collective-permute-start.11 = (bf16[128,640]{1,0:T(8,128)(2,1)S(1)}, bf16[128,640]{1,0:T(8,128)(2,1)S(1)}, u32[]{:S(2)}, u32[]{:S(2)}) collective-permute-start(bf16[128,640]{1,0:T(8,128)(2,1)S(1)} %add.37), channel_id=1, source_target_pairs={{0,32},{64,96},{128,160},{192,224},{256,288},{320,352},{384,416},{... | collective-permute-start | bytes 491528 | tf_op jit(solution)/shard_map/ppermute | solution.py:280
  77.4 3.8 %collective-permute-done.11 = bf16[128,640]{1,0:T(8,128)(2,1)S(1)} collective-permute-done((bf16[128,640]{1,0:T(8,128)(2,1)S(1)}, bf16[128,640]{1,0:T(8,128)(2,1)S(1)}, u32[]{:S(2)}, u32[]{:S(2)}) %collective-permute-start.11) | collective-permute-done | bytes 163872 | tf_op jit(solution)/shard_map/ppermute | solution.py:280
  81.2 0.0 collective-permute-done.13
  81.2 0.0 collective-permute-done.12.w1
  81.2 2.5 %collective-permute-start.16 = (bf16[160,1920]{1,0:T(8,128)(2,1)S(1)}, bf16[160,1920]{1,0:T(8,128)(2,1)S(1)}, u32[]{:S(2)}, u32[]{:S(2)}) collective-permute-start(bf16[160,1920]{1,0:T(8,128)(2,1)S(1)} %constant_dynamic-update-slice_fusion.w2), channel_id=1, source_target_pairs={{0,1},{1,0},{2,3},{3,2},{4,5},{5,4},{6,7},{7,6},{8,9},{9,8},{10,11... | collective-permute-start | bytes 1843208 | tf_op jit(solution)/shard_map/ppermute | solution.py:27
  83.7 1.3 %collective-permute-start.14 = (bf16[128,640]{1,0:T(8,128)(2,1)S(1)}, bf16[128,640]{1,0:T(8,128)(2,1)S(1)}, u32[]{:S(2)}, u32[]{:S(2)}) collective-permute-start(bf16[128,640]{1,0:T(8,128)(2,1)S(1)} %add.38), channel_id=1, source_target_pairs={{0,16},{32,48},{64,80},{96,112},{128,144},{160,176},{192,208},{224... | collective-permute-start | bytes 491528 | tf_op jit(solution)/shard_map/ppermute | solution.py:280
  85.0 1.9 %collective-permute-start.15 = (bf16[128,640]{1,0:T(8,128)(2,1)S(1)}, bf16[128,640]{1,0:T(8,128)(2,1)S(1)}, u32[]{:S(2)}, u32[]{:S(2)}) collective-permute-start(bf16[128,640]{1,0:T(8,128)(2,1)S(1)} %broadcast_select_fusion.p0), channel_id=1, source_target_pairs={{0,2},{1,3},{2,0},{3,1},{4,6},{5,7},{6,4},{7,5},{8,10},{9,11},{10,... | collective-permute-start | bytes 491528 | tf_op jit(solution)/shard_map/ppermute | solution.py:27
  87.0 1.9 %collective-permute-done.14 = bf16[128,640]{1,0:T(8,128)(2,1)S(1)} collective-permute-done((bf16[128,640]{1,0:T(8,128)(2,1)S(1)}, bf16[128,640]{1,0:T(8,128)(2,1)S(1)}, u32[]{:S(2)}, u32[]{:S(2)}) %collective-permute-start.14) | collective-permute-done | bytes 163872 | tf_op jit(solution)/shard_map/ppermute | solution.py:280
  88.9 3.9 %collective-permute-done.15.p2 = bf16[128,640]{1,0:T(8,128)(2,1)S(1)} collective-permute-done((bf16[128,640]{1,0:T(8,128)(2,1)S(1)}, bf16[128,640]{1,0:T(8,128)(2,1)S(1)}, u32[]{:S(2)}, u32[]{:S(2)}) %collective-permute-start.15) | collective-permute-done | bytes 163872 | tf_op jit(solution)/shard_map/ppermute | solution.py:27
  92.7 0.0 collective-permute-done.16.w3
  92.7 1.3 %collective-permute-start.17 = (bf16[128,640]{1,0:T(8,128)(2,1)S(1)}, bf16[128,640]{1,0:T(8,128)(2,1)S(1)}, u32[]{:S(2)}, u32[]{:S(2)}) collective-permute-start(bf16[128,640]{1,0:T(8,128)(2,1)S(1)} %add.39), channel_id=1, source_target_pairs={{0,8},{16,24},{32,40},{48,56},{64,72},{80,88},{96,104},{112,120},{... | collective-permute-start | bytes 491528 | tf_op jit(solution)/shard_map/ppermute | solution.py:280
  94.0 2.7 %collective-permute-start.18 = (bf16[128,640]{1,0:T(8,128)(2,1)S(1)}, bf16[128,640]{1,0:T(8,128)(2,1)S(1)}, u32[]{:S(2)}, u32[]{:S(2)}) collective-permute-start(bf16[128,640]{1,0:T(8,128)(2,1)S(1)} %collective-permute-done.15.p2), channel_id=1, source_target_pairs={{0,1},{1,0},{2,3},{3,2},{4,5},{5,4},{6,7},{7,6},{8,9},{9,8},{10,11... | collective-permute-start | bytes 491528 | tf_op jit(solution)/shard_map/ppermute | solution.py:27
  96.8 0.3 collective-permute-done.17
  97.1 0.6 collective-permute-done.18.p3
  97.8 1.3 %collective-permute-start.19 = (bf16[128,640]{1,0:T(8,128)(2,1)S(1)}, bf16[128,640]{1,0:T(8,128)(2,1)S(1)}, u32[]{:S(2)}, u32[]{:S(2)}) collective-permute-start(bf16[128,640]{1,0:T(8,128)(2,1)S(1)} %add.40), channel_id=1, source_target_pairs={{0,4},{8,12},{16,20},{24,28},{32,36},{40,44},{48,52},{56,60},{64,6... | collective-permute-start | bytes 491528 | tf_op jit(solution)/shard_map/ppermute | solution.py:280
  99.1 3.6 %shard_map.67 = (bf16[128,640]{1,0:T(8,128)(2,1)S(1)}, f32[128,8]{1,0:T(8,128)S(1)}, f32[128,8]{1,0:T(8,128)S(1)}, f32[128,640]{1,0:T(8,128)S(1)}, bf16[640,1920]{1,0:T(8,128)(2,1)S(1)}) custom-call(s32[1]{0:T(128)} %bitcast.me_ref, bf16[128,640]{1,0:T(8,128)(2,1)S(1)} %get-tuple-element.54.own, bf16[128,640]{1,0:T(8,128)(2,1)S(1)} %broadcast_select_fusion.p0, ...), custom_call_target="tpu_custom_call" | custom-call | flops 1006632960 | bytes 6234116 | tf_op jit(solution)/shard_map/pallas_call | solution.py:217
  102.6 0.0 collective-permute-done.19
  102.7 1.9 %collective-permute-start.20 = (bf16[128,640]{1,0:T(8,128)(2,1)S(1)}, bf16[128,640]{1,0:T(8,128)(2,1)S(1)}, u32[]{:S(2)}, u32[]{:S(2)}) collective-permute-start(bf16[128,640]{1,0:T(8,128)(2,1)S(1)} %add.41.a0), channel_id=1, source_target_pairs={{0,2},{1,3},{2,0},{3,1},{4,6},{5,7},{6,4},{7,5},{8,10},{9,11},{10,... | collective-permute-start | bytes 491528 | tf_op jit(solution)/shard_map/ppermute | solution.py:27
  104.6 3.1 %collective-permute-start.22 = (bf16[128,640]{1,0:T(8,128)(2,1)S(1)}, bf16[128,640]{1,0:T(8,128)(2,1)S(1)}, u32[]{:S(2)}, u32[]{:S(2)}) collective-permute-start(bf16[128,640]{1,0:T(8,128)(2,1)S(1)} %add.41.a0), channel_id=1, source_target_pairs={{0,1},{1,0},{2,3},{3,2},{4,5},{5,4},{6,7},{7,6},{8,9},{9,8},{10,11... | collective-permute-start | bytes 491528 | tf_op jit(solution)/shard_map/ppermute | solution.py:27
  107.8 1.8 %collective-permute-done.20.a0 = bf16[128,640]{1,0:T(8,128)(2,1)S(1)} collective-permute-done((bf16[128,640]{1,0:T(8,128)(2,1)S(1)}, bf16[128,640]{1,0:T(8,128)(2,1)S(1)}, u32[]{:S(2)}, u32[]{:S(2)}) %collective-permute-start.20) | collective-permute-done | bytes 163872 | tf_op jit(solution)/shard_map/ppermute | solution.py:27
  109.5 3.8 %collective-permute-start.21 = (bf16[128,640]{1,0:T(8,128)(2,1)S(1)}, bf16[128,640]{1,0:T(8,128)(2,1)S(1)}, u32[]{:S(2)}, u32[]{:S(2)}) collective-permute-start(bf16[128,640]{1,0:T(8,128)(2,1)S(1)} %collective-permute-done.20.a0), channel_id=1, source_target_pairs={{0,1},{1,0},{2,3},{3,2},{4,5},{5,4},{6,7},{7,6},{8,9},{9,8},{10,11... | collective-permute-start | bytes 491528 | tf_op jit(solution)/shard_map/ppermute | solution.py:27
  113.3 0.0 collective-permute-done.22.a1
  113.3 2.9 %shard_map.68 = (f32[128,8]{1,0:T(8,128)S(1)}, f32[128,8]{1,0:T(8,128)S(1)}, f32[128,640]{1,0:T(8,128)S(1)}) custom-call(bf16[128,640]{1,0:T(8,128)(2,1)S(1)} %get-tuple-element.55.query, bf16[128,640]{1,0:T(8,128)(2,1)S(1)} %add.41.a0, bf16[128,640]{1,0:T(8,128)(2,1)S(1)} %collective-permute-done.22.a1, bf16[640,1920]{1,0:T(8,128)(2,1)S(1)} %get-tuple-element.58.weight, ...), custom_call_target="tpu_custom_call" | custom-call | flops 503316480 | bytes 3620864 | tf_op jit(solution)/shard_map/pallas_call | solution.py:217
  116.2 0.0 collective-permute-done.21.a1
  116.3 4.1 %shard_map.69 = bf16[128,640]{1,0:T(8,128)(2,1)} custom-call(bf16[128,640]{1,0:T(8,128)(2,1)S(1)} %get-tuple-element.55.query, bf16[128,640]{1,0:T(8,128)(2,1)S(1)} %collective-permute-done.20.a0, bf16[128,640]{1,0:T(8,128)(2,1)S(1)} %collective-permute-done.21.a1, bf16[640,1920]{1,0:T(8,128)(2,1)S(1)} %get-tuple-element.58.weight, ...), custom_call_target="tpu_custom_call" | custom-call | flops 503316480 | bytes 3612672 | tf_op jit(solution)/shard_map/pallas_call | solution.py:217
  (20 shorter events, 0.5 us)
Async XLA Ops:
  0.0 28.4 %copy-start.4 = (f32[640]{0:T(1024)S(1)}, f32[640]{0:T(1024)}, u32[]{:S(2)}) copy-start(f32[640]{0:T(1024)} %param.9) | copy-start | bytes 7684
  0.0 28.4 %copy-start.5 = (f32[640]{0:T(1024)S(1)}, f32[640]{0:T(1024)}, u32[]{:S(2)}) copy-start(f32[640]{0:T(1024)} %param.10) | copy-start | bytes 7684
  0.0 10.1 %collective-permute-start = (bf16[128,640]{1,0:T(8,128)(2,1)}, bf16[128,640]{1,0:T(8,128)(2,1)S(1)}, u32[]{:S(2)}, u32[]{:S(2)}) collective-permute-start(bf16[128,640]{1,0:T(8,128)(2,1)} %bitcast.6), channel_id=1, source_target_pairs={{0,1},{1,0},{2,3},{3,2},{4,5},{5,4},{6,7},{7,6},{8,9},{9,8},{10,11... | collective-permute-start | bytes 491528 | tf_op jit(solution)/shard_map/ppermute | solution.py:27
  10.1 0.9 copy-start
  11.1 22.7 %copy-start.1 = (bf16[1,4,32,640]{3,2,1,0:T(8,128)(2,1)S(1)}, bf16[1,4,32,640]{3,2,1,0:T(8,128)(2,1)}, u32[]{:S(2)}) copy-start(bf16[1,4,32,640]{3,2,1,0:T(8,128)(2,1)} %param.6) | copy-start | bytes 491524
  11.3 6.7 %collective-permute-start.1 = (bf16[2,128,160]{2,1,0:T(8,128)(2,1)S(1)}, bf16[2,128,160]{2,1,0:T(8,128)(2,1)S(1)}, u32[]{:S(2)}, u32[]{:S(2)}) collective-permute-start(bf16[2,128,160]{2,1,0:T(8,128)(2,1)S(1)} %get-tuple-element.36), channel_id=1, source_target_pairs={{0,2},{1,3},{2,0},{3,1},{4,6},{5,7},{6,4},{7,5},{8,10},{9,11},{10,... | collective-permute-start | bytes 245768 | tf_op jit(solution)/shard_map/ppermute | solution.py:27
  18.0 1.5 %copy-start.3 = (bf16[9,160,640]{2,1,0:T(8,128)(2,1)S(1)}, bf16[9,160,640]{2,1,0:T(8,128)(2,1)}, u32[]{:S(2)}) copy-start(bf16[9,160,640]{2,1,0:T(8,128)(2,1)} %param.8) | copy-start | bytes 5529604
  19.5 26.7 %copy-start.2 = (bf16[160,1920]{1,0:T(8,128)(2,1)S(1)}, bf16[160,1920]{1,0:T(8,128)(2,1)}, u32[]{:S(2)}) copy-start(bf16[160,1920]{1,0:T(8,128)(2,1)} %w0.1) | copy-start | bytes 1843204
  22.2 4.3 %collective-permute-start.2 = (bf16[2,128,640]{2,1,0:T(8,128)(2,1)S(1)}, bf16[2,128,640]{2,1,0:T(8,128)(2,1)S(1)}, u32[]{:S(2)}, u32[]{:S(2)}) collective-permute-start(bf16[2,128,640]{2,1,0:T(8,128)(2,1)S(1)} %get-tuple-element.38), channel_id=1, source_target_pairs={{0,1},{1,0},{2,3},{3,2},{4,5},{5,4},{6,7},{7,6},{8,9},{9,8},{10,11... | collective-permute-start | bytes 983048 | tf_op jit(solution)/shard_map/ppermute | solution.py:27
  26.5 7.3 %collective-permute-start.3 = (bf16[128,640]{1,0:T(8,128)(2,1)S(1)}, bf16[128,640]{1,0:T(8,128)(2,1)S(1)}, u32[]{:S(2)}, u32[]{:S(2)}) collective-permute-start(bf16[128,640]{1,0:T(8,128)(2,1)S(1)} %fusion), channel_id=1, source_target_pairs={{0,2},{1,3},{2,0},{3,1},{4,6},{5,7},{6,4},{7,5},{8,10},{9,11},{10,... | collective-permute-start | bytes 491528 | tf_op jit(solution)/shard_map/ppermute | solution.py:27
  34.1 3.9 %collective-permute-start.4 = (bf16[128,640]{1,0:T(8,128)(2,1)S(1)}, bf16[128,640]{1,0:T(8,128)(2,1)S(1)}, u32[]{:S(2)}, u32[]{:S(2)}) collective-permute-start(bf16[128,640]{1,0:T(8,128)(2,1)S(1)} %broadcast_select_fusion.1), channel_id=1, source_target_pairs={{0,256},{1,257},{2,258},{3,259}} | collective-permute-start | bytes 491528 | tf_op jit(solution)/shard_map/ppermute | solution.py:280
  38.0 13.5 %collective-permute-start.5 = (bf16[128,640]{1,0:T(8,128)(2,1)S(1)}, bf16[128,640]{1,0:T(8,128)(2,1)S(1)}, u32[]{:S(2)}, u32[]{:S(2)}) collective-permute-start(bf16[128,640]{1,0:T(8,128)(2,1)S(1)} %fusion.2), channel_id=1, source_target_pairs={{0,128},{256,384},{1,129},{257,385},{2,130},{258,386},{3,131},{259... | collective-permute-start | bytes 491528 | tf_op jit(solution)/shard_map/ppermute | solution.py:280
  44.9 6.7 %collective-permute-start.6 = (bf16[128,640]{1,0:T(8,128)(2,1)S(1)}, bf16[128,640]{1,0:T(8,128)(2,1)S(1)}, u32[]{:S(2)}, u32[]{:S(2)}) collective-permute-start(bf16[128,640]{1,0:T(8,128)(2,1)S(1)} %get-tuple-element.54.own), channel_id=1, source_target_pairs={{0,4},{4,8},{8,12},{12,16},{16,20},{20,24},{24,28},{28,32},{32,36}... | collective-permute-start | bytes 491528 | tf_op jit(solution)/shard_map/ppermute | solution.py:282
  46.2 8.7 %collective-permute-start.7 = (bf16[48,1920]{1,0:T(8,128)(2,1)S(1)}, bf16[48,1920]{1,0:T(8,128)(2,1)S(1)}, u32[]{:S(2)}, u32[]{:S(2)}) collective-permute-start(bf16[48,1920]{1,0:T(8,128)(2,1)S(1)} %get-tuple-element.41), channel_id=1, source_target_pairs={{0,258},{1,259},{2,256},{3,257},{4,262},{5,263},{6,260},{7,261},{8... | collective-permute-start | bytes 552968 | tf_op jit(solution)/shard_map/ppermute | solution.py:277
  55.0 14.7 %collective-permute-start.10 = (bf16[48,1920]{1,0:T(8,128)(2,1)S(1)}, bf16[48,1920]{1,0:T(8,128)(2,1)S(1)}, u32[]{:S(2)}, u32[]{:S(2)}) collective-permute-start(bf16[48,1920]{1,0:T(8,128)(2,1)S(1)} %get-tuple-element.44), channel_id=1, source_target_pairs={{0,258},{1,259},{2,256},{3,257},{4,262},{5,263},{6,260},{7,261},{8... | collective-permute-start | bytes 552968 | tf_op jit(solution)/shard_map/ppermute | solution.py:277
  61.5 7.2 %collective-permute-start.8 = (bf16[128,640]{1,0:T(8,128)(2,1)S(1)}, bf16[128,640]{1,0:T(8,128)(2,1)S(1)}, u32[]{:S(2)}, u32[]{:S(2)}) collective-permute-start(bf16[128,640]{1,0:T(8,128)(2,1)S(1)} %add.36), channel_id=1, source_target_pairs={{0,64},{128,192},{256,320},{384,448},{1,65},{129,193},{257,321},{3... | collective-permute-start | bytes 491528 | tf_op jit(solution)/shard_map/ppermute | solution.py:280
  62.8 6.9 %collective-permute-start.9 = (bf16[128,640]{1,0:T(8,128)(2,1)S(1)}, bf16[128,640]{1,0:T(8,128)(2,1)S(1)}, u32[]{:S(2)}, u32[]{:S(2)}) collective-permute-start(bf16[128,640]{1,0:T(8,128)(2,1)S(1)} %broadcast_select_fusion.p0), channel_id=1, source_target_pairs={{0,1},{1,0},{2,3},{3,2},{4,5},{5,4},{6,7},{7,6},{8,9},{9,8},{10,11... | collective-permute-start | bytes 491528 | tf_op jit(solution)/shard_map/ppermute | solution.py:27
  69.7 11.5 %collective-permute-start.13 = (bf16[64,1920]{1,0:T(8,128)(2,1)S(1)}, bf16[64,1920]{1,0:T(8,128)(2,1)S(1)}, u32[]{:S(2)}, u32[]{:S(2)}) collective-permute-start(bf16[64,1920]{1,0:T(8,128)(2,1)S(1)} %slice.19), channel_id=1, source_target_pairs={{0,258},{1,259},{2,256},{3,257},{4,262},{5,263},{6,260},{7,261},{8... | collective-permute-start | bytes 737288 | tf_op jit(solution)/shard_map/ppermute | solution.py:277
  71.6 9.6 %collective-permute-start.12 = (bf16[160,1920]{1,0:T(8,128)(2,1)S(1)}, bf16[160,1920]{1,0:T(8,128)(2,1)S(1)}, u32[]{:S(2)}, u32[]{:S(2)}) collective-permute-start(bf16[160,1920]{1,0:T(8,128)(2,1)S(1)} %copy-done.2), channel_id=1, source_target_pairs={{0,1},{1,0},{2,3},{3,2},{4,5},{5,4},{6,7},{7,6},{8,9},{9,8},{10,11... | collective-permute-start | bytes 1843208 | tf_op jit(solution)/shard_map/ppermute | solution.py:27
  76.0 5.1 %collective-permute-start.11 = (bf16[128,640]{1,0:T(8,128)(2,1)S(1)}, bf16[128,640]{1,0:T(8,128)(2,1)S(1)}, u32[]{:S(2)}, u32[]{:S(2)}) collective-permute-start(bf16[128,640]{1,0:T(8,128)(2,1)S(1)} %add.37), channel_id=1, source_target_pairs={{0,32},{64,96},{128,160},{192,224},{256,288},{320,352},{384,416},{... | collective-permute-start | bytes 491528 | tf_op jit(solution)/shard_map/ppermute | solution.py:280
  81.2 11.5 %collective-permute-start.16 = (bf16[160,1920]{1,0:T(8,128)(2,1)S(1)}, bf16[160,1920]{1,0:T(8,128)(2,1)S(1)}, u32[]{:S(2)}, u32[]{:S(2)}) collective-permute-start(bf16[160,1920]{1,0:T(8,128)(2,1)S(1)} %constant_dynamic-update-slice_fusion.w2), channel_id=1, source_target_pairs={{0,1},{1,0},{2,3},{3,2},{4,5},{5,4},{6,7},{7,6},{8,9},{9,8},{10,11... | collective-permute-start | bytes 1843208 | tf_op jit(solution)/shard_map/ppermute | solution.py:27
  83.7 5.1 %collective-permute-start.14 = (bf16[128,640]{1,0:T(8,128)(2,1)S(1)}, bf16[128,640]{1,0:T(8,128)(2,1)S(1)}, u32[]{:S(2)}, u32[]{:S(2)}) collective-permute-start(bf16[128,640]{1,0:T(8,128)(2,1)S(1)} %add.38), channel_id=1, source_target_pairs={{0,16},{32,48},{64,80},{96,112},{128,144},{160,176},{192,208},{224... | collective-permute-start | bytes 491528 | tf_op jit(solution)/shard_map/ppermute | solution.py:280
  85.0 7.7 %collective-permute-start.15 = (bf16[128,640]{1,0:T(8,128)(2,1)S(1)}, bf16[128,640]{1,0:T(8,128)(2,1)S(1)}, u32[]{:S(2)}, u32[]{:S(2)}) collective-permute-start(bf16[128,640]{1,0:T(8,128)(2,1)S(1)} %broadcast_select_fusion.p0), channel_id=1, source_target_pairs={{0,2},{1,3},{2,0},{3,1},{4,6},{5,7},{6,4},{7,5},{8,10},{9,11},{10,... | collective-permute-start | bytes 491528 | tf_op jit(solution)/shard_map/ppermute | solution.py:27
  92.7 4.3 %collective-permute-start.17 = (bf16[128,640]{1,0:T(8,128)(2,1)S(1)}, bf16[128,640]{1,0:T(8,128)(2,1)S(1)}, u32[]{:S(2)}, u32[]{:S(2)}) collective-permute-start(bf16[128,640]{1,0:T(8,128)(2,1)S(1)} %add.39), channel_id=1, source_target_pairs={{0,8},{16,24},{32,40},{48,56},{64,72},{80,88},{96,104},{112,120},{... | collective-permute-start | bytes 491528 | tf_op jit(solution)/shard_map/ppermute | solution.py:280
  94.0 3.7 %collective-permute-start.18 = (bf16[128,640]{1,0:T(8,128)(2,1)S(1)}, bf16[128,640]{1,0:T(8,128)(2,1)S(1)}, u32[]{:S(2)}, u32[]{:S(2)}) collective-permute-start(bf16[128,640]{1,0:T(8,128)(2,1)S(1)} %collective-permute-done.15.p2), channel_id=1, source_target_pairs={{0,1},{1,0},{2,3},{3,2},{4,5},{5,4},{6,7},{7,6},{8,9},{9,8},{10,11... | collective-permute-start | bytes 491528 | tf_op jit(solution)/shard_map/ppermute | solution.py:27
  97.8 4.9 %collective-permute-start.19 = (bf16[128,640]{1,0:T(8,128)(2,1)S(1)}, bf16[128,640]{1,0:T(8,128)(2,1)S(1)}, u32[]{:S(2)}, u32[]{:S(2)}) collective-permute-start(bf16[128,640]{1,0:T(8,128)(2,1)S(1)} %add.40), channel_id=1, source_target_pairs={{0,4},{8,12},{16,20},{24,28},{32,36},{40,44},{48,52},{56,60},{64,6... | collective-permute-start | bytes 491528 | tf_op jit(solution)/shard_map/ppermute | solution.py:280
  102.7 6.8 %collective-permute-start.20 = (bf16[128,640]{1,0:T(8,128)(2,1)S(1)}, bf16[128,640]{1,0:T(8,128)(2,1)S(1)}, u32[]{:S(2)}, u32[]{:S(2)}) collective-permute-start(bf16[128,640]{1,0:T(8,128)(2,1)S(1)} %add.41.a0), channel_id=1, source_target_pairs={{0,2},{1,3},{2,0},{3,1},{4,6},{5,7},{6,4},{7,5},{8,10},{9,11},{10,... | collective-permute-start | bytes 491528 | tf_op jit(solution)/shard_map/ppermute | solution.py:27
  104.6 8.7 %collective-permute-start.22 = (bf16[128,640]{1,0:T(8,128)(2,1)S(1)}, bf16[128,640]{1,0:T(8,128)(2,1)S(1)}, u32[]{:S(2)}, u32[]{:S(2)}) collective-permute-start(bf16[128,640]{1,0:T(8,128)(2,1)S(1)} %add.41.a0), channel_id=1, source_target_pairs={{0,1},{1,0},{2,3},{3,2},{4,5},{5,4},{6,7},{7,6},{8,9},{9,8},{10,11... | collective-permute-start | bytes 491528 | tf_op jit(solution)/shard_map/ppermute | solution.py:27
  109.5 6.7 %collective-permute-start.21 = (bf16[128,640]{1,0:T(8,128)(2,1)S(1)}, bf16[128,640]{1,0:T(8,128)(2,1)S(1)}, u32[]{:S(2)}, u32[]{:S(2)}) collective-permute-start(bf16[128,640]{1,0:T(8,128)(2,1)S(1)} %collective-permute-done.20.a0), channel_id=1, source_target_pairs={{0,1},{1,0},{2,3},{3,2},{4,5},{5,4},{6,7},{7,6},{8,9},{9,8},{10,11... | collective-permute-start | bytes 491528 | tf_op jit(solution)/shard_map/ppermute | solution.py:27

commit v6 on v5

--- a/solution.py
+++ b/solution.py
@@ -9,7 +9,6 @@
 HEADS = 8
 GROUPS = 32
 EPS = 1e-05
-BOTH = ("tm", "rows")
 HBM = pl.BlockSpec(memory_space=pltpu.HBM)
 VMEM = pl.BlockSpec(memory_space=pltpu.VMEM)
 SMEM = pl.BlockSpec(memory_space=pltpu.SMEM)
@@ -37,6 +36,12 @@
     return x, core, chip, to_rows(chip, 1)
 
 
+def fetch_kernel(source, out, landed):
+    load = pltpu.make_async_copy(source, out, landed)
+    load.start()
+    load.wait()
+
+
 def split_kernel(share, me_ref, own, core, mine, away):
     for out, want in ((mine, me_ref[0]), (away, me_ref[0] ^ 2)):
         for block in range(4):
@@ -48,10 +53,8 @@
 
 
 def conv_kernel(
-    width, me_ref, mine, came, gain, weight_hbm, pool, keep, send, x_ref, taps, acc, weight, landed
+    width, me_ref, mine, came, gain, weight, pool, keep, send, x_ref, taps, acc
 ):
-    load = pltpu.make_async_copy(weight_hbm, weight, landed)
-    load.start()
     me = me_ref[0]
     blocks = (mine[0], mine[1], came[0], came[1])
     cells, chans = x_ref.shape
@@ -83,7 +86,6 @@
     taps[width : width + cells, :] = jnp.concatenate([before, act, after], axis=1).astype(
         jnp.bfloat16
     )
-    load.wait()
     acc[...] = sum(
         jnp.dot(
             taps[row * width : row * width + cells, :],
@@ -236,26 +238,31 @@
     bf16, f32 = jnp.bfloat16, jnp.float32
     lat = latents.reshape(part, chans)
 
+    fetched = lambda x: call(
+        fetch_kernel, [shape(x.shape, x.dtype)], [x], [pltpu.SemaphoreType.DMA], hbm=(0,)
+    )[0]
+    lat_core = to_rows(lat, 1)
+    lat = fetched(lat)
     mine, away = call(
         functools.partial(split_kernel, share),
         [shape((2, part, share), bf16)] * 2,
-        [me.reshape(1), lat, to_rows(lat, 1)],
+        [me.reshape(1), lat, lat_core],
     )
     came = to_rows(away, 2)
+    weight_core = to_rows(after(qkv_weight, away), 1)
+    taps_weight = fetched(after(conv_weight.reshape(3, 3 * share, chans), away))
+    came = after(came, weight_core, taps_weight)
     group = jnp.arange(share) // (chans // GROUPS)
     pool = (group[:, None] == group[None, :]).astype(f32)
     keep, send = call(
         functools.partial(conv_kernel, width),
         [shape((2, part, chans), f32), shape((2, part, chans), bf16)],
-        [me.reshape(1), mine, came, gn_gain.reshape(4, share), conv_weight.reshape(3, 3 * share, chans), pool],
+        [me.reshape(1), mine, came, gn_gain.reshape(4, share), taps_weight, pool],
         [
             pltpu.VMEM((cells, share), f32),
             pltpu.VMEM((cells + 2 * width, 3 * share), bf16),
             pltpu.VMEM((cells, chans), f32),
-            pltpu.VMEM((3, 3 * share, chans), bf16),
-            pltpu.SemaphoreType.DMA,
         ],
-        hbm=(4,),
         flops=2 * cells * 9 * share * chans,
     )
     core = to_rows(send, 1)
@@ -268,34 +275,26 @@
     )
 
     devices = lax.axis_size("tm")
-    far = [
-        (tm * 4 + row, (tm + devices // 2) % devices * 4 + (row ^ 2))
-        for tm in range(devices)
-        for row in range(4)
-    ]
-    cut = share // 3 // 16 * 16
-    chunk = lambda low, high, done: lax.ppermute(after(qkv_weight[low:high], done), BOTH, far)
     routes = tree_levels(devices)
     routes = routes + [[]] * (7 - len(routes))
     tree = lambda level, x: x + lax.ppermute(x, "tm", routes[level])
+    cut = share // 4
+    chunk = lambda at, done: to_rows(after(qkv_weight[at * cut : (at + 1) * cut], done), 2)
+    prev = lax.ppermute(feats, "tm", [(i, i + 1) for i in range(devices - 1)])
+    chunks = [chunk(0, feats)]
     anchor = tree(0, jnp.where(first, feats, jnp.zeros_like(feats)))
-    prev = lax.ppermute(after(feats, anchor), "tm", [(i, i + 1) for i in range(devices - 1)])
-    chunk0 = chunk(0, cut, anchor)
-    anchor = tree(1, anchor)
-    prev = jnp.where(first, feats, prev)
-    anchor = after(anchor, prev, chunk0)
-    chunk1 = chunk(cut, 2 * cut, anchor)
-    prev_core = to_rows(after(prev, anchor), 1)
-    anchor = after(tree(2, anchor), prev_core, chunk1)
-    chunk2 = chunk(2 * cut, share, anchor)
-    weight_core = to_rows(after(qkv_weight, anchor), 1)
-    anchor = after(tree(3, anchor), weight_core, chunk2)
+    prev = jnp.where(first, feats, after(prev, anchor))
+    anchor = after(anchor, prev, chunks[0])
+    for level in (1, 2, 3):
+        chunks.append(chunk(level, anchor))
+        anchor = after(tree(level, anchor), chunks[level])
+    weight_chip = jnp.concatenate(chunks, axis=0)
     prev_chip = to_rows(after(prev, anchor), 2)
-    weight_chip = jnp.concatenate([chunk0, chunk1, chunk2], axis=0)
     weight_last = to_rows(after(weight_chip, anchor), 1)
     anchor = after(tree(4, anchor), prev_chip, weight_last)
+    prev_core = to_rows(after(prev, anchor), 1)
     prev_last = to_rows(after(prev_chip, anchor), 1)
-    anchor = after(tree(5, anchor), prev_last)
+    anchor = after(tree(5, anchor), prev_core, prev_last)
     prev = (prev, prev_core, prev_chip, prev_last)
     qkv = [qkv_weight, weight_core, weight_chip, weight_last]
 

time: 121 us -> 122 us (level)
  starting transfers between devices: 71.6 us -> 74.5 us
  waiting for transfers between devices: 30.7 us -> 28.1 us
    ppermute x4 -> x1, starting transfers between devices: 15 us -> 1.3 us  [on_device(): prev = lax.ppermute(feats, 'tm', [(i, i + 1) for i in range(devices - 1)])]
    ppermute x12 -> x16, starting transfers between devices: 42 us -> 53.5 us  [to_rows(): return lax.ppermute(x, 'rows', [(i, i ^ flip) for i in range(4)])]
    ppermute x12 -> x16, waiting for transfers between devices: 18.9 us -> 25.5 us  [to_rows(): return lax.ppermute(x, 'rows', [(i, i ^ flip) for i in range(4)])]
    ppermute x7, waiting for transfers between devices: 8.51 us -> 1.97 us  [on_device(): tree = lambda level, x: x + lax.ppermute(x, 'tm', routes[level])]
    ppermute x7, starting transfers between devices: 14.7 us -> 19.7 us  [on_device(): tree = lambda level, x: x + lax.ppermute(x, 'tm', routes[level])]
    ppermute x4 -> x1, waiting for transfers between devices: 3.36 us -> 0.59 us  [on_device(): prev = lax.ppermute(feats, 'tm', [(i, i + 1) for i in range(devices - 1)])]
    pallas_call x6 -> x8, Pallas kernels: 13.7 us -> 13.8 us  [call(): pl.pallas_call(kernel, out_shape=list(outs), in_specs=specs, out_specs=[V...]
    unnamed x14 -> x13, local copies, waits for them, and re-layouts: 2.47 us -> 2.48 us
  transfers between devices with their start and end apart: 23 -> 24, of which waited for: 13 -> 15; matrix products, arithmetic and copies ran while one was open for 1% -> 1% of each run, Pallas kernels for 5% -> 6%
where the time goes in v6:
time: 122 us; the launch traced here: 121 us
  starting transfers between devices  74.5 us (61%)
  waiting for transfers between devices  28.1 us (23%)
  Pallas kernels  13.8 us (11%)
  local copies, waits for them, and re-layouts  3.32 us (3%)
    ppermute x16, starting transfers between devices, to_rows(): return lax.ppermute(x, 'rows', [(i, i ^ flip) for i in range(4)])  53.5 us
    ppermute x16, waiting for transfers between devices, to_rows(): return lax.ppermute(x, 'rows', [(i, i ^ flip) for i in range(4)])  25.5 us
    ppermute x7, starting transfers between devices, on_device(): tree = lambda level, x: x + lax.ppermute(x, 'tm', routes[level])  19.7 us
    pallas_call x8, Pallas kernels, call(): pl.pallas_call(kernel, out_shape=list(outs), in_specs=specs, out_specs=[V...  13.8 us
    unnamed x13, local copies, waits for them, and re-layouts  2.48 us
  transfers between devices with their start and end apart: 24, of which 15 were waited for; matrix products, arithmetic and copies ran while one was open for 1% of the time, Pallas kernels for 6%

profile of v6, /device:TPU:1, one launch (start us, length us, event | category | flops | bytes accessed | tf_op | source)
XLA Modules:
  0.0 120.6 jit_solution(4961767932967989380)
XLA Ops:
  0.0 8.8 %collective-permute-start = (bf16[128,640]{1,0:T(8,128)(2,1)}, bf16[128,640]{1,0:T(8,128)(2,1)S(1)}, u32[]{:S(2)}, u32[]{:S(2)}) collective-permute-start(bf16[128,640]{1,0:T(8,128)(2,1)} %bitcast.7), channel_id=1, source_target_pairs={{0,1},{1,0},{2,3},{3,2},{4,5},{5,4},{6,7},{7,6},{8,9},{9,8},{10,11... | collective-permute-start | bytes 491528 | tf_op jit(solution)/shard_map/ppermute | solution.py:26
  8.8 0.0 copy-start.2
  8.8 0.9 copy-done.2
  9.7 0.2 shard_map.64.own.lat
  9.9 0.1 collective-permute-done.core
  10.0 0.2 shard_map.65
  10.2 2.2 %collective-permute-start.2 = (bf16[160,1920]{1,0:T(8,128)(2,1)}, bf16[160,1920]{1,0:T(8,128)(2,1)S(1)}, u32[]{:S(2)}, u32[]{:S(2)}) collective-permute-start(bf16[160,1920]{1,0:T(8,128)(2,1)} %w0.1), channel_id=1, source_target_pairs={{0,1},{1,0},{2,3},{3,2},{4,5},{5,4},{6,7},{7,6},{8,9},{9,8},{10,11... | collective-permute-start | bytes 1843208 | tf_op jit(solution)/shard_map/ppermute | solution.py:26
  12.4 1.9 %collective-permute-start.1 = (bf16[2,128,160]{2,1,0:T(8,128)(2,1)S(1)}, bf16[2,128,160]{2,1,0:T(8,128)(2,1)S(1)}, u32[]{:S(2)}, u32[]{:S(2)}) collective-permute-start(bf16[2,128,160]{2,1,0:T(8,128)(2,1)S(1)} %get-tuple-element.40), channel_id=1, source_target_pairs={{0,2},{1,3},{2,0},{3,1},{4,6},{5,7},{6,4},{7,5},{8,10},{9,11},{10,... | collective-permute-start | bytes 245768 | tf_op jit(solution)/shard_map/ppermute | solution.py:26
  14.4 0.1 compare_convert_fusion.pool
  14.5 0.8 reshape.55.gain
  15.2 1.5 %copy-done = bf16[9,160,640]{2,1,0:T(8,128)(2,1)S(1)} copy-done((bf16[9,160,640]{2,1,0:T(8,128)(2,1)S(1)}, bf16[9,160,640]{2,1,0:T(8,128)(2,1)}, u32[]{:S(2)}) %copy-start) | copy-done | bytes 1843224
  16.7 0.1 shard_map.66.weight
  16.9 2.3 %collective-permute-done.1.came = bf16[2,128,160]{2,1,0:T(8,128)(2,1)S(1)} collective-permute-done((bf16[2,128,160]{2,1,0:T(8,128)(2,1)S(1)}, bf16[2,128,160]{2,1,0:T(8,128)(2,1)S(1)}, u32[]{:S(2)}, u32[]{:S(2)}) %collective-permute-start.1) | collective-permute-done | bytes 81952 | tf_op jit(solution)/shard_map/ppermute | solution.py:26
  19.2 0.0 collective-permute-done.2.w1
  19.2 2.4 %shard_map.67 = (f32[2,128,640]{2,1,0:T(8,128)S(1)}, bf16[2,128,640]{2,1,0:T(8,128)(2,1)S(1)}) custom-call(s32[1]{0:T(128)} %bitcast.me_ref, bf16[2,128,160]{2,1,0:T(8,128)(2,1)S(1)} %get-tuple-element.39.mine, bf16[2,128,160]{2,1,0:T(8,128)(2,1)S(1)} %collective-permute-done.1.came, f32[4,160]{1,0:T(4,128)S(1)} %reshape.55.gain, ...), custom_call_target="tpu_custom_call" | custom-call | flops 943718400 | bytes 3095044 | tf_op jit(solution)/shard_map/pallas_call | solution.py:219
  21.6 0.0 copy-start.1
  21.6 3.1 %collective-permute-start.3 = (bf16[2,128,640]{2,1,0:T(8,128)(2,1)S(1)}, bf16[2,128,640]{2,1,0:T(8,128)(2,1)S(1)}, u32[]{:S(2)}, u32[]{:S(2)}) collective-permute-start(bf16[2,128,640]{2,1,0:T(8,128)(2,1)S(1)} %get-tuple-element.45), channel_id=1, source_target_pairs={{0,1},{1,0},{2,3},{3,2},{4,5},{5,4},{6,7},{7,6},{8,9},{9,8},{10,11... | collective-permute-start | bytes 983048 | tf_op jit(solution)/shard_map/ppermute | solution.py:26
  24.7 1.2 %collective-permute-done.3.core = bf16[2,128,640]{2,1,0:T(8,128)(2,1)S(1)} collective-permute-done((bf16[2,128,640]{2,1,0:T(8,128)(2,1)S(1)}, bf16[2,128,640]{2,1,0:T(8,128)(2,1)S(1)}, u32[]{:S(2)}, u32[]{:S(2)}) %collective-permute-start.3) | collective-permute-done | bytes 327712 | tf_op jit(solution)/shard_map/ppermute | solution.py:26
  26.0 1.9 %collective-permute-start.4 = (bf16[128,640]{1,0:T(8,128)(2,1)S(1)}, bf16[128,640]{1,0:T(8,128)(2,1)S(1)}, u32[]{:S(2)}, u32[]{:S(2)}) collective-permute-start(bf16[128,640]{1,0:T(8,128)(2,1)S(1)} %fusion), channel_id=1, source_target_pairs={{0,2},{1,3},{2,0},{3,1},{4,6},{5,7},{6,4},{7,5},{8,10},{9,11},{10,... | collective-permute-start | bytes 491528 | tf_op jit(solution)/shard_map/ppermute | solution.py:26
  27.9 0.0 copy-done.3
  27.9 5.3 %collective-permute-done.4.chip = bf16[128,640]{1,0:T(8,128)(2,1)S(1)} collective-permute-done((bf16[128,640]{1,0:T(8,128)(2,1)S(1)}, bf16[128,640]{1,0:T(8,128)(2,1)S(1)}, u32[]{:S(2)}, u32[]{:S(2)}) %collective-permute-start.4) | collective-permute-done | bytes 163872 | tf_op jit(solution)/shard_map/ppermute | solution.py:26
  33.3 0.3 shard_map.68
  33.6 1.3 %collective-permute-start.5 = (bf16[128,640]{1,0:T(8,128)(2,1)S(1)}, bf16[128,640]{1,0:T(8,128)(2,1)S(1)}, u32[]{:S(2)}, u32[]{:S(2)}) collective-permute-start(bf16[128,640]{1,0:T(8,128)(2,1)S(1)} %broadcast_select_fusion.1), channel_id=1, source_target_pairs={{0,256},{1,257},{2,258},{3,259}} | collective-permute-start | bytes 491528 | tf_op jit(solution)/shard_map/ppermute | solution.py:280
  34.9 0.0 copy-done.1
  35.0 1.3 %collective-permute-start.6 = (bf16[128,640]{1,0:T(8,128)(2,1)S(1)}, bf16[128,640]{1,0:T(8,128)(2,1)S(1)}, u32[]{:S(2)}, u32[]{:S(2)}) collective-permute-start(bf16[128,640]{1,0:T(8,128)(2,1)S(1)} %get-tuple-element.62.own), channel_id=1, source_target_pairs={{0,4},{4,8},{8,12},{12,16},{16,20},{20,24},{24,28},{28,32},{32,36}... | collective-permute-start | bytes 491528 | tf_op jit(solution)/shard_map/ppermute | solution.py:283
  36.3 1.9 %collective-permute-start.7 = (bf16[40,1920]{1,0:T(8,128)(2,1)S(1)}, bf16[40,1920]{1,0:T(8,128)(2,1)S(1)}, u32[]{:S(2)}, u32[]{:S(2)}) collective-permute-start(bf16[40,1920]{1,0:T(8,128)(2,1)S(1)} %get-tuple-element.48), channel_id=1, source_target_pairs={{0,2},{1,3},{2,0},{3,1},{4,6},{5,7},{6,4},{7,5},{8,10},{9,11},{10,... | collective-permute-start | bytes 460808 | tf_op jit(solution)/shard_map/ppermute | solution.py:26
  38.2 0.0 collective-permute-done.5
  38.2 0.6 collective-permute-done.6
  38.8 3.4 %collective-permute-done.7 = bf16[40,1920]{1,0:T(8,128)(2,1)S(1)} collective-permute-done((bf16[40,1920]{1,0:T(8,128)(2,1)S(1)}, bf16[40,1920]{1,0:T(8,128)(2,1)S(1)}, u32[]{:S(2)}, u32[]{:S(2)}) %collective-permute-start.7) | collective-permute-done | bytes 153632 | tf_op jit(solution)/shard_map/ppermute | solution.py:26
  42.2 11.9 %collective-permute-start.8 = (bf16[128,640]{1,0:T(8,128)(2,1)S(1)}, bf16[128,640]{1,0:T(8,128)(2,1)S(1)}, u32[]{:S(2)}, u32[]{:S(2)}) collective-permute-start(bf16[128,640]{1,0:T(8,128)(2,1)S(1)} %fusion.2), channel_id=1, source_target_pairs={{0,128},{256,384},{1,129},{257,385},{2,130},{258,386},{3,131},{259... | collective-permute-start | bytes 491528 | tf_op jit(solution)/shard_map/ppermute | solution.py:280
  54.1 3.2 %collective-permute-start.9 = (bf16[40,1920]{1,0:T(8,128)(2,1)S(1)}, bf16[40,1920]{1,0:T(8,128)(2,1)S(1)}, u32[]{:S(2)}, u32[]{:S(2)}) collective-permute-start(bf16[40,1920]{1,0:T(8,128)(2,1)S(1)} %get-tuple-element.50), channel_id=1, source_target_pairs={{0,2},{1,3},{2,0},{3,1},{4,6},{5,7},{6,4},{7,5},{8,10},{9,11},{10,... | collective-permute-start | bytes 460808 | tf_op jit(solution)/shard_map/ppermute | solution.py:26
  57.4 0.0 collective-permute-done.8
  57.4 2.7 %collective-permute-done.9 = bf16[40,1920]{1,0:T(8,128)(2,1)S(1)} collective-permute-done((bf16[40,1920]{1,0:T(8,128)(2,1)S(1)}, bf16[40,1920]{1,0:T(8,128)(2,1)S(1)}, u32[]{:S(2)}, u32[]{:S(2)}) %collective-permute-start.9) | collective-permute-done | bytes 153632 | tf_op jit(solution)/shard_map/ppermute | solution.py:26
  60.1 1.3 %collective-permute-start.10 = (bf16[128,640]{1,0:T(8,128)(2,1)S(1)}, bf16[128,640]{1,0:T(8,128)(2,1)S(1)}, u32[]{:S(2)}, u32[]{:S(2)}) collective-permute-start(bf16[128,640]{1,0:T(8,128)(2,1)S(1)} %add.36), channel_id=1, source_target_pairs={{0,64},{128,192},{256,320},{384,448},{1,65},{129,193},{257,321},{3... | collective-permute-start | bytes 491528 | tf_op jit(solution)/shard_map/ppermute | solution.py:280
  61.4 3.2 %collective-permute-start.11 = (bf16[40,1920]{1,0:T(8,128)(2,1)S(1)}, bf16[40,1920]{1,0:T(8,128)(2,1)S(1)}, u32[]{:S(2)}, u32[]{:S(2)}) collective-permute-start(bf16[40,1920]{1,0:T(8,128)(2,1)S(1)} %get-tuple-element.52), channel_id=1, source_target_pairs={{0,2},{1,3},{2,0},{3,1},{4,6},{5,7},{6,4},{7,5},{8,10},{9,11},{10,... | collective-permute-start | bytes 460808 | tf_op jit(solution)/shard_map/ppermute | solution.py:26
  64.6 0.0 collective-permute-done.10
  64.7 2.7 %collective-permute-done.11 = bf16[40,1920]{1,0:T(8,128)(2,1)S(1)} collective-permute-done((bf16[40,1920]{1,0:T(8,128)(2,1)S(1)}, bf16[40,1920]{1,0:T(8,128)(2,1)S(1)}, u32[]{:S(2)}, u32[]{:S(2)}) %collective-permute-start.11) | collective-permute-done | bytes 153632 | tf_op jit(solution)/shard_map/ppermute | solution.py:26
  67.4 3.2 %collective-permute-start.13 = (bf16[40,1920]{1,0:T(8,128)(2,1)S(1)}, bf16[40,1920]{1,0:T(8,128)(2,1)S(1)}, u32[]{:S(2)}, u32[]{:S(2)}) collective-permute-start(bf16[40,1920]{1,0:T(8,128)(2,1)S(1)} %get-tuple-element.54), channel_id=1, source_target_pairs={{0,2},{1,3},{2,0},{3,1},{4,6},{5,7},{6,4},{7,5},{8,10},{9,11},{10,... | collective-permute-start | bytes 460808 | tf_op jit(solution)/shard_map/ppermute | solution.py:26
  70.6 1.3 %collective-permute-start.12 = (bf16[128,640]{1,0:T(8,128)(2,1)S(1)}, bf16[128,640]{1,0:T(8,128)(2,1)S(1)}, u32[]{:S(2)}, u32[]{:S(2)}) collective-permute-start(bf16[128,640]{1,0:T(8,128)(2,1)S(1)} %add.37), channel_id=1, source_target_pairs={{0,32},{64,96},{128,160},{192,224},{256,288},{320,352},{384,416},{... | collective-permute-start | bytes 491528 | tf_op jit(solution)/shard_map/ppermute | solution.py:280
  71.9 1.4 %collective-permute-done.13 = bf16[40,1920]{1,0:T(8,128)(2,1)S(1)} collective-permute-done((bf16[40,1920]{1,0:T(8,128)(2,1)S(1)}, bf16[40,1920]{1,0:T(8,128)(2,1)S(1)}, u32[]{:S(2)}, u32[]{:S(2)}) %collective-permute-start.13) | collective-permute-done | bytes 153632 | tf_op jit(solution)/shard_map/ppermute | solution.py:26
  73.3 0.8 collective-permute-done.12
  74.2 7.5 %collective-permute-start.16 = (bf16[160,1920]{1,0:T(8,128)(2,1)S(1)}, bf16[160,1920]{1,0:T(8,128)(2,1)S(1)}, u32[]{:S(2)}, u32[]{:S(2)}) collective-permute-start(bf16[160,1920]{1,0:T(8,128)(2,1)S(1)} %constant_dynamic-update-slice_fusion.w2), channel_id=1, source_target_pairs={{0,1},{1,0},{2,3},{3,2},{4,5},{5,4},{6,7},{7,6},{8,9},{9,8},{10,11... | collective-permute-start | bytes 1843208 | tf_op jit(solution)/shard_map/ppermute | solution.py:26
  81.6 1.3 %collective-permute-start.14 = (bf16[128,640]{1,0:T(8,128)(2,1)S(1)}, bf16[128,640]{1,0:T(8,128)(2,1)S(1)}, u32[]{:S(2)}, u32[]{:S(2)}) collective-permute-start(bf16[128,640]{1,0:T(8,128)(2,1)S(1)} %add.38), channel_id=1, source_target_pairs={{0,16},{32,48},{64,80},{96,112},{128,144},{160,176},{192,208},{224... | collective-permute-start | bytes 491528 | tf_op jit(solution)/shard_map/ppermute | solution.py:280
  82.9 2.7 %collective-permute-start.15 = (bf16[128,640]{1,0:T(8,128)(2,1)S(1)}, bf16[128,640]{1,0:T(8,128)(2,1)S(1)}, u32[]{:S(2)}, u32[]{:S(2)}) collective-permute-start(bf16[128,640]{1,0:T(8,128)(2,1)S(1)} %broadcast_select_fusion.p0), channel_id=1, source_target_pairs={{0,2},{1,3},{2,0},{3,1},{4,6},{5,7},{6,4},{7,5},{8,10},{9,11},{10,... | collective-permute-start | bytes 491528 | tf_op jit(solution)/shard_map/ppermute | solution.py:26
  85.7 1.1 collective-permute-done.14
  86.8 3.9 %collective-permute-done.15.p2 = bf16[128,640]{1,0:T(8,128)(2,1)S(1)} collective-permute-done((bf16[128,640]{1,0:T(8,128)(2,1)S(1)}, bf16[128,640]{1,0:T(8,128)(2,1)S(1)}, u32[]{:S(2)}, u32[]{:S(2)}) %collective-permute-start.15) | collective-permute-done | bytes 163872 | tf_op jit(solution)/shard_map/ppermute | solution.py:26
  90.7 0.0 collective-permute-done.16.w3
  90.7 1.3 %collective-permute-start.17 = (bf16[128,640]{1,0:T(8,128)(2,1)S(1)}, bf16[128,640]{1,0:T(8,128)(2,1)S(1)}, u32[]{:S(2)}, u32[]{:S(2)}) collective-permute-start(bf16[128,640]{1,0:T(8,128)(2,1)S(1)} %add.39), channel_id=1, source_target_pairs={{0,8},{16,24},{32,40},{48,56},{64,72},{80,88},{96,104},{112,120},{... | collective-permute-start | bytes 491528 | tf_op jit(solution)/shard_map/ppermute | solution.py:280
  92.0 2.7 %collective-permute-start.18 = (bf16[128,640]{1,0:T(8,128)(2,1)S(1)}, bf16[128,640]{1,0:T(8,128)(2,1)S(1)}, u32[]{:S(2)}, u32[]{:S(2)}) collective-permute-start(bf16[128,640]{1,0:T(8,128)(2,1)S(1)} %broadcast_select_fusion.p0), channel_id=1, source_target_pairs={{0,1},{1,0},{2,3},{3,2},{4,5},{5,4},{6,7},{7,6},{8,9},{9,8},{10,11... | collective-permute-start | bytes 491528 | tf_op jit(solution)/shard_map/ppermute | solution.py:26
  94.7 1.9 %collective-permute-start.19 = (bf16[128,640]{1,0:T(8,128)(2,1)S(1)}, bf16[128,640]{1,0:T(8,128)(2,1)S(1)}, u32[]{:S(2)}, u32[]{:S(2)}) collective-permute-start(bf16[128,640]{1,0:T(8,128)(2,1)S(1)} %collective-permute-done.15.p2), channel_id=1, source_target_pairs={{0,1},{1,0},{2,3},{3,2},{4,5},{5,4},{6,7},{7,6},{8,9},{9,8},{10,11... | collective-permute-start | bytes 491528 | tf_op jit(solution)/shard_map/ppermute | solution.py:26
  96.6 0.0 collective-permute-done.17
  96.7 0.0 collective-permute-done.18.p1
  96.7 1.3 %collective-permute-done.19.p3 = bf16[128,640]{1,0:T(8,128)(2,1)S(1)} collective-permute-done((bf16[128,640]{1,0:T(8,128)(2,1)S(1)}, bf16[128,640]{1,0:T(8,128)(2,1)S(1)}, u32[]{:S(2)}, u32[]{:S(2)}) %collective-permute-start.19) | collective-permute-done | bytes 163872 | tf_op jit(solution)/shard_map/ppermute | solution.py:26
  98.0 1.3 %collective-permute-start.20 = (bf16[128,640]{1,0:T(8,128)(2,1)S(1)}, bf16[128,640]{1,0:T(8,128)(2,1)S(1)}, u32[]{:S(2)}, u32[]{:S(2)}) collective-permute-start(bf16[128,640]{1,0:T(8,128)(2,1)S(1)} %add.40), channel_id=1, source_target_pairs={{0,4},{8,12},{16,20},{24,28},{32,36},{40,44},{48,52},{56,60},{64,6... | collective-permute-start | bytes 491528 | tf_op jit(solution)/shard_map/ppermute | solution.py:280
  99.3 3.6 %shard_map.69 = (bf16[128,640]{1,0:T(8,128)(2,1)S(1)}, f32[128,8]{1,0:T(8,128)S(1)}, f32[128,8]{1,0:T(8,128)S(1)}, f32[128,640]{1,0:T(8,128)S(1)}, bf16[640,1920]{1,0:T(8,128)(2,1)S(1)}) custom-call(s32[1]{0:T(128)} %bitcast.me_ref, bf16[128,640]{1,0:T(8,128)(2,1)S(1)} %get-tuple-element.62.own, bf16[128,640]{1,0:T(8,128)(2,1)S(1)} %broadcast_select_fusion.p0, ...), custom_call_target="tpu_custom_call" | custom-call | flops 1006632960 | bytes 6234116 | tf_op jit(solution)/shard_map/pallas_call | solution.py:219
  102.8 0.1 collective-permute-done.20
  103.0 2.7 %collective-permute-start.21 = (bf16[128,640]{1,0:T(8,128)(2,1)S(1)}, bf16[128,640]{1,0:T(8,128)(2,1)S(1)}, u32[]{:S(2)}, u32[]{:S(2)}) collective-permute-start(bf16[128,640]{1,0:T(8,128)(2,1)S(1)} %add.41.a0), channel_id=1, source_target_pairs={{0,2},{1,3},{2,0},{3,1},{4,6},{5,7},{6,4},{7,5},{8,10},{9,11},{10,... | collective-permute-start | bytes 491528 | tf_op jit(solution)/shard_map/ppermute | solution.py:26
  105.7 2.9 %collective-permute-start.23 = (bf16[128,640]{1,0:T(8,128)(2,1)S(1)}, bf16[128,640]{1,0:T(8,128)(2,1)S(1)}, u32[]{:S(2)}, u32[]{:S(2)}) collective-permute-start(bf16[128,640]{1,0:T(8,128)(2,1)S(1)} %add.41.a0), channel_id=1, source_target_pairs={{0,1},{1,0},{2,3},{3,2},{4,5},{5,4},{6,7},{7,6},{8,9},{9,8},{10,11... | collective-permute-start | bytes 491528 | tf_op jit(solution)/shard_map/ppermute | solution.py:26
  108.6 1.3 %collective-permute-done.21.a0 = bf16[128,640]{1,0:T(8,128)(2,1)S(1)} collective-permute-done((bf16[128,640]{1,0:T(8,128)(2,1)S(1)}, bf16[128,640]{1,0:T(8,128)(2,1)S(1)}, u32[]{:S(2)}, u32[]{:S(2)}) %collective-permute-start.21) | collective-permute-done | bytes 163872 | tf_op jit(solution)/shard_map/ppermute | solution.py:26
  109.9 3.7 %collective-permute-start.22 = (bf16[128,640]{1,0:T(8,128)(2,1)S(1)}, bf16[128,640]{1,0:T(8,128)(2,1)S(1)}, u32[]{:S(2)}, u32[]{:S(2)}) collective-permute-start(bf16[128,640]{1,0:T(8,128)(2,1)S(1)} %collective-permute-done.21.a0), channel_id=1, source_target_pairs={{0,1},{1,0},{2,3},{3,2},{4,5},{5,4},{6,7},{7,6},{8,9},{9,8},{10,11... | collective-permute-start | bytes 491528 | tf_op jit(solution)/shard_map/ppermute | solution.py:26
  113.6 0.0 collective-permute-done.23.a1
  113.6 2.9 %shard_map.70 = (f32[128,8]{1,0:T(8,128)S(1)}, f32[128,8]{1,0:T(8,128)S(1)}, f32[128,640]{1,0:T(8,128)S(1)}) custom-call(bf16[128,640]{1,0:T(8,128)(2,1)S(1)} %get-tuple-element.63.query, bf16[128,640]{1,0:T(8,128)(2,1)S(1)} %add.41.a0, bf16[128,640]{1,0:T(8,128)(2,1)S(1)} %collective-permute-done.23.a1, bf16[640,1920]{1,0:T(8,128)(2,1)S(1)} %get-tuple-element.66.weight, ...), custom_call_target="tpu_custom_call" | custom-call | flops 503316480 | bytes 3620864 | tf_op jit(solution)/shard_map/pallas_call | solution.py:219
  116.5 0.0 collective-permute-done.22.a1
  116.5 4.1 %shard_map.71 = bf16[128,640]{1,0:T(8,128)(2,1)} custom-call(bf16[128,640]{1,0:T(8,128)(2,1)S(1)} %get-tuple-element.63.query, bf16[128,640]{1,0:T(8,128)(2,1)S(1)} %collective-permute-done.21.a0, bf16[128,640]{1,0:T(8,128)(2,1)S(1)} %collective-permute-done.22.a1, bf16[640,1920]{1,0:T(8,128)(2,1)S(1)} %get-tuple-element.66.weight, ...), custom_call_target="tpu_custom_call" | custom-call | flops 503316480 | bytes 3612672 | tf_op jit(solution)/shard_map/pallas_call | solution.py:219
  (22 shorter events, 0.5 us)
Async XLA Ops:
  0.0 10.0 %collective-permute-start = (bf16[128,640]{1,0:T(8,128)(2,1)}, bf16[128,640]{1,0:T(8,128)(2,1)S(1)}, u32[]{:S(2)}, u32[]{:S(2)}) collective-permute-start(bf16[128,640]{1,0:T(8,128)(2,1)} %bitcast.7), channel_id=1, source_target_pairs={{0,1},{1,0},{2,3},{3,2},{4,5},{5,4},{6,7},{7,6},{8,9},{9,8},{10,11... | collective-permute-start | bytes 491528 | tf_op jit(solution)/shard_map/ppermute | solution.py:26
  8.8 0.9 copy-start.2
  10.2 9.0 %collective-permute-start.2 = (bf16[160,1920]{1,0:T(8,128)(2,1)}, bf16[160,1920]{1,0:T(8,128)(2,1)S(1)}, u32[]{:S(2)}, u32[]{:S(2)}) collective-permute-start(bf16[160,1920]{1,0:T(8,128)(2,1)} %w0.1), channel_id=1, source_target_pairs={{0,1},{1,0},{2,3},{3,2},{4,5},{5,4},{6,7},{7,6},{8,9},{9,8},{10,11... | collective-permute-start | bytes 1843208 | tf_op jit(solution)/shard_map/ppermute | solution.py:26
  12.4 6.8 %collective-permute-start.1 = (bf16[2,128,160]{2,1,0:T(8,128)(2,1)S(1)}, bf16[2,128,160]{2,1,0:T(8,128)(2,1)S(1)}, u32[]{:S(2)}, u32[]{:S(2)}) collective-permute-start(bf16[2,128,160]{2,1,0:T(8,128)(2,1)S(1)} %get-tuple-element.40), channel_id=1, source_target_pairs={{0,2},{1,3},{2,0},{3,1},{4,6},{5,7},{6,4},{7,5},{8,10},{9,11},{10,... | collective-permute-start | bytes 245768 | tf_op jit(solution)/shard_map/ppermute | solution.py:26
  15.2 1.5 %copy-start = (bf16[9,160,640]{2,1,0:T(8,128)(2,1)S(1)}, bf16[9,160,640]{2,1,0:T(8,128)(2,1)}, u32[]{:S(2)}) copy-start(bf16[9,160,640]{2,1,0:T(8,128)(2,1)} %param.8) | copy-start | bytes 5529604
  19.2 8.7 %copy-start.3 = (f32[640]{0:T(1024)S(1)}, f32[640]{0:T(1024)}, u32[]{:S(2)}) copy-start(f32[640]{0:T(1024)} %param.9) | copy-start | bytes 7684
  19.2 8.7 %copy-start.4 = (f32[640]{0:T(1024)S(1)}, f32[640]{0:T(1024)}, u32[]{:S(2)}) copy-start(f32[640]{0:T(1024)} %param.10) | copy-start | bytes 7684
  21.6 13.3 %copy-start.1 = (bf16[160,1920]{1,0:T(8,128)(2,1)S(1)}, bf16[160,1920]{1,0:T(8,128)(2,1)}, u32[]{:S(2)}) copy-start(bf16[160,1920]{1,0:T(8,128)(2,1)} %w0.1) | copy-start | bytes 1843204
  21.6 4.3 %collective-permute-start.3 = (bf16[2,128,640]{2,1,0:T(8,128)(2,1)S(1)}, bf16[2,128,640]{2,1,0:T(8,128)(2,1)S(1)}, u32[]{:S(2)}, u32[]{:S(2)}) collective-permute-start(bf16[2,128,640]{2,1,0:T(8,128)(2,1)S(1)} %get-tuple-element.45), channel_id=1, source_target_pairs={{0,1},{1,0},{2,3},{3,2},{4,5},{5,4},{6,7},{7,6},{8,9},{9,8},{10,11... | collective-permute-start | bytes 983048 | tf_op jit(solution)/shard_map/ppermute | solution.py:26
  26.0 7.3 %collective-permute-start.4 = (bf16[128,640]{1,0:T(8,128)(2,1)S(1)}, bf16[128,640]{1,0:T(8,128)(2,1)S(1)}, u32[]{:S(2)}, u32[]{:S(2)}) collective-permute-start(bf16[128,640]{1,0:T(8,128)(2,1)S(1)} %fusion), channel_id=1, source_target_pairs={{0,2},{1,3},{2,0},{3,1},{4,6},{5,7},{6,4},{7,5},{8,10},{9,11},{10,... | collective-permute-start | bytes 491528 | tf_op jit(solution)/shard_map/ppermute | solution.py:26
  33.6 4.6 %collective-permute-start.5 = (bf16[128,640]{1,0:T(8,128)(2,1)S(1)}, bf16[128,640]{1,0:T(8,128)(2,1)S(1)}, u32[]{:S(2)}, u32[]{:S(2)}) collective-permute-start(bf16[128,640]{1,0:T(8,128)(2,1)S(1)} %broadcast_select_fusion.1), channel_id=1, source_target_pairs={{0,256},{1,257},{2,258},{3,259}} | collective-permute-start | bytes 491528 | tf_op jit(solution)/shard_map/ppermute | solution.py:280
  35.0 3.9 %collective-permute-start.6 = (bf16[128,640]{1,0:T(8,128)(2,1)S(1)}, bf16[128,640]{1,0:T(8,128)(2,1)S(1)}, u32[]{:S(2)}, u32[]{:S(2)}) collective-permute-start(bf16[128,640]{1,0:T(8,128)(2,1)S(1)} %get-tuple-element.62.own), channel_id=1, source_target_pairs={{0,4},{4,8},{8,12},{12,16},{16,20},{20,24},{24,28},{28,32},{32,36}... | collective-permute-start | bytes 491528 | tf_op jit(solution)/shard_map/ppermute | solution.py:283
  36.3 6.0 %collective-permute-start.7 = (bf16[40,1920]{1,0:T(8,128)(2,1)S(1)}, bf16[40,1920]{1,0:T(8,128)(2,1)S(1)}, u32[]{:S(2)}, u32[]{:S(2)}) collective-permute-start(bf16[40,1920]{1,0:T(8,128)(2,1)S(1)} %get-tuple-element.48), channel_id=1, source_target_pairs={{0,2},{1,3},{2,0},{3,1},{4,6},{5,7},{6,4},{7,5},{8,10},{9,11},{10,... | collective-permute-start | bytes 460808 | tf_op jit(solution)/shard_map/ppermute | solution.py:26
  42.2 15.2 %collective-permute-start.8 = (bf16[128,640]{1,0:T(8,128)(2,1)S(1)}, bf16[128,640]{1,0:T(8,128)(2,1)S(1)}, u32[]{:S(2)}, u32[]{:S(2)}) collective-permute-start(bf16[128,640]{1,0:T(8,128)(2,1)S(1)} %fusion.2), channel_id=1, source_target_pairs={{0,128},{256,384},{1,129},{257,385},{2,130},{258,386},{3,131},{259... | collective-permute-start | bytes 491528 | tf_op jit(solution)/shard_map/ppermute | solution.py:280
  54.1 6.0 %collective-permute-start.9 = (bf16[40,1920]{1,0:T(8,128)(2,1)S(1)}, bf16[40,1920]{1,0:T(8,128)(2,1)S(1)}, u32[]{:S(2)}, u32[]{:S(2)}) collective-permute-start(bf16[40,1920]{1,0:T(8,128)(2,1)S(1)} %get-tuple-element.50), channel_id=1, source_target_pairs={{0,2},{1,3},{2,0},{3,1},{4,6},{5,7},{6,4},{7,5},{8,10},{9,11},{10,... | collective-permute-start | bytes 460808 | tf_op jit(solution)/shard_map/ppermute | solution.py:26
  60.1 4.5 %collective-permute-start.10 = (bf16[128,640]{1,0:T(8,128)(2,1)S(1)}, bf16[128,640]{1,0:T(8,128)(2,1)S(1)}, u32[]{:S(2)}, u32[]{:S(2)}) collective-permute-start(bf16[128,640]{1,0:T(8,128)(2,1)S(1)} %add.36), channel_id=1, source_target_pairs={{0,64},{128,192},{256,320},{384,448},{1,65},{129,193},{257,321},{3... | collective-permute-start | bytes 491528 | tf_op jit(solution)/shard_map/ppermute | solution.py:280
  61.4 6.0 %collective-permute-start.11 = (bf16[40,1920]{1,0:T(8,128)(2,1)S(1)}, bf16[40,1920]{1,0:T(8,128)(2,1)S(1)}, u32[]{:S(2)}, u32[]{:S(2)}) collective-permute-start(bf16[40,1920]{1,0:T(8,128)(2,1)S(1)} %get-tuple-element.52), channel_id=1, source_target_pairs={{0,2},{1,3},{2,0},{3,1},{4,6},{5,7},{6,4},{7,5},{8,10},{9,11},{10,... | collective-permute-start | bytes 460808 | tf_op jit(solution)/shard_map/ppermute | solution.py:26
  67.4 5.9 %collective-permute-start.13 = (bf16[40,1920]{1,0:T(8,128)(2,1)S(1)}, bf16[40,1920]{1,0:T(8,128)(2,1)S(1)}, u32[]{:S(2)}, u32[]{:S(2)}) collective-permute-start(bf16[40,1920]{1,0:T(8,128)(2,1)S(1)} %get-tuple-element.54), channel_id=1, source_target_pairs={{0,2},{1,3},{2,0},{3,1},{4,6},{5,7},{6,4},{7,5},{8,10},{9,11},{10,... | collective-permute-start | bytes 460808 | tf_op jit(solution)/shard_map/ppermute | solution.py:26
  70.6 3.5 %collective-permute-start.12 = (bf16[128,640]{1,0:T(8,128)(2,1)S(1)}, bf16[128,640]{1,0:T(8,128)(2,1)S(1)}, u32[]{:S(2)}, u32[]{:S(2)}) collective-permute-start(bf16[128,640]{1,0:T(8,128)(2,1)S(1)} %add.37), channel_id=1, source_target_pairs={{0,32},{64,96},{128,160},{192,224},{256,288},{320,352},{384,416},{... | collective-permute-start | bytes 491528 | tf_op jit(solution)/shard_map/ppermute | solution.py:280
  74.2 16.5 %collective-permute-start.16 = (bf16[160,1920]{1,0:T(8,128)(2,1)S(1)}, bf16[160,1920]{1,0:T(8,128)(2,1)S(1)}, u32[]{:S(2)}, u32[]{:S(2)}) collective-permute-start(bf16[160,1920]{1,0:T(8,128)(2,1)S(1)} %constant_dynamic-update-slice_fusion.w2), channel_id=1, source_target_pairs={{0,1},{1,0},{2,3},{3,2},{4,5},{5,4},{6,7},{7,6},{8,9},{9,8},{10,11... | collective-permute-start | bytes 1843208 | tf_op jit(solution)/shard_map/ppermute | solution.py:26
  81.6 5.1 %collective-permute-start.14 = (bf16[128,640]{1,0:T(8,128)(2,1)S(1)}, bf16[128,640]{1,0:T(8,128)(2,1)S(1)}, u32[]{:S(2)}, u32[]{:S(2)}) collective-permute-start(bf16[128,640]{1,0:T(8,128)(2,1)S(1)} %add.38), channel_id=1, source_target_pairs={{0,16},{32,48},{64,80},{96,112},{128,144},{160,176},{192,208},{224... | collective-permute-start | bytes 491528 | tf_op jit(solution)/shard_map/ppermute | solution.py:280
  82.9 7.7 %collective-permute-start.15 = (bf16[128,640]{1,0:T(8,128)(2,1)S(1)}, bf16[128,640]{1,0:T(8,128)(2,1)S(1)}, u32[]{:S(2)}, u32[]{:S(2)}) collective-permute-start(bf16[128,640]{1,0:T(8,128)(2,1)S(1)} %broadcast_select_fusion.p0), channel_id=1, source_target_pairs={{0,2},{1,3},{2,0},{3,1},{4,6},{5,7},{6,4},{7,5},{8,10},{9,11},{10,... | collective-permute-start | bytes 491528 | tf_op jit(solution)/shard_map/ppermute | solution.py:26
  90.7 5.9 %collective-permute-start.17 = (bf16[128,640]{1,0:T(8,128)(2,1)S(1)}, bf16[128,640]{1,0:T(8,128)(2,1)S(1)}, u32[]{:S(2)}, u32[]{:S(2)}) collective-permute-start(bf16[128,640]{1,0:T(8,128)(2,1)S(1)} %add.39), channel_id=1, source_target_pairs={{0,8},{16,24},{32,40},{48,56},{64,72},{80,88},{96,104},{112,120},{... | collective-permute-start | bytes 491528 | tf_op jit(solution)/shard_map/ppermute | solution.py:280
  92.0 4.7 %collective-permute-start.18 = (bf16[128,640]{1,0:T(8,128)(2,1)S(1)}, bf16[128,640]{1,0:T(8,128)(2,1)S(1)}, u32[]{:S(2)}, u32[]{:S(2)}) collective-permute-start(bf16[128,640]{1,0:T(8,128)(2,1)S(1)} %broadcast_select_fusion.p0), channel_id=1, source_target_pairs={{0,1},{1,0},{2,3},{3,2},{4,5},{5,4},{6,7},{7,6},{8,9},{9,8},{10,11... | collective-permute-start | bytes 491528 | tf_op jit(solution)/shard_map/ppermute | solution.py:26
  94.7 3.3 %collective-permute-start.19 = (bf16[128,640]{1,0:T(8,128)(2,1)S(1)}, bf16[128,640]{1,0:T(8,128)(2,1)S(1)}, u32[]{:S(2)}, u32[]{:S(2)}) collective-permute-start(bf16[128,640]{1,0:T(8,128)(2,1)S(1)} %collective-permute-done.15.p2), channel_id=1, source_target_pairs={{0,1},{1,0},{2,3},{3,2},{4,5},{5,4},{6,7},{7,6},{8,9},{9,8},{10,11... | collective-permute-start | bytes 491528 | tf_op jit(solution)/shard_map/ppermute | solution.py:26
  98.0 5.0 %collective-permute-start.20 = (bf16[128,640]{1,0:T(8,128)(2,1)S(1)}, bf16[128,640]{1,0:T(8,128)(2,1)S(1)}, u32[]{:S(2)}, u32[]{:S(2)}) collective-permute-start(bf16[128,640]{1,0:T(8,128)(2,1)S(1)} %add.40), channel_id=1, source_target_pairs={{0,4},{8,12},{16,20},{24,28},{32,36},{40,44},{48,52},{56,60},{64,6... | collective-permute-start | bytes 491528 | tf_op jit(solution)/shard_map/ppermute | solution.py:280
  103.0 6.9 %collective-permute-start.21 = (bf16[128,640]{1,0:T(8,128)(2,1)S(1)}, bf16[128,640]{1,0:T(8,128)(2,1)S(1)}, u32[]{:S(2)}, u32[]{:S(2)}) collective-permute-start(bf16[128,640]{1,0:T(8,128)(2,1)S(1)} %add.41.a0), channel_id=1, source_target_pairs={{0,2},{1,3},{2,0},{3,1},{4,6},{5,7},{6,4},{7,5},{8,10},{9,11},{10,... | collective-permute-start | bytes 491528 | tf_op jit(solution)/shard_map/ppermute | solution.py:26
  105.7 7.9 %collective-permute-start.23 = (bf16[128,640]{1,0:T(8,128)(2,1)S(1)}, bf16[128,640]{1,0:T(8,128)(2,1)S(1)}, u32[]{:S(2)}, u32[]{:S(2)}) collective-permute-start(bf16[128,640]{1,0:T(8,128)(2,1)S(1)} %add.41.a0), channel_id=1, source_target_pairs={{0,1},{1,0},{2,3},{3,2},{4,5},{5,4},{6,7},{7,6},{8,9},{9,8},{10,11... | collective-permute-start | bytes 491528 | tf_op jit(solution)/shard_map/ppermute | solution.py:26
  109.9 6.6 %collective-permute-start.22 = (bf16[128,640]{1,0:T(8,128)(2,1)S(1)}, bf16[128,640]{1,0:T(8,128)(2,1)S(1)}, u32[]{:S(2)}, u32[]{:S(2)}) collective-permute-start(bf16[128,640]{1,0:T(8,128)(2,1)S(1)} %collective-permute-done.21.a0), channel_id=1, source_target_pairs={{0,1},{1,0},{2,3},{3,2},{4,5},{5,4},{6,7},{7,6},{8,9},{9,8},{10,11... | collective-permute-start | bytes 491528 | tf_op jit(solution)/shard_map/ppermute | solution.py:26

commit v7 on v6

--- a/solution.py
+++ b/solution.py
@@ -28,12 +28,6 @@
 
 def after(x, *done):
     return lax.optimization_barrier((x, *done))[0]
-
-
-def gathered(x):
-    core = to_rows(x, 1)
-    chip = to_rows(x, 2)
-    return x, core, chip, to_rows(chip, 1)
 
 
 def fetch_kernel(source, out, landed):
@@ -141,22 +135,14 @@
     )
 
 
-def prev_kernel(
-    me_ref, own, p0, p1, p2, p3, w0, w1, w2, w3, query, top, den, acc, weight, joined, keys, vals
-):
-    me = me_ref[0]
-    part, chans = own.shape
-    share = w0.shape[0]
-    for flip, shard in enumerate((w0, w1, w2, w3)):
-        at = pl.multiple_of((me ^ flip) * share, share)
-        weight[pl.ds(at, share), :] = shard[...]
+def first_kernel(feats, a0, a1, weight, query, top, den, acc, joined, keys, vals):
+    chans = feats.shape[1]
     head_dim = chans // HEADS
     scale = head_dim ** (-0.5)
     query[...] = jnp.dot(
-        own[...], weight[:, :chans], preferred_element_type=jnp.float32
+        feats[...], weight[:, :chans], preferred_element_type=jnp.float32
     ).astype(jnp.bfloat16)
-    project((p0, p1, p2, p3), weight, joined, keys, vals)
-    acc[...] = jnp.zeros_like(acc)
+    project((a0, a1), weight, joined, keys, vals)
     for head in range(HEADS):
         window, inside = head_window(head, head_dim, chans)
         s = scores_of(query, keys, head, window, inside)
@@ -189,10 +175,10 @@
 
 
 def more_kernel(
-    query, a0, a1, weight, top, den, acc, new_top, new_den, new_acc, joined, keys, vals
+    query, a0, weight, top, den, acc, new_top, new_den, new_acc, joined, keys, vals
 ):
     for head, window, inside, peak, total, out in attend(
-        (a0, a1), query, weight, top, den, acc, joined, keys, vals
+        (a0,), query, weight, top, den, acc, joined, keys, vals
     ):
         new_top[:, head : head + 1] = peak
         new_den[:, head : head + 1] = total
@@ -200,10 +186,10 @@
 
 
 def last_kernel(
-    query, a0, a1, weight, top, den, acc, residual, restyled, joined, keys, vals, mixed
+    query, a0, weight, top, den, acc, residual, restyled, joined, keys, vals, mixed
 ):
     for head, window, inside, _, total, out in attend(
-        (a0, a1), query, weight, top, den, acc, joined, keys, vals
+        (a0,), query, weight, top, den, acc, joined, keys, vals
     ):
         mixed[:, window] = jnp.where(inside, out / total, mixed[:, window])
     restyled[...] = (residual[...].astype(jnp.float32) + mixed[...]).astype(jnp.bfloat16)
@@ -238,6 +224,7 @@
     bf16, f32 = jnp.bfloat16, jnp.float32
     lat = latents.reshape(part, chans)
 
+    weight = lax.all_gather(qkv_weight, "rows", axis=0, tiled=True)
     fetched = lambda x: call(
         fetch_kernel, [shape(x.shape, x.dtype)], [x], [pltpu.SemaphoreType.DMA], hbm=(0,)
     )[0]
@@ -249,9 +236,8 @@
         [me.reshape(1), lat, lat_core],
     )
     came = to_rows(away, 2)
-    weight_core = to_rows(after(qkv_weight, away), 1)
     taps_weight = fetched(after(conv_weight.reshape(3, 3 * share, chans), away))
-    came = after(came, weight_core, taps_weight)
+    came = after(came, taps_weight)
     group = jnp.arange(share) // (chans // GROUPS)
     pool = (group[:, None] == group[None, :]).astype(f32)
     keep, send = call(
@@ -275,29 +261,19 @@
     )
 
     devices = lax.axis_size("tm")
-    routes = tree_levels(devices)
-    routes = routes + [[]] * (7 - len(routes))
-    tree = lambda level, x: x + lax.ppermute(x, "tm", routes[level])
-    cut = share // 4
-    chunk = lambda at, done: to_rows(after(qkv_weight[at * cut : (at + 1) * cut], done), 2)
     prev = lax.ppermute(feats, "tm", [(i, i + 1) for i in range(devices - 1)])
-    chunks = [chunk(0, feats)]
-    anchor = tree(0, jnp.where(first, feats, jnp.zeros_like(feats)))
+    anchor = jnp.where(first, feats, jnp.zeros_like(feats))
+    for level, route in enumerate(tree_levels(devices)):
+        anchor = anchor + lax.ppermute(anchor, "tm", route)
+        if level == 0:
+            anchor = after(anchor, prev)
     prev = jnp.where(first, feats, after(prev, anchor))
-    anchor = after(anchor, prev, chunks[0])
-    for level in (1, 2, 3):
-        chunks.append(chunk(level, anchor))
-        anchor = after(tree(level, anchor), chunks[level])
-    weight_chip = jnp.concatenate(chunks, axis=0)
-    prev_chip = to_rows(after(prev, anchor), 2)
-    weight_last = to_rows(after(weight_chip, anchor), 1)
-    anchor = after(tree(4, anchor), prev_chip, weight_last)
-    prev_core = to_rows(after(prev, anchor), 1)
-    prev_last = to_rows(after(prev_chip, anchor), 1)
-    anchor = after(tree(5, anchor), prev_core, prev_last)
-    prev = (prev, prev_core, prev_chip, prev_last)
-    qkv = [qkv_weight, weight_core, weight_chip, weight_last]
-
+    weight = fetched(after(weight, anchor))
+
+    own = jnp.concatenate([prev, anchor], axis=0)
+    core = to_rows(own, 1)
+    chip = to_rows(own, 2)
+    keys = 2 * part
     scratch = lambda keys: [pltpu.VMEM((keys, chans), bf16)] * 3
     flops = lambda keys: 2 * keys * chans * 2 * chans + 4 * part * keys * chans
     state = [
@@ -305,27 +281,27 @@
         shape((part, HEADS), f32),
         shape((part, chans), f32),
     ]
-    query, *prior, weight = call(
-        prev_kernel,
-        [shape((part, chans), bf16), *state, shape((chans, 3 * chans), bf16)],
-        [me.reshape(1), after(feats, anchor), *prev, *qkv],
-        scratch(cells),
-        flops=flops(cells),
-    )
-    anchor, anchor_core, anchor_chip, anchor_last = gathered(after(tree(6, anchor), prior[2]))
+    query, *prior = call(
+        first_kernel,
+        [shape((part, chans), bf16), *state],
+        [feats, own, core, weight],
+        scratch(2 * keys),
+        flops=flops(2 * keys),
+    )
+    last = to_rows(after(chip, query), 1)
     prior = call(
         more_kernel,
         state,
-        [query, anchor, anchor_core, weight, *prior],
-        scratch(2 * part),
-        flops=flops(2 * part),
+        [query, chip, weight, *prior],
+        scratch(keys),
+        flops=flops(keys),
     )
     (restyled,) = call(
         last_kernel,
         [shape((part, chans), bf16)],
-        [query, anchor_chip, anchor_last, weight, *prior, residual],
-        scratch(2 * part) + [pltpu.VMEM((part, chans), f32)],
-        flops=flops(2 * part),
+        [query, last, weight, *prior, residual],
+        scratch(keys) + [pltpu.VMEM((part, chans), f32)],
+        flops=flops(keys),
     )
     return restyled.reshape(1, rows_dev, width, chans)
 

time: 122 us -> 126 us (1.033)
  the two profiles are of different devices: /device:TPU:1 before, /device:TPU:495 now
where the time goes in v7:
time: 126 us
  waiting for transfers between devices  57.9 us (46%)
  starting transfers between devices  34.7 us (28%)
  Pallas kernels  13.8 us (11%)
  between operations  13.8 us (11%)
  local copies, waits for them, and re-layouts  4.88 us (4%)
    ppermute x7, waiting for transfers between devices, on_device(): anchor = anchor + lax.ppermute(anchor, 'tm', route)  36.5 us
    ppermute x7, starting transfers between devices, to_rows(): return lax.ppermute(x, 'rows', [(i, i ^ flip) for i in range(4)])  27.5 us
    ppermute x7, waiting for transfers between devices, to_rows(): return lax.ppermute(x, 'rows', [(i, i ^ flip) for i in range(4)])  16.2 us
    pallas_call x9, Pallas kernels, call(): pl.pallas_call(kernel, out_shape=list(outs), in_specs=specs, out_specs=[V...  13.8 us
    ppermute x7, starting transfers between devices, on_device(): anchor = anchor + lax.ppermute(anchor, 'tm', route)  5.31 us
    ppermute x1, waiting for transfers between devices, on_device(): prev = lax.ppermute(feats, 'tm', [(i, i + 1) for i in range(devices - 1)])  4.49 us
    unnamed x10, local copies, waits for them, and re-layouts  4.11 us
  transfers between devices with their start and end apart: 16, of which 7 were waited for; matrix products, arithmetic and copies ran while one was open for 1% of the time, Pallas kernels for 8%

profile of v7, /device:TPU:495, one launch (start us, length us, event | category | flops | bytes accessed | tf_op | source)
XLA Modules:
  0.0 125.6 jit_solution(6950768973199357028)
XLA Ops:
  6.5 0.0 all-gather.2.cloned.1.call-start
  6.5 0.7 all-gather.2.cloned.1.call-update
  7.3 2.6 %collective-permute-start = (bf16[128,640]{1,0:T(8,128)(2,1)}, bf16[128,640]{1,0:T(8,128)(2,1)S(1)}, u32[]{:S(2)}, u32[]{:S(2)}) collective-permute-start(bf16[128,640]{1,0:T(8,128)(2,1)} %bitcast.7), channel_id=1, source_target_pairs={{0,1},{1,0},{2,3},{3,2},{4,5},{5,4},{6,7},{7,6},{8,9},{9,8},{10,11... | collective-permute-start | bytes 491528 | tf_op jit(solution)/shard_map/ppermute | solution.py:26
  9.8 0.0 copy-start.2
  9.9 0.9 copy-done.2
  10.8 0.2 shard_map.64.own.lat
  11.0 0.1 collective-permute-done.core
  11.1 0.2 shard_map.65
  11.3 2.1 %collective-permute-start.1 = (bf16[2,128,160]{2,1,0:T(8,128)(2,1)S(1)}, bf16[2,128,160]{2,1,0:T(8,128)(2,1)S(1)}, u32[]{:S(2)}, u32[]{:S(2)}) collective-permute-start(bf16[2,128,160]{2,1,0:T(8,128)(2,1)S(1)} %get-tuple-element.25), channel_id=1, source_target_pairs={{0,2},{1,3},{2,0},{3,1},{4,6},{5,7},{6,4},{7,5},{8,10},{9,11},{10,... | collective-permute-start | bytes 245768 | tf_op jit(solution)/shard_map/ppermute | solution.py:26
  13.4 0.1 compare_convert_fusion.pool
  13.5 0.8 reshape.54.gain
  14.2 0.0 copy-start.1
  14.2 1.5 %copy-done.1 = bf16[9,160,640]{2,1,0:T(8,128)(2,1)S(1)} copy-done((bf16[9,160,640]{2,1,0:T(8,128)(2,1)S(1)}, bf16[9,160,640]{2,1,0:T(8,128)(2,1)}, u32[]{:S(2)}) %copy-start.1) | copy-done | bytes 1843224
  15.7 0.1 shard_map.66.weight
  15.9 0.0 copy-start.3
  15.9 0.0 copy-start.4
  15.9 2.1 %collective-permute-done.1.came = bf16[2,128,160]{2,1,0:T(8,128)(2,1)S(1)} collective-permute-done((bf16[2,128,160]{2,1,0:T(8,128)(2,1)S(1)}, bf16[2,128,160]{2,1,0:T(8,128)(2,1)S(1)}, u32[]{:S(2)}, u32[]{:S(2)}) %collective-permute-start.1) | collective-permute-done | bytes 81952 | tf_op jit(solution)/shard_map/ppermute | solution.py:26
  18.0 2.4 %shard_map.67 = (f32[2,128,640]{2,1,0:T(8,128)S(1)}, bf16[2,128,640]{2,1,0:T(8,128)(2,1)S(1)}) custom-call(s32[1]{0:T(128)} %bitcast.1.me_ref, bf16[2,128,160]{2,1,0:T(8,128)(2,1)S(1)} %get-tuple-element.24.mine, bf16[2,128,160]{2,1,0:T(8,128)(2,1)S(1)} %collective-permute-done.1.came, f32[4,160]{1,0:T(4,128)S(1)} %reshape.54.gain, ...), custom_call_target="tpu_custom_call" | custom-call | flops 943718400 | bytes 3095044 | tf_op jit(solution)/shard_map/pallas_call | solution.py:205
  20.4 3.0 %collective-permute-start.2 = (bf16[2,128,640]{2,1,0:T(8,128)(2,1)S(1)}, bf16[2,128,640]{2,1,0:T(8,128)(2,1)S(1)}, u32[]{:S(2)}, u32[]{:S(2)}) collective-permute-start(bf16[2,128,640]{2,1,0:T(8,128)(2,1)S(1)} %get-tuple-element.29), channel_id=1, source_target_pairs={{0,1},{1,0},{2,3},{3,2},{4,5},{5,4},{6,7},{7,6},{8,9},{9,8},{10,11... | collective-permute-start | bytes 983048 | tf_op jit(solution)/shard_map/ppermute | solution.py:26
  23.4 1.2 collective-permute-done.2.core
  24.6 2.1 %collective-permute-start.3 = (bf16[128,640]{1,0:T(8,128)(2,1)S(1)}, bf16[128,640]{1,0:T(8,128)(2,1)S(1)}, u32[]{:S(2)}, u32[]{:S(2)}) collective-permute-start(bf16[128,640]{1,0:T(8,128)(2,1)S(1)} %fusion), channel_id=1, source_target_pairs={{0,2},{1,3},{2,0},{3,1},{4,6},{5,7},{6,4},{7,5},{8,10},{9,11},{10,... | collective-permute-start | bytes 491528 | tf_op jit(solution)/shard_map/ppermute | solution.py:26
  26.7 0.0 copy-done.3
  26.8 0.0 copy-done.4
  26.8 8.9 %collective-permute-done.3.chip = bf16[128,640]{1,0:T(8,128)(2,1)S(1)} collective-permute-done((bf16[128,640]{1,0:T(8,128)(2,1)S(1)}, bf16[128,640]{1,0:T(8,128)(2,1)S(1)}, u32[]{:S(2)}, u32[]{:S(2)}) %collective-permute-start.3) | collective-permute-done | bytes 163872 | tf_op jit(solution)/shard_map/ppermute | solution.py:26
  35.7 0.3 shard_map.68
  36.0 0.7 collective-permute-start.5
  36.7 1.9 %collective-permute-start.4 = (bf16[128,640]{1,0:T(8,128)(2,1)S(1)}, bf16[128,640]{1,0:T(8,128)(2,1)S(1)}, u32[]{:S(2)}, u32[]{:S(2)}) collective-permute-start(bf16[128,640]{1,0:T(8,128)(2,1)S(1)} %get-tuple-element.30.feats), channel_id=1, source_target_pairs={{0,4},{4,8},{8,12},{12,16},{16,20},{20,24},{24,28},{28,32},{32,36}... | collective-permute-start | bytes 491528 | tf_op jit(solution)/shard_map/ppermute | solution.py:264
  38.6 0.0 collective-permute-done.5
  38.7 4.5 %collective-permute-done.4 = bf16[128,640]{1,0:T(8,128)(2,1)S(1)} collective-permute-done((bf16[128,640]{1,0:T(8,128)(2,1)S(1)}, bf16[128,640]{1,0:T(8,128)(2,1)S(1)}, u32[]{:S(2)}, u32[]{:S(2)}) %collective-permute-start.4) | collective-permute-done | bytes 163872 | tf_op jit(solution)/shard_map/ppermute | solution.py:264
  43.2 0.7 collective-permute-start.6
  43.9 0.0 collective-permute-done.6
  43.9 0.7 collective-permute-start.7
  44.6 0.0 collective-permute-done.7
  44.7 0.7 collective-permute-start.8
  45.3 0.0 collective-permute-done.8
  45.4 0.7 collective-permute-start.9
  46.1 0.0 collective-permute-done.9
  46.1 0.7 collective-permute-start.10
  46.8 0.0 collective-permute-done.10
  46.9 1.3 %collective-permute-start.11 = (bf16[128,640]{1,0:T(8,128)(2,1)S(1)}, bf16[128,640]{1,0:T(8,128)(2,1)S(1)}, u32[]{:S(2)}, u32[]{:S(2)}) collective-permute-start(bf16[128,640]{1,0:T(8,128)(2,1)S(1)} %add.40), channel_id=1, source_target_pairs={{0,4},{8,12},{16,20},{24,28},{32,36},{40,44},{48,52},{56,60},{64,6... | collective-permute-start | bytes 491528 | tf_op jit(solution)/shard_map/ppermute | solution.py:267
  48.2 36.5 %collective-permute-done.11 = bf16[128,640]{1,0:T(8,128)(2,1)S(1)} collective-permute-done((bf16[128,640]{1,0:T(8,128)(2,1)S(1)}, bf16[128,640]{1,0:T(8,128)(2,1)S(1)}, u32[]{:S(2)}, u32[]{:S(2)}) %collective-permute-start.11) | collective-permute-done | bytes 163872 | tf_op jit(solution)/shard_map/ppermute | solution.py:267
  84.8 13.1 %collective-permute-start.12 = (bf16[256,640]{1,0:T(8,128)(2,1)S(1)}, bf16[256,640]{1,0:T(8,128)(2,1)S(1)}, u32[]{:S(2)}, u32[]{:S(2)}) collective-permute-start(bf16[256,640]{1,0:T(8,128)(2,1)S(1)} %pad_maximum_fusion.a0), channel_id=1, source_target_pairs={{0,1},{1,0},{2,3},{3,2},{4,5},{5,4},{6,7},{7,6},{8,9},{9,8},{10,11... | collective-permute-start | bytes 983048 | tf_op jit(solution)/shard_map/ppermute | solution.py:26
  97.9 1.9 %collective-permute-start.13 = (bf16[256,640]{1,0:T(8,128)(2,1)S(1)}, bf16[256,640]{1,0:T(8,128)(2,1)S(1)}, u32[]{:S(2)}, u32[]{:S(2)}) collective-permute-start(bf16[256,640]{1,0:T(8,128)(2,1)S(1)} %pad_maximum_fusion.a0), channel_id=1, source_target_pairs={{0,2},{1,3},{2,0},{3,1},{4,6},{5,7},{6,4},{7,5},{8,10},{9,11},{10,... | collective-permute-start | bytes 983048 | tf_op jit(solution)/shard_map/ppermute | solution.py:26
  99.8 0.0 all-gather.2.cloned.1.call-done.source
  99.9 0.0 copy-start
  99.9 1.7 %copy-done = bf16[640,1920]{1,0:T(8,128)(2,1)S(1)} copy-done((bf16[640,1920]{1,0:T(8,128)(2,1)S(1)}, bf16[640,1920]{1,0:T(8,128)(2,1)}, u32[]{:S(2)}) %copy-start) | copy-done | bytes 2457624
  101.5 0.3 shard_map.69.weight
  101.8 0.0 collective-permute-done.12.a1
  101.9 3.4 %shard_map.70 = (bf16[128,640]{1,0:T(8,128)(2,1)S(1)}, f32[128,8]{1,0:T(8,128)S(1)}, f32[128,8]{1,0:T(8,128)S(1)}, f32[128,640]{1,0:T(8,128)S(1)}) custom-call(bf16[128,640]{1,0:T(8,128)(2,1)S(1)} %get-tuple-element.30.feats, bf16[256,640]{1,0:T(8,128)(2,1)S(1)} %pad_maximum_fusion.a0, bf16[256,640]{1,0:T(8,128)(2,1)S(1)} %collective-permute-done.12.a1, ...), custom_call_target="tpu_custom_call" | custom-call | flops 1006632960 | bytes 3776512 | tf_op jit(solution)/shard_map/pallas_call | solution.py:205
  105.3 3.9 %collective-permute-done.13.a0 = bf16[256,640]{1,0:T(8,128)(2,1)S(1)} collective-permute-done((bf16[256,640]{1,0:T(8,128)(2,1)S(1)}, bf16[256,640]{1,0:T(8,128)(2,1)S(1)}, u32[]{:S(2)}, u32[]{:S(2)}) %collective-permute-start.13) | collective-permute-done | bytes 327712 | tf_op jit(solution)/shard_map/ppermute | solution.py:26
  109.1 2.7 %collective-permute-start.14 = (bf16[256,640]{1,0:T(8,128)(2,1)S(1)}, bf16[256,640]{1,0:T(8,128)(2,1)S(1)}, u32[]{:S(2)}, u32[]{:S(2)}) collective-permute-start(bf16[256,640]{1,0:T(8,128)(2,1)S(1)} %collective-permute-done.13.a0), channel_id=1, source_target_pairs={{0,1},{1,0},{2,3},{3,2},{4,5},{5,4},{6,7},{7,6},{8,9},{9,8},{10,11... | collective-permute-start | bytes 983048 | tf_op jit(solution)/shard_map/ppermute | solution.py:26
  111.8 2.9 %shard_map.71 = (f32[128,8]{1,0:T(8,128)S(1)}, f32[128,8]{1,0:T(8,128)S(1)}, f32[128,640]{1,0:T(8,128)S(1)}) custom-call(bf16[128,640]{1,0:T(8,128)(2,1)S(1)} %get-tuple-element.34.query, bf16[256,640]{1,0:T(8,128)(2,1)S(1)} %collective-permute-done.13.a0, bf16[640,1920]{1,0:T(8,128)(2,1)S(1)} %shard_map.69.weight, f32[128,8]{1,0:T(8,128)S(1)} %get-tuple-element.36.top, ...), custom_call_target="tpu_custom_call" | custom-call | flops 503316480 | bytes 3620864 | tf_op jit(solution)/shard_map/pallas_call | solution.py:205
  114.7 0.0 collective-permute-done.14.a0
  114.7 4.1 %shard_map.72 = bf16[128,640]{1,0:T(8,128)(2,1)} custom-call(bf16[128,640]{1,0:T(8,128)(2,1)S(1)} %get-tuple-element.34.query, bf16[256,640]{1,0:T(8,128)(2,1)S(1)} %collective-permute-done.14.a0, bf16[640,1920]{1,0:T(8,128)(2,1)S(1)} %shard_map.69.weight, f32[128,8]{1,0:T(8,128)S(1)} %get-tuple-element.39.top, f32[128,8]{1,0:T(8,128)S(1)} %get-tuple-element.40.den, ...), custom_call_target="tpu_custom_call" | custom-call | flops 503316480 | bytes 3612672 | tf_op jit(solution)/shard_map/pallas_call | solution.py:205
  (14 shorter events, 0.4 us)
Async XLA Ops:
  6.5 93.3 %all-gather.2.cloned.1.call-start = ((), (), s32[]{:S(2)}) async-start(), calls=%async_computation | async-start | bytes 3072000 | tf_op jit(solution)/shard_map/all_gather | solution.py:227
  7.3 3.8 %collective-permute-start = (bf16[128,640]{1,0:T(8,128)(2,1)}, bf16[128,640]{1,0:T(8,128)(2,1)S(1)}, u32[]{:S(2)}, u32[]{:S(2)}) collective-permute-start(bf16[128,640]{1,0:T(8,128)(2,1)} %bitcast.7), channel_id=1, source_target_pairs={{0,1},{1,0},{2,3},{3,2},{4,5},{5,4},{6,7},{7,6},{8,9},{9,8},{10,11... | collective-permute-start | bytes 491528 | tf_op jit(solution)/shard_map/ppermute | solution.py:26
  9.8 0.9 copy-start.2
  11.3 6.7 %collective-permute-start.1 = (bf16[2,128,160]{2,1,0:T(8,128)(2,1)S(1)}, bf16[2,128,160]{2,1,0:T(8,128)(2,1)S(1)}, u32[]{:S(2)}, u32[]{:S(2)}) collective-permute-start(bf16[2,128,160]{2,1,0:T(8,128)(2,1)S(1)} %get-tuple-element.25), channel_id=1, source_target_pairs={{0,2},{1,3},{2,0},{3,1},{4,6},{5,7},{6,4},{7,5},{8,10},{9,11},{10,... | collective-permute-start | bytes 245768 | tf_op jit(solution)/shard_map/ppermute | solution.py:26
  14.2 1.5 %copy-start.1 = (bf16[9,160,640]{2,1,0:T(8,128)(2,1)S(1)}, bf16[9,160,640]{2,1,0:T(8,128)(2,1)}, u32[]{:S(2)}) copy-start(bf16[9,160,640]{2,1,0:T(8,128)(2,1)} %param.8) | copy-start | bytes 5529604
  15.9 10.9 %copy-start.3 = (f32[640]{0:T(1024)S(1)}, f32[640]{0:T(1024)}, u32[]{:S(2)}) copy-start(f32[640]{0:T(1024)} %param.9) | copy-start | bytes 7684
  15.9 10.9 %copy-start.4 = (f32[640]{0:T(1024)S(1)}, f32[640]{0:T(1024)}, u32[]{:S(2)}) copy-start(f32[640]{0:T(1024)} %param.10) | copy-start | bytes 7684
  20.4 4.3 %collective-permute-start.2 = (bf16[2,128,640]{2,1,0:T(8,128)(2,1)S(1)}, bf16[2,128,640]{2,1,0:T(8,128)(2,1)S(1)}, u32[]{:S(2)}, u32[]{:S(2)}) collective-permute-start(bf16[2,128,640]{2,1,0:T(8,128)(2,1)S(1)} %get-tuple-element.29), channel_id=1, source_target_pairs={{0,1},{1,0},{2,3},{3,2},{4,5},{5,4},{6,7},{7,6},{8,9},{9,8},{10,11... | collective-permute-start | bytes 983048 | tf_op jit(solution)/shard_map/ppermute | solution.py:26
  24.6 11.1 %collective-permute-start.3 = (bf16[128,640]{1,0:T(8,128)(2,1)S(1)}, bf16[128,640]{1,0:T(8,128)(2,1)S(1)}, u32[]{:S(2)}, u32[]{:S(2)}) collective-permute-start(bf16[128,640]{1,0:T(8,128)(2,1)S(1)} %fusion), channel_id=1, source_target_pairs={{0,2},{1,3},{2,0},{3,1},{4,6},{5,7},{6,4},{7,5},{8,10},{9,11},{10,... | collective-permute-start | bytes 491528 | tf_op jit(solution)/shard_map/ppermute | solution.py:26
  36.0 2.6 %collective-permute-start.5 = (bf16[128,640]{1,0:T(8,128)(2,1)S(1)}, bf16[128,640]{1,0:T(8,128)(2,1)S(1)}, u32[]{:S(2)}, u32[]{:S(2)}) collective-permute-start(bf16[128,640]{1,0:T(8,128)(2,1)S(1)} %broadcast_select_fusion.1), channel_id=1, source_target_pairs={{0,256},{1,257},{2,258},{3,259}} | collective-permute-start | bytes 491528 | tf_op jit(solution)/shard_map/ppermute | solution.py:267
  36.7 6.5 %collective-permute-start.4 = (bf16[128,640]{1,0:T(8,128)(2,1)S(1)}, bf16[128,640]{1,0:T(8,128)(2,1)S(1)}, u32[]{:S(2)}, u32[]{:S(2)}) collective-permute-start(bf16[128,640]{1,0:T(8,128)(2,1)S(1)} %get-tuple-element.30.feats), channel_id=1, source_target_pairs={{0,4},{4,8},{8,12},{12,16},{16,20},{20,24},{24,28},{28,32},{32,36}... | collective-permute-start | bytes 491528 | tf_op jit(solution)/shard_map/ppermute | solution.py:264
  43.2 0.7 collective-permute-start.6
  43.9 0.7 collective-permute-start.7
  44.7 0.7 collective-permute-start.8
  45.4 0.7 collective-permute-start.9
  46.1 0.7 collective-permute-start.10
  46.9 37.8 %collective-permute-start.11 = (bf16[128,640]{1,0:T(8,128)(2,1)S(1)}, bf16[128,640]{1,0:T(8,128)(2,1)S(1)}, u32[]{:S(2)}, u32[]{:S(2)}) collective-permute-start(bf16[128,640]{1,0:T(8,128)(2,1)S(1)} %add.40), channel_id=1, source_target_pairs={{0,4},{8,12},{16,20},{24,28},{32,36},{40,44},{48,52},{56,60},{64,6... | collective-permute-start | bytes 491528 | tf_op jit(solution)/shard_map/ppermute | solution.py:267
  84.8 17.1 %collective-permute-start.12 = (bf16[256,640]{1,0:T(8,128)(2,1)S(1)}, bf16[256,640]{1,0:T(8,128)(2,1)S(1)}, u32[]{:S(2)}, u32[]{:S(2)}) collective-permute-start(bf16[256,640]{1,0:T(8,128)(2,1)S(1)} %pad_maximum_fusion.a0), channel_id=1, source_target_pairs={{0,1},{1,0},{2,3},{3,2},{4,5},{5,4},{6,7},{7,6},{8,9},{9,8},{10,11... | collective-permute-start | bytes 983048 | tf_op jit(solution)/shard_map/ppermute | solution.py:26
  97.9 11.2 %collective-permute-start.13 = (bf16[256,640]{1,0:T(8,128)(2,1)S(1)}, bf16[256,640]{1,0:T(8,128)(2,1)S(1)}, u32[]{:S(2)}, u32[]{:S(2)}) collective-permute-start(bf16[256,640]{1,0:T(8,128)(2,1)S(1)} %pad_maximum_fusion.a0), channel_id=1, source_target_pairs={{0,2},{1,3},{2,0},{3,1},{4,6},{5,7},{6,4},{7,5},{8,10},{9,11},{10,... | collective-permute-start | bytes 983048 | tf_op jit(solution)/shard_map/ppermute | solution.py:26
  99.9 1.7 %copy-start = (bf16[640,1920]{1,0:T(8,128)(2,1)S(1)}, bf16[640,1920]{1,0:T(8,128)(2,1)}, u32[]{:S(2)}) copy-start(bf16[640,1920]{1,0:T(8,128)(2,1)} %all-gather.2.cloned.1.call-done.source) | copy-start | bytes 7372804
  109.1 5.6 %collective-permute-start.14 = (bf16[256,640]{1,0:T(8,128)(2,1)S(1)}, bf16[256,640]{1,0:T(8,128)(2,1)S(1)}, u32[]{:S(2)}, u32[]{:S(2)}) collective-permute-start(bf16[256,640]{1,0:T(8,128)(2,1)S(1)} %collective-permute-done.13.a0), channel_id=1, source_target_pairs={{0,1},{1,0},{2,3},{3,2},{4,5},{5,4},{6,7},{7,6},{8,9},{9,8},{10,11... | collective-permute-start | bytes 983048 | tf_op jit(solution)/shard_map/ppermute | solution.py:26
Sparse Core Ops, SparseCore 0:
  9.5 41.6 all-gather.1

commit v8 on v7

--- a/solution.py
+++ b/solution.py
@@ -15,10 +15,13 @@
 
 
 def tree_levels(devices):
-    levels, step = [], devices // 2
-    while step:
-        levels.append([(tm, tm + step) for tm in range(0, devices, 2 * step)])
-        step //= 2
+    steps = []
+    while 2 ** len(steps) < devices:
+        steps.insert(0, 2 ** len(steps))
+    levels, known = [], [0]
+    for step in steps[1:] + steps[:1]:
+        levels.append([(tm, tm + step) for tm in known])
+        known = known + [tm + step for tm in known]
     return levels
 
 
@@ -135,8 +138,15 @@
     )
 
 
-def first_kernel(feats, a0, a1, weight, query, top, den, acc, joined, keys, vals):
+def first_kernel(
+    me_ref, feats, a0, a1, w0, w1, w2, w3, query, top, den, acc, weight, joined, keys, vals
+):
+    me = me_ref[0]
     chans = feats.shape[1]
+    share = w0.shape[0]
+    for flip, shard in enumerate((w0, w1, w2, w3)):
+        at = pl.multiple_of((me ^ flip) * share, share)
+        weight[pl.ds(at, share), :] = shard[...]
     head_dim = chans // HEADS
     scale = head_dim ** (-0.5)
     query[...] = jnp.dot(
@@ -224,7 +234,6 @@
     bf16, f32 = jnp.bfloat16, jnp.float32
     lat = latents.reshape(part, chans)
 
-    weight = lax.all_gather(qkv_weight, "rows", axis=0, tiled=True)
     fetched = lambda x: call(
         fetch_kernel, [shape(x.shape, x.dtype)], [x], [pltpu.SemaphoreType.DMA], hbm=(0,)
     )[0]
@@ -236,8 +245,9 @@
         [me.reshape(1), lat, lat_core],
     )
     came = to_rows(away, 2)
+    weight_core = to_rows(after(qkv_weight, away), 1)
     taps_weight = fetched(after(conv_weight.reshape(3, 3 * share, chans), away))
-    came = after(came, taps_weight)
+    came = after(came, weight_core, taps_weight)
     group = jnp.arange(share) // (chans // GROUPS)
     pool = (group[:, None] == group[None, :]).astype(f32)
     keep, send = call(
@@ -261,14 +271,24 @@
     )
 
     devices = lax.axis_size("tm")
+    routes = tree_levels(devices)
     prev = lax.ppermute(feats, "tm", [(i, i + 1) for i in range(devices - 1)])
+    weight_chip = to_rows(after(qkv_weight, feats), 2)
+
+    def levels(anchor, which):
+        for route in which:
+            anchor = anchor + lax.ppermute(anchor, "tm", route)
+        return anchor
+
+    trips = 1 + jnp.minimum(lax.axis_index("tm"), 0)
     anchor = jnp.where(first, feats, jnp.zeros_like(feats))
-    for level, route in enumerate(tree_levels(devices)):
-        anchor = anchor + lax.ppermute(anchor, "tm", route)
-        if level == 0:
-            anchor = after(anchor, prev)
+    anchor = lax.fori_loop(0, trips, lambda _, a: levels(a, routes[:4]), anchor)
+    anchor = after(anchor, prev, weight_chip)
+    weight_last = to_rows(after(weight_chip, anchor), 1)
+    anchor = after(levels(anchor, routes[4:5]), weight_last)
+    anchor = levels(anchor, routes[5:])
     prev = jnp.where(first, feats, after(prev, anchor))
-    weight = fetched(after(weight, anchor))
+    shards = [qkv_weight, weight_core, weight_chip, weight_last]
 
     own = jnp.concatenate([prev, anchor], axis=0)
     core = to_rows(own, 1)
@@ -281,10 +301,10 @@
         shape((part, HEADS), f32),
         shape((part, chans), f32),
     ]
-    query, *prior = call(
+    query, *prior, weight = call(
         first_kernel,
-        [shape((part, chans), bf16), *state],
-        [feats, own, core, weight],
+        [shape((part, chans), bf16), *state, shape((chans, 3 * chans), bf16)],
+        [me.reshape(1), feats, own, core, *shards],
         scratch(2 * keys),
         flops=flops(2 * keys),
     )

time: 126 us -> 117 us (0.929)
  the two profiles are of different devices: /device:TPU:495 before, /device:TPU:503 now
where the time goes in v8:
time: 117 us
  waiting for transfers between devices  62.5 us (53%)
  starting transfers between devices  36.2 us (31%)
  Pallas kernels  13.8 us (12%)
  local copies, waits for them, and re-layouts  3.2 us (3%)
    ppermute x7, waiting for transfers between devices, levels(): anchor = anchor + lax.ppermute(anchor, 'tm', route)  40.9 us
    ppermute x10, starting transfers between devices, to_rows(): return lax.ppermute(x, 'rows', [(i, i ^ flip) for i in range(4)])  29.6 us
    ppermute x10, waiting for transfers between devices, to_rows(): return lax.ppermute(x, 'rows', [(i, i ^ flip) for i in range(4)])  19.6 us
    pallas_call x8, Pallas kernels, call(): pl.pallas_call(kernel, out_shape=list(outs), in_specs=specs, out_specs=[V...  13.8 us
    ppermute x7, starting transfers between devices, levels(): anchor = anchor + lax.ppermute(anchor, 'tm', route)  5.31 us
    unnamed x10, local copies, waits for them, and re-layouts  2.43 us
  transfers between devices with their start and end apart: 18, of which 9 were waited for; matrix products, arithmetic and copies ran while one was open for 1% of the time, Pallas kernels for 6%

profile of v8, /device:TPU:503, one launch (start us, length us, event | category | flops | bytes accessed | tf_op | source)
XLA Modules:
  0.0 116.7 jit_solution(4063896789317600340)
XLA Ops:
  0.0 2.6 %collective-permute-start.4 = (bf16[128,640]{1,0:T(8,128)(2,1)}, bf16[128,640]{1,0:T(8,128)(2,1)S(1)}, u32[]{:S(2)}, u32[]{:S(2)}) collective-permute-start(bf16[128,640]{1,0:T(8,128)(2,1)} %bitcast.7), channel_id=1, source_target_pairs={{0,1},{1,0},{2,3},{3,2},{4,5},{5,4},{6,7},{7,6},{8,9},{9,8},{10,11... | collective-permute-start | bytes 491528 | tf_op jit(solution)/shard_map/ppermute | solution.py:29
  2.6 0.0 copy-start.1
  2.6 0.9 copy-done.1
  3.5 0.2 shard_map.64.own.lat
  3.7 0.1 collective-permute-done.4.core
  3.8 0.2 shard_map.65
  4.0 2.2 %collective-permute-start.6 = (bf16[160,1920]{1,0:T(8,128)(2,1)}, bf16[160,1920]{1,0:T(8,128)(2,1)S(1)}, u32[]{:S(2)}, u32[]{:S(2)}) collective-permute-start(bf16[160,1920]{1,0:T(8,128)(2,1)} %w0.1), channel_id=1, source_target_pairs={{0,1},{1,0},{2,3},{3,2},{4,5},{5,4},{6,7},{7,6},{8,9},{9,8},{10,11... | collective-permute-start | bytes 1843208 | tf_op jit(solution)/shard_map/ppermute | solution.py:29
  6.2 2.9 %collective-permute-start.5 = (bf16[2,128,160]{2,1,0:T(8,128)(2,1)S(1)}, bf16[2,128,160]{2,1,0:T(8,128)(2,1)S(1)}, u32[]{:S(2)}, u32[]{:S(2)}) collective-permute-start(bf16[2,128,160]{2,1,0:T(8,128)(2,1)S(1)} %get-tuple-element.47), channel_id=1, source_target_pairs={{0,2},{1,3},{2,0},{3,1},{4,6},{5,7},{6,4},{7,5},{8,10},{9,11},{10,... | collective-permute-start | bytes 245768 | tf_op jit(solution)/shard_map/ppermute | solution.py:29
  9.2 0.1 compare_convert_fusion.pool
  9.2 0.8 reshape.55.gain
  10.0 0.0 copy-start
  10.0 1.5 %copy-done = bf16[9,160,640]{2,1,0:T(8,128)(2,1)S(1)} copy-done((bf16[9,160,640]{2,1,0:T(8,128)(2,1)S(1)}, bf16[9,160,640]{2,1,0:T(8,128)(2,1)}, u32[]{:S(2)}) %copy-start) | copy-done | bytes 1843224
  11.5 0.1 shard_map.66.weight
  11.7 1.3 %collective-permute-done.5.came = bf16[2,128,160]{2,1,0:T(8,128)(2,1)S(1)} collective-permute-done((bf16[2,128,160]{2,1,0:T(8,128)(2,1)S(1)}, bf16[2,128,160]{2,1,0:T(8,128)(2,1)S(1)}, u32[]{:S(2)}, u32[]{:S(2)}) %collective-permute-start.5) | collective-permute-done | bytes 81952 | tf_op jit(solution)/shard_map/ppermute | solution.py:29
  13.0 0.0 collective-permute-done.6.w1
  13.0 0.0 copy-start.3
  13.0 0.0 copy-start.4
  13.0 2.4 %shard_map.67 = (f32[2,128,640]{2,1,0:T(8,128)S(1)}, bf16[2,128,640]{2,1,0:T(8,128)(2,1)S(1)}) custom-call(s32[1]{0:T(128)} %bitcast.me_ref, bf16[2,128,160]{2,1,0:T(8,128)(2,1)S(1)} %get-tuple-element.46.mine, bf16[2,128,160]{2,1,0:T(8,128)(2,1)S(1)} %collective-permute-done.5.came, f32[4,160]{1,0:T(4,128)S(1)} %reshape.55.gain, ...), custom_call_target="tpu_custom_call" | custom-call | flops 943718400 | bytes 3095044 | tf_op jit(solution)/shard_map/pallas_call | solution.py:215
  15.4 0.0 copy-start.2
  15.4 3.1 %collective-permute-start.7 = (bf16[2,128,640]{2,1,0:T(8,128)(2,1)S(1)}, bf16[2,128,640]{2,1,0:T(8,128)(2,1)S(1)}, u32[]{:S(2)}, u32[]{:S(2)}) collective-permute-start(bf16[2,128,640]{2,1,0:T(8,128)(2,1)S(1)} %get-tuple-element.52), channel_id=1, source_target_pairs={{0,1},{1,0},{2,3},{3,2},{4,5},{5,4},{6,7},{7,6},{8,9},{9,8},{10,11... | collective-permute-start | bytes 983048 | tf_op jit(solution)/shard_map/ppermute | solution.py:29
  18.5 1.2 %collective-permute-done.7.core = bf16[2,128,640]{2,1,0:T(8,128)(2,1)S(1)} collective-permute-done((bf16[2,128,640]{2,1,0:T(8,128)(2,1)S(1)}, bf16[2,128,640]{2,1,0:T(8,128)(2,1)S(1)}, u32[]{:S(2)}, u32[]{:S(2)}) %collective-permute-start.7) | collective-permute-done | bytes 327712 | tf_op jit(solution)/shard_map/ppermute | solution.py:29
  19.8 2.9 %collective-permute-start.8 = (bf16[128,640]{1,0:T(8,128)(2,1)S(1)}, bf16[128,640]{1,0:T(8,128)(2,1)S(1)}, u32[]{:S(2)}, u32[]{:S(2)}) collective-permute-start(bf16[128,640]{1,0:T(8,128)(2,1)S(1)} %fusion), channel_id=1, source_target_pairs={{0,2},{1,3},{2,0},{3,1},{4,6},{5,7},{6,4},{7,5},{8,10},{9,11},{10,... | collective-permute-start | bytes 491528 | tf_op jit(solution)/shard_map/ppermute | solution.py:29
  22.7 0.0 copy-done.3
  22.7 0.0 copy-done.4
  22.7 4.4 %collective-permute-done.8.chip = bf16[128,640]{1,0:T(8,128)(2,1)S(1)} collective-permute-done((bf16[128,640]{1,0:T(8,128)(2,1)S(1)}, bf16[128,640]{1,0:T(8,128)(2,1)S(1)}, u32[]{:S(2)}, u32[]{:S(2)}) %collective-permute-start.8) | collective-permute-done | bytes 163872 | tf_op jit(solution)/shard_map/ppermute | solution.py:29
  27.1 0.3 shard_map.68
  27.4 0.0 copy-done.2
  27.4 2.9 %collective-permute-start.10 = (bf16[160,1920]{1,0:T(8,128)(2,1)S(1)}, bf16[160,1920]{1,0:T(8,128)(2,1)S(1)}, u32[]{:S(2)}, u32[]{:S(2)}) collective-permute-start(bf16[160,1920]{1,0:T(8,128)(2,1)S(1)} %copy-done.2), channel_id=1, source_target_pairs={{0,2},{1,3},{2,0},{3,1},{4,6},{5,7},{6,4},{7,5},{8,10},{9,11},{10,... | collective-permute-start | bytes 1843208 | tf_op jit(solution)/shard_map/ppermute | solution.py:29
  30.3 1.3 %collective-permute-start.9 = (bf16[128,640]{1,0:T(8,128)(2,1)S(1)}, bf16[128,640]{1,0:T(8,128)(2,1)S(1)}, u32[]{:S(2)}, u32[]{:S(2)}) collective-permute-start(bf16[128,640]{1,0:T(8,128)(2,1)S(1)} %get-tuple-element.53.feats), channel_id=1, source_target_pairs={{0,4},{4,8},{8,12},{12,16},{16,20},{20,24},{24,28},{28,32},{32,36}... | collective-permute-start | bytes 491528 | tf_op jit(solution)/shard_map/ppermute | solution.py:275
  31.6 3.0 %while.10 = (s32[]{:T(128)}, bf16[128,640]{1,0:T(8,128)(2,1)S(1)}, s32[]{:T(128)}, s32[]{:T(128)}) while((s32[]{:T(128)}, bf16[128,640]{1,0:T(8,128)(2,1)S(1)}, s32[]{:T(128)}, s32[]{:T(128)}) %tuple.36), condition=%wide.region_1.2_spmd, body=%wide.region_0.1_spmd.sunk | while | flops 327682 | bytes 4587733 | solution.py:285
  31.6 0.7 collective-permute-start
  32.3 0.0 collective-permute-done
  32.4 0.7 collective-permute-start.1
  33.0 0.0 collective-permute-done.1
  33.1 0.7 collective-permute-start.2
  33.8 0.0 collective-permute-done.2
  33.8 0.7 collective-permute-start.3
  34.5 0.0 collective-permute-done.3
  34.6 2.0 %collective-permute-done.9 = bf16[128,640]{1,0:T(8,128)(2,1)S(1)} collective-permute-done((bf16[128,640]{1,0:T(8,128)(2,1)S(1)}, bf16[128,640]{1,0:T(8,128)(2,1)S(1)}, u32[]{:S(2)}, u32[]{:S(2)}) %collective-permute-start.9) | collective-permute-done | bytes 163872 | tf_op jit(solution)/shard_map/ppermute | solution.py:275
  36.6 6.8 %collective-permute-done.10.w2 = bf16[160,1920]{1,0:T(8,128)(2,1)S(1)} collective-permute-done((bf16[160,1920]{1,0:T(8,128)(2,1)S(1)}, bf16[160,1920]{1,0:T(8,128)(2,1)S(1)}, u32[]{:S(2)}, u32[]{:S(2)}) %collective-permute-start.10) | collective-permute-done | bytes 614432 | tf_op jit(solution)/shard_map/ppermute | solution.py:29
  43.4 4.0 %collective-permute-start.12 = (bf16[160,1920]{1,0:T(8,128)(2,1)S(1)}, bf16[160,1920]{1,0:T(8,128)(2,1)S(1)}, u32[]{:S(2)}, u32[]{:S(2)}) collective-permute-start(bf16[160,1920]{1,0:T(8,128)(2,1)S(1)} %collective-permute-done.10.w2), channel_id=1, source_target_pairs={{0,1},{1,0},{2,3},{3,2},{4,5},{5,4},{6,7},{7,6},{8,9},{9,8},{10,11... | collective-permute-start | bytes 1843208 | tf_op jit(solution)/shard_map/ppermute | solution.py:29
  47.4 0.7 collective-permute-start.11
  48.1 0.0 collective-permute-done.11
  48.2 0.9 collective-permute-done.12.w3
  49.1 0.7 collective-permute-start.13
  49.7 0.0 collective-permute-done.13
  49.8 1.3 %collective-permute-start.14 = (bf16[128,640]{1,0:T(8,128)(2,1)S(1)}, bf16[128,640]{1,0:T(8,128)(2,1)S(1)}, u32[]{:S(2)}, u32[]{:S(2)}) collective-permute-start(bf16[128,640]{1,0:T(8,128)(2,1)S(1)} %add.43), channel_id=1, source_target_pairs={{0,256},{128,384},{64,320},{192,448},{32,288},{160,416},{96,352},{... | collective-permute-start | bytes 491528 | tf_op jit(solution)/shard_map/ppermute | solution.py:280
  51.1 40.8 %collective-permute-done.14 = bf16[128,640]{1,0:T(8,128)(2,1)S(1)} collective-permute-done((bf16[128,640]{1,0:T(8,128)(2,1)S(1)}, bf16[128,640]{1,0:T(8,128)(2,1)S(1)}, u32[]{:S(2)}, u32[]{:S(2)}) %collective-permute-start.14) | collective-permute-done | bytes 163872 | tf_op jit(solution)/shard_map/ppermute | solution.py:280
  92.1 3.7 %collective-permute-start.15 = (bf16[256,640]{1,0:T(8,128)(2,1)S(1)}, bf16[256,640]{1,0:T(8,128)(2,1)S(1)}, u32[]{:S(2)}, u32[]{:S(2)}) collective-permute-start(bf16[256,640]{1,0:T(8,128)(2,1)S(1)} %pad_maximum_fusion.a0), channel_id=1, source_target_pairs={{0,1},{1,0},{2,3},{3,2},{4,5},{5,4},{6,7},{7,6},{8,9},{9,8},{10,11... | collective-permute-start | bytes 983048 | tf_op jit(solution)/shard_map/ppermute | solution.py:29
  95.7 2.7 %collective-permute-start.16 = (bf16[256,640]{1,0:T(8,128)(2,1)S(1)}, bf16[256,640]{1,0:T(8,128)(2,1)S(1)}, u32[]{:S(2)}, u32[]{:S(2)}) collective-permute-start(bf16[256,640]{1,0:T(8,128)(2,1)S(1)} %pad_maximum_fusion.a0), channel_id=1, source_target_pairs={{0,2},{1,3},{2,0},{3,1},{4,6},{5,7},{6,4},{7,5},{8,10},{9,11},{10,... | collective-permute-start | bytes 983048 | tf_op jit(solution)/shard_map/ppermute | solution.py:29
  98.4 0.0 collective-permute-done.15.a1
  98.5 3.6 %shard_map.69 = (bf16[128,640]{1,0:T(8,128)(2,1)S(1)}, f32[128,8]{1,0:T(8,128)S(1)}, f32[128,8]{1,0:T(8,128)S(1)}, f32[128,640]{1,0:T(8,128)S(1)}, bf16[640,1920]{1,0:T(8,128)(2,1)S(1)}) custom-call(s32[1]{0:T(128)} %bitcast.me_ref, bf16[128,640]{1,0:T(8,128)(2,1)S(1)} %get-tuple-element.53.feats, bf16[256,640]{1,0:T(8,128)(2,1)S(1)} %pad_maximum_fusion.a0, ...), custom_call_target="tpu_custom_call" | custom-call | flops 1006632960 | bytes 6234116 | tf_op jit(solution)/shard_map/pallas_call | solution.py:215
  102.0 4.9 %collective-permute-done.16.a0 = bf16[256,640]{1,0:T(8,128)(2,1)S(1)} collective-permute-done((bf16[256,640]{1,0:T(8,128)(2,1)S(1)}, bf16[256,640]{1,0:T(8,128)(2,1)S(1)}, u32[]{:S(2)}, u32[]{:S(2)}) %collective-permute-start.16) | collective-permute-done | bytes 327712 | tf_op jit(solution)/shard_map/ppermute | solution.py:29
  107.0 2.7 %collective-permute-start.17 = (bf16[256,640]{1,0:T(8,128)(2,1)S(1)}, bf16[256,640]{1,0:T(8,128)(2,1)S(1)}, u32[]{:S(2)}, u32[]{:S(2)}) collective-permute-start(bf16[256,640]{1,0:T(8,128)(2,1)S(1)} %collective-permute-done.16.a0), channel_id=1, source_target_pairs={{0,1},{1,0},{2,3},{3,2},{4,5},{5,4},{6,7},{7,6},{8,9},{9,8},{10,11... | collective-permute-start | bytes 983048 | tf_op jit(solution)/shard_map/ppermute | solution.py:29
  109.7 2.9 %shard_map.70 = (f32[128,8]{1,0:T(8,128)S(1)}, f32[128,8]{1,0:T(8,128)S(1)}, f32[128,640]{1,0:T(8,128)S(1)}) custom-call(bf16[128,640]{1,0:T(8,128)(2,1)S(1)} %get-tuple-element.60.query, bf16[256,640]{1,0:T(8,128)(2,1)S(1)} %collective-permute-done.16.a0, bf16[640,1920]{1,0:T(8,128)(2,1)S(1)} %get-tuple-element.62.weight, ...), custom_call_target="tpu_custom_call" | custom-call | flops 503316480 | bytes 3620864 | tf_op jit(solution)/shard_map/pallas_call | solution.py:215
  112.6 0.0 collective-permute-done.17.a0
  112.6 4.1 %shard_map.71 = bf16[128,640]{1,0:T(8,128)(2,1)} custom-call(bf16[128,640]{1,0:T(8,128)(2,1)S(1)} %get-tuple-element.60.query, bf16[256,640]{1,0:T(8,128)(2,1)S(1)} %collective-permute-done.17.a0, bf16[640,1920]{1,0:T(8,128)(2,1)S(1)} %get-tuple-element.62.weight, f32[128,8]{1,0:T(8,128)S(1)} %get-tuple-element.66.top, f32[128,8]{1,0:T(8,128)S(1)} %get-tuple-element.67.den, ...), custom_call_target="tpu_custom_call" | custom-call | flops 503316480 | bytes 3612672 | tf_op jit(solution)/shard_map/pallas_call | solution.py:215
  (14 shorter events, 0.4 us)
Async XLA Ops:
  0.0 3.8 %collective-permute-start.4 = (bf16[128,640]{1,0:T(8,128)(2,1)}, bf16[128,640]{1,0:T(8,128)(2,1)S(1)}, u32[]{:S(2)}, u32[]{:S(2)}) collective-permute-start(bf16[128,640]{1,0:T(8,128)(2,1)} %bitcast.7), channel_id=1, source_target_pairs={{0,1},{1,0},{2,3},{3,2},{4,5},{5,4},{6,7},{7,6},{8,9},{9,8},{10,11... | collective-permute-start | bytes 491528 | tf_op jit(solution)/shard_map/ppermute | solution.py:29
  2.6 0.9 copy-start.1
  4.0 9.0 %collective-permute-start.6 = (bf16[160,1920]{1,0:T(8,128)(2,1)}, bf16[160,1920]{1,0:T(8,128)(2,1)S(1)}, u32[]{:S(2)}, u32[]{:S(2)}) collective-permute-start(bf16[160,1920]{1,0:T(8,128)(2,1)} %w0.1), channel_id=1, source_target_pairs={{0,1},{1,0},{2,3},{3,2},{4,5},{5,4},{6,7},{7,6},{8,9},{9,8},{10,11... | collective-permute-start | bytes 1843208 | tf_op jit(solution)/shard_map/ppermute | solution.py:29
  6.2 6.8 %collective-permute-start.5 = (bf16[2,128,160]{2,1,0:T(8,128)(2,1)S(1)}, bf16[2,128,160]{2,1,0:T(8,128)(2,1)S(1)}, u32[]{:S(2)}, u32[]{:S(2)}) collective-permute-start(bf16[2,128,160]{2,1,0:T(8,128)(2,1)S(1)} %get-tuple-element.47), channel_id=1, source_target_pairs={{0,2},{1,3},{2,0},{3,1},{4,6},{5,7},{6,4},{7,5},{8,10},{9,11},{10,... | collective-permute-start | bytes 245768 | tf_op jit(solution)/shard_map/ppermute | solution.py:29
  10.0 1.5 %copy-start = (bf16[9,160,640]{2,1,0:T(8,128)(2,1)S(1)}, bf16[9,160,640]{2,1,0:T(8,128)(2,1)}, u32[]{:S(2)}) copy-start(bf16[9,160,640]{2,1,0:T(8,128)(2,1)} %param.10) | copy-start | bytes 5529604
  13.0 9.7 %copy-start.3 = (f32[640]{0:T(1024)S(1)}, f32[640]{0:T(1024)}, u32[]{:S(2)}) copy-start(f32[640]{0:T(1024)} %param.11) | copy-start | bytes 7684
  13.0 9.7 %copy-start.4 = (f32[640]{0:T(1024)S(1)}, f32[640]{0:T(1024)}, u32[]{:S(2)}) copy-start(f32[640]{0:T(1024)} %param.12) | copy-start | bytes 7684
  15.4 12.0 %copy-start.2 = (bf16[160,1920]{1,0:T(8,128)(2,1)S(1)}, bf16[160,1920]{1,0:T(8,128)(2,1)}, u32[]{:S(2)}) copy-start(bf16[160,1920]{1,0:T(8,128)(2,1)} %w0.1) | copy-start | bytes 1843204
  15.4 4.3 %collective-permute-start.7 = (bf16[2,128,640]{2,1,0:T(8,128)(2,1)S(1)}, bf16[2,128,640]{2,1,0:T(8,128)(2,1)S(1)}, u32[]{:S(2)}, u32[]{:S(2)}) collective-permute-start(bf16[2,128,640]{2,1,0:T(8,128)(2,1)S(1)} %get-tuple-element.52), channel_id=1, source_target_pairs={{0,1},{1,0},{2,3},{3,2},{4,5},{5,4},{6,7},{7,6},{8,9},{9,8},{10,11... | collective-permute-start | bytes 983048 | tf_op jit(solution)/shard_map/ppermute | solution.py:29
  19.8 7.3 %collective-permute-start.8 = (bf16[128,640]{1,0:T(8,128)(2,1)S(1)}, bf16[128,640]{1,0:T(8,128)(2,1)S(1)}, u32[]{:S(2)}, u32[]{:S(2)}) collective-permute-start(bf16[128,640]{1,0:T(8,128)(2,1)S(1)} %fusion), channel_id=1, source_target_pairs={{0,2},{1,3},{2,0},{3,1},{4,6},{5,7},{6,4},{7,5},{8,10},{9,11},{10,... | collective-permute-start | bytes 491528 | tf_op jit(solution)/shard_map/ppermute | solution.py:29
  27.4 16.0 %collective-permute-start.10 = (bf16[160,1920]{1,0:T(8,128)(2,1)S(1)}, bf16[160,1920]{1,0:T(8,128)(2,1)S(1)}, u32[]{:S(2)}, u32[]{:S(2)}) collective-permute-start(bf16[160,1920]{1,0:T(8,128)(2,1)S(1)} %copy-done.2), channel_id=1, source_target_pairs={{0,2},{1,3},{2,0},{3,1},{4,6},{5,7},{6,4},{7,5},{8,10},{9,11},{10,... | collective-permute-start | bytes 1843208 | tf_op jit(solution)/shard_map/ppermute | solution.py:29
  30.3 6.4 %collective-permute-start.9 = (bf16[128,640]{1,0:T(8,128)(2,1)S(1)}, bf16[128,640]{1,0:T(8,128)(2,1)S(1)}, u32[]{:S(2)}, u32[]{:S(2)}) collective-permute-start(bf16[128,640]{1,0:T(8,128)(2,1)S(1)} %get-tuple-element.53.feats), channel_id=1, source_target_pairs={{0,4},{4,8},{8,12},{12,16},{16,20},{20,24},{24,28},{28,32},{32,36}... | collective-permute-start | bytes 491528 | tf_op jit(solution)/shard_map/ppermute | solution.py:275
  31.6 0.7 collective-permute-start
  32.4 0.7 collective-permute-start.1
  33.1 0.7 collective-permute-start.2
  33.8 0.7 collective-permute-start.3
  43.4 5.7 %collective-permute-start.12 = (bf16[160,1920]{1,0:T(8,128)(2,1)S(1)}, bf16[160,1920]{1,0:T(8,128)(2,1)S(1)}, u32[]{:S(2)}, u32[]{:S(2)}) collective-permute-start(bf16[160,1920]{1,0:T(8,128)(2,1)S(1)} %collective-permute-done.10.w2), channel_id=1, source_target_pairs={{0,1},{1,0},{2,3},{3,2},{4,5},{5,4},{6,7},{7,6},{8,9},{9,8},{10,11... | collective-permute-start | bytes 1843208 | tf_op jit(solution)/shard_map/ppermute | solution.py:29
  47.4 0.7 collective-permute-start.11
  49.1 0.7 collective-permute-start.13
  49.8 42.1 %collective-permute-start.14 = (bf16[128,640]{1,0:T(8,128)(2,1)S(1)}, bf16[128,640]{1,0:T(8,128)(2,1)S(1)}, u32[]{:S(2)}, u32[]{:S(2)}) collective-permute-start(bf16[128,640]{1,0:T(8,128)(2,1)S(1)} %add.43), channel_id=1, source_target_pairs={{0,256},{128,384},{64,320},{192,448},{32,288},{160,416},{96,352},{... | collective-permute-start | bytes 491528 | tf_op jit(solution)/shard_map/ppermute | solution.py:280
  92.1 6.4 %collective-permute-start.15 = (bf16[256,640]{1,0:T(8,128)(2,1)S(1)}, bf16[256,640]{1,0:T(8,128)(2,1)S(1)}, u32[]{:S(2)}, u32[]{:S(2)}) collective-permute-start(bf16[256,640]{1,0:T(8,128)(2,1)S(1)} %pad_maximum_fusion.a0), channel_id=1, source_target_pairs={{0,1},{1,0},{2,3},{3,2},{4,5},{5,4},{6,7},{7,6},{8,9},{9,8},{10,11... | collective-permute-start | bytes 983048 | tf_op jit(solution)/shard_map/ppermute | solution.py:29
  95.7 11.2 %collective-permute-start.16 = (bf16[256,640]{1,0:T(8,128)(2,1)S(1)}, bf16[256,640]{1,0:T(8,128)(2,1)S(1)}, u32[]{:S(2)}, u32[]{:S(2)}) collective-permute-start(bf16[256,640]{1,0:T(8,128)(2,1)S(1)} %pad_maximum_fusion.a0), channel_id=1, source_target_pairs={{0,2},{1,3},{2,0},{3,1},{4,6},{5,7},{6,4},{7,5},{8,10},{9,11},{10,... | collective-permute-start | bytes 983048 | tf_op jit(solution)/shard_map/ppermute | solution.py:29
  107.0 5.6 %collective-permute-start.17 = (bf16[256,640]{1,0:T(8,128)(2,1)S(1)}, bf16[256,640]{1,0:T(8,128)(2,1)S(1)}, u32[]{:S(2)}, u32[]{:S(2)}) collective-permute-start(bf16[256,640]{1,0:T(8,128)(2,1)S(1)} %collective-permute-done.16.a0), channel_id=1, source_target_pairs={{0,1},{1,0},{2,3},{3,2},{4,5},{5,4},{6,7},{7,6},{8,9},{9,8},{10,11... | collective-permute-start | bytes 983048 | tf_op jit(solution)/shard_map/ppermute | solution.py:29

commit v9 on v8

--- a/solution.py
+++ b/solution.py
@@ -128,14 +128,55 @@
         ).astype(jnp.bfloat16)
 
 
-def scores_of(query, keys, head, window, inside):
-    q_head = jnp.where(inside, query[:, window], 0)
-    return lax.dot_general(
-        q_head,
-        keys[:, window],
-        (((1,), (1,)), ((), ())),
-        preferred_element_type=jnp.float32,
-    )
+def attend(blocks, query, weight, joined, keys, vals, state=None):
+    chans = query.shape[1]
+    head_dim = chans // HEADS
+    scale = head_dim ** (-0.5)
+    project(blocks, weight, joined, keys, vals)
+    heads = []
+    for head in range(HEADS):
+        window, inside = head_window(head, head_dim, chans)
+        s = lax.dot_general(
+            jnp.where(inside, query[:, window], 0),
+            keys[:, window],
+            (((1,), (1,)), ((), ())),
+            preferred_element_type=jnp.float32,
+        )
+        peak = jnp.max(s, axis=1, keepdims=True)
+        if state is not None:
+            old = state[0][:, head : head + 1]
+            peak = jnp.maximum(old, peak)
+            factor = jnp.exp((old - peak) * scale)
+        w = jnp.exp((s - peak) * scale)
+        total = jnp.sum(w, axis=1, keepdims=True)
+        out = jnp.dot(
+            w.astype(jnp.bfloat16), vals[:, window], preferred_element_type=jnp.float32
+        )
+        if state is not None:
+            total = state[1][:, head : head + 1] * factor + total
+            out = state[2][:, window] * factor + out
+        heads.append((peak, total, out))
+    return heads
+
+
+def tiles_of(outs, chans):
+    for low in range(0, chans, 128):
+        tile = None
+        for head, out in enumerate(outs):
+            window, inside = head_window(head, chans // HEADS, chans)
+            if window.start <= low < window.stop:
+                at = low - window.start
+                part = out[:, at : at + 128]
+                tile = part if tile is None else jnp.where(inside[:, at : at + 128], part, tile)
+        yield slice(low, low + 128), tile
+
+
+def keep_state(heads, top, den, acc):
+    for head, (peak, total, _) in enumerate(heads):
+        top[:, head : head + 1] = peak
+        den[:, head : head + 1] = total
+    for tile, value in tiles_of([out for _, _, out in heads], acc.shape[1]):
+        acc[:, tile] = value
 
 
 def first_kernel(
@@ -147,62 +188,22 @@
     for flip, shard in enumerate((w0, w1, w2, w3)):
         at = pl.multiple_of((me ^ flip) * share, share)
         weight[pl.ds(at, share), :] = shard[...]
-    head_dim = chans // HEADS
-    scale = head_dim ** (-0.5)
     query[...] = jnp.dot(
         feats[...], weight[:, :chans], preferred_element_type=jnp.float32
     ).astype(jnp.bfloat16)
-    project((a0, a1), weight, joined, keys, vals)
-    for head in range(HEADS):
-        window, inside = head_window(head, head_dim, chans)
-        s = scores_of(query, keys, head, window, inside)
-        peak = jnp.max(s, axis=1, keepdims=True)
-        w = jnp.exp((s - peak) * scale)
-        top[:, head : head + 1] = peak
-        den[:, head : head + 1] = jnp.sum(w, axis=1, keepdims=True)
-        out = jnp.dot(
-            w.astype(jnp.bfloat16), vals[:, window], preferred_element_type=jnp.float32
-        )
-        acc[:, window] = jnp.where(inside, out, acc[:, window])
-
-
-def attend(blocks, query, weight, top, den, acc, joined, keys, vals):
-    head_dim = query.shape[1] // HEADS
-    scale = head_dim ** (-0.5)
-    project(blocks, weight, joined, keys, vals)
-    for head in range(HEADS):
-        window, inside = head_window(head, head_dim, query.shape[1])
-        s = scores_of(query, keys, head, window, inside)
-        old = top[:, head : head + 1]
-        peak = jnp.maximum(old, jnp.max(s, axis=1, keepdims=True))
-        factor = jnp.exp((old - peak) * scale)
-        w = jnp.exp((s - peak) * scale)
-        total = den[:, head : head + 1] * factor + jnp.sum(w, axis=1, keepdims=True)
-        out = jnp.dot(
-            w.astype(jnp.bfloat16), vals[:, window], preferred_element_type=jnp.float32
-        )
-        yield head, window, inside, peak, total, acc[:, window] * factor + out
-
-
-def more_kernel(
-    query, a0, weight, top, den, acc, new_top, new_den, new_acc, joined, keys, vals
-):
-    for head, window, inside, peak, total, out in attend(
-        (a0,), query, weight, top, den, acc, joined, keys, vals
-    ):
-        new_top[:, head : head + 1] = peak
-        new_den[:, head : head + 1] = total
-        new_acc[:, window] = jnp.where(inside, out, new_acc[:, window])
-
-
-def last_kernel(
-    query, a0, weight, top, den, acc, residual, restyled, joined, keys, vals, mixed
-):
-    for head, window, inside, _, total, out in attend(
-        (a0,), query, weight, top, den, acc, joined, keys, vals
-    ):
-        mixed[:, window] = jnp.where(inside, out / total, mixed[:, window])
-    restyled[...] = (residual[...].astype(jnp.float32) + mixed[...]).astype(jnp.bfloat16)
+    keep_state(attend((a0, a1), query, weight, joined, keys, vals), top, den, acc)
+
+
+def more_kernel(query, a0, weight, top, den, acc, new_top, new_den, new_acc, joined, keys, vals):
+    heads = attend((a0,), query, weight, joined, keys, vals, (top, den, acc))
+    keep_state(heads, new_top, new_den, new_acc)
+
+
+def last_kernel(query, a0, weight, top, den, acc, residual, restyled, joined, keys, vals):
+    heads = attend((a0,), query, weight, joined, keys, vals, (top, den, acc))
+    mixed = [out / total for _, total, out in heads]
+    for tile, value in tiles_of(mixed, restyled.shape[1]):
+        restyled[:, tile] = (residual[:, tile].astype(jnp.float32) + value).astype(jnp.bfloat16)
 
 
 def call(kernel, outs, ins, scratch=(), flops=0, limit=24, hbm=()):
@@ -272,7 +273,6 @@
 
     devices = lax.axis_size("tm")
     routes = tree_levels(devices)
-    prev = lax.ppermute(feats, "tm", [(i, i + 1) for i in range(devices - 1)])
     weight_chip = to_rows(after(qkv_weight, feats), 2)
 
     def levels(anchor, which):
@@ -283,10 +283,12 @@
     trips = 1 + jnp.minimum(lax.axis_index("tm"), 0)
     anchor = jnp.where(first, feats, jnp.zeros_like(feats))
     anchor = lax.fori_loop(0, trips, lambda _, a: levels(a, routes[:4]), anchor)
-    anchor = after(anchor, prev, weight_chip)
+    anchor = after(anchor, weight_chip)
     weight_last = to_rows(after(weight_chip, anchor), 1)
     anchor = after(levels(anchor, routes[4:5]), weight_last)
-    anchor = levels(anchor, routes[5:])
+    prev = lax.ppermute(after(feats, anchor), "tm", [(i, i + 1) for i in range(devices - 1)])
+    anchor = after(levels(anchor, routes[5:6]), prev)
+    anchor = levels(anchor, routes[6:])
     prev = jnp.where(first, feats, after(prev, anchor))
     shards = [qkv_weight, weight_core, weight_chip, weight_last]
 
@@ -320,7 +322,7 @@
         last_kernel,
         [shape((part, chans), bf16)],
         [query, last, weight, *prior, residual],
-        scratch(keys) + [pltpu.VMEM((part, chans), f32)],
+        scratch(keys),
         flops=flops(keys),
     )
     return restyled.reshape(1, rows_dev, width, chans)

time: 117 us -> 117 us (level)
  the two profiles are of different devices: /device:TPU:503 before, /device:TPU:497 now
where the time goes in v9:
time: 117 us; the launch traced here: 116 us
  waiting for transfers between devices  60.3 us (52%)
  starting transfers between devices  38.4 us (33%)
  Pallas kernels  13.6 us (12%)
  local copies, waits for them, and re-layouts  3.2 us (3%)
    ppermute x7, waiting for transfers between devices, levels(): anchor = anchor + lax.ppermute(anchor, 'tm', route)  31.1 us
    ppermute x10, starting transfers between devices, to_rows(): return lax.ppermute(x, 'rows', [(i, i ^ flip) for i in range(4)])  30 us
    ppermute x10, waiting for transfers between devices, to_rows(): return lax.ppermute(x, 'rows', [(i, i ^ flip) for i in range(4)])  22.9 us
    pallas_call x8, Pallas kernels, call(): pl.pallas_call(kernel, out_shape=list(outs), in_specs=specs, out_specs=[V...  13.6 us
    ppermute x1, waiting for transfers between devices, on_device(): lax.ppermute(after(feats, anchor), 'tm', [(i, i + 1) for i in range(devic...  6.23 us
    ppermute x7, starting transfers between devices, levels(): anchor = anchor + lax.ppermute(anchor, 'tm', route)  5.29 us
    ppermute x1, starting transfers between devices, on_device(): lax.ppermute(after(feats, anchor), 'tm', [(i, i + 1) for i in range(devic...  3.12 us
    unnamed x10, local copies, waits for them, and re-layouts  2.43 us
  transfers between devices with their start and end apart: 18, of which 9 were waited for; matrix products, arithmetic and copies ran while one was open for 1% of the time, Pallas kernels for 6%

profile of v9, /device:TPU:497, one launch (start us, length us, event | category | flops | bytes accessed | tf_op | source)
XLA Modules:
  0.0 116.4 jit_solution(15666693072524754530)
XLA Ops:
  0.0 2.6 %collective-permute-start.4 = (bf16[128,640]{1,0:T(8,128)(2,1)}, bf16[128,640]{1,0:T(8,128)(2,1)S(1)}, u32[]{:S(2)}, u32[]{:S(2)}) collective-permute-start(bf16[128,640]{1,0:T(8,128)(2,1)} %bitcast.7), channel_id=1, source_target_pairs={{0,1},{1,0},{2,3},{3,2},{4,5},{5,4},{6,7},{7,6},{8,9},{9,8},{10,11... | collective-permute-start | bytes 491528 | tf_op jit(solution)/shard_map/ppermute | solution.py:29
  2.6 0.0 copy-start.1
  2.6 0.9 copy-done.1
  3.5 0.2 shard_map.64.own.lat
  3.7 0.1 collective-permute-done.4.core
  3.8 0.2 shard_map.65
  4.0 2.2 %collective-permute-start.6 = (bf16[160,1920]{1,0:T(8,128)(2,1)}, bf16[160,1920]{1,0:T(8,128)(2,1)S(1)}, u32[]{:S(2)}, u32[]{:S(2)}) collective-permute-start(bf16[160,1920]{1,0:T(8,128)(2,1)} %w0.1), channel_id=1, source_target_pairs={{0,1},{1,0},{2,3},{3,2},{4,5},{5,4},{6,7},{7,6},{8,9},{9,8},{10,11... | collective-permute-start | bytes 1843208 | tf_op jit(solution)/shard_map/ppermute | solution.py:29
  6.2 2.9 %collective-permute-start.5 = (bf16[2,128,160]{2,1,0:T(8,128)(2,1)S(1)}, bf16[2,128,160]{2,1,0:T(8,128)(2,1)S(1)}, u32[]{:S(2)}, u32[]{:S(2)}) collective-permute-start(bf16[2,128,160]{2,1,0:T(8,128)(2,1)S(1)} %get-tuple-element.49), channel_id=1, source_target_pairs={{0,2},{1,3},{2,0},{3,1},{4,6},{5,7},{6,4},{7,5},{8,10},{9,11},{10,... | collective-permute-start | bytes 245768 | tf_op jit(solution)/shard_map/ppermute | solution.py:29
  9.2 0.1 compare_convert_fusion.pool
  9.2 0.8 reshape.55.gain
  10.0 0.0 copy-start
  10.0 1.5 %copy-done = bf16[9,160,640]{2,1,0:T(8,128)(2,1)S(1)} copy-done((bf16[9,160,640]{2,1,0:T(8,128)(2,1)S(1)}, bf16[9,160,640]{2,1,0:T(8,128)(2,1)}, u32[]{:S(2)}) %copy-start) | copy-done | bytes 1843224
  11.5 0.1 shard_map.66.weight
  11.7 1.3 %collective-permute-done.5.came = bf16[2,128,160]{2,1,0:T(8,128)(2,1)S(1)} collective-permute-done((bf16[2,128,160]{2,1,0:T(8,128)(2,1)S(1)}, bf16[2,128,160]{2,1,0:T(8,128)(2,1)S(1)}, u32[]{:S(2)}, u32[]{:S(2)}) %collective-permute-start.5) | collective-permute-done | bytes 81952 | tf_op jit(solution)/shard_map/ppermute | solution.py:29
  13.0 0.0 collective-permute-done.6.w1
  13.0 0.0 copy-start.3
  13.0 0.0 copy-start.4
  13.0 2.4 %shard_map.67 = (f32[2,128,640]{2,1,0:T(8,128)S(1)}, bf16[2,128,640]{2,1,0:T(8,128)(2,1)S(1)}) custom-call(s32[1]{0:T(128)} %bitcast.me_ref, bf16[2,128,160]{2,1,0:T(8,128)(2,1)S(1)} %get-tuple-element.48.mine, bf16[2,128,160]{2,1,0:T(8,128)(2,1)S(1)} %collective-permute-done.5.came, f32[4,160]{1,0:T(4,128)S(1)} %reshape.55.gain, ...), custom_call_target="tpu_custom_call" | custom-call | flops 943718400 | bytes 3095044 | tf_op jit(solution)/shard_map/pallas_call | solution.py:216
  15.4 0.0 copy-start.2
  15.4 3.1 %collective-permute-start.7 = (bf16[2,128,640]{2,1,0:T(8,128)(2,1)S(1)}, bf16[2,128,640]{2,1,0:T(8,128)(2,1)S(1)}, u32[]{:S(2)}, u32[]{:S(2)}) collective-permute-start(bf16[2,128,640]{2,1,0:T(8,128)(2,1)S(1)} %get-tuple-element.54), channel_id=1, source_target_pairs={{0,1},{1,0},{2,3},{3,2},{4,5},{5,4},{6,7},{7,6},{8,9},{9,8},{10,11... | collective-permute-start | bytes 983048 | tf_op jit(solution)/shard_map/ppermute | solution.py:29
  18.5 1.2 %collective-permute-done.7.core = bf16[2,128,640]{2,1,0:T(8,128)(2,1)S(1)} collective-permute-done((bf16[2,128,640]{2,1,0:T(8,128)(2,1)S(1)}, bf16[2,128,640]{2,1,0:T(8,128)(2,1)S(1)}, u32[]{:S(2)}, u32[]{:S(2)}) %collective-permute-start.7) | collective-permute-done | bytes 327712 | tf_op jit(solution)/shard_map/ppermute | solution.py:29
  19.8 2.9 %collective-permute-start.8 = (bf16[128,640]{1,0:T(8,128)(2,1)S(1)}, bf16[128,640]{1,0:T(8,128)(2,1)S(1)}, u32[]{:S(2)}, u32[]{:S(2)}) collective-permute-start(bf16[128,640]{1,0:T(8,128)(2,1)S(1)} %fusion), channel_id=1, source_target_pairs={{0,2},{1,3},{2,0},{3,1},{4,6},{5,7},{6,4},{7,5},{8,10},{9,11},{10,... | collective-permute-start | bytes 491528 | tf_op jit(solution)/shard_map/ppermute | solution.py:29
  22.7 0.0 copy-done.3
  22.7 0.0 copy-done.4
  22.7 4.4 %collective-permute-done.8.chip = bf16[128,640]{1,0:T(8,128)(2,1)S(1)} collective-permute-done((bf16[128,640]{1,0:T(8,128)(2,1)S(1)}, bf16[128,640]{1,0:T(8,128)(2,1)S(1)}, u32[]{:S(2)}, u32[]{:S(2)}) %collective-permute-start.8) | collective-permute-done | bytes 163872 | tf_op jit(solution)/shard_map/ppermute | solution.py:29
  27.1 0.3 shard_map.68
  27.4 0.0 copy-done.2
  27.4 2.9 %collective-permute-start.9 = (bf16[160,1920]{1,0:T(8,128)(2,1)S(1)}, bf16[160,1920]{1,0:T(8,128)(2,1)S(1)}, u32[]{:S(2)}, u32[]{:S(2)}) collective-permute-start(bf16[160,1920]{1,0:T(8,128)(2,1)S(1)} %copy-done.2), channel_id=1, source_target_pairs={{0,2},{1,3},{2,0},{3,1},{4,6},{5,7},{6,4},{7,5},{8,10},{9,11},{10,... | collective-permute-start | bytes 1843208 | tf_op jit(solution)/shard_map/ppermute | solution.py:29
  30.3 3.0 %while.10 = (s32[]{:T(128)}, bf16[128,640]{1,0:T(8,128)(2,1)S(1)}, s32[]{:T(128)}, s32[]{:T(128)}) while((s32[]{:T(128)}, bf16[128,640]{1,0:T(8,128)(2,1)S(1)}, s32[]{:T(128)}, s32[]{:T(128)}) %tuple.40), condition=%wide.region_1.2_spmd, body=%wide.region_0.1_spmd.sunk | while | flops 327682 | bytes 4587733 | solution.py:285
  30.3 0.7 collective-permute-start
  31.0 0.0 collective-permute-done
  31.1 0.7 collective-permute-start.1
  31.7 0.0 collective-permute-done.1
  31.8 0.7 collective-permute-start.2
  32.5 0.0 collective-permute-done.2
  32.5 0.7 collective-permute-start.3
  33.2 0.0 collective-permute-done.3
  33.3 10.1 %collective-permute-done.9.w2 = bf16[160,1920]{1,0:T(8,128)(2,1)S(1)} collective-permute-done((bf16[160,1920]{1,0:T(8,128)(2,1)S(1)}, bf16[160,1920]{1,0:T(8,128)(2,1)S(1)}, u32[]{:S(2)}, u32[]{:S(2)}) %collective-permute-start.9) | collective-permute-done | bytes 614432 | tf_op jit(solution)/shard_map/ppermute | solution.py:29
  43.4 4.0 %collective-permute-start.11 = (bf16[160,1920]{1,0:T(8,128)(2,1)S(1)}, bf16[160,1920]{1,0:T(8,128)(2,1)S(1)}, u32[]{:S(2)}, u32[]{:S(2)}) collective-permute-start(bf16[160,1920]{1,0:T(8,128)(2,1)S(1)} %collective-permute-done.9.w2), channel_id=1, source_target_pairs={{0,1},{1,0},{2,3},{3,2},{4,5},{5,4},{6,7},{7,6},{8,9},{9,8},{10,11... | collective-permute-start | bytes 1843208 | tf_op jit(solution)/shard_map/ppermute | solution.py:29
  47.4 0.7 collective-permute-start.10
  48.1 0.0 collective-permute-done.10
  48.2 0.9 collective-permute-done.11.w3
  49.1 0.7 collective-permute-start.13
  49.7 3.1 %collective-permute-start.12 = (bf16[128,640]{1,0:T(8,128)(2,1)S(1)}, bf16[128,640]{1,0:T(8,128)(2,1)S(1)}, u32[]{:S(2)}, u32[]{:S(2)}) collective-permute-start(bf16[128,640]{1,0:T(8,128)(2,1)S(1)} %get-tuple-element.61.feats), channel_id=1, source_target_pairs={{0,4},{4,8},{8,12},{12,16},{16,20},{20,24},{24,28},{28,32},{32,36}... | collective-permute-start | bytes 491528 | tf_op jit(solution)/shard_map/ppermute | solution.py:289
  52.9 0.0 collective-permute-done.13
  52.9 6.2 %collective-permute-done.12 = bf16[128,640]{1,0:T(8,128)(2,1)S(1)} collective-permute-done((bf16[128,640]{1,0:T(8,128)(2,1)S(1)}, bf16[128,640]{1,0:T(8,128)(2,1)S(1)}, u32[]{:S(2)}, u32[]{:S(2)}) %collective-permute-start.12) | collective-permute-done | bytes 163872 | tf_op jit(solution)/shard_map/ppermute | solution.py:289
  59.2 1.3 %collective-permute-start.14 = (bf16[128,640]{1,0:T(8,128)(2,1)S(1)}, bf16[128,640]{1,0:T(8,128)(2,1)S(1)}, u32[]{:S(2)}, u32[]{:S(2)}) collective-permute-start(bf16[128,640]{1,0:T(8,128)(2,1)S(1)} %add.43), channel_id=1, source_target_pairs={{0,256},{128,384},{64,320},{192,448},{32,288},{160,416},{96,352},{... | collective-permute-start | bytes 491528 | tf_op jit(solution)/shard_map/ppermute | solution.py:280
  60.5 31.1 %collective-permute-done.14 = bf16[128,640]{1,0:T(8,128)(2,1)S(1)} collective-permute-done((bf16[128,640]{1,0:T(8,128)(2,1)S(1)}, bf16[128,640]{1,0:T(8,128)(2,1)S(1)}, u32[]{:S(2)}, u32[]{:S(2)}) %collective-permute-start.14) | collective-permute-done | bytes 163872 | tf_op jit(solution)/shard_map/ppermute | solution.py:280
  91.7 4.0 %collective-permute-start.15 = (bf16[256,640]{1,0:T(8,128)(2,1)S(1)}, bf16[256,640]{1,0:T(8,128)(2,1)S(1)}, u32[]{:S(2)}, u32[]{:S(2)}) collective-permute-start(bf16[256,640]{1,0:T(8,128)(2,1)S(1)} %pad_maximum_fusion.a0), channel_id=1, source_target_pairs={{0,1},{1,0},{2,3},{3,2},{4,5},{5,4},{6,7},{7,6},{8,9},{9,8},{10,11... | collective-permute-start | bytes 983048 | tf_op jit(solution)/shard_map/ppermute | solution.py:29
  95.7 2.7 %collective-permute-start.16 = (bf16[256,640]{1,0:T(8,128)(2,1)S(1)}, bf16[256,640]{1,0:T(8,128)(2,1)S(1)}, u32[]{:S(2)}, u32[]{:S(2)}) collective-permute-start(bf16[256,640]{1,0:T(8,128)(2,1)S(1)} %pad_maximum_fusion.a0), channel_id=1, source_target_pairs={{0,2},{1,3},{2,0},{3,1},{4,6},{5,7},{6,4},{7,5},{8,10},{9,11},{10,... | collective-permute-start | bytes 983048 | tf_op jit(solution)/shard_map/ppermute | solution.py:29
  98.4 0.0 collective-permute-done.15.a1
  98.4 3.6 %shard_map.69 = (bf16[128,640]{1,0:T(8,128)(2,1)S(1)}, f32[128,8]{1,0:T(8,128)S(1)}, f32[128,8]{1,0:T(8,128)S(1)}, f32[128,640]{1,0:T(8,128)S(1)}, bf16[640,1920]{1,0:T(8,128)(2,1)S(1)}) custom-call(s32[1]{0:T(128)} %bitcast.me_ref, bf16[128,640]{1,0:T(8,128)(2,1)S(1)} %get-tuple-element.61.feats, bf16[256,640]{1,0:T(8,128)(2,1)S(1)} %pad_maximum_fusion.a0, ...), custom_call_target="tpu_custom_call" | custom-call | flops 1006632960 | bytes 6234116 | tf_op jit(solution)/shard_map/pallas_call | solution.py:216
  102.0 4.9 %collective-permute-done.16.a0 = bf16[256,640]{1,0:T(8,128)(2,1)S(1)} collective-permute-done((bf16[256,640]{1,0:T(8,128)(2,1)S(1)}, bf16[256,640]{1,0:T(8,128)(2,1)S(1)}, u32[]{:S(2)}, u32[]{:S(2)}) %collective-permute-start.16) | collective-permute-done | bytes 327712 | tf_op jit(solution)/shard_map/ppermute | solution.py:29
  106.9 2.7 %collective-permute-start.17 = (bf16[256,640]{1,0:T(8,128)(2,1)S(1)}, bf16[256,640]{1,0:T(8,128)(2,1)S(1)}, u32[]{:S(2)}, u32[]{:S(2)}) collective-permute-start(bf16[256,640]{1,0:T(8,128)(2,1)S(1)} %collective-permute-done.16.a0), channel_id=1, source_target_pairs={{0,1},{1,0},{2,3},{3,2},{4,5},{5,4},{6,7},{7,6},{8,9},{9,8},{10,11... | collective-permute-start | bytes 983048 | tf_op jit(solution)/shard_map/ppermute | solution.py:29
  109.6 2.9 %shard_map.70 = (f32[128,8]{1,0:T(8,128)S(1)}, f32[128,8]{1,0:T(8,128)S(1)}, f32[128,640]{1,0:T(8,128)S(1)}) custom-call(bf16[128,640]{1,0:T(8,128)(2,1)S(1)} %get-tuple-element.64.query, bf16[256,640]{1,0:T(8,128)(2,1)S(1)} %collective-permute-done.16.a0, bf16[640,1920]{1,0:T(8,128)(2,1)S(1)} %get-tuple-element.66.weight, ...), custom_call_target="tpu_custom_call" | custom-call | flops 503316480 | bytes 3620864 | tf_op jit(solution)/shard_map/pallas_call | solution.py:216
  112.6 0.0 collective-permute-done.17.a0
  112.6 3.8 %shard_map.71 = bf16[128,640]{1,0:T(8,128)(2,1)} custom-call(bf16[128,640]{1,0:T(8,128)(2,1)S(1)} %get-tuple-element.64.query, bf16[256,640]{1,0:T(8,128)(2,1)S(1)} %collective-permute-done.17.a0, bf16[640,1920]{1,0:T(8,128)(2,1)S(1)} %get-tuple-element.66.weight, f32[128,8]{1,0:T(8,128)S(1)} %get-tuple-element.70.top, f32[128,8]{1,0:T(8,128)S(1)} %get-tuple-element.71.den, ...), custom_call_target="tpu_custom_call" | custom-call | flops 503316480 | bytes 3612672 | tf_op jit(solution)/shard_map/pallas_call | solution.py:216
  (14 shorter events, 0.5 us)
Async XLA Ops:
  0.0 3.8 %collective-permute-start.4 = (bf16[128,640]{1,0:T(8,128)(2,1)}, bf16[128,640]{1,0:T(8,128)(2,1)S(1)}, u32[]{:S(2)}, u32[]{:S(2)}) collective-permute-start(bf16[128,640]{1,0:T(8,128)(2,1)} %bitcast.7), channel_id=1, source_target_pairs={{0,1},{1,0},{2,3},{3,2},{4,5},{5,4},{6,7},{7,6},{8,9},{9,8},{10,11... | collective-permute-start | bytes 491528 | tf_op jit(solution)/shard_map/ppermute | solution.py:29
  2.6 0.9 copy-start.1
  4.0 9.0 %collective-permute-start.6 = (bf16[160,1920]{1,0:T(8,128)(2,1)}, bf16[160,1920]{1,0:T(8,128)(2,1)S(1)}, u32[]{:S(2)}, u32[]{:S(2)}) collective-permute-start(bf16[160,1920]{1,0:T(8,128)(2,1)} %w0.1), channel_id=1, source_target_pairs={{0,1},{1,0},{2,3},{3,2},{4,5},{5,4},{6,7},{7,6},{8,9},{9,8},{10,11... | collective-permute-start | bytes 1843208 | tf_op jit(solution)/shard_map/ppermute | solution.py:29
  6.2 6.8 %collective-permute-start.5 = (bf16[2,128,160]{2,1,0:T(8,128)(2,1)S(1)}, bf16[2,128,160]{2,1,0:T(8,128)(2,1)S(1)}, u32[]{:S(2)}, u32[]{:S(2)}) collective-permute-start(bf16[2,128,160]{2,1,0:T(8,128)(2,1)S(1)} %get-tuple-element.49), channel_id=1, source_target_pairs={{0,2},{1,3},{2,0},{3,1},{4,6},{5,7},{6,4},{7,5},{8,10},{9,11},{10,... | collective-permute-start | bytes 245768 | tf_op jit(solution)/shard_map/ppermute | solution.py:29
  10.0 1.5 %copy-start = (bf16[9,160,640]{2,1,0:T(8,128)(2,1)S(1)}, bf16[9,160,640]{2,1,0:T(8,128)(2,1)}, u32[]{:S(2)}) copy-start(bf16[9,160,640]{2,1,0:T(8,128)(2,1)} %param.10) | copy-start | bytes 5529604
  13.0 9.7 %copy-start.3 = (f32[640]{0:T(1024)S(1)}, f32[640]{0:T(1024)}, u32[]{:S(2)}) copy-start(f32[640]{0:T(1024)} %param.11) | copy-start | bytes 7684
  13.0 9.7 %copy-start.4 = (f32[640]{0:T(1024)S(1)}, f32[640]{0:T(1024)}, u32[]{:S(2)}) copy-start(f32[640]{0:T(1024)} %param.12) | copy-start | bytes 7684
  15.4 12.0 %copy-start.2 = (bf16[160,1920]{1,0:T(8,128)(2,1)S(1)}, bf16[160,1920]{1,0:T(8,128)(2,1)}, u32[]{:S(2)}) copy-start(bf16[160,1920]{1,0:T(8,128)(2,1)} %w0.1) | copy-start | bytes 1843204
  15.4 4.3 %collective-permute-start.7 = (bf16[2,128,640]{2,1,0:T(8,128)(2,1)S(1)}, bf16[2,128,640]{2,1,0:T(8,128)(2,1)S(1)}, u32[]{:S(2)}, u32[]{:S(2)}) collective-permute-start(bf16[2,128,640]{2,1,0:T(8,128)(2,1)S(1)} %get-tuple-element.54), channel_id=1, source_target_pairs={{0,1},{1,0},{2,3},{3,2},{4,5},{5,4},{6,7},{7,6},{8,9},{9,8},{10,11... | collective-permute-start | bytes 983048 | tf_op jit(solution)/shard_map/ppermute | solution.py:29
  19.8 7.3 %collective-permute-start.8 = (bf16[128,640]{1,0:T(8,128)(2,1)S(1)}, bf16[128,640]{1,0:T(8,128)(2,1)S(1)}, u32[]{:S(2)}, u32[]{:S(2)}) collective-permute-start(bf16[128,640]{1,0:T(8,128)(2,1)S(1)} %fusion), channel_id=1, source_target_pairs={{0,2},{1,3},{2,0},{3,1},{4,6},{5,7},{6,4},{7,5},{8,10},{9,11},{10,... | collective-permute-start | bytes 491528 | tf_op jit(solution)/shard_map/ppermute | solution.py:29
  27.4 16.0 %collective-permute-start.9 = (bf16[160,1920]{1,0:T(8,128)(2,1)S(1)}, bf16[160,1920]{1,0:T(8,128)(2,1)S(1)}, u32[]{:S(2)}, u32[]{:S(2)}) collective-permute-start(bf16[160,1920]{1,0:T(8,128)(2,1)S(1)} %copy-done.2), channel_id=1, source_target_pairs={{0,2},{1,3},{2,0},{3,1},{4,6},{5,7},{6,4},{7,5},{8,10},{9,11},{10,... | collective-permute-start | bytes 1843208 | tf_op jit(solution)/shard_map/ppermute | solution.py:29
  30.3 0.7 collective-permute-start
  31.1 0.7 collective-permute-start.1
  31.8 0.7 collective-permute-start.2
  32.5 0.7 collective-permute-start.3
  43.4 5.7 %collective-permute-start.11 = (bf16[160,1920]{1,0:T(8,128)(2,1)S(1)}, bf16[160,1920]{1,0:T(8,128)(2,1)S(1)}, u32[]{:S(2)}, u32[]{:S(2)}) collective-permute-start(bf16[160,1920]{1,0:T(8,128)(2,1)S(1)} %collective-permute-done.9.w2), channel_id=1, source_target_pairs={{0,1},{1,0},{2,3},{3,2},{4,5},{5,4},{6,7},{7,6},{8,9},{9,8},{10,11... | collective-permute-start | bytes 1843208 | tf_op jit(solution)/shard_map/ppermute | solution.py:29
  47.4 0.7 collective-permute-start.10
  49.1 3.8 %collective-permute-start.13 = (bf16[128,640]{1,0:T(8,128)(2,1)S(1)}, bf16[128,640]{1,0:T(8,128)(2,1)S(1)}, u32[]{:S(2)}, u32[]{:S(2)}) collective-permute-start(bf16[128,640]{1,0:T(8,128)(2,1)S(1)} %add.42), channel_id=1, source_target_pairs={{0,4},{128,132},{64,68},{192,196},{32,36},{160,164},{96,100},{224,... | collective-permute-start | bytes 491528 | tf_op jit(solution)/shard_map/ppermute | solution.py:280
  49.7 9.4 %collective-permute-start.12 = (bf16[128,640]{1,0:T(8,128)(2,1)S(1)}, bf16[128,640]{1,0:T(8,128)(2,1)S(1)}, u32[]{:S(2)}, u32[]{:S(2)}) collective-permute-start(bf16[128,640]{1,0:T(8,128)(2,1)S(1)} %get-tuple-element.61.feats), channel_id=1, source_target_pairs={{0,4},{4,8},{8,12},{12,16},{16,20},{20,24},{24,28},{28,32},{32,36}... | collective-permute-start | bytes 491528 | tf_op jit(solution)/shard_map/ppermute | solution.py:289
  59.2 32.4 %collective-permute-start.14 = (bf16[128,640]{1,0:T(8,128)(2,1)S(1)}, bf16[128,640]{1,0:T(8,128)(2,1)S(1)}, u32[]{:S(2)}, u32[]{:S(2)}) collective-permute-start(bf16[128,640]{1,0:T(8,128)(2,1)S(1)} %add.43), channel_id=1, source_target_pairs={{0,256},{128,384},{64,320},{192,448},{32,288},{160,416},{96,352},{... | collective-permute-start | bytes 491528 | tf_op jit(solution)/shard_map/ppermute | solution.py:280
  91.7 6.7 %collective-permute-start.15 = (bf16[256,640]{1,0:T(8,128)(2,1)S(1)}, bf16[256,640]{1,0:T(8,128)(2,1)S(1)}, u32[]{:S(2)}, u32[]{:S(2)}) collective-permute-start(bf16[256,640]{1,0:T(8,128)(2,1)S(1)} %pad_maximum_fusion.a0), channel_id=1, source_target_pairs={{0,1},{1,0},{2,3},{3,2},{4,5},{5,4},{6,7},{7,6},{8,9},{9,8},{10,11... | collective-permute-start | bytes 983048 | tf_op jit(solution)/shard_map/ppermute | solution.py:29
  95.7 11.2 %collective-permute-start.16 = (bf16[256,640]{1,0:T(8,128)(2,1)S(1)}, bf16[256,640]{1,0:T(8,128)(2,1)S(1)}, u32[]{:S(2)}, u32[]{:S(2)}) collective-permute-start(bf16[256,640]{1,0:T(8,128)(2,1)S(1)} %pad_maximum_fusion.a0), channel_id=1, source_target_pairs={{0,2},{1,3},{2,0},{3,1},{4,6},{5,7},{6,4},{7,5},{8,10},{9,11},{10,... | collective-permute-start | bytes 983048 | tf_op jit(solution)/shard_map/ppermute | solution.py:29
  106.9 5.6 %collective-permute-start.17 = (bf16[256,640]{1,0:T(8,128)(2,1)S(1)}, bf16[256,640]{1,0:T(8,128)(2,1)S(1)}, u32[]{:S(2)}, u32[]{:S(2)}) collective-permute-start(bf16[256,640]{1,0:T(8,128)(2,1)S(1)} %collective-permute-done.16.a0), channel_id=1, source_target_pairs={{0,1},{1,0},{2,3},{3,2},{4,5},{5,4},{6,7},{7,6},{8,9},{9,8},{10,11... | collective-permute-start | bytes 983048 | tf_op jit(solution)/shard_map/ppermute | solution.py:29

commit v10 on v9

--- a/solution.py
+++ b/solution.py
@@ -17,9 +17,9 @@
 def tree_levels(devices):
     steps = []
     while 2 ** len(steps) < devices:
-        steps.insert(0, 2 ** len(steps))
+        steps.append(2 ** len(steps))
     levels, known = [], [0]
-    for step in steps[1:] + steps[:1]:
+    for step in steps[1::-1] + steps[-2:1:-1] + steps[max(2, len(steps) - 1) :]:
         levels.append([(tm, tm + step) for tm in known])
         known = known + [tm + step for tm in known]
     return levels
@@ -273,6 +273,7 @@
 
     devices = lax.axis_size("tm")
     routes = tree_levels(devices)
+    prev = lax.ppermute(feats, "tm", [(i, i + 1) for i in range(devices - 1)])
     weight_chip = to_rows(after(qkv_weight, feats), 2)
 
     def levels(anchor, which):
@@ -283,12 +284,10 @@
     trips = 1 + jnp.minimum(lax.axis_index("tm"), 0)
     anchor = jnp.where(first, feats, jnp.zeros_like(feats))
     anchor = lax.fori_loop(0, trips, lambda _, a: levels(a, routes[:4]), anchor)
-    anchor = after(anchor, weight_chip)
+    anchor = after(anchor, prev, weight_chip)
     weight_last = to_rows(after(weight_chip, anchor), 1)
     anchor = after(levels(anchor, routes[4:5]), weight_last)
-    prev = lax.ppermute(after(feats, anchor), "tm", [(i, i + 1) for i in range(devices - 1)])
-    anchor = after(levels(anchor, routes[5:6]), prev)
-    anchor = levels(anchor, routes[6:])
+    anchor = levels(anchor, routes[5:])
     prev = jnp.where(first, feats, after(prev, anchor))
     shards = [qkv_weight, weight_core, weight_chip, weight_last]
 

time: 117 us -> 107 us (0.915)
  the two profiles are of different devices: /device:TPU:497 before, /device:TPU:511 now
where the time goes in v10:
time: 107 us
  waiting for transfers between devices  55 us (51%)
  starting transfers between devices  33.9 us (32%)
  Pallas kernels  13.6 us (13%)
  local copies, waits for them, and re-layouts  3.2 us (3%)
    ppermute x7, waiting for transfers between devices, levels(): anchor = anchor + lax.ppermute(anchor, 'tm', route)  31 us
    ppermute x10, starting transfers between devices, to_rows(): return lax.ppermute(x, 'rows', [(i, i ^ flip) for i in range(4)])  27.3 us
    ppermute x10, waiting for transfers between devices, to_rows(): return lax.ppermute(x, 'rows', [(i, i ^ flip) for i in range(4)])  22 us
    pallas_call x8, Pallas kernels, call(): pl.pallas_call(kernel, out_shape=list(outs), in_specs=specs, out_specs=[V...  13.6 us
    ppermute x7, starting transfers between devices, levels(): anchor = anchor + lax.ppermute(anchor, 'tm', route)  5.31 us
    unnamed x10, local copies, waits for them, and re-layouts  2.43 us
  transfers between devices with their start and end apart: 18, of which 9 were waited for; matrix products, arithmetic and copies ran while one was open for 1% of the time, Pallas kernels for 6%

profile of v10, /device:TPU:511, one launch (start us, length us, event | category | flops | bytes accessed | tf_op | source)
XLA Modules:
  0.0 106.6 jit_solution(7309562659227232357)
XLA Ops:
  0.0 2.6 %collective-permute-start.4 = (bf16[128,640]{1,0:T(8,128)(2,1)}, bf16[128,640]{1,0:T(8,128)(2,1)S(1)}, u32[]{:S(2)}, u32[]{:S(2)}) collective-permute-start(bf16[128,640]{1,0:T(8,128)(2,1)} %bitcast.7), channel_id=1, source_target_pairs={{0,1},{1,0},{2,3},{3,2},{4,5},{5,4},{6,7},{7,6},{8,9},{9,8},{10,11... | collective-permute-start | bytes 491528 | tf_op jit(solution)/shard_map/ppermute | solution.py:29
  2.6 0.0 copy-start.1
  2.6 0.9 copy-done.1
  3.5 0.2 shard_map.64.own.lat
  3.7 0.1 collective-permute-done.4.core
  3.8 0.2 shard_map.65
  4.0 2.2 %collective-permute-start.6 = (bf16[160,1920]{1,0:T(8,128)(2,1)}, bf16[160,1920]{1,0:T(8,128)(2,1)S(1)}, u32[]{:S(2)}, u32[]{:S(2)}) collective-permute-start(bf16[160,1920]{1,0:T(8,128)(2,1)} %w0.1), channel_id=1, source_target_pairs={{0,1},{1,0},{2,3},{3,2},{4,5},{5,4},{6,7},{7,6},{8,9},{9,8},{10,11... | collective-permute-start | bytes 1843208 | tf_op jit(solution)/shard_map/ppermute | solution.py:29
  6.2 2.4 %collective-permute-start.5 = (bf16[2,128,160]{2,1,0:T(8,128)(2,1)S(1)}, bf16[2,128,160]{2,1,0:T(8,128)(2,1)S(1)}, u32[]{:S(2)}, u32[]{:S(2)}) collective-permute-start(bf16[2,128,160]{2,1,0:T(8,128)(2,1)S(1)} %get-tuple-element.47), channel_id=1, source_target_pairs={{0,2},{1,3},{2,0},{3,1},{4,6},{5,7},{6,4},{7,5},{8,10},{9,11},{10,... | collective-permute-start | bytes 245768 | tf_op jit(solution)/shard_map/ppermute | solution.py:29
  8.6 0.1 compare_convert_fusion.pool
  8.7 0.8 reshape.55.gain
  9.5 0.0 copy-start
  9.5 1.5 %copy-done = bf16[9,160,640]{2,1,0:T(8,128)(2,1)S(1)} copy-done((bf16[9,160,640]{2,1,0:T(8,128)(2,1)S(1)}, bf16[9,160,640]{2,1,0:T(8,128)(2,1)}, u32[]{:S(2)}) %copy-start) | copy-done | bytes 1843224
  11.0 0.1 shard_map.66.weight
  11.1 1.9 %collective-permute-done.5.came = bf16[2,128,160]{2,1,0:T(8,128)(2,1)S(1)} collective-permute-done((bf16[2,128,160]{2,1,0:T(8,128)(2,1)S(1)}, bf16[2,128,160]{2,1,0:T(8,128)(2,1)S(1)}, u32[]{:S(2)}, u32[]{:S(2)}) %collective-permute-start.5) | collective-permute-done | bytes 81952 | tf_op jit(solution)/shard_map/ppermute | solution.py:29
  13.0 0.0 collective-permute-done.6.w1
  13.0 0.0 copy-start.3
  13.0 0.0 copy-start.4
  13.0 2.4 %shard_map.67 = (f32[2,128,640]{2,1,0:T(8,128)S(1)}, bf16[2,128,640]{2,1,0:T(8,128)(2,1)S(1)}) custom-call(s32[1]{0:T(128)} %bitcast.me_ref, bf16[2,128,160]{2,1,0:T(8,128)(2,1)S(1)} %get-tuple-element.46.mine, bf16[2,128,160]{2,1,0:T(8,128)(2,1)S(1)} %collective-permute-done.5.came, f32[4,160]{1,0:T(4,128)S(1)} %reshape.55.gain, ...), custom_call_target="tpu_custom_call" | custom-call | flops 943718400 | bytes 3095044 | tf_op jit(solution)/shard_map/pallas_call | solution.py:216
  15.4 0.0 copy-start.2
  15.4 3.1 %collective-permute-start.7 = (bf16[2,128,640]{2,1,0:T(8,128)(2,1)S(1)}, bf16[2,128,640]{2,1,0:T(8,128)(2,1)S(1)}, u32[]{:S(2)}, u32[]{:S(2)}) collective-permute-start(bf16[2,128,640]{2,1,0:T(8,128)(2,1)S(1)} %get-tuple-element.52), channel_id=1, source_target_pairs={{0,1},{1,0},{2,3},{3,2},{4,5},{5,4},{6,7},{7,6},{8,9},{9,8},{10,11... | collective-permute-start | bytes 983048 | tf_op jit(solution)/shard_map/ppermute | solution.py:29
  18.5 1.2 %collective-permute-done.7.core = bf16[2,128,640]{2,1,0:T(8,128)(2,1)S(1)} collective-permute-done((bf16[2,128,640]{2,1,0:T(8,128)(2,1)S(1)}, bf16[2,128,640]{2,1,0:T(8,128)(2,1)S(1)}, u32[]{:S(2)}, u32[]{:S(2)}) %collective-permute-start.7) | collective-permute-done | bytes 327712 | tf_op jit(solution)/shard_map/ppermute | solution.py:29
  19.8 2.4 %collective-permute-start.8 = (bf16[128,640]{1,0:T(8,128)(2,1)S(1)}, bf16[128,640]{1,0:T(8,128)(2,1)S(1)}, u32[]{:S(2)}, u32[]{:S(2)}) collective-permute-start(bf16[128,640]{1,0:T(8,128)(2,1)S(1)} %fusion), channel_id=1, source_target_pairs={{0,2},{1,3},{2,0},{3,1},{4,6},{5,7},{6,4},{7,5},{8,10},{9,11},{10,... | collective-permute-start | bytes 491528 | tf_op jit(solution)/shard_map/ppermute | solution.py:29
  22.1 0.0 copy-done.3
  22.2 0.0 copy-done.4
  22.2 4.9 %collective-permute-done.8.chip = bf16[128,640]{1,0:T(8,128)(2,1)S(1)} collective-permute-done((bf16[128,640]{1,0:T(8,128)(2,1)S(1)}, bf16[128,640]{1,0:T(8,128)(2,1)S(1)}, u32[]{:S(2)}, u32[]{:S(2)}) %collective-permute-start.8) | collective-permute-done | bytes 163872 | tf_op jit(solution)/shard_map/ppermute | solution.py:29
  27.1 0.3 shard_map.68
  27.3 0.0 copy-done.2
  27.4 2.4 %collective-permute-start.10 = (bf16[160,1920]{1,0:T(8,128)(2,1)S(1)}, bf16[160,1920]{1,0:T(8,128)(2,1)S(1)}, u32[]{:S(2)}, u32[]{:S(2)}) collective-permute-start(bf16[160,1920]{1,0:T(8,128)(2,1)S(1)} %copy-done.2), channel_id=1, source_target_pairs={{0,2},{1,3},{2,0},{3,1},{4,6},{5,7},{6,4},{7,5},{8,10},{9,11},{10,... | collective-permute-start | bytes 1843208 | tf_op jit(solution)/shard_map/ppermute | solution.py:29
  29.8 1.3 %collective-permute-start.9 = (bf16[128,640]{1,0:T(8,128)(2,1)S(1)}, bf16[128,640]{1,0:T(8,128)(2,1)S(1)}, u32[]{:S(2)}, u32[]{:S(2)}) collective-permute-start(bf16[128,640]{1,0:T(8,128)(2,1)S(1)} %get-tuple-element.53.feats), channel_id=1, source_target_pairs={{0,4},{4,8},{8,12},{12,16},{16,20},{20,24},{24,28},{28,32},{32,36}... | collective-permute-start | bytes 491528 | tf_op jit(solution)/shard_map/ppermute | solution.py:276
  31.1 3.0 %while.10 = (s32[]{:T(128)}, bf16[128,640]{1,0:T(8,128)(2,1)S(1)}, s32[]{:T(128)}, s32[]{:T(128)}) while((s32[]{:T(128)}, bf16[128,640]{1,0:T(8,128)(2,1)S(1)}, s32[]{:T(128)}, s32[]{:T(128)}) %tuple.36), condition=%wide.region_1.2_spmd, body=%wide.region_0.1_spmd.sunk | while | flops 327682 | bytes 4587733 | solution.py:286
  31.1 0.7 collective-permute-start
  31.8 0.0 collective-permute-done
  31.8 0.7 collective-permute-start.1
  32.5 0.0 collective-permute-done.1
  32.6 0.7 collective-permute-start.2
  33.3 0.0 collective-permute-done.2
  33.3 0.7 collective-permute-start.3
  34.0 0.0 collective-permute-done.3
  34.1 2.0 %collective-permute-done.9 = bf16[128,640]{1,0:T(8,128)(2,1)S(1)} collective-permute-done((bf16[128,640]{1,0:T(8,128)(2,1)S(1)}, bf16[128,640]{1,0:T(8,128)(2,1)S(1)}, u32[]{:S(2)}, u32[]{:S(2)}) %collective-permute-start.9) | collective-permute-done | bytes 163872 | tf_op jit(solution)/shard_map/ppermute | solution.py:276
  36.1 7.3 %collective-permute-done.10.w2 = bf16[160,1920]{1,0:T(8,128)(2,1)S(1)} collective-permute-done((bf16[160,1920]{1,0:T(8,128)(2,1)S(1)}, bf16[160,1920]{1,0:T(8,128)(2,1)S(1)}, u32[]{:S(2)}, u32[]{:S(2)}) %collective-permute-start.10) | collective-permute-done | bytes 614432 | tf_op jit(solution)/shard_map/ppermute | solution.py:29
  43.4 4.0 %collective-permute-start.12 = (bf16[160,1920]{1,0:T(8,128)(2,1)S(1)}, bf16[160,1920]{1,0:T(8,128)(2,1)S(1)}, u32[]{:S(2)}, u32[]{:S(2)}) collective-permute-start(bf16[160,1920]{1,0:T(8,128)(2,1)S(1)} %collective-permute-done.10.w2), channel_id=1, source_target_pairs={{0,1},{1,0},{2,3},{3,2},{4,5},{5,4},{6,7},{7,6},{8,9},{9,8},{10,11... | collective-permute-start | bytes 1843208 | tf_op jit(solution)/shard_map/ppermute | solution.py:29
  47.4 0.7 collective-permute-start.11
  48.1 0.0 collective-permute-done.11
  48.2 0.9 collective-permute-done.12.w3
  49.1 0.7 collective-permute-start.13
  49.7 0.0 collective-permute-done.13
  49.8 1.3 %collective-permute-start.14 = (bf16[128,640]{1,0:T(8,128)(2,1)S(1)}, bf16[128,640]{1,0:T(8,128)(2,1)S(1)}, u32[]{:S(2)}, u32[]{:S(2)}) collective-permute-start(bf16[128,640]{1,0:T(8,128)(2,1)S(1)} %add.43), channel_id=1, source_target_pairs={{0,256},{8,264},{4,260},{12,268},{128,384},{136,392},{132,388},{14... | collective-permute-start | bytes 491528 | tf_op jit(solution)/shard_map/ppermute | solution.py:281
  51.1 31.0 %collective-permute-done.14 = bf16[128,640]{1,0:T(8,128)(2,1)S(1)} collective-permute-done((bf16[128,640]{1,0:T(8,128)(2,1)S(1)}, bf16[128,640]{1,0:T(8,128)(2,1)S(1)}, u32[]{:S(2)}, u32[]{:S(2)}) %collective-permute-start.14) | collective-permute-done | bytes 163872 | tf_op jit(solution)/shard_map/ppermute | solution.py:281
  82.2 3.7 %collective-permute-start.15 = (bf16[256,640]{1,0:T(8,128)(2,1)S(1)}, bf16[256,640]{1,0:T(8,128)(2,1)S(1)}, u32[]{:S(2)}, u32[]{:S(2)}) collective-permute-start(bf16[256,640]{1,0:T(8,128)(2,1)S(1)} %pad_maximum_fusion.a0), channel_id=1, source_target_pairs={{0,1},{1,0},{2,3},{3,2},{4,5},{5,4},{6,7},{7,6},{8,9},{9,8},{10,11... | collective-permute-start | bytes 983048 | tf_op jit(solution)/shard_map/ppermute | solution.py:29
  85.9 1.9 %collective-permute-start.16 = (bf16[256,640]{1,0:T(8,128)(2,1)S(1)}, bf16[256,640]{1,0:T(8,128)(2,1)S(1)}, u32[]{:S(2)}, u32[]{:S(2)}) collective-permute-start(bf16[256,640]{1,0:T(8,128)(2,1)S(1)} %pad_maximum_fusion.a0), channel_id=1, source_target_pairs={{0,2},{1,3},{2,0},{3,1},{4,6},{5,7},{6,4},{7,5},{8,10},{9,11},{10,... | collective-permute-start | bytes 983048 | tf_op jit(solution)/shard_map/ppermute | solution.py:29
  87.8 0.0 collective-permute-done.15.a1
  87.8 3.6 %shard_map.69 = (bf16[128,640]{1,0:T(8,128)(2,1)S(1)}, f32[128,8]{1,0:T(8,128)S(1)}, f32[128,8]{1,0:T(8,128)S(1)}, f32[128,640]{1,0:T(8,128)S(1)}, bf16[640,1920]{1,0:T(8,128)(2,1)S(1)}) custom-call(s32[1]{0:T(128)} %bitcast.me_ref, bf16[128,640]{1,0:T(8,128)(2,1)S(1)} %get-tuple-element.53.feats, bf16[256,640]{1,0:T(8,128)(2,1)S(1)} %pad_maximum_fusion.a0, ...), custom_call_target="tpu_custom_call" | custom-call | flops 1006632960 | bytes 6234116 | tf_op jit(solution)/shard_map/pallas_call | solution.py:216
  91.4 5.7 %collective-permute-done.16.a0 = bf16[256,640]{1,0:T(8,128)(2,1)S(1)} collective-permute-done((bf16[256,640]{1,0:T(8,128)(2,1)S(1)}, bf16[256,640]{1,0:T(8,128)(2,1)S(1)}, u32[]{:S(2)}, u32[]{:S(2)}) %collective-permute-start.16) | collective-permute-done | bytes 327712 | tf_op jit(solution)/shard_map/ppermute | solution.py:29
  97.1 2.7 %collective-permute-start.17 = (bf16[256,640]{1,0:T(8,128)(2,1)S(1)}, bf16[256,640]{1,0:T(8,128)(2,1)S(1)}, u32[]{:S(2)}, u32[]{:S(2)}) collective-permute-start(bf16[256,640]{1,0:T(8,128)(2,1)S(1)} %collective-permute-done.16.a0), channel_id=1, source_target_pairs={{0,1},{1,0},{2,3},{3,2},{4,5},{5,4},{6,7},{7,6},{8,9},{9,8},{10,11... | collective-permute-start | bytes 983048 | tf_op jit(solution)/shard_map/ppermute | solution.py:29
  99.8 2.9 %shard_map.70 = (f32[128,8]{1,0:T(8,128)S(1)}, f32[128,8]{1,0:T(8,128)S(1)}, f32[128,640]{1,0:T(8,128)S(1)}) custom-call(bf16[128,640]{1,0:T(8,128)(2,1)S(1)} %get-tuple-element.60.query, bf16[256,640]{1,0:T(8,128)(2,1)S(1)} %collective-permute-done.16.a0, bf16[640,1920]{1,0:T(8,128)(2,1)S(1)} %get-tuple-element.62.weight, ...), custom_call_target="tpu_custom_call" | custom-call | flops 503316480 | bytes 3620864 | tf_op jit(solution)/shard_map/pallas_call | solution.py:216
  102.8 0.0 collective-permute-done.17.a0
  102.8 3.8 %shard_map.71 = bf16[128,640]{1,0:T(8,128)(2,1)} custom-call(bf16[128,640]{1,0:T(8,128)(2,1)S(1)} %get-tuple-element.60.query, bf16[256,640]{1,0:T(8,128)(2,1)S(1)} %collective-permute-done.17.a0, bf16[640,1920]{1,0:T(8,128)(2,1)S(1)} %get-tuple-element.62.weight, f32[128,8]{1,0:T(8,128)S(1)} %get-tuple-element.66.top, f32[128,8]{1,0:T(8,128)S(1)} %get-tuple-element.67.den, ...), custom_call_target="tpu_custom_call" | custom-call | flops 503316480 | bytes 3612672 | tf_op jit(solution)/shard_map/pallas_call | solution.py:216
  (14 shorter events, 0.5 us)
Async XLA Ops:
  0.0 3.8 %collective-permute-start.4 = (bf16[128,640]{1,0:T(8,128)(2,1)}, bf16[128,640]{1,0:T(8,128)(2,1)S(1)}, u32[]{:S(2)}, u32[]{:S(2)}) collective-permute-start(bf16[128,640]{1,0:T(8,128)(2,1)} %bitcast.7), channel_id=1, source_target_pairs={{0,1},{1,0},{2,3},{3,2},{4,5},{5,4},{6,7},{7,6},{8,9},{9,8},{10,11... | collective-permute-start | bytes 491528 | tf_op jit(solution)/shard_map/ppermute | solution.py:29
  2.6 0.9 copy-start.1
  4.0 9.0 %collective-permute-start.6 = (bf16[160,1920]{1,0:T(8,128)(2,1)}, bf16[160,1920]{1,0:T(8,128)(2,1)S(1)}, u32[]{:S(2)}, u32[]{:S(2)}) collective-permute-start(bf16[160,1920]{1,0:T(8,128)(2,1)} %w0.1), channel_id=1, source_target_pairs={{0,1},{1,0},{2,3},{3,2},{4,5},{5,4},{6,7},{7,6},{8,9},{9,8},{10,11... | collective-permute-start | bytes 1843208 | tf_op jit(solution)/shard_map/ppermute | solution.py:29
  6.2 6.8 %collective-permute-start.5 = (bf16[2,128,160]{2,1,0:T(8,128)(2,1)S(1)}, bf16[2,128,160]{2,1,0:T(8,128)(2,1)S(1)}, u32[]{:S(2)}, u32[]{:S(2)}) collective-permute-start(bf16[2,128,160]{2,1,0:T(8,128)(2,1)S(1)} %get-tuple-element.47), channel_id=1, source_target_pairs={{0,2},{1,3},{2,0},{3,1},{4,6},{5,7},{6,4},{7,5},{8,10},{9,11},{10,... | collective-permute-start | bytes 245768 | tf_op jit(solution)/shard_map/ppermute | solution.py:29
  9.5 1.5 %copy-start = (bf16[9,160,640]{2,1,0:T(8,128)(2,1)S(1)}, bf16[9,160,640]{2,1,0:T(8,128)(2,1)}, u32[]{:S(2)}) copy-start(bf16[9,160,640]{2,1,0:T(8,128)(2,1)} %param.10) | copy-start | bytes 5529604
  13.0 9.1 %copy-start.3 = (f32[640]{0:T(1024)S(1)}, f32[640]{0:T(1024)}, u32[]{:S(2)}) copy-start(f32[640]{0:T(1024)} %param.11) | copy-start | bytes 7684
  13.0 9.2 %copy-start.4 = (f32[640]{0:T(1024)S(1)}, f32[640]{0:T(1024)}, u32[]{:S(2)}) copy-start(f32[640]{0:T(1024)} %param.12) | copy-start | bytes 7684
  15.4 12.0 %copy-start.2 = (bf16[160,1920]{1,0:T(8,128)(2,1)S(1)}, bf16[160,1920]{1,0:T(8,128)(2,1)}, u32[]{:S(2)}) copy-start(bf16[160,1920]{1,0:T(8,128)(2,1)} %w0.1) | copy-start | bytes 1843204
  15.4 4.3 %collective-permute-start.7 = (bf16[2,128,640]{2,1,0:T(8,128)(2,1)S(1)}, bf16[2,128,640]{2,1,0:T(8,128)(2,1)S(1)}, u32[]{:S(2)}, u32[]{:S(2)}) collective-permute-start(bf16[2,128,640]{2,1,0:T(8,128)(2,1)S(1)} %get-tuple-element.52), channel_id=1, source_target_pairs={{0,1},{1,0},{2,3},{3,2},{4,5},{5,4},{6,7},{7,6},{8,9},{9,8},{10,11... | collective-permute-start | bytes 983048 | tf_op jit(solution)/shard_map/ppermute | solution.py:29
  19.8 7.3 %collective-permute-start.8 = (bf16[128,640]{1,0:T(8,128)(2,1)S(1)}, bf16[128,640]{1,0:T(8,128)(2,1)S(1)}, u32[]{:S(2)}, u32[]{:S(2)}) collective-permute-start(bf16[128,640]{1,0:T(8,128)(2,1)S(1)} %fusion), channel_id=1, source_target_pairs={{0,2},{1,3},{2,0},{3,1},{4,6},{5,7},{6,4},{7,5},{8,10},{9,11},{10,... | collective-permute-start | bytes 491528 | tf_op jit(solution)/shard_map/ppermute | solution.py:29
  27.4 16.0 %collective-permute-start.10 = (bf16[160,1920]{1,0:T(8,128)(2,1)S(1)}, bf16[160,1920]{1,0:T(8,128)(2,1)S(1)}, u32[]{:S(2)}, u32[]{:S(2)}) collective-permute-start(bf16[160,1920]{1,0:T(8,128)(2,1)S(1)} %copy-done.2), channel_id=1, source_target_pairs={{0,2},{1,3},{2,0},{3,1},{4,6},{5,7},{6,4},{7,5},{8,10},{9,11},{10,... | collective-permute-start | bytes 1843208 | tf_op jit(solution)/shard_map/ppermute | solution.py:29
  29.8 6.4 %collective-permute-start.9 = (bf16[128,640]{1,0:T(8,128)(2,1)S(1)}, bf16[128,640]{1,0:T(8,128)(2,1)S(1)}, u32[]{:S(2)}, u32[]{:S(2)}) collective-permute-start(bf16[128,640]{1,0:T(8,128)(2,1)S(1)} %get-tuple-element.53.feats), channel_id=1, source_target_pairs={{0,4},{4,8},{8,12},{12,16},{16,20},{20,24},{24,28},{28,32},{32,36}... | collective-permute-start | bytes 491528 | tf_op jit(solution)/shard_map/ppermute | solution.py:276
  31.1 0.7 collective-permute-start
  31.8 0.7 collective-permute-start.1
  32.6 0.7 collective-permute-start.2
  33.3 0.7 collective-permute-start.3
  43.4 5.7 %collective-permute-start.12 = (bf16[160,1920]{1,0:T(8,128)(2,1)S(1)}, bf16[160,1920]{1,0:T(8,128)(2,1)S(1)}, u32[]{:S(2)}, u32[]{:S(2)}) collective-permute-start(bf16[160,1920]{1,0:T(8,128)(2,1)S(1)} %collective-permute-done.10.w2), channel_id=1, source_target_pairs={{0,1},{1,0},{2,3},{3,2},{4,5},{5,4},{6,7},{7,6},{8,9},{9,8},{10,11... | collective-permute-start | bytes 1843208 | tf_op jit(solution)/shard_map/ppermute | solution.py:29
  47.4 0.7 collective-permute-start.11
  49.1 0.7 collective-permute-start.13
  49.8 32.3 %collective-permute-start.14 = (bf16[128,640]{1,0:T(8,128)(2,1)S(1)}, bf16[128,640]{1,0:T(8,128)(2,1)S(1)}, u32[]{:S(2)}, u32[]{:S(2)}) collective-permute-start(bf16[128,640]{1,0:T(8,128)(2,1)S(1)} %add.43), channel_id=1, source_target_pairs={{0,256},{8,264},{4,260},{12,268},{128,384},{136,392},{132,388},{14... | collective-permute-start | bytes 491528 | tf_op jit(solution)/shard_map/ppermute | solution.py:281
  82.2 5.6 %collective-permute-start.15 = (bf16[256,640]{1,0:T(8,128)(2,1)S(1)}, bf16[256,640]{1,0:T(8,128)(2,1)S(1)}, u32[]{:S(2)}, u32[]{:S(2)}) collective-permute-start(bf16[256,640]{1,0:T(8,128)(2,1)S(1)} %pad_maximum_fusion.a0), channel_id=1, source_target_pairs={{0,1},{1,0},{2,3},{3,2},{4,5},{5,4},{6,7},{7,6},{8,9},{9,8},{10,11... | collective-permute-start | bytes 983048 | tf_op jit(solution)/shard_map/ppermute | solution.py:29
  85.9 11.2 %collective-permute-start.16 = (bf16[256,640]{1,0:T(8,128)(2,1)S(1)}, bf16[256,640]{1,0:T(8,128)(2,1)S(1)}, u32[]{:S(2)}, u32[]{:S(2)}) collective-permute-start(bf16[256,640]{1,0:T(8,128)(2,1)S(1)} %pad_maximum_fusion.a0), channel_id=1, source_target_pairs={{0,2},{1,3},{2,0},{3,1},{4,6},{5,7},{6,4},{7,5},{8,10},{9,11},{10,... | collective-permute-start | bytes 983048 | tf_op jit(solution)/shard_map/ppermute | solution.py:29
  97.1 5.6 %collective-permute-start.17 = (bf16[256,640]{1,0:T(8,128)(2,1)S(1)}, bf16[256,640]{1,0:T(8,128)(2,1)S(1)}, u32[]{:S(2)}, u32[]{:S(2)}) collective-permute-start(bf16[256,640]{1,0:T(8,128)(2,1)S(1)} %collective-permute-done.16.a0), channel_id=1, source_target_pairs={{0,1},{1,0},{2,3},{3,2},{4,5},{5,4},{6,7},{7,6},{8,9},{9,8},{10,11... | collective-permute-start | bytes 983048 | tf_op jit(solution)/shard_map/ppermute | solution.py:29

commit v11 on v10

--- a/solution.py
+++ b/solution.py
@@ -119,9 +119,11 @@
 
 
 def project(blocks, weight, joined, keys, vals):
-    part, chans = blocks[0].shape
-    for at, block in enumerate(blocks):
-        joined[at * part : (at + 1) * part, :] = block[...]
+    chans = joined.shape[1]
+    at = 0
+    for block in blocks:
+        joined[at : at + block.shape[0], :] = block[...]
+        at += block.shape[0]
     for out, first in ((keys, chans), (vals, 2 * chans)):
         out[...] = jnp.dot(
             joined[...], weight[:, first : first + chans], preferred_element_type=jnp.float32
@@ -180,7 +182,7 @@
 
 
 def first_kernel(
-    me_ref, feats, a0, a1, w0, w1, w2, w3, query, top, den, acc, weight, joined, keys, vals
+    me_ref, feats, a0, a1, a2, w0, w1, w2, w3, query, top, den, acc, weight, joined, keys, vals
 ):
     me = me_ref[0]
     chans = feats.shape[1]
@@ -191,7 +193,7 @@
     query[...] = jnp.dot(
         feats[...], weight[:, :chans], preferred_element_type=jnp.float32
     ).astype(jnp.bfloat16)
-    keep_state(attend((a0, a1), query, weight, joined, keys, vals), top, den, acc)
+    keep_state(attend((a0, a1, a2), query, weight, joined, keys, vals), top, den, acc)
 
 
 def more_kernel(query, a0, weight, top, den, acc, new_top, new_den, new_acc, joined, keys, vals):
@@ -201,7 +203,7 @@
 
 def last_kernel(query, a0, weight, top, den, acc, residual, restyled, joined, keys, vals):
     heads = attend((a0,), query, weight, joined, keys, vals, (top, den, acc))
-    mixed = [out / total for _, total, out in heads]
+    mixed = [out * (1.0 / total) for _, total, out in heads]
     for tile, value in tiles_of(mixed, restyled.shape[1]):
         restyled[:, tile] = (residual[:, tile].astype(jnp.float32) + value).astype(jnp.bfloat16)
 
@@ -276,24 +278,27 @@
     prev = lax.ppermute(feats, "tm", [(i, i + 1) for i in range(devices - 1)])
     weight_chip = to_rows(after(qkv_weight, feats), 2)
 
+    trips = 1 + jnp.minimum(lax.axis_index("tm"), 0)
+
     def levels(anchor, which):
         for route in which:
             anchor = anchor + lax.ppermute(anchor, "tm", route)
         return anchor
 
-    trips = 1 + jnp.minimum(lax.axis_index("tm"), 0)
-    anchor = jnp.where(first, feats, jnp.zeros_like(feats))
-    anchor = lax.fori_loop(0, trips, lambda _, a: levels(a, routes[:4]), anchor)
+    def looped(anchor, which):
+        return lax.fori_loop(0, trips, lambda _, a: levels(a, which), anchor)
+
+    anchor = looped(jnp.where(first, feats, jnp.zeros_like(feats)), routes[:4])
     anchor = after(anchor, prev, weight_chip)
     weight_last = to_rows(after(weight_chip, anchor), 1)
-    anchor = after(levels(anchor, routes[4:5]), weight_last)
-    anchor = levels(anchor, routes[5:])
+    anchor = after(looped(anchor, routes[4:6]), weight_last)
+    anchor = levels(anchor, routes[6:])
     prev = jnp.where(first, feats, after(prev, anchor))
     shards = [qkv_weight, weight_core, weight_chip, weight_last]
 
     own = jnp.concatenate([prev, anchor], axis=0)
-    core = to_rows(own, 1)
     chip = to_rows(own, 2)
+    core = [to_rows(prev, 1), to_rows(anchor, 1)]
     keys = 2 * part
     scratch = lambda keys: [pltpu.VMEM((keys, chans), bf16)] * 3
     flops = lambda keys: 2 * keys * chans * 2 * chans + 4 * part * keys * chans
@@ -305,7 +310,7 @@
     query, *prior, weight = call(
         first_kernel,
         [shape((part, chans), bf16), *state, shape((chans, 3 * chans), bf16)],
-        [me.reshape(1), feats, own, core, *shards],
+        [me.reshape(1), feats, own, *core, *shards],
         scratch(2 * keys),
         flops=flops(2 * keys),
     )

time: 107 us -> 105 us (0.981)
  the two profiles are of different devices: /device:TPU:511 before, /device:TPU:503 now
where the time goes in v11:
time: 105 us
  waiting for transfers between devices  47.7 us (45%)
  starting transfers between devices  39.4 us (38%)
  Pallas kernels  13.5 us (13%)
  local copies, waits for them, and re-layouts  3.2 us (3%)
    ppermute x11, starting transfers between devices, to_rows(): return lax.ppermute(x, 'rows', [(i, i ^ flip) for i in range(4)])  32.8 us
    ppermute x7, waiting for transfers between devices, levels(): anchor = anchor + lax.ppermute(anchor, 'tm', route)  30.4 us
    ppermute x11, waiting for transfers between devices, to_rows(): return lax.ppermute(x, 'rows', [(i, i ^ flip) for i in range(4)])  15.3 us
    pallas_call x8, Pallas kernels, call(): pl.pallas_call(kernel, out_shape=list(outs), in_specs=specs, out_specs=[V...  13.5 us
    ppermute x7, starting transfers between devices, levels(): anchor = anchor + lax.ppermute(anchor, 'tm', route)  5.31 us
    unnamed x10, local copies, waits for them, and re-layouts  2.43 us
  transfers between devices with their start and end apart: 19, of which 9 were waited for; matrix products, arithmetic and copies ran while one was open for 1% of the time, Pallas kernels for 7%

profile of v11, /device:TPU:503, one launch (start us, length us, event | category | flops | bytes accessed | tf_op | source)
XLA Modules:
  0.0 104.8 jit_solution(12823644852428190028)
XLA Ops:
  0.0 2.6 %collective-permute-start.6 = (bf16[128,640]{1,0:T(8,128)(2,1)}, bf16[128,640]{1,0:T(8,128)(2,1)S(1)}, u32[]{:S(2)}, u32[]{:S(2)}) collective-permute-start(bf16[128,640]{1,0:T(8,128)(2,1)} %bitcast.7), channel_id=1, source_target_pairs={{0,1},{1,0},{2,3},{3,2},{4,5},{5,4},{6,7},{7,6},{8,9},{9,8},{10,11... | collective-permute-start | bytes 491528 | tf_op jit(solution)/shard_map/ppermute | solution.py:29
  2.6 0.0 copy-start.1
  2.6 0.9 copy-done.1
  3.5 0.2 shard_map.64.own.lat
  3.7 0.1 collective-permute-done.6.core
  3.8 0.2 shard_map.65
  4.0 2.2 %collective-permute-start.8 = (bf16[160,1920]{1,0:T(8,128)(2,1)}, bf16[160,1920]{1,0:T(8,128)(2,1)S(1)}, u32[]{:S(2)}, u32[]{:S(2)}) collective-permute-start(bf16[160,1920]{1,0:T(8,128)(2,1)} %w0.1), channel_id=1, source_target_pairs={{0,1},{1,0},{2,3},{3,2},{4,5},{5,4},{6,7},{7,6},{8,9},{9,8},{10,11... | collective-permute-start | bytes 1843208 | tf_op jit(solution)/shard_map/ppermute | solution.py:29
  6.2 2.9 %collective-permute-start.7 = (bf16[2,128,160]{2,1,0:T(8,128)(2,1)S(1)}, bf16[2,128,160]{2,1,0:T(8,128)(2,1)S(1)}, u32[]{:S(2)}, u32[]{:S(2)}) collective-permute-start(bf16[2,128,160]{2,1,0:T(8,128)(2,1)S(1)} %get-tuple-element.65), channel_id=1, source_target_pairs={{0,2},{1,3},{2,0},{3,1},{4,6},{5,7},{6,4},{7,5},{8,10},{9,11},{10,... | collective-permute-start | bytes 245768 | tf_op jit(solution)/shard_map/ppermute | solution.py:29
  9.2 0.1 compare_convert_fusion.pool
  9.2 0.8 reshape.55.gain
  10.0 0.0 copy-start
  10.0 1.5 %copy-done = bf16[9,160,640]{2,1,0:T(8,128)(2,1)S(1)} copy-done((bf16[9,160,640]{2,1,0:T(8,128)(2,1)S(1)}, bf16[9,160,640]{2,1,0:T(8,128)(2,1)}, u32[]{:S(2)}) %copy-start) | copy-done | bytes 1843224
  11.5 0.1 shard_map.66.weight
  11.7 1.3 %collective-permute-done.7.came = bf16[2,128,160]{2,1,0:T(8,128)(2,1)S(1)} collective-permute-done((bf16[2,128,160]{2,1,0:T(8,128)(2,1)S(1)}, bf16[2,128,160]{2,1,0:T(8,128)(2,1)S(1)}, u32[]{:S(2)}, u32[]{:S(2)}) %collective-permute-start.7) | collective-permute-done | bytes 81952 | tf_op jit(solution)/shard_map/ppermute | solution.py:29
  13.0 0.0 collective-permute-done.8.w1
  13.0 0.0 copy-start.3
  13.0 0.0 copy-start.4
  13.0 2.4 %shard_map.67 = (f32[2,128,640]{2,1,0:T(8,128)S(1)}, bf16[2,128,640]{2,1,0:T(8,128)(2,1)S(1)}) custom-call(s32[1]{0:T(128)} %bitcast.me_ref, bf16[2,128,160]{2,1,0:T(8,128)(2,1)S(1)} %get-tuple-element.64.mine, bf16[2,128,160]{2,1,0:T(8,128)(2,1)S(1)} %collective-permute-done.7.came, f32[4,160]{1,0:T(4,128)S(1)} %reshape.55.gain, ...), custom_call_target="tpu_custom_call" | custom-call | flops 943718400 | bytes 3095044 | tf_op jit(solution)/shard_map/pallas_call | solution.py:218
  15.4 0.0 copy-start.2
  15.4 3.1 %collective-permute-start.9 = (bf16[2,128,640]{2,1,0:T(8,128)(2,1)S(1)}, bf16[2,128,640]{2,1,0:T(8,128)(2,1)S(1)}, u32[]{:S(2)}, u32[]{:S(2)}) collective-permute-start(bf16[2,128,640]{2,1,0:T(8,128)(2,1)S(1)} %get-tuple-element.70), channel_id=1, source_target_pairs={{0,1},{1,0},{2,3},{3,2},{4,5},{5,4},{6,7},{7,6},{8,9},{9,8},{10,11... | collective-permute-start | bytes 983048 | tf_op jit(solution)/shard_map/ppermute | solution.py:29
  18.5 1.2 %collective-permute-done.9.core = bf16[2,128,640]{2,1,0:T(8,128)(2,1)S(1)} collective-permute-done((bf16[2,128,640]{2,1,0:T(8,128)(2,1)S(1)}, bf16[2,128,640]{2,1,0:T(8,128)(2,1)S(1)}, u32[]{:S(2)}, u32[]{:S(2)}) %collective-permute-start.9) | collective-permute-done | bytes 327712 | tf_op jit(solution)/shard_map/ppermute | solution.py:29
  19.8 2.9 %collective-permute-start.10 = (bf16[128,640]{1,0:T(8,128)(2,1)S(1)}, bf16[128,640]{1,0:T(8,128)(2,1)S(1)}, u32[]{:S(2)}, u32[]{:S(2)}) collective-permute-start(bf16[128,640]{1,0:T(8,128)(2,1)S(1)} %fusion), channel_id=1, source_target_pairs={{0,2},{1,3},{2,0},{3,1},{4,6},{5,7},{6,4},{7,5},{8,10},{9,11},{10,... | collective-permute-start | bytes 491528 | tf_op jit(solution)/shard_map/ppermute | solution.py:29
  22.7 0.0 copy-done.3
  22.7 0.0 copy-done.4
  22.7 4.4 %collective-permute-done.10.chip = bf16[128,640]{1,0:T(8,128)(2,1)S(1)} collective-permute-done((bf16[128,640]{1,0:T(8,128)(2,1)S(1)}, bf16[128,640]{1,0:T(8,128)(2,1)S(1)}, u32[]{:S(2)}, u32[]{:S(2)}) %collective-permute-start.10) | collective-permute-done | bytes 163872 | tf_op jit(solution)/shard_map/ppermute | solution.py:29
  27.1 0.3 shard_map.68
  27.4 0.0 copy-done.2
  27.4 2.9 %collective-permute-start.12 = (bf16[160,1920]{1,0:T(8,128)(2,1)S(1)}, bf16[160,1920]{1,0:T(8,128)(2,1)S(1)}, u32[]{:S(2)}, u32[]{:S(2)}) collective-permute-start(bf16[160,1920]{1,0:T(8,128)(2,1)S(1)} %copy-done.2), channel_id=1, source_target_pairs={{0,2},{1,3},{2,0},{3,1},{4,6},{5,7},{6,4},{7,5},{8,10},{9,11},{10,... | collective-permute-start | bytes 1843208 | tf_op jit(solution)/shard_map/ppermute | solution.py:29
  30.3 1.3 %collective-permute-start.11 = (bf16[128,640]{1,0:T(8,128)(2,1)S(1)}, bf16[128,640]{1,0:T(8,128)(2,1)S(1)}, u32[]{:S(2)}, u32[]{:S(2)}) collective-permute-start(bf16[128,640]{1,0:T(8,128)(2,1)S(1)} %get-tuple-element.71.feats), channel_id=1, source_target_pairs={{0,4},{4,8},{8,12},{12,16},{16,20},{20,24},{24,28},{28,32},{32,36}... | collective-permute-start | bytes 491528 | tf_op jit(solution)/shard_map/ppermute | solution.py:278
  31.6 3.0 %while.20 = (s32[]{:T(128)}, bf16[128,640]{1,0:T(8,128)(2,1)S(1)}, s32[]{:T(128)}, s32[]{:T(128)}) while((s32[]{:T(128)}, bf16[128,640]{1,0:T(8,128)(2,1)S(1)}, s32[]{:T(128)}, s32[]{:T(128)}) %tuple.49), condition=%wide.region_1.2_spmd, body=%wide.region_0.1_spmd.sunk | while | flops 327682 | bytes 4587733 | solution.py:289
  31.6 0.7 collective-permute-start
  32.3 0.0 collective-permute-done
  32.4 0.7 collective-permute-start.1
  33.0 0.0 collective-permute-done.1
  33.1 0.7 collective-permute-start.2
  33.8 0.0 collective-permute-done.2
  33.8 0.7 collective-permute-start.3
  34.5 0.0 collective-permute-done.3
  34.6 2.0 %collective-permute-done.11 = bf16[128,640]{1,0:T(8,128)(2,1)S(1)} collective-permute-done((bf16[128,640]{1,0:T(8,128)(2,1)S(1)}, bf16[128,640]{1,0:T(8,128)(2,1)S(1)}, u32[]{:S(2)}, u32[]{:S(2)}) %collective-permute-start.11) | collective-permute-done | bytes 163872 | tf_op jit(solution)/shard_map/ppermute | solution.py:278
  36.6 6.8 %collective-permute-done.12.w2 = bf16[160,1920]{1,0:T(8,128)(2,1)S(1)} collective-permute-done((bf16[160,1920]{1,0:T(8,128)(2,1)S(1)}, bf16[160,1920]{1,0:T(8,128)(2,1)S(1)}, u32[]{:S(2)}, u32[]{:S(2)}) %collective-permute-start.12) | collective-permute-done | bytes 614432 | tf_op jit(solution)/shard_map/ppermute | solution.py:29
  43.4 4.0 %collective-permute-start.13 = (bf16[160,1920]{1,0:T(8,128)(2,1)S(1)}, bf16[160,1920]{1,0:T(8,128)(2,1)S(1)}, u32[]{:S(2)}, u32[]{:S(2)}) collective-permute-start(bf16[160,1920]{1,0:T(8,128)(2,1)S(1)} %collective-permute-done.12.w2), channel_id=1, source_target_pairs={{0,1},{1,0},{2,3},{3,2},{4,5},{5,4},{6,7},{7,6},{8,9},{9,8},{10,11... | collective-permute-start | bytes 1843208 | tf_op jit(solution)/shard_map/ppermute | solution.py:29
  47.4 1.5 %while.21 = (s32[]{:T(128)}, bf16[128,640]{1,0:T(8,128)(2,1)S(1)}, s32[]{:T(128)}, s32[]{:T(128)}) while((s32[]{:T(128)}, bf16[128,640]{1,0:T(8,128)(2,1)S(1)}, s32[]{:T(128)}, s32[]{:T(128)}) %tuple.52), condition=%wide.region_3.4_spmd, body=%wide.region_2.3_spmd.sunk | while | flops 163842 | bytes 2293893 | solution.py:289
  47.4 0.7 collective-permute-start.4
  48.1 0.0 collective-permute-done.4
  48.2 0.7 collective-permute-start.5
  48.9 0.0 collective-permute-done.5
  48.9 0.1 collective-permute-done.13.w3
  49.1 1.3 %collective-permute-start.14 = (bf16[128,640]{1,0:T(8,128)(2,1)S(1)}, bf16[128,640]{1,0:T(8,128)(2,1)S(1)}, u32[]{:S(2)}, u32[]{:S(2)}) collective-permute-start(bf16[128,640]{1,0:T(8,128)(2,1)S(1)} %get-tuple-element.77), channel_id=1, source_target_pairs={{0,256},{8,264},{4,260},{12,268},{128,384},{136,392},{132,388},{14... | collective-permute-start | bytes 491528 | tf_op jit(solution)/shard_map/ppermute | solution.py:285
  50.4 30.4 %collective-permute-done.14 = bf16[128,640]{1,0:T(8,128)(2,1)S(1)} collective-permute-done((bf16[128,640]{1,0:T(8,128)(2,1)S(1)}, bf16[128,640]{1,0:T(8,128)(2,1)S(1)}, u32[]{:S(2)}, u32[]{:S(2)}) %collective-permute-start.14) | collective-permute-done | bytes 163872 | tf_op jit(solution)/shard_map/ppermute | solution.py:285
  80.9 4.3 %collective-permute-start.17 = (bf16[256,640]{1,0:T(8,128)(2,1)S(1)}, bf16[256,640]{1,0:T(8,128)(2,1)S(1)}, u32[]{:S(2)}, u32[]{:S(2)}) collective-permute-start(bf16[256,640]{1,0:T(8,128)(2,1)S(1)} %pad_maximum_fusion.a0), channel_id=1, source_target_pairs={{0,2},{1,3},{2,0},{3,1},{4,6},{5,7},{6,4},{7,5},{8,10},{9,11},{10,... | collective-permute-start | bytes 983048 | tf_op jit(solution)/shard_map/ppermute | solution.py:29
  85.2 3.9 %collective-permute-start.15 = (bf16[128,640]{1,0:T(8,128)(2,1)S(1)}, bf16[128,640]{1,0:T(8,128)(2,1)S(1)}, u32[]{:S(2)}, u32[]{:S(2)}) collective-permute-start(bf16[128,640]{1,0:T(8,128)(2,1)S(1)} %broadcast_select_fusion), channel_id=1, source_target_pairs={{0,1},{1,0},{2,3},{3,2},{4,5},{5,4},{6,7},{7,6},{8,9},{9,8},{10,11... | collective-permute-start | bytes 491528 | tf_op jit(solution)/shard_map/ppermute | solution.py:29
  89.1 1.9 %collective-permute-start.16 = (bf16[128,640]{1,0:T(8,128)(2,1)S(1)}, bf16[128,640]{1,0:T(8,128)(2,1)S(1)}, u32[]{:S(2)}, u32[]{:S(2)}) collective-permute-start(bf16[128,640]{1,0:T(8,128)(2,1)S(1)} %add.45), channel_id=1, source_target_pairs={{0,1},{1,0},{2,3},{3,2},{4,5},{5,4},{6,7},{7,6},{8,9},{9,8},{10,11... | collective-permute-start | bytes 491528 | tf_op jit(solution)/shard_map/ppermute | solution.py:29
  91.0 0.0 collective-permute-done.15.a1
  91.0 1.4 %collective-permute-done.16.a2 = bf16[128,640]{1,0:T(8,128)(2,1)S(1)} collective-permute-done((bf16[128,640]{1,0:T(8,128)(2,1)S(1)}, bf16[128,640]{1,0:T(8,128)(2,1)S(1)}, u32[]{:S(2)}, u32[]{:S(2)}) %collective-permute-start.16) | collective-permute-done | bytes 163872 | tf_op jit(solution)/shard_map/ppermute | solution.py:29
  92.4 3.6 %shard_map.69 = (bf16[128,640]{1,0:T(8,128)(2,1)S(1)}, f32[128,8]{1,0:T(8,128)S(1)}, f32[128,8]{1,0:T(8,128)S(1)}, f32[128,640]{1,0:T(8,128)S(1)}, bf16[640,1920]{1,0:T(8,128)(2,1)S(1)}) custom-call(s32[1]{0:T(128)} %bitcast.me_ref, bf16[128,640]{1,0:T(8,128)(2,1)S(1)} %get-tuple-element.71.feats, bf16[256,640]{1,0:T(8,128)(2,1)S(1)} %pad_maximum_fusion.a0, ...), custom_call_target="tpu_custom_call" | custom-call | flops 1006632960 | bytes 6234116 | tf_op jit(solution)/shard_map/pallas_call | solution.py:218
  96.0 0.0 collective-permute-done.17.a0
  96.0 2.1 %collective-permute-start.18 = (bf16[256,640]{1,0:T(8,128)(2,1)S(1)}, bf16[256,640]{1,0:T(8,128)(2,1)S(1)}, u32[]{:S(2)}, u32[]{:S(2)}) collective-permute-start(bf16[256,640]{1,0:T(8,128)(2,1)S(1)} %collective-permute-done.17.a0), channel_id=1, source_target_pairs={{0,1},{1,0},{2,3},{3,2},{4,5},{5,4},{6,7},{7,6},{8,9},{9,8},{10,11... | collective-permute-start | bytes 983048 | tf_op jit(solution)/shard_map/ppermute | solution.py:29
  98.1 2.9 %shard_map.70 = (f32[128,8]{1,0:T(8,128)S(1)}, f32[128,8]{1,0:T(8,128)S(1)}, f32[128,640]{1,0:T(8,128)S(1)}) custom-call(bf16[128,640]{1,0:T(8,128)(2,1)S(1)} %get-tuple-element.79.query, bf16[256,640]{1,0:T(8,128)(2,1)S(1)} %collective-permute-done.17.a0, bf16[640,1920]{1,0:T(8,128)(2,1)S(1)} %get-tuple-element.81.weight, ...), custom_call_target="tpu_custom_call" | custom-call | flops 503316480 | bytes 3620864 | tf_op jit(solution)/shard_map/pallas_call | solution.py:218
  101.0 0.0 collective-permute-done.18.a0
  101.0 3.8 %shard_map.71 = bf16[128,640]{1,0:T(8,128)(2,1)} custom-call(bf16[128,640]{1,0:T(8,128)(2,1)S(1)} %get-tuple-element.79.query, bf16[256,640]{1,0:T(8,128)(2,1)S(1)} %collective-permute-done.18.a0, bf16[640,1920]{1,0:T(8,128)(2,1)S(1)} %get-tuple-element.81.weight, f32[128,8]{1,0:T(8,128)S(1)} %get-tuple-element.85.top, f32[128,8]{1,0:T(8,128)S(1)} %get-tuple-element.86.den, ...), custom_call_target="tpu_custom_call" | custom-call | flops 503316480 | bytes 3612672 | tf_op jit(solution)/shard_map/pallas_call | solution.py:218
  (14 shorter events, 0.4 us)
Async XLA Ops:
  0.0 3.8 %collective-permute-start.6 = (bf16[128,640]{1,0:T(8,128)(2,1)}, bf16[128,640]{1,0:T(8,128)(2,1)S(1)}, u32[]{:S(2)}, u32[]{:S(2)}) collective-permute-start(bf16[128,640]{1,0:T(8,128)(2,1)} %bitcast.7), channel_id=1, source_target_pairs={{0,1},{1,0},{2,3},{3,2},{4,5},{5,4},{6,7},{7,6},{8,9},{9,8},{10,11... | collective-permute-start | bytes 491528 | tf_op jit(solution)/shard_map/ppermute | solution.py:29
  2.6 0.9 copy-start.1
  4.0 9.0 %collective-permute-start.8 = (bf16[160,1920]{1,0:T(8,128)(2,1)}, bf16[160,1920]{1,0:T(8,128)(2,1)S(1)}, u32[]{:S(2)}, u32[]{:S(2)}) collective-permute-start(bf16[160,1920]{1,0:T(8,128)(2,1)} %w0.1), channel_id=1, source_target_pairs={{0,1},{1,0},{2,3},{3,2},{4,5},{5,4},{6,7},{7,6},{8,9},{9,8},{10,11... | collective-permute-start | bytes 1843208 | tf_op jit(solution)/shard_map/ppermute | solution.py:29
  6.2 6.8 %collective-permute-start.7 = (bf16[2,128,160]{2,1,0:T(8,128)(2,1)S(1)}, bf16[2,128,160]{2,1,0:T(8,128)(2,1)S(1)}, u32[]{:S(2)}, u32[]{:S(2)}) collective-permute-start(bf16[2,128,160]{2,1,0:T(8,128)(2,1)S(1)} %get-tuple-element.65), channel_id=1, source_target_pairs={{0,2},{1,3},{2,0},{3,1},{4,6},{5,7},{6,4},{7,5},{8,10},{9,11},{10,... | collective-permute-start | bytes 245768 | tf_op jit(solution)/shard_map/ppermute | solution.py:29
  10.0 1.5 %copy-start = (bf16[9,160,640]{2,1,0:T(8,128)(2,1)S(1)}, bf16[9,160,640]{2,1,0:T(8,128)(2,1)}, u32[]{:S(2)}) copy-start(bf16[9,160,640]{2,1,0:T(8,128)(2,1)} %param.12) | copy-start | bytes 5529604
  13.0 9.7 %copy-start.3 = (f32[640]{0:T(1024)S(1)}, f32[640]{0:T(1024)}, u32[]{:S(2)}) copy-start(f32[640]{0:T(1024)} %param.13) | copy-start | bytes 7684
  13.0 9.7 %copy-start.4 = (f32[640]{0:T(1024)S(1)}, f32[640]{0:T(1024)}, u32[]{:S(2)}) copy-start(f32[640]{0:T(1024)} %param.14) | copy-start | bytes 7684
  15.4 12.0 %copy-start.2 = (bf16[160,1920]{1,0:T(8,128)(2,1)S(1)}, bf16[160,1920]{1,0:T(8,128)(2,1)}, u32[]{:S(2)}) copy-start(bf16[160,1920]{1,0:T(8,128)(2,1)} %w0.1) | copy-start | bytes 1843204
  15.4 4.3 %collective-permute-start.9 = (bf16[2,128,640]{2,1,0:T(8,128)(2,1)S(1)}, bf16[2,128,640]{2,1,0:T(8,128)(2,1)S(1)}, u32[]{:S(2)}, u32[]{:S(2)}) collective-permute-start(bf16[2,128,640]{2,1,0:T(8,128)(2,1)S(1)} %get-tuple-element.70), channel_id=1, source_target_pairs={{0,1},{1,0},{2,3},{3,2},{4,5},{5,4},{6,7},{7,6},{8,9},{9,8},{10,11... | collective-permute-start | bytes 983048 | tf_op jit(solution)/shard_map/ppermute | solution.py:29
  19.8 7.3 %collective-permute-start.10 = (bf16[128,640]{1,0:T(8,128)(2,1)S(1)}, bf16[128,640]{1,0:T(8,128)(2,1)S(1)}, u32[]{:S(2)}, u32[]{:S(2)}) collective-permute-start(bf16[128,640]{1,0:T(8,128)(2,1)S(1)} %fusion), channel_id=1, source_target_pairs={{0,2},{1,3},{2,0},{3,1},{4,6},{5,7},{6,4},{7,5},{8,10},{9,11},{10,... | collective-permute-start | bytes 491528 | tf_op jit(solution)/shard_map/ppermute | solution.py:29
  27.4 16.0 %collective-permute-start.12 = (bf16[160,1920]{1,0:T(8,128)(2,1)S(1)}, bf16[160,1920]{1,0:T(8,128)(2,1)S(1)}, u32[]{:S(2)}, u32[]{:S(2)}) collective-permute-start(bf16[160,1920]{1,0:T(8,128)(2,1)S(1)} %copy-done.2), channel_id=1, source_target_pairs={{0,2},{1,3},{2,0},{3,1},{4,6},{5,7},{6,4},{7,5},{8,10},{9,11},{10,... | collective-permute-start | bytes 1843208 | tf_op jit(solution)/shard_map/ppermute | solution.py:29
  30.3 6.4 %collective-permute-start.11 = (bf16[128,640]{1,0:T(8,128)(2,1)S(1)}, bf16[128,640]{1,0:T(8,128)(2,1)S(1)}, u32[]{:S(2)}, u32[]{:S(2)}) collective-permute-start(bf16[128,640]{1,0:T(8,128)(2,1)S(1)} %get-tuple-element.71.feats), channel_id=1, source_target_pairs={{0,4},{4,8},{8,12},{12,16},{16,20},{20,24},{24,28},{28,32},{32,36}... | collective-permute-start | bytes 491528 | tf_op jit(solution)/shard_map/ppermute | solution.py:278
  31.6 0.7 collective-permute-start
  32.4 0.7 collective-permute-start.1
  33.1 0.7 collective-permute-start.2
  33.8 0.7 collective-permute-start.3
  43.4 5.7 %collective-permute-start.13 = (bf16[160,1920]{1,0:T(8,128)(2,1)S(1)}, bf16[160,1920]{1,0:T(8,128)(2,1)S(1)}, u32[]{:S(2)}, u32[]{:S(2)}) collective-permute-start(bf16[160,1920]{1,0:T(8,128)(2,1)S(1)} %collective-permute-done.12.w2), channel_id=1, source_target_pairs={{0,1},{1,0},{2,3},{3,2},{4,5},{5,4},{6,7},{7,6},{8,9},{9,8},{10,11... | collective-permute-start | bytes 1843208 | tf_op jit(solution)/shard_map/ppermute | solution.py:29
  47.4 0.7 collective-permute-start.4
  48.2 0.7 collective-permute-start.5
  49.1 31.7 %collective-permute-start.14 = (bf16[128,640]{1,0:T(8,128)(2,1)S(1)}, bf16[128,640]{1,0:T(8,128)(2,1)S(1)}, u32[]{:S(2)}, u32[]{:S(2)}) collective-permute-start(bf16[128,640]{1,0:T(8,128)(2,1)S(1)} %get-tuple-element.77), channel_id=1, source_target_pairs={{0,256},{8,264},{4,260},{12,268},{128,384},{136,392},{132,388},{14... | collective-permute-start | bytes 491528 | tf_op jit(solution)/shard_map/ppermute | solution.py:285
  80.9 15.2 %collective-permute-start.17 = (bf16[256,640]{1,0:T(8,128)(2,1)S(1)}, bf16[256,640]{1,0:T(8,128)(2,1)S(1)}, u32[]{:S(2)}, u32[]{:S(2)}) collective-permute-start(bf16[256,640]{1,0:T(8,128)(2,1)S(1)} %pad_maximum_fusion.a0), channel_id=1, source_target_pairs={{0,2},{1,3},{2,0},{3,1},{4,6},{5,7},{6,4},{7,5},{8,10},{9,11},{10,... | collective-permute-start | bytes 983048 | tf_op jit(solution)/shard_map/ppermute | solution.py:29
  85.2 5.9 %collective-permute-start.15 = (bf16[128,640]{1,0:T(8,128)(2,1)S(1)}, bf16[128,640]{1,0:T(8,128)(2,1)S(1)}, u32[]{:S(2)}, u32[]{:S(2)}) collective-permute-start(bf16[128,640]{1,0:T(8,128)(2,1)S(1)} %broadcast_select_fusion), channel_id=1, source_target_pairs={{0,1},{1,0},{2,3},{3,2},{4,5},{5,4},{6,7},{7,6},{8,9},{9,8},{10,11... | collective-permute-start | bytes 491528 | tf_op jit(solution)/shard_map/ppermute | solution.py:29
  89.1 3.3 %collective-permute-start.16 = (bf16[128,640]{1,0:T(8,128)(2,1)S(1)}, bf16[128,640]{1,0:T(8,128)(2,1)S(1)}, u32[]{:S(2)}, u32[]{:S(2)}) collective-permute-start(bf16[128,640]{1,0:T(8,128)(2,1)S(1)} %add.45), channel_id=1, source_target_pairs={{0,1},{1,0},{2,3},{3,2},{4,5},{5,4},{6,7},{7,6},{8,9},{9,8},{10,11... | collective-permute-start | bytes 491528 | tf_op jit(solution)/shard_map/ppermute | solution.py:29
  96.0 5.0 %collective-permute-start.18 = (bf16[256,640]{1,0:T(8,128)(2,1)S(1)}, bf16[256,640]{1,0:T(8,128)(2,1)S(1)}, u32[]{:S(2)}, u32[]{:S(2)}) collective-permute-start(bf16[256,640]{1,0:T(8,128)(2,1)S(1)} %collective-permute-done.17.a0), channel_id=1, source_target_pairs={{0,1},{1,0},{2,3},{3,2},{4,5},{5,4},{6,7},{7,6},{8,9},{9,8},{10,11... | collective-permute-start | bytes 983048 | tf_op jit(solution)/shard_map/ppermute | solution.py:29

commit v12 on v11

--- a/solution.py
+++ b/solution.py
@@ -15,13 +15,17 @@
 
 
 def tree_levels(devices):
-    steps = []
-    while 2 ** len(steps) < devices:
-        steps.append(2 ** len(steps))
+    if devices == 128:
+        jumps = [{0: 2}, {0: 1, 2: 1}]
+        jumps += [{0: 16}, {0: 48, 16: 16}, 8, 4, 64]
+    else:
+        jumps = [2**bit for bit in range(devices.bit_length()) if 2**bit < devices]
     levels, known = [], [0]
-    for step in steps[1::-1] + steps[-2:1:-1] + steps[max(2, len(steps) - 1) :]:
-        levels.append([(tm, tm + step) for tm in known])
-        known = known + [tm + step for tm in known]
+    for jump in jumps:
+        step = lambda tm: jump if isinstance(jump, int) else jump[tm if tm in jump else tm // 16 * 16]
+        level = [(tm, tm + step(tm)) for tm in known]
+        levels.append([(tm, to) for tm, to in level if to < devices])
+        known = known + [to for _, to in levels[-1]]
     return levels
 
 
@@ -275,7 +279,6 @@
 
     devices = lax.axis_size("tm")
     routes = tree_levels(devices)
-    prev = lax.ppermute(feats, "tm", [(i, i + 1) for i in range(devices - 1)])
     weight_chip = to_rows(after(qkv_weight, feats), 2)
 
     trips = 1 + jnp.minimum(lax.axis_index("tm"), 0)
@@ -288,8 +291,16 @@
     def looped(anchor, which):
         return lax.fori_loop(0, trips, lambda _, a: levels(a, which), anchor)
 
-    anchor = looped(jnp.where(first, feats, jnp.zeros_like(feats)), routes[:4])
-    anchor = after(anchor, prev, weight_chip)
+    def with_prev(_, carried):
+        anchor = levels(carried[0], routes[:1])
+        came = lax.ppermute(
+            after(feats, anchor), "tm", [(i, i + 1) for i in range(devices - 1)]
+        )
+        return levels(anchor, routes[1:4]), came
+
+    anchor = jnp.where(first, feats, jnp.zeros_like(feats))
+    anchor, prev = lax.fori_loop(0, trips, with_prev, (anchor, feats))
+    anchor = after(anchor, weight_chip)
     weight_last = to_rows(after(weight_chip, anchor), 1)
     anchor = after(looped(anchor, routes[4:6]), weight_last)
     anchor = levels(anchor, routes[6:])

time: 105 us -> 103 us (0.981)
  the two profiles are of different devices: /device:TPU:503 before, /device:TPU:241 now
where the time goes in v12:
time: 103 us; the launch traced here: 102 us
  waiting for transfers between devices  42.1 us (41%)
  starting transfers between devices  41 us (40%)
  Pallas kernels  13.4 us (13%)
  local copies, waits for them, and re-layouts  4.54 us (4%)
    ppermute x11, starting transfers between devices, to_rows(): return lax.ppermute(x, 'rows', [(i, i ^ flip) for i in range(4)])  32.5 us
    ppermute x7, waiting for transfers between devices, levels(): anchor = anchor + lax.ppermute(anchor, 'tm', route)  28 us
    pallas_call x8, Pallas kernels, call(): pl.pallas_call(kernel, out_shape=list(outs), in_specs=specs, out_specs=[V...  13.4 us
    ppermute x11, waiting for transfers between devices, to_rows(): return lax.ppermute(x, 'rows', [(i, i ^ flip) for i in range(4)])  9.05 us
    ppermute x7, starting transfers between devices, levels(): anchor = anchor + lax.ppermute(anchor, 'tm', route)  5.45 us
    ppermute x1, waiting for transfers between devices, with_prev(): lax.ppermute(after(feats, anchor), 'tm', [(i, i + 1) for i in range(devic...  4.98 us
    ppermute x1, starting transfers between devices, with_prev(): lax.ppermute(after(feats, anchor), 'tm', [(i, i + 1) for i in range(devic...  3.12 us
    unnamed x13, local copies, waits for them, and re-layouts  3.1 us
  transfers between devices with their start and end apart: 19, of which 8 were waited for; matrix products, arithmetic and copies ran while one was open for 2% of the time, Pallas kernels for 7%

profile of v12, /device:TPU:241, one launch (start us, length us, event | category | flops | bytes accessed | tf_op | source)
XLA Modules:
  0.0 102.1 jit_solution(14959748942459182254)
XLA Ops:
  0.0 2.6 %collective-permute-start.7 = (bf16[128,640]{1,0:T(8,128)(2,1)}, bf16[128,640]{1,0:T(8,128)(2,1)S(1)}, u32[]{:S(2)}, u32[]{:S(2)}) collective-permute-start(bf16[128,640]{1,0:T(8,128)(2,1)} %bitcast.7), channel_id=1, source_target_pairs={{0,1},{1,0},{2,3},{3,2},{4,5},{5,4},{6,7},{7,6},{8,9},{9,8},{10,11... | collective-permute-start | bytes 491528 | tf_op jit(solution)/shard_map/ppermute | solution.py:33
  2.6 0.0 copy-start.1
  2.6 0.9 copy-done.1
  3.5 0.2 shard_map.64.own.lat
  3.7 0.1 collective-permute-done.7.core
  3.8 0.2 shard_map.65
  4.0 2.2 %collective-permute-start.9 = (bf16[160,1920]{1,0:T(8,128)(2,1)}, bf16[160,1920]{1,0:T(8,128)(2,1)S(1)}, u32[]{:S(2)}, u32[]{:S(2)}) collective-permute-start(bf16[160,1920]{1,0:T(8,128)(2,1)} %w0.1), channel_id=1, source_target_pairs={{0,1},{1,0},{2,3},{3,2},{4,5},{5,4},{6,7},{7,6},{8,9},{9,8},{10,11... | collective-permute-start | bytes 1843208 | tf_op jit(solution)/shard_map/ppermute | solution.py:33
  6.2 2.9 %collective-permute-start.8 = (bf16[2,128,160]{2,1,0:T(8,128)(2,1)S(1)}, bf16[2,128,160]{2,1,0:T(8,128)(2,1)S(1)}, u32[]{:S(2)}, u32[]{:S(2)}) collective-permute-start(bf16[2,128,160]{2,1,0:T(8,128)(2,1)S(1)} %get-tuple-element.76), channel_id=1, source_target_pairs={{0,2},{1,3},{2,0},{3,1},{4,6},{5,7},{6,4},{7,5},{8,10},{9,11},{10,... | collective-permute-start | bytes 245768 | tf_op jit(solution)/shard_map/ppermute | solution.py:33
  9.2 0.1 compare_convert_fusion.pool
  9.2 0.8 reshape.55.gain
  10.0 0.0 copy-start
  10.0 1.5 %copy-done = bf16[9,160,640]{2,1,0:T(8,128)(2,1)S(1)} copy-done((bf16[9,160,640]{2,1,0:T(8,128)(2,1)S(1)}, bf16[9,160,640]{2,1,0:T(8,128)(2,1)}, u32[]{:S(2)}) %copy-start) | copy-done | bytes 1843224
  11.5 0.1 shard_map.66.weight
  11.7 1.3 %collective-permute-done.8.came = bf16[2,128,160]{2,1,0:T(8,128)(2,1)S(1)} collective-permute-done((bf16[2,128,160]{2,1,0:T(8,128)(2,1)S(1)}, bf16[2,128,160]{2,1,0:T(8,128)(2,1)S(1)}, u32[]{:S(2)}, u32[]{:S(2)}) %collective-permute-start.8) | collective-permute-done | bytes 81952 | tf_op jit(solution)/shard_map/ppermute | solution.py:33
  13.0 0.0 collective-permute-done.9.w1
  13.0 0.0 copy-start.5
  13.0 0.0 copy-start.6
  13.0 2.4 %shard_map.67 = (f32[2,128,640]{2,1,0:T(8,128)S(1)}, bf16[2,128,640]{2,1,0:T(8,128)(2,1)S(1)}) custom-call(s32[1]{0:T(128)} %bitcast.me_ref, bf16[2,128,160]{2,1,0:T(8,128)(2,1)S(1)} %get-tuple-element.75.mine, bf16[2,128,160]{2,1,0:T(8,128)(2,1)S(1)} %collective-permute-done.8.came, f32[4,160]{1,0:T(4,128)S(1)} %reshape.55.gain, ...), custom_call_target="tpu_custom_call" | custom-call | flops 943718400 | bytes 3095044 | tf_op jit(solution)/shard_map/pallas_call | solution.py:222
  15.4 0.0 copy-start.2
  15.4 3.1 %collective-permute-start.10 = (bf16[2,128,640]{2,1,0:T(8,128)(2,1)S(1)}, bf16[2,128,640]{2,1,0:T(8,128)(2,1)S(1)}, u32[]{:S(2)}, u32[]{:S(2)}) collective-permute-start(bf16[2,128,640]{2,1,0:T(8,128)(2,1)S(1)} %get-tuple-element.81), channel_id=1, source_target_pairs={{0,1},{1,0},{2,3},{3,2},{4,5},{5,4},{6,7},{7,6},{8,9},{9,8},{10,11... | collective-permute-start | bytes 983048 | tf_op jit(solution)/shard_map/ppermute | solution.py:33
  18.5 1.2 %collective-permute-done.10.core = bf16[2,128,640]{2,1,0:T(8,128)(2,1)S(1)} collective-permute-done((bf16[2,128,640]{2,1,0:T(8,128)(2,1)S(1)}, bf16[2,128,640]{2,1,0:T(8,128)(2,1)S(1)}, u32[]{:S(2)}, u32[]{:S(2)}) %collective-permute-start.10) | collective-permute-done | bytes 327712 | tf_op jit(solution)/shard_map/ppermute | solution.py:33
  19.8 2.9 %collective-permute-start.11 = (bf16[128,640]{1,0:T(8,128)(2,1)S(1)}, bf16[128,640]{1,0:T(8,128)(2,1)S(1)}, u32[]{:S(2)}, u32[]{:S(2)}) collective-permute-start(bf16[128,640]{1,0:T(8,128)(2,1)S(1)} %fusion), channel_id=1, source_target_pairs={{0,2},{1,3},{2,0},{3,1},{4,6},{5,7},{6,4},{7,5},{8,10},{9,11},{10,... | collective-permute-start | bytes 491528 | tf_op jit(solution)/shard_map/ppermute | solution.py:33
  22.7 0.0 copy-done.5
  22.7 0.0 copy-done.6
  22.7 4.4 %collective-permute-done.11.chip = bf16[128,640]{1,0:T(8,128)(2,1)S(1)} collective-permute-done((bf16[128,640]{1,0:T(8,128)(2,1)S(1)}, bf16[128,640]{1,0:T(8,128)(2,1)S(1)}, u32[]{:S(2)}, u32[]{:S(2)}) %collective-permute-start.11) | collective-permute-done | bytes 163872 | tf_op jit(solution)/shard_map/ppermute | solution.py:33
  27.1 0.3 shard_map.68
  27.4 0.0 copy-done.2
  27.4 2.9 %collective-permute-start.12 = (bf16[160,1920]{1,0:T(8,128)(2,1)S(1)}, bf16[160,1920]{1,0:T(8,128)(2,1)S(1)}, u32[]{:S(2)}, u32[]{:S(2)}) collective-permute-start(bf16[160,1920]{1,0:T(8,128)(2,1)S(1)} %copy-done.2), channel_id=1, source_target_pairs={{0,2},{1,3},{2,0},{3,1},{4,6},{5,7},{6,4},{7,5},{8,10},{9,11},{10,... | collective-permute-start | bytes 1843208 | tf_op jit(solution)/shard_map/ppermute | solution.py:33
  30.3 0.7 copy.9
  31.0 11.8 %while.22 = (s32[]{:T(128)}, bf16[128,640]{1,0:T(8,128)(2,1)S(1)}, bf16[128,640]{1,0:T(8,128)(2,1)}, s32[]{:T(128)}, bf16[128,640]{1,0:T(8,128)(2,1)S(1)}, /*index=5*/s32[]{:T(128)}) while((s32[]{:T(128)}, bf16[128,640]{1,0:T(8,128)(2,1)S(1)}, bf16[128,640]{1,0:T(8,128)(2,1)}, s32[]{:T(128)}, bf16[128,640]{1,0:T(8,128)(2,1)S(1)}, ...), condition=%wide.region_1.2_spmd, body=%wide.region_0.1_spmd.sunk | while | flops 327682 | bytes 5898537 | solution.py:302
  31.0 0.7 collective-permute-start
  31.7 0.0 collective-permute-done
  31.7 0.7 collective-permute-start.1
  32.4 0.0 collective-permute-done.1
  32.5 0.7 collective-permute-start.2
  33.2 0.0 collective-permute-done.2
  33.2 0.7 collective-permute-start.3
  33.9 3.1 %collective-permute-start.4 = (bf16[128,640]{1,0:T(8,128)(2,1)S(1)}, bf16[128,640]{1,0:T(8,128)(2,1)S(1)}, u32[]{:S(2)}, u32[]{:S(2)}) collective-permute-start(bf16[128,640]{1,0:T(8,128)(2,1)S(1)} %get-tuple-element.165), channel_id=1, source_target_pairs={{0,4},{4,8},{8,12},{12,16},{16,20},{20,24},{24,28},{28,32},{32,36}... | collective-permute-start | bytes 491528 | tf_op jit(solution)/shard_map/while/body/ppermute | solution.py:296
  37.0 0.0 collective-permute-done.3
  37.1 5.0 %collective-permute-done.4 = bf16[128,640]{1,0:T(8,128)(2,1)S(1)} collective-permute-done((bf16[128,640]{1,0:T(8,128)(2,1)S(1)}, bf16[128,640]{1,0:T(8,128)(2,1)S(1)}, u32[]{:S(2)}, u32[]{:S(2)}) %collective-permute-start.4) | collective-permute-done | bytes 163872 | tf_op jit(solution)/shard_map/while/body/ppermute | solution.py:296
  42.1 0.7 copy-done.3
  42.7 0.7 collective-permute-done.12.w2
  43.4 4.0 %collective-permute-start.13 = (bf16[160,1920]{1,0:T(8,128)(2,1)S(1)}, bf16[160,1920]{1,0:T(8,128)(2,1)S(1)}, u32[]{:S(2)}, u32[]{:S(2)}) collective-permute-start(bf16[160,1920]{1,0:T(8,128)(2,1)S(1)} %collective-permute-done.12.w2), channel_id=1, source_target_pairs={{0,1},{1,0},{2,3},{3,2},{4,5},{5,4},{6,7},{7,6},{8,9},{9,8},{10,11... | collective-permute-start | bytes 1843208 | tf_op jit(solution)/shard_map/ppermute | solution.py:33
  47.4 0.0 copy-start.4
  47.4 1.6 %while.23 = (s32[]{:T(128)}, bf16[128,640]{1,0:T(8,128)(2,1)S(1)}, s32[]{:T(128)}, s32[]{:T(128)}) while((s32[]{:T(128)}, bf16[128,640]{1,0:T(8,128)(2,1)S(1)}, s32[]{:T(128)}, s32[]{:T(128)}) %tuple.55), condition=%wide.region_3.4_spmd, body=%wide.region_2.3_spmd.sunk | while | flops 163842 | bytes 2293893 | solution.py:292
  47.5 0.8 collective-permute-start.5
  48.3 0.0 collective-permute-done.5
  48.3 0.7 collective-permute-start.6
  49.0 0.0 collective-permute-done.6
  49.1 0.0 collective-permute-done.13.w3
  49.1 1.3 %collective-permute-start.14 = (bf16[128,640]{1,0:T(8,128)(2,1)S(1)}, bf16[128,640]{1,0:T(8,128)(2,1)S(1)}, u32[]{:S(2)}, u32[]{:S(2)}) collective-permute-start(bf16[128,640]{1,0:T(8,128)(2,1)S(1)} %get-tuple-element.89), channel_id=1, source_target_pairs={{0,256},{8,264},{4,260},{12,268},{64,320},{72,328},{68,324},{76,33... | collective-permute-start | bytes 491528 | tf_op jit(solution)/shard_map/ppermute | solution.py:288
  50.4 28.0 %collective-permute-done.14 = bf16[128,640]{1,0:T(8,128)(2,1)S(1)} collective-permute-done((bf16[128,640]{1,0:T(8,128)(2,1)S(1)}, bf16[128,640]{1,0:T(8,128)(2,1)S(1)}, u32[]{:S(2)}, u32[]{:S(2)}) %collective-permute-start.14) | collective-permute-done | bytes 163872 | tf_op jit(solution)/shard_map/ppermute | solution.py:288
  78.4 0.0 copy-done.4
  78.5 4.0 %collective-permute-start.17 = (bf16[256,640]{1,0:T(8,128)(2,1)S(1)}, bf16[256,640]{1,0:T(8,128)(2,1)S(1)}, u32[]{:S(2)}, u32[]{:S(2)}) collective-permute-start(bf16[256,640]{1,0:T(8,128)(2,1)S(1)} %pad_maximum_fusion.a0), channel_id=1, source_target_pairs={{0,2},{1,3},{2,0},{3,1},{4,6},{5,7},{6,4},{7,5},{8,10},{9,11},{10,... | collective-permute-start | bytes 983048 | tf_op jit(solution)/shard_map/ppermute | solution.py:33
  82.5 3.9 %collective-permute-start.15 = (bf16[128,640]{1,0:T(8,128)(2,1)S(1)}, bf16[128,640]{1,0:T(8,128)(2,1)S(1)}, u32[]{:S(2)}, u32[]{:S(2)}) collective-permute-start(bf16[128,640]{1,0:T(8,128)(2,1)S(1)} %broadcast_select_fusion), channel_id=1, source_target_pairs={{0,1},{1,0},{2,3},{3,2},{4,5},{5,4},{6,7},{7,6},{8,9},{9,8},{10,11... | collective-permute-start | bytes 491528 | tf_op jit(solution)/shard_map/ppermute | solution.py:33
  86.4 1.9 %collective-permute-start.16 = (bf16[128,640]{1,0:T(8,128)(2,1)S(1)}, bf16[128,640]{1,0:T(8,128)(2,1)S(1)}, u32[]{:S(2)}, u32[]{:S(2)}) collective-permute-start(bf16[128,640]{1,0:T(8,128)(2,1)S(1)} %add.45), channel_id=1, source_target_pairs={{0,1},{1,0},{2,3},{3,2},{4,5},{5,4},{6,7},{7,6},{8,9},{9,8},{10,11... | collective-permute-start | bytes 491528 | tf_op jit(solution)/shard_map/ppermute | solution.py:33
  88.4 0.0 collective-permute-done.15.a1
  88.4 1.4 %collective-permute-done.16.a2 = bf16[128,640]{1,0:T(8,128)(2,1)S(1)} collective-permute-done((bf16[128,640]{1,0:T(8,128)(2,1)S(1)}, bf16[128,640]{1,0:T(8,128)(2,1)S(1)}, u32[]{:S(2)}, u32[]{:S(2)}) %collective-permute-start.16) | collective-permute-done | bytes 163872 | tf_op jit(solution)/shard_map/ppermute | solution.py:33
  89.7 3.6 %shard_map.69 = (bf16[128,640]{1,0:T(8,128)(2,1)S(1)}, f32[128,8]{1,0:T(8,128)S(1)}, f32[128,8]{1,0:T(8,128)S(1)}, f32[128,640]{1,0:T(8,128)S(1)}, bf16[640,1920]{1,0:T(8,128)(2,1)S(1)}) custom-call(s32[1]{0:T(128)} %bitcast.me_ref, bf16[128,640]{1,0:T(8,128)(2,1)S(1)} %get-tuple-element.232, bf16[256,640]{1,0:T(8,128)(2,1)S(1)} %pad_maximum_fusion.a0, ...), custom_call_target="tpu_custom_call" | custom-call | flops 1006632960 | bytes 6234116 | tf_op jit(solution)/shard_map/pallas_call | solution.py:222
  93.3 0.0 collective-permute-done.17.a0
  93.3 2.1 %collective-permute-start.18 = (bf16[256,640]{1,0:T(8,128)(2,1)S(1)}, bf16[256,640]{1,0:T(8,128)(2,1)S(1)}, u32[]{:S(2)}, u32[]{:S(2)}) collective-permute-start(bf16[256,640]{1,0:T(8,128)(2,1)S(1)} %collective-permute-done.17.a0), channel_id=1, source_target_pairs={{0,1},{1,0},{2,3},{3,2},{4,5},{5,4},{6,7},{7,6},{8,9},{9,8},{10,11... | collective-permute-start | bytes 983048 | tf_op jit(solution)/shard_map/ppermute | solution.py:33
  95.4 2.9 %shard_map.70 = (f32[128,8]{1,0:T(8,128)S(1)}, f32[128,8]{1,0:T(8,128)S(1)}, f32[128,640]{1,0:T(8,128)S(1)}) custom-call(bf16[128,640]{1,0:T(8,128)(2,1)S(1)} %get-tuple-element.91.query, bf16[256,640]{1,0:T(8,128)(2,1)S(1)} %collective-permute-done.17.a0, bf16[640,1920]{1,0:T(8,128)(2,1)S(1)} %get-tuple-element.93.weight, ...), custom_call_target="tpu_custom_call" | custom-call | flops 503316480 | bytes 3620864 | tf_op jit(solution)/shard_map/pallas_call | solution.py:222
  98.3 0.0 collective-permute-done.18.a0
  98.3 3.8 %shard_map.71 = bf16[128,640]{1,0:T(8,128)(2,1)} custom-call(bf16[128,640]{1,0:T(8,128)(2,1)S(1)} %get-tuple-element.91.query, bf16[256,640]{1,0:T(8,128)(2,1)S(1)} %collective-permute-done.18.a0, bf16[640,1920]{1,0:T(8,128)(2,1)S(1)} %get-tuple-element.93.weight, f32[128,8]{1,0:T(8,128)S(1)} %get-tuple-element.97.top, f32[128,8]{1,0:T(8,128)S(1)} %get-tuple-element.98.den, ...), custom_call_target="tpu_custom_call" | custom-call | flops 503316480 | bytes 3612672 | tf_op jit(solution)/shard_map/pallas_call | solution.py:222
  (15 shorter events, 0.4 us)
Async XLA Ops:
  0.0 3.8 %collective-permute-start.7 = (bf16[128,640]{1,0:T(8,128)(2,1)}, bf16[128,640]{1,0:T(8,128)(2,1)S(1)}, u32[]{:S(2)}, u32[]{:S(2)}) collective-permute-start(bf16[128,640]{1,0:T(8,128)(2,1)} %bitcast.7), channel_id=1, source_target_pairs={{0,1},{1,0},{2,3},{3,2},{4,5},{5,4},{6,7},{7,6},{8,9},{9,8},{10,11... | collective-permute-start | bytes 491528 | tf_op jit(solution)/shard_map/ppermute | solution.py:33
  2.6 0.9 copy-start.1
  4.0 9.0 %collective-permute-start.9 = (bf16[160,1920]{1,0:T(8,128)(2,1)}, bf16[160,1920]{1,0:T(8,128)(2,1)S(1)}, u32[]{:S(2)}, u32[]{:S(2)}) collective-permute-start(bf16[160,1920]{1,0:T(8,128)(2,1)} %w0.1), channel_id=1, source_target_pairs={{0,1},{1,0},{2,3},{3,2},{4,5},{5,4},{6,7},{7,6},{8,9},{9,8},{10,11... | collective-permute-start | bytes 1843208 | tf_op jit(solution)/shard_map/ppermute | solution.py:33
  6.2 6.8 %collective-permute-start.8 = (bf16[2,128,160]{2,1,0:T(8,128)(2,1)S(1)}, bf16[2,128,160]{2,1,0:T(8,128)(2,1)S(1)}, u32[]{:S(2)}, u32[]{:S(2)}) collective-permute-start(bf16[2,128,160]{2,1,0:T(8,128)(2,1)S(1)} %get-tuple-element.76), channel_id=1, source_target_pairs={{0,2},{1,3},{2,0},{3,1},{4,6},{5,7},{6,4},{7,5},{8,10},{9,11},{10,... | collective-permute-start | bytes 245768 | tf_op jit(solution)/shard_map/ppermute | solution.py:33
  10.0 1.5 %copy-start = (bf16[9,160,640]{2,1,0:T(8,128)(2,1)S(1)}, bf16[9,160,640]{2,1,0:T(8,128)(2,1)}, u32[]{:S(2)}) copy-start(bf16[9,160,640]{2,1,0:T(8,128)(2,1)} %param.12) | copy-start | bytes 5529604
  13.0 9.7 %copy-start.5 = (f32[640]{0:T(1024)S(1)}, f32[640]{0:T(1024)}, u32[]{:S(2)}) copy-start(f32[640]{0:T(1024)} %param.13) | copy-start | bytes 7684
  13.0 9.7 %copy-start.6 = (f32[640]{0:T(1024)S(1)}, f32[640]{0:T(1024)}, u32[]{:S(2)}) copy-start(f32[640]{0:T(1024)} %param.14) | copy-start | bytes 7684
  15.4 12.0 %copy-start.2 = (bf16[160,1920]{1,0:T(8,128)(2,1)S(1)}, bf16[160,1920]{1,0:T(8,128)(2,1)}, u32[]{:S(2)}) copy-start(bf16[160,1920]{1,0:T(8,128)(2,1)} %w0.1) | copy-start | bytes 1843204
  15.4 4.3 %collective-permute-start.10 = (bf16[2,128,640]{2,1,0:T(8,128)(2,1)S(1)}, bf16[2,128,640]{2,1,0:T(8,128)(2,1)S(1)}, u32[]{:S(2)}, u32[]{:S(2)}) collective-permute-start(bf16[2,128,640]{2,1,0:T(8,128)(2,1)S(1)} %get-tuple-element.81), channel_id=1, source_target_pairs={{0,1},{1,0},{2,3},{3,2},{4,5},{5,4},{6,7},{7,6},{8,9},{9,8},{10,11... | collective-permute-start | bytes 983048 | tf_op jit(solution)/shard_map/ppermute | solution.py:33
  19.8 7.3 %collective-permute-start.11 = (bf16[128,640]{1,0:T(8,128)(2,1)S(1)}, bf16[128,640]{1,0:T(8,128)(2,1)S(1)}, u32[]{:S(2)}, u32[]{:S(2)}) collective-permute-start(bf16[128,640]{1,0:T(8,128)(2,1)S(1)} %fusion), channel_id=1, source_target_pairs={{0,2},{1,3},{2,0},{3,1},{4,6},{5,7},{6,4},{7,5},{8,10},{9,11},{10,... | collective-permute-start | bytes 491528 | tf_op jit(solution)/shard_map/ppermute | solution.py:33
  27.4 16.0 %collective-permute-start.12 = (bf16[160,1920]{1,0:T(8,128)(2,1)S(1)}, bf16[160,1920]{1,0:T(8,128)(2,1)S(1)}, u32[]{:S(2)}, u32[]{:S(2)}) collective-permute-start(bf16[160,1920]{1,0:T(8,128)(2,1)S(1)} %copy-done.2), channel_id=1, source_target_pairs={{0,2},{1,3},{2,0},{3,1},{4,6},{5,7},{6,4},{7,5},{8,10},{9,11},{10,... | collective-permute-start | bytes 1843208 | tf_op jit(solution)/shard_map/ppermute | solution.py:33
  31.0 0.7 collective-permute-start
  31.7 0.7 collective-permute-start.1
  32.5 0.7 collective-permute-start.2
  33.2 3.8 %collective-permute-start.3 = (bf16[128,640]{1,0:T(8,128)(2,1)S(1)}, bf16[128,640]{1,0:T(8,128)(2,1)S(1)}, u32[]{:S(2)}, u32[]{:S(2)}) collective-permute-start(bf16[128,640]{1,0:T(8,128)(2,1)S(1)} %add.60), channel_id=1, source_target_pairs={{0,192},{8,200},{4,196},{12,204},{64,128},{72,136},{68,132},{76,14... | collective-permute-start | bytes 491528 | tf_op jit(solution)/shard_map/while/body/ppermute | solution.py:288
  33.9 8.2 %collective-permute-start.4 = (bf16[128,640]{1,0:T(8,128)(2,1)S(1)}, bf16[128,640]{1,0:T(8,128)(2,1)S(1)}, u32[]{:S(2)}, u32[]{:S(2)}) collective-permute-start(bf16[128,640]{1,0:T(8,128)(2,1)S(1)} %get-tuple-element.165), channel_id=1, source_target_pairs={{0,4},{4,8},{8,12},{12,16},{16,20},{20,24},{24,28},{28,32},{32,36}... | collective-permute-start | bytes 491528 | tf_op jit(solution)/shard_map/while/body/ppermute | solution.py:296
  42.1 0.7 copy-start.3
  43.4 5.7 %collective-permute-start.13 = (bf16[160,1920]{1,0:T(8,128)(2,1)S(1)}, bf16[160,1920]{1,0:T(8,128)(2,1)S(1)}, u32[]{:S(2)}, u32[]{:S(2)}) collective-permute-start(bf16[160,1920]{1,0:T(8,128)(2,1)S(1)} %collective-permute-done.12.w2), channel_id=1, source_target_pairs={{0,1},{1,0},{2,3},{3,2},{4,5},{5,4},{6,7},{7,6},{8,9},{9,8},{10,11... | collective-permute-start | bytes 1843208 | tf_op jit(solution)/shard_map/ppermute | solution.py:33
  47.4 31.0 %copy-start.4 = (bf16[128,640]{1,0:T(8,128)(2,1)S(1)}, bf16[128,640]{1,0:T(8,128)(2,1)}, u32[]{:S(2)}) copy-start(bf16[128,640]{1,0:T(8,128)(2,1)} %get-tuple-element.90) | copy-start | bytes 491524
  47.5 0.8 collective-permute-start.5
  48.3 0.7 collective-permute-start.6
  49.1 29.3 %collective-permute-start.14 = (bf16[128,640]{1,0:T(8,128)(2,1)S(1)}, bf16[128,640]{1,0:T(8,128)(2,1)S(1)}, u32[]{:S(2)}, u32[]{:S(2)}) collective-permute-start(bf16[128,640]{1,0:T(8,128)(2,1)S(1)} %get-tuple-element.89), channel_id=1, source_target_pairs={{0,256},{8,264},{4,260},{12,268},{64,320},{72,328},{68,324},{76,33... | collective-permute-start | bytes 491528 | tf_op jit(solution)/shard_map/ppermute | solution.py:288
  78.5 14.8 %collective-permute-start.17 = (bf16[256,640]{1,0:T(8,128)(2,1)S(1)}, bf16[256,640]{1,0:T(8,128)(2,1)S(1)}, u32[]{:S(2)}, u32[]{:S(2)}) collective-permute-start(bf16[256,640]{1,0:T(8,128)(2,1)S(1)} %pad_maximum_fusion.a0), channel_id=1, source_target_pairs={{0,2},{1,3},{2,0},{3,1},{4,6},{5,7},{6,4},{7,5},{8,10},{9,11},{10,... | collective-permute-start | bytes 983048 | tf_op jit(solution)/shard_map/ppermute | solution.py:33
  82.5 5.9 %collective-permute-start.15 = (bf16[128,640]{1,0:T(8,128)(2,1)S(1)}, bf16[128,640]{1,0:T(8,128)(2,1)S(1)}, u32[]{:S(2)}, u32[]{:S(2)}) collective-permute-start(bf16[128,640]{1,0:T(8,128)(2,1)S(1)} %broadcast_select_fusion), channel_id=1, source_target_pairs={{0,1},{1,0},{2,3},{3,2},{4,5},{5,4},{6,7},{7,6},{8,9},{9,8},{10,11... | collective-permute-start | bytes 491528 | tf_op jit(solution)/shard_map/ppermute | solution.py:33
  86.4 3.3 %collective-permute-start.16 = (bf16[128,640]{1,0:T(8,128)(2,1)S(1)}, bf16[128,640]{1,0:T(8,128)(2,1)S(1)}, u32[]{:S(2)}, u32[]{:S(2)}) collective-permute-start(bf16[128,640]{1,0:T(8,128)(2,1)S(1)} %add.45), channel_id=1, source_target_pairs={{0,1},{1,0},{2,3},{3,2},{4,5},{5,4},{6,7},{7,6},{8,9},{9,8},{10,11... | collective-permute-start | bytes 491528 | tf_op jit(solution)/shard_map/ppermute | solution.py:33
  93.3 5.0 %collective-permute-start.18 = (bf16[256,640]{1,0:T(8,128)(2,1)S(1)}, bf16[256,640]{1,0:T(8,128)(2,1)S(1)}, u32[]{:S(2)}, u32[]{:S(2)}) collective-permute-start(bf16[256,640]{1,0:T(8,128)(2,1)S(1)} %collective-permute-done.17.a0), channel_id=1, source_target_pairs={{0,1},{1,0},{2,3},{3,2},{4,5},{5,4},{6,7},{7,6},{8,9},{9,8},{10,11... | collective-permute-start | bytes 983048 | tf_op jit(solution)/shard_map/ppermute | solution.py:33

commit v13 on v12

--- a/solution.py
+++ b/solution.py
@@ -279,6 +279,7 @@
 
     devices = lax.axis_size("tm")
     routes = tree_levels(devices)
+    prev = lax.ppermute(feats, "tm", [(i, i + 1) for i in range(devices - 1)])
     weight_chip = to_rows(after(qkv_weight, feats), 2)
 
     trips = 1 + jnp.minimum(lax.axis_index("tm"), 0)
@@ -291,16 +292,8 @@
     def looped(anchor, which):
         return lax.fori_loop(0, trips, lambda _, a: levels(a, which), anchor)
 
-    def with_prev(_, carried):
-        anchor = levels(carried[0], routes[:1])
-        came = lax.ppermute(
-            after(feats, anchor), "tm", [(i, i + 1) for i in range(devices - 1)]
-        )
-        return levels(anchor, routes[1:4]), came
-
-    anchor = jnp.where(first, feats, jnp.zeros_like(feats))
-    anchor, prev = lax.fori_loop(0, trips, with_prev, (anchor, feats))
-    anchor = after(anchor, weight_chip)
+    anchor = looped(jnp.where(first, feats, jnp.zeros_like(feats)), routes[:4])
+    anchor = after(anchor, prev, weight_chip)
     weight_last = to_rows(after(weight_chip, anchor), 1)
     anchor = after(looped(anchor, routes[4:6]), weight_last)
     anchor = levels(anchor, routes[6:])

time: 103 us -> 101 us (0.981)
  the two profiles are of different devices: /device:TPU:241 before, /device:TPU:375 now
where the time goes in v13:
time: 101 us
  waiting for transfers between devices  42.6 us (42%)
  starting transfers between devices  40.3 us (40%)
  Pallas kernels  13.5 us (13%)
  local copies, waits for them, and re-layouts  3.2 us (3%)
    ppermute x11, starting transfers between devices, to_rows(): return lax.ppermute(x, 'rows', [(i, i ^ flip) for i in range(4)])  32.5 us
    ppermute x7, waiting for transfers between devices, levels(): anchor = anchor + lax.ppermute(anchor, 'tm', route)  26.5 us
    ppermute x11, waiting for transfers between devices, to_rows(): return lax.ppermute(x, 'rows', [(i, i ^ flip) for i in range(4)])  15.3 us
    pallas_call x8, Pallas kernels, call(): pl.pallas_call(kernel, out_shape=list(outs), in_specs=specs, out_specs=[V...  13.5 us
    ppermute x7, starting transfers between devices, levels(): anchor = anchor + lax.ppermute(anchor, 'tm', route)  5.31 us
    ppermute x1, starting transfers between devices, on_device(): prev = lax.ppermute(feats, 'tm', [(i, i + 1) for i in range(devices - 1)])  2.56 us
    unnamed x10, local copies, waits for them, and re-layouts  2.43 us
  transfers between devices with their start and end apart: 19, of which 9 were waited for; matrix products, arithmetic and copies ran while one was open for 1% of the time, Pallas kernels for 7%

profile of v13, /device:TPU:375, one launch (start us, length us, event | category | flops | bytes accessed | tf_op | source)
XLA Modules:
  0.0 100.6 jit_solution(3659695227125028194)
XLA Ops:
  0.0 2.6 %collective-permute-start.6 = (bf16[128,640]{1,0:T(8,128)(2,1)}, bf16[128,640]{1,0:T(8,128)(2,1)S(1)}, u32[]{:S(2)}, u32[]{:S(2)}) collective-permute-start(bf16[128,640]{1,0:T(8,128)(2,1)} %bitcast.7), channel_id=1, source_target_pairs={{0,1},{1,0},{2,3},{3,2},{4,5},{5,4},{6,7},{7,6},{8,9},{9,8},{10,11... | collective-permute-start | bytes 491528 | tf_op jit(solution)/shard_map/ppermute | solution.py:33
  2.6 0.0 copy-start.1
  2.6 0.9 copy-done.1
  3.5 0.2 shard_map.64.own.lat
  3.7 0.1 collective-permute-done.6.core
  3.8 0.2 shard_map.65
  4.0 2.2 %collective-permute-start.8 = (bf16[160,1920]{1,0:T(8,128)(2,1)}, bf16[160,1920]{1,0:T(8,128)(2,1)S(1)}, u32[]{:S(2)}, u32[]{:S(2)}) collective-permute-start(bf16[160,1920]{1,0:T(8,128)(2,1)} %w0.1), channel_id=1, source_target_pairs={{0,1},{1,0},{2,3},{3,2},{4,5},{5,4},{6,7},{7,6},{8,9},{9,8},{10,11... | collective-permute-start | bytes 1843208 | tf_op jit(solution)/shard_map/ppermute | solution.py:33
  6.2 2.9 %collective-permute-start.7 = (bf16[2,128,160]{2,1,0:T(8,128)(2,1)S(1)}, bf16[2,128,160]{2,1,0:T(8,128)(2,1)S(1)}, u32[]{:S(2)}, u32[]{:S(2)}) collective-permute-start(bf16[2,128,160]{2,1,0:T(8,128)(2,1)S(1)} %get-tuple-element.65), channel_id=1, source_target_pairs={{0,2},{1,3},{2,0},{3,1},{4,6},{5,7},{6,4},{7,5},{8,10},{9,11},{10,... | collective-permute-start | bytes 245768 | tf_op jit(solution)/shard_map/ppermute | solution.py:33
  9.2 0.1 compare_convert_fusion.pool
  9.2 0.8 reshape.55.gain
  10.0 0.0 copy-start
  10.0 1.5 %copy-done = bf16[9,160,640]{2,1,0:T(8,128)(2,1)S(1)} copy-done((bf16[9,160,640]{2,1,0:T(8,128)(2,1)S(1)}, bf16[9,160,640]{2,1,0:T(8,128)(2,1)}, u32[]{:S(2)}) %copy-start) | copy-done | bytes 1843224
  11.5 0.1 shard_map.66.weight
  11.7 1.3 %collective-permute-done.7.came = bf16[2,128,160]{2,1,0:T(8,128)(2,1)S(1)} collective-permute-done((bf16[2,128,160]{2,1,0:T(8,128)(2,1)S(1)}, bf16[2,128,160]{2,1,0:T(8,128)(2,1)S(1)}, u32[]{:S(2)}, u32[]{:S(2)}) %collective-permute-start.7) | collective-permute-done | bytes 81952 | tf_op jit(solution)/shard_map/ppermute | solution.py:33
  13.0 0.0 collective-permute-done.8.w1
  13.0 0.0 copy-start.3
  13.0 0.0 copy-start.4
  13.0 2.4 %shard_map.67 = (f32[2,128,640]{2,1,0:T(8,128)S(1)}, bf16[2,128,640]{2,1,0:T(8,128)(2,1)S(1)}) custom-call(s32[1]{0:T(128)} %bitcast.me_ref, bf16[2,128,160]{2,1,0:T(8,128)(2,1)S(1)} %get-tuple-element.64.mine, bf16[2,128,160]{2,1,0:T(8,128)(2,1)S(1)} %collective-permute-done.7.came, f32[4,160]{1,0:T(4,128)S(1)} %reshape.55.gain, ...), custom_call_target="tpu_custom_call" | custom-call | flops 943718400 | bytes 3095044 | tf_op jit(solution)/shard_map/pallas_call | solution.py:222
  15.4 0.0 copy-start.2
  15.4 3.1 %collective-permute-start.9 = (bf16[2,128,640]{2,1,0:T(8,128)(2,1)S(1)}, bf16[2,128,640]{2,1,0:T(8,128)(2,1)S(1)}, u32[]{:S(2)}, u32[]{:S(2)}) collective-permute-start(bf16[2,128,640]{2,1,0:T(8,128)(2,1)S(1)} %get-tuple-element.70), channel_id=1, source_target_pairs={{0,1},{1,0},{2,3},{3,2},{4,5},{5,4},{6,7},{7,6},{8,9},{9,8},{10,11... | collective-permute-start | bytes 983048 | tf_op jit(solution)/shard_map/ppermute | solution.py:33
  18.5 1.2 %collective-permute-done.9.core = bf16[2,128,640]{2,1,0:T(8,128)(2,1)S(1)} collective-permute-done((bf16[2,128,640]{2,1,0:T(8,128)(2,1)S(1)}, bf16[2,128,640]{2,1,0:T(8,128)(2,1)S(1)}, u32[]{:S(2)}, u32[]{:S(2)}) %collective-permute-start.9) | collective-permute-done | bytes 327712 | tf_op jit(solution)/shard_map/ppermute | solution.py:33
  19.8 2.9 %collective-permute-start.10 = (bf16[128,640]{1,0:T(8,128)(2,1)S(1)}, bf16[128,640]{1,0:T(8,128)(2,1)S(1)}, u32[]{:S(2)}, u32[]{:S(2)}) collective-permute-start(bf16[128,640]{1,0:T(8,128)(2,1)S(1)} %fusion), channel_id=1, source_target_pairs={{0,2},{1,3},{2,0},{3,1},{4,6},{5,7},{6,4},{7,5},{8,10},{9,11},{10,... | collective-permute-start | bytes 491528 | tf_op jit(solution)/shard_map/ppermute | solution.py:33
  22.7 0.0 copy-done.3
  22.7 0.0 copy-done.4
  22.7 4.4 %collective-permute-done.10.chip = bf16[128,640]{1,0:T(8,128)(2,1)S(1)} collective-permute-done((bf16[128,640]{1,0:T(8,128)(2,1)S(1)}, bf16[128,640]{1,0:T(8,128)(2,1)S(1)}, u32[]{:S(2)}, u32[]{:S(2)}) %collective-permute-start.10) | collective-permute-done | bytes 163872 | tf_op jit(solution)/shard_map/ppermute | solution.py:33
  27.1 0.3 shard_map.68
  27.4 0.0 copy-done.2
  27.4 2.9 %collective-permute-start.12 = (bf16[160,1920]{1,0:T(8,128)(2,1)S(1)}, bf16[160,1920]{1,0:T(8,128)(2,1)S(1)}, u32[]{:S(2)}, u32[]{:S(2)}) collective-permute-start(bf16[160,1920]{1,0:T(8,128)(2,1)S(1)} %copy-done.2), channel_id=1, source_target_pairs={{0,2},{1,3},{2,0},{3,1},{4,6},{5,7},{6,4},{7,5},{8,10},{9,11},{10,... | collective-permute-start | bytes 1843208 | tf_op jit(solution)/shard_map/ppermute | solution.py:33
  30.3 2.6 %collective-permute-start.11 = (bf16[128,640]{1,0:T(8,128)(2,1)S(1)}, bf16[128,640]{1,0:T(8,128)(2,1)S(1)}, u32[]{:S(2)}, u32[]{:S(2)}) collective-permute-start(bf16[128,640]{1,0:T(8,128)(2,1)S(1)} %get-tuple-element.71.feats), channel_id=1, source_target_pairs={{0,4},{4,8},{8,12},{12,16},{16,20},{20,24},{24,28},{28,32},{32,36}... | collective-permute-start | bytes 491528 | tf_op jit(solution)/shard_map/ppermute | solution.py:282
  32.9 3.0 %while.20 = (s32[]{:T(128)}, bf16[128,640]{1,0:T(8,128)(2,1)S(1)}, s32[]{:T(128)}, s32[]{:T(128)}) while((s32[]{:T(128)}, bf16[128,640]{1,0:T(8,128)(2,1)S(1)}, s32[]{:T(128)}, s32[]{:T(128)}) %tuple.49), condition=%wide.region_1.2_spmd, body=%wide.region_0.1_spmd.sunk | while | flops 327682 | bytes 4587733 | solution.py:293
  32.9 0.7 collective-permute-start
  33.6 0.0 collective-permute-done
  33.6 0.7 collective-permute-start.1
  34.3 0.0 collective-permute-done.1
  34.4 0.7 collective-permute-start.2
  35.1 0.0 collective-permute-done.2
  35.1 0.7 collective-permute-start.3
  35.8 0.0 collective-permute-done.3
  35.9 0.8 collective-permute-done.11
  36.6 6.8 %collective-permute-done.12.w2 = bf16[160,1920]{1,0:T(8,128)(2,1)S(1)} collective-permute-done((bf16[160,1920]{1,0:T(8,128)(2,1)S(1)}, bf16[160,1920]{1,0:T(8,128)(2,1)S(1)}, u32[]{:S(2)}, u32[]{:S(2)}) %collective-permute-start.12) | collective-permute-done | bytes 614432 | tf_op jit(solution)/shard_map/ppermute | solution.py:33
  43.4 4.0 %collective-permute-start.13 = (bf16[160,1920]{1,0:T(8,128)(2,1)S(1)}, bf16[160,1920]{1,0:T(8,128)(2,1)S(1)}, u32[]{:S(2)}, u32[]{:S(2)}) collective-permute-start(bf16[160,1920]{1,0:T(8,128)(2,1)S(1)} %collective-permute-done.12.w2), channel_id=1, source_target_pairs={{0,1},{1,0},{2,3},{3,2},{4,5},{5,4},{6,7},{7,6},{8,9},{9,8},{10,11... | collective-permute-start | bytes 1843208 | tf_op jit(solution)/shard_map/ppermute | solution.py:33
  47.4 1.5 %while.21 = (s32[]{:T(128)}, bf16[128,640]{1,0:T(8,128)(2,1)S(1)}, s32[]{:T(128)}, s32[]{:T(128)}) while((s32[]{:T(128)}, bf16[128,640]{1,0:T(8,128)(2,1)S(1)}, s32[]{:T(128)}, s32[]{:T(128)}) %tuple.52), condition=%wide.region_3.4_spmd, body=%wide.region_2.3_spmd.sunk | while | flops 163842 | bytes 2293893 | solution.py:293
  47.4 0.7 collective-permute-start.4
  48.1 0.0 collective-permute-done.4
  48.2 0.7 collective-permute-start.5
  48.9 0.0 collective-permute-done.5
  48.9 0.1 collective-permute-done.13.w3
  49.1 1.3 %collective-permute-start.14 = (bf16[128,640]{1,0:T(8,128)(2,1)S(1)}, bf16[128,640]{1,0:T(8,128)(2,1)S(1)}, u32[]{:S(2)}, u32[]{:S(2)}) collective-permute-start(bf16[128,640]{1,0:T(8,128)(2,1)S(1)} %get-tuple-element.77), channel_id=1, source_target_pairs={{0,256},{8,264},{4,260},{12,268},{64,320},{72,328},{68,324},{76,33... | collective-permute-start | bytes 491528 | tf_op jit(solution)/shard_map/ppermute | solution.py:289
  50.4 26.5 %collective-permute-done.14 = bf16[128,640]{1,0:T(8,128)(2,1)S(1)} collective-permute-done((bf16[128,640]{1,0:T(8,128)(2,1)S(1)}, bf16[128,640]{1,0:T(8,128)(2,1)S(1)}, u32[]{:S(2)}, u32[]{:S(2)}) %collective-permute-start.14) | collective-permute-done | bytes 163872 | tf_op jit(solution)/shard_map/ppermute | solution.py:289
  77.0 4.0 %collective-permute-start.17 = (bf16[256,640]{1,0:T(8,128)(2,1)S(1)}, bf16[256,640]{1,0:T(8,128)(2,1)S(1)}, u32[]{:S(2)}, u32[]{:S(2)}) collective-permute-start(bf16[256,640]{1,0:T(8,128)(2,1)S(1)} %pad_maximum_fusion.a0), channel_id=1, source_target_pairs={{0,2},{1,3},{2,0},{3,1},{4,6},{5,7},{6,4},{7,5},{8,10},{9,11},{10,... | collective-permute-start | bytes 983048 | tf_op jit(solution)/shard_map/ppermute | solution.py:33
  81.0 3.9 %collective-permute-start.15 = (bf16[128,640]{1,0:T(8,128)(2,1)S(1)}, bf16[128,640]{1,0:T(8,128)(2,1)S(1)}, u32[]{:S(2)}, u32[]{:S(2)}) collective-permute-start(bf16[128,640]{1,0:T(8,128)(2,1)S(1)} %broadcast_select_fusion), channel_id=1, source_target_pairs={{0,1},{1,0},{2,3},{3,2},{4,5},{5,4},{6,7},{7,6},{8,9},{9,8},{10,11... | collective-permute-start | bytes 491528 | tf_op jit(solution)/shard_map/ppermute | solution.py:33
  84.9 1.9 %collective-permute-start.16 = (bf16[128,640]{1,0:T(8,128)(2,1)S(1)}, bf16[128,640]{1,0:T(8,128)(2,1)S(1)}, u32[]{:S(2)}, u32[]{:S(2)}) collective-permute-start(bf16[128,640]{1,0:T(8,128)(2,1)S(1)} %add.45), channel_id=1, source_target_pairs={{0,1},{1,0},{2,3},{3,2},{4,5},{5,4},{6,7},{7,6},{8,9},{9,8},{10,11... | collective-permute-start | bytes 491528 | tf_op jit(solution)/shard_map/ppermute | solution.py:33
  86.9 0.0 collective-permute-done.15.a1
  86.9 1.4 %collective-permute-done.16.a2 = bf16[128,640]{1,0:T(8,128)(2,1)S(1)} collective-permute-done((bf16[128,640]{1,0:T(8,128)(2,1)S(1)}, bf16[128,640]{1,0:T(8,128)(2,1)S(1)}, u32[]{:S(2)}, u32[]{:S(2)}) %collective-permute-start.16) | collective-permute-done | bytes 163872 | tf_op jit(solution)/shard_map/ppermute | solution.py:33
  88.2 3.6 %shard_map.69 = (bf16[128,640]{1,0:T(8,128)(2,1)S(1)}, f32[128,8]{1,0:T(8,128)S(1)}, f32[128,8]{1,0:T(8,128)S(1)}, f32[128,640]{1,0:T(8,128)S(1)}, bf16[640,1920]{1,0:T(8,128)(2,1)S(1)}) custom-call(s32[1]{0:T(128)} %bitcast.me_ref, bf16[128,640]{1,0:T(8,128)(2,1)S(1)} %get-tuple-element.71.feats, bf16[256,640]{1,0:T(8,128)(2,1)S(1)} %pad_maximum_fusion.a0, ...), custom_call_target="tpu_custom_call" | custom-call | flops 1006632960 | bytes 6234116 | tf_op jit(solution)/shard_map/pallas_call | solution.py:222
  91.8 0.0 collective-permute-done.17.a0
  91.8 2.1 %collective-permute-start.18 = (bf16[256,640]{1,0:T(8,128)(2,1)S(1)}, bf16[256,640]{1,0:T(8,128)(2,1)S(1)}, u32[]{:S(2)}, u32[]{:S(2)}) collective-permute-start(bf16[256,640]{1,0:T(8,128)(2,1)S(1)} %collective-permute-done.17.a0), channel_id=1, source_target_pairs={{0,1},{1,0},{2,3},{3,2},{4,5},{5,4},{6,7},{7,6},{8,9},{9,8},{10,11... | collective-permute-start | bytes 983048 | tf_op jit(solution)/shard_map/ppermute | solution.py:33
  93.9 2.9 %shard_map.70 = (f32[128,8]{1,0:T(8,128)S(1)}, f32[128,8]{1,0:T(8,128)S(1)}, f32[128,640]{1,0:T(8,128)S(1)}) custom-call(bf16[128,640]{1,0:T(8,128)(2,1)S(1)} %get-tuple-element.79.query, bf16[256,640]{1,0:T(8,128)(2,1)S(1)} %collective-permute-done.17.a0, bf16[640,1920]{1,0:T(8,128)(2,1)S(1)} %get-tuple-element.81.weight, ...), custom_call_target="tpu_custom_call" | custom-call | flops 503316480 | bytes 3620864 | tf_op jit(solution)/shard_map/pallas_call | solution.py:222
  96.8 0.0 collective-permute-done.18.a0
  96.9 3.8 %shard_map.71 = bf16[128,640]{1,0:T(8,128)(2,1)} custom-call(bf16[128,640]{1,0:T(8,128)(2,1)S(1)} %get-tuple-element.79.query, bf16[256,640]{1,0:T(8,128)(2,1)S(1)} %collective-permute-done.18.a0, bf16[640,1920]{1,0:T(8,128)(2,1)S(1)} %get-tuple-element.81.weight, f32[128,8]{1,0:T(8,128)S(1)} %get-tuple-element.85.top, f32[128,8]{1,0:T(8,128)S(1)} %get-tuple-element.86.den, ...), custom_call_target="tpu_custom_call" | custom-call | flops 503316480 | bytes 3612672 | tf_op jit(solution)/shard_map/pallas_call | solution.py:222
  (14 shorter events, 0.4 us)
Async XLA Ops:
  0.0 3.8 %collective-permute-start.6 = (bf16[128,640]{1,0:T(8,128)(2,1)}, bf16[128,640]{1,0:T(8,128)(2,1)S(1)}, u32[]{:S(2)}, u32[]{:S(2)}) collective-permute-start(bf16[128,640]{1,0:T(8,128)(2,1)} %bitcast.7), channel_id=1, source_target_pairs={{0,1},{1,0},{2,3},{3,2},{4,5},{5,4},{6,7},{7,6},{8,9},{9,8},{10,11... | collective-permute-start | bytes 491528 | tf_op jit(solution)/shard_map/ppermute | solution.py:33
  2.6 0.9 copy-start.1
  4.0 9.0 %collective-permute-start.8 = (bf16[160,1920]{1,0:T(8,128)(2,1)}, bf16[160,1920]{1,0:T(8,128)(2,1)S(1)}, u32[]{:S(2)}, u32[]{:S(2)}) collective-permute-start(bf16[160,1920]{1,0:T(8,128)(2,1)} %w0.1), channel_id=1, source_target_pairs={{0,1},{1,0},{2,3},{3,2},{4,5},{5,4},{6,7},{7,6},{8,9},{9,8},{10,11... | collective-permute-start | bytes 1843208 | tf_op jit(solution)/shard_map/ppermute | solution.py:33
  6.2 6.8 %collective-permute-start.7 = (bf16[2,128,160]{2,1,0:T(8,128)(2,1)S(1)}, bf16[2,128,160]{2,1,0:T(8,128)(2,1)S(1)}, u32[]{:S(2)}, u32[]{:S(2)}) collective-permute-start(bf16[2,128,160]{2,1,0:T(8,128)(2,1)S(1)} %get-tuple-element.65), channel_id=1, source_target_pairs={{0,2},{1,3},{2,0},{3,1},{4,6},{5,7},{6,4},{7,5},{8,10},{9,11},{10,... | collective-permute-start | bytes 245768 | tf_op jit(solution)/shard_map/ppermute | solution.py:33
  10.0 1.5 %copy-start = (bf16[9,160,640]{2,1,0:T(8,128)(2,1)S(1)}, bf16[9,160,640]{2,1,0:T(8,128)(2,1)}, u32[]{:S(2)}) copy-start(bf16[9,160,640]{2,1,0:T(8,128)(2,1)} %param.12) | copy-start | bytes 5529604
  13.0 9.7 %copy-start.3 = (f32[640]{0:T(1024)S(1)}, f32[640]{0:T(1024)}, u32[]{:S(2)}) copy-start(f32[640]{0:T(1024)} %param.13) | copy-start | bytes 7684
  13.0 9.7 %copy-start.4 = (f32[640]{0:T(1024)S(1)}, f32[640]{0:T(1024)}, u32[]{:S(2)}) copy-start(f32[640]{0:T(1024)} %param.14) | copy-start | bytes 7684
  15.4 12.0 %copy-start.2 = (bf16[160,1920]{1,0:T(8,128)(2,1)S(1)}, bf16[160,1920]{1,0:T(8,128)(2,1)}, u32[]{:S(2)}) copy-start(bf16[160,1920]{1,0:T(8,128)(2,1)} %w0.1) | copy-start | bytes 1843204
  15.4 4.3 %collective-permute-start.9 = (bf16[2,128,640]{2,1,0:T(8,128)(2,1)S(1)}, bf16[2,128,640]{2,1,0:T(8,128)(2,1)S(1)}, u32[]{:S(2)}, u32[]{:S(2)}) collective-permute-start(bf16[2,128,640]{2,1,0:T(8,128)(2,1)S(1)} %get-tuple-element.70), channel_id=1, source_target_pairs={{0,1},{1,0},{2,3},{3,2},{4,5},{5,4},{6,7},{7,6},{8,9},{9,8},{10,11... | collective-permute-start | bytes 983048 | tf_op jit(solution)/shard_map/ppermute | solution.py:33
  19.8 7.3 %collective-permute-start.10 = (bf16[128,640]{1,0:T(8,128)(2,1)S(1)}, bf16[128,640]{1,0:T(8,128)(2,1)S(1)}, u32[]{:S(2)}, u32[]{:S(2)}) collective-permute-start(bf16[128,640]{1,0:T(8,128)(2,1)S(1)} %fusion), channel_id=1, source_target_pairs={{0,2},{1,3},{2,0},{3,1},{4,6},{5,7},{6,4},{7,5},{8,10},{9,11},{10,... | collective-permute-start | bytes 491528 | tf_op jit(solution)/shard_map/ppermute | solution.py:33
  27.4 16.0 %collective-permute-start.12 = (bf16[160,1920]{1,0:T(8,128)(2,1)S(1)}, bf16[160,1920]{1,0:T(8,128)(2,1)S(1)}, u32[]{:S(2)}, u32[]{:S(2)}) collective-permute-start(bf16[160,1920]{1,0:T(8,128)(2,1)S(1)} %copy-done.2), channel_id=1, source_target_pairs={{0,2},{1,3},{2,0},{3,1},{4,6},{5,7},{6,4},{7,5},{8,10},{9,11},{10,... | collective-permute-start | bytes 1843208 | tf_op jit(solution)/shard_map/ppermute | solution.py:33
  30.3 6.4 %collective-permute-start.11 = (bf16[128,640]{1,0:T(8,128)(2,1)S(1)}, bf16[128,640]{1,0:T(8,128)(2,1)S(1)}, u32[]{:S(2)}, u32[]{:S(2)}) collective-permute-start(bf16[128,640]{1,0:T(8,128)(2,1)S(1)} %get-tuple-element.71.feats), channel_id=1, source_target_pairs={{0,4},{4,8},{8,12},{12,16},{16,20},{20,24},{24,28},{28,32},{32,36}... | collective-permute-start | bytes 491528 | tf_op jit(solution)/shard_map/ppermute | solution.py:282
  32.9 0.7 collective-permute-start
  33.6 0.7 collective-permute-start.1
  34.4 0.7 collective-permute-start.2
  35.1 0.7 collective-permute-start.3
  43.4 5.7 %collective-permute-start.13 = (bf16[160,1920]{1,0:T(8,128)(2,1)S(1)}, bf16[160,1920]{1,0:T(8,128)(2,1)S(1)}, u32[]{:S(2)}, u32[]{:S(2)}) collective-permute-start(bf16[160,1920]{1,0:T(8,128)(2,1)S(1)} %collective-permute-done.12.w2), channel_id=1, source_target_pairs={{0,1},{1,0},{2,3},{3,2},{4,5},{5,4},{6,7},{7,6},{8,9},{9,8},{10,11... | collective-permute-start | bytes 1843208 | tf_op jit(solution)/shard_map/ppermute | solution.py:33
  47.4 0.7 collective-permute-start.4
  48.2 0.7 collective-permute-start.5
  49.1 27.8 %collective-permute-start.14 = (bf16[128,640]{1,0:T(8,128)(2,1)S(1)}, bf16[128,640]{1,0:T(8,128)(2,1)S(1)}, u32[]{:S(2)}, u32[]{:S(2)}) collective-permute-start(bf16[128,640]{1,0:T(8,128)(2,1)S(1)} %get-tuple-element.77), channel_id=1, source_target_pairs={{0,256},{8,264},{4,260},{12,268},{64,320},{72,328},{68,324},{76,33... | collective-permute-start | bytes 491528 | tf_op jit(solution)/shard_map/ppermute | solution.py:289
  77.0 14.8 %collective-permute-start.17 = (bf16[256,640]{1,0:T(8,128)(2,1)S(1)}, bf16[256,640]{1,0:T(8,128)(2,1)S(1)}, u32[]{:S(2)}, u32[]{:S(2)}) collective-permute-start(bf16[256,640]{1,0:T(8,128)(2,1)S(1)} %pad_maximum_fusion.a0), channel_id=1, source_target_pairs={{0,2},{1,3},{2,0},{3,1},{4,6},{5,7},{6,4},{7,5},{8,10},{9,11},{10,... | collective-permute-start | bytes 983048 | tf_op jit(solution)/shard_map/ppermute | solution.py:33
  81.0 5.9 %collective-permute-start.15 = (bf16[128,640]{1,0:T(8,128)(2,1)S(1)}, bf16[128,640]{1,0:T(8,128)(2,1)S(1)}, u32[]{:S(2)}, u32[]{:S(2)}) collective-permute-start(bf16[128,640]{1,0:T(8,128)(2,1)S(1)} %broadcast_select_fusion), channel_id=1, source_target_pairs={{0,1},{1,0},{2,3},{3,2},{4,5},{5,4},{6,7},{7,6},{8,9},{9,8},{10,11... | collective-permute-start | bytes 491528 | tf_op jit(solution)/shard_map/ppermute | solution.py:33
  84.9 3.3 %collective-permute-start.16 = (bf16[128,640]{1,0:T(8,128)(2,1)S(1)}, bf16[128,640]{1,0:T(8,128)(2,1)S(1)}, u32[]{:S(2)}, u32[]{:S(2)}) collective-permute-start(bf16[128,640]{1,0:T(8,128)(2,1)S(1)} %add.45), channel_id=1, source_target_pairs={{0,1},{1,0},{2,3},{3,2},{4,5},{5,4},{6,7},{7,6},{8,9},{9,8},{10,11... | collective-permute-start | bytes 491528 | tf_op jit(solution)/shard_map/ppermute | solution.py:33
  91.8 5.0 %collective-permute-start.18 = (bf16[256,640]{1,0:T(8,128)(2,1)S(1)}, bf16[256,640]{1,0:T(8,128)(2,1)S(1)}, u32[]{:S(2)}, u32[]{:S(2)}) collective-permute-start(bf16[256,640]{1,0:T(8,128)(2,1)S(1)} %collective-permute-done.17.a0), channel_id=1, source_target_pairs={{0,1},{1,0},{2,3},{3,2},{4,5},{5,4},{6,7},{7,6},{8,9},{9,8},{10,11... | collective-permute-start | bytes 983048 | tf_op jit(solution)/shard_map/ppermute | solution.py:33

commit v14 on v13

--- a/solution.py
+++ b/solution.py
@@ -186,14 +186,15 @@
 
 
 def first_kernel(
-    me_ref, feats, a0, a1, a2, w0, w1, w2, w3, query, top, den, acc, weight, joined, keys, vals
+    me_ref, feats, a0, a1, a2, w0, c0, c1, c2, c3, w2, w3, query, top, den, acc, weight, joined, keys, vals
 ):
     me = me_ref[0]
     chans = feats.shape[1]
     share = w0.shape[0]
-    for flip, shard in enumerate((w0, w1, w2, w3)):
+    for flip, pieces in enumerate(((w0,), (c0, c1, c2, c3), (w2,), (w3,))):
+        shard = jnp.concatenate([piece[...] for piece in pieces], axis=0)
         at = pl.multiple_of((me ^ flip) * share, share)
-        weight[pl.ds(at, share), :] = shard[...]
+        weight[pl.ds(at, share), :] = shard
     query[...] = jnp.dot(
         feats[...], weight[:, :chans], preferred_element_type=jnp.float32
     ).astype(jnp.bfloat16)
@@ -252,9 +253,8 @@
         [me.reshape(1), lat, lat_core],
     )
     came = to_rows(away, 2)
-    weight_core = to_rows(after(qkv_weight, away), 1)
     taps_weight = fetched(after(conv_weight.reshape(3, 3 * share, chans), away))
-    came = after(came, weight_core, taps_weight)
+    came = after(came, taps_weight)
     group = jnp.arange(share) // (chans // GROUPS)
     pool = (group[:, None] == group[None, :]).astype(f32)
     keep, send = call(
@@ -270,7 +270,10 @@
     )
     core = to_rows(send, 1)
     half = (keep[1] + core[1].astype(f32)).astype(bf16)
-    chip = to_rows(half, 2)
+    cut = share // 4
+    chunk = lambda at, done: to_rows(after(qkv_weight[at * cut : (at + 1) * cut], done), 1)
+    chunks = [chunk(at, half) for at in range(3)]
+    chip = after(to_rows(half, 2), *chunks)
     residual, feats = call(
         norm_kernel,
         [shape((part, chans), bf16)] * 2,
@@ -296,9 +299,10 @@
     anchor = after(anchor, prev, weight_chip)
     weight_last = to_rows(after(weight_chip, anchor), 1)
     anchor = after(looped(anchor, routes[4:6]), weight_last)
-    anchor = levels(anchor, routes[6:])
+    chunks.append(chunk(3, anchor))
+    anchor = after(levels(anchor, routes[6:]), chunks[3])
     prev = jnp.where(first, feats, after(prev, anchor))
-    shards = [qkv_weight, weight_core, weight_chip, weight_last]
+    shards = [qkv_weight, *chunks, weight_chip, weight_last]
 
     own = jnp.concatenate([prev, anchor], axis=0)
     chip = to_rows(own, 2)

time: 101 us -> 102 us (level)
  starting transfers between devices: 40.3 us -> 44.5 us
  waiting for transfers between devices: 42.6 us -> 39.1 us
    ppermute x11 -> x14, starting transfers between devices: 32.5 us -> 36.7 us  [to_rows(): return lax.ppermute(x, 'rows', [(i, i ^ flip) for i in range(4)])]
    ppermute x11 -> x14, waiting for transfers between devices: 15.3 us -> 12.6 us  [to_rows(): return lax.ppermute(x, 'rows', [(i, i ^ flip) for i in range(4)])]
    ppermute x7, waiting for transfers between devices: 26.5 us -> 25.1 us  [levels(): anchor = anchor + lax.ppermute(anchor, 'tm', route)]
  transfers between devices with their start and end apart: 19 -> 22, of which waited for: 9 -> 9; matrix products, arithmetic and copies ran while one was open for 1% -> 1% of each run, Pallas kernels for 7% -> 7%
where the time goes in v14:
time: 102 us; the launch traced here: 101 us
  starting transfers between devices  44.5 us (44%)
  waiting for transfers between devices  39.1 us (38%)
  Pallas kernels  13.5 us (13%)
  local copies, waits for them, and re-layouts  3.25 us (3%)
    ppermute x14, starting transfers between devices, to_rows(): return lax.ppermute(x, 'rows', [(i, i ^ flip) for i in range(4)])  36.7 us
    ppermute x7, waiting for transfers between devices, levels(): anchor = anchor + lax.ppermute(anchor, 'tm', route)  25.1 us
    pallas_call x8, Pallas kernels, call(): pl.pallas_call(kernel, out_shape=list(outs), in_specs=specs, out_specs=[V...  13.5 us
    ppermute x14, waiting for transfers between devices, to_rows(): return lax.ppermute(x, 'rows', [(i, i ^ flip) for i in range(4)])  12.6 us
    ppermute x7, starting transfers between devices, levels(): anchor = anchor + lax.ppermute(anchor, 'tm', route)  5.31 us
    ppermute x1, starting transfers between devices, on_device(): prev = lax.ppermute(feats, 'tm', [(i, i + 1) for i in range(devices - 1)])  2.56 us
    unnamed x10, local copies, waits for them, and re-layouts  2.42 us
  transfers between devices with their start and end apart: 22, of which 9 were waited for; matrix products, arithmetic and copies ran while one was open for 1% of the time, Pallas kernels for 7%

profile of v14, /device:TPU:375, one launch (start us, length us, event | category | flops | bytes accessed | tf_op | source)
XLA Modules:
  0.0 101.4 jit_solution(12494542786021456236)
XLA Ops:
  0.0 2.6 %collective-permute-start.6 = (bf16[128,640]{1,0:T(8,128)(2,1)}, bf16[128,640]{1,0:T(8,128)(2,1)S(1)}, u32[]{:S(2)}, u32[]{:S(2)}) collective-permute-start(bf16[128,640]{1,0:T(8,128)(2,1)} %bitcast.7), channel_id=1, source_target_pairs={{0,1},{1,0},{2,3},{3,2},{4,5},{5,4},{6,7},{7,6},{8,9},{9,8},{10,11... | collective-permute-start | bytes 491528 | tf_op jit(solution)/shard_map/ppermute | solution.py:33
  2.6 0.0 copy-start.2
  2.6 0.9 copy-done.2
  3.5 0.2 shard_map.64.own.lat
  3.7 0.1 collective-permute-done.6.core
  3.8 0.2 shard_map.65
  4.0 2.9 %collective-permute-start.7 = (bf16[2,128,160]{2,1,0:T(8,128)(2,1)S(1)}, bf16[2,128,160]{2,1,0:T(8,128)(2,1)S(1)}, u32[]{:S(2)}, u32[]{:S(2)}) collective-permute-start(bf16[2,128,160]{2,1,0:T(8,128)(2,1)S(1)} %get-tuple-element.70), channel_id=1, source_target_pairs={{0,2},{1,3},{2,0},{3,1},{4,6},{5,7},{6,4},{7,5},{8,10},{9,11},{10,... | collective-permute-start | bytes 245768 | tf_op jit(solution)/shard_map/ppermute | solution.py:33
  6.9 0.1 compare_convert_fusion.pool
  7.0 0.8 reshape.55.gain
  7.8 0.0 copy-start
  7.8 1.5 %copy-done = bf16[9,160,640]{2,1,0:T(8,128)(2,1)S(1)} copy-done((bf16[9,160,640]{2,1,0:T(8,128)(2,1)S(1)}, bf16[9,160,640]{2,1,0:T(8,128)(2,1)}, u32[]{:S(2)}) %copy-start) | copy-done | bytes 1843224
  9.3 0.1 shard_map.66.weight
  9.4 1.3 %collective-permute-done.7.came = bf16[2,128,160]{2,1,0:T(8,128)(2,1)S(1)} collective-permute-done((bf16[2,128,160]{2,1,0:T(8,128)(2,1)S(1)}, bf16[2,128,160]{2,1,0:T(8,128)(2,1)S(1)}, u32[]{:S(2)}, u32[]{:S(2)}) %collective-permute-start.7) | collective-permute-done | bytes 81952 | tf_op jit(solution)/shard_map/ppermute | solution.py:33
  10.7 0.0 copy-start.1
  10.7 2.4 %shard_map.67 = (f32[2,128,640]{2,1,0:T(8,128)S(1)}, bf16[2,128,640]{2,1,0:T(8,128)(2,1)S(1)}) custom-call(s32[1]{0:T(128)} %bitcast.me_ref, bf16[2,128,160]{2,1,0:T(8,128)(2,1)S(1)} %get-tuple-element.69.mine, bf16[2,128,160]{2,1,0:T(8,128)(2,1)S(1)} %collective-permute-done.7.came, f32[4,160]{1,0:T(4,128)S(1)} %reshape.55.gain, ...), custom_call_target="tpu_custom_call" | custom-call | flops 943718400 | bytes 3095044 | tf_op jit(solution)/shard_map/pallas_call | solution.py:223
  13.1 3.0 %collective-permute-start.8 = (bf16[2,128,640]{2,1,0:T(8,128)(2,1)S(1)}, bf16[2,128,640]{2,1,0:T(8,128)(2,1)S(1)}, u32[]{:S(2)}, u32[]{:S(2)}) collective-permute-start(bf16[2,128,640]{2,1,0:T(8,128)(2,1)S(1)} %get-tuple-element.74), channel_id=1, source_target_pairs={{0,1},{1,0},{2,3},{3,2},{4,5},{5,4},{6,7},{7,6},{8,9},{9,8},{10,11... | collective-permute-start | bytes 983048 | tf_op jit(solution)/shard_map/ppermute | solution.py:33
  16.1 1.2 %collective-permute-done.8.core = bf16[2,128,640]{2,1,0:T(8,128)(2,1)S(1)} collective-permute-done((bf16[2,128,640]{2,1,0:T(8,128)(2,1)S(1)}, bf16[2,128,640]{2,1,0:T(8,128)(2,1)S(1)}, u32[]{:S(2)}, u32[]{:S(2)}) %collective-permute-start.8) | collective-permute-done | bytes 327712 | tf_op jit(solution)/shard_map/ppermute | solution.py:33
  17.4 2.9 %collective-permute-start.9 = (bf16[128,640]{1,0:T(8,128)(2,1)S(1)}, bf16[128,640]{1,0:T(8,128)(2,1)S(1)}, u32[]{:S(2)}, u32[]{:S(2)}) collective-permute-start(bf16[128,640]{1,0:T(8,128)(2,1)S(1)} %fusion), channel_id=1, source_target_pairs={{0,2},{1,3},{2,0},{3,1},{4,6},{5,7},{6,4},{7,5},{8,10},{9,11},{10,... | collective-permute-start | bytes 491528 | tf_op jit(solution)/shard_map/ppermute | solution.py:33
  20.3 0.0 copy-done.1
  20.4 2.6 %collective-permute-start.10 = (bf16[40,1920]{1,0:T(8,128)(2,1)S(1)}, bf16[40,1920]{1,0:T(8,128)(2,1)S(1)}, u32[]{:S(2)}, u32[]{:S(2)}) collective-permute-start(bf16[40,1920]{1,0:T(8,128)(2,1)S(1)} %get-tuple-element.75), channel_id=1, source_target_pairs={{0,1},{1,0},{2,3},{3,2},{4,5},{5,4},{6,7},{7,6},{8,9},{9,8},{10,11... | collective-permute-start | bytes 460808 | tf_op jit(solution)/shard_map/ppermute | solution.py:33
  23.0 1.9 %collective-permute-start.11 = (bf16[40,1920]{1,0:T(8,128)(2,1)S(1)}, bf16[40,1920]{1,0:T(8,128)(2,1)S(1)}, u32[]{:S(2)}, u32[]{:S(2)}) collective-permute-start(bf16[40,1920]{1,0:T(8,128)(2,1)S(1)} %get-tuple-element.76), channel_id=1, source_target_pairs={{0,1},{1,0},{2,3},{3,2},{4,5},{5,4},{6,7},{7,6},{8,9},{9,8},{10,11... | collective-permute-start | bytes 460808 | tf_op jit(solution)/shard_map/ppermute | solution.py:33
  24.9 2.4 %collective-permute-start.12 = (bf16[40,1920]{1,0:T(8,128)(2,1)S(1)}, bf16[40,1920]{1,0:T(8,128)(2,1)S(1)}, u32[]{:S(2)}, u32[]{:S(2)}) collective-permute-start(bf16[40,1920]{1,0:T(8,128)(2,1)S(1)} %get-tuple-element.77), channel_id=1, source_target_pairs={{0,1},{1,0},{2,3},{3,2},{4,5},{5,4},{6,7},{7,6},{8,9},{9,8},{10,11... | collective-permute-start | bytes 460808 | tf_op jit(solution)/shard_map/ppermute | solution.py:33
  27.3 0.0 copy-done.3
  27.3 0.0 copy-done.4
  27.3 0.0 collective-permute-done.10.c0
  27.3 0.0 collective-permute-done.11.c1
  27.4 0.9 collective-permute-done.12.c2
  28.3 0.0 collective-permute-done.9.chip
  28.3 0.3 shard_map.68
  28.6 2.4 %collective-permute-start.14 = (bf16[160,1920]{1,0:T(8,128)(2,1)S(1)}, bf16[160,1920]{1,0:T(8,128)(2,1)S(1)}, u32[]{:S(2)}, u32[]{:S(2)}) collective-permute-start(bf16[160,1920]{1,0:T(8,128)(2,1)S(1)} %copy-done.1), channel_id=1, source_target_pairs={{0,2},{1,3},{2,0},{3,1},{4,6},{5,7},{6,4},{7,5},{8,10},{9,11},{10,... | collective-permute-start | bytes 1843208 | tf_op jit(solution)/shard_map/ppermute | solution.py:33
  31.0 2.6 %collective-permute-start.13 = (bf16[128,640]{1,0:T(8,128)(2,1)S(1)}, bf16[128,640]{1,0:T(8,128)(2,1)S(1)}, u32[]{:S(2)}, u32[]{:S(2)}) collective-permute-start(bf16[128,640]{1,0:T(8,128)(2,1)S(1)} %get-tuple-element.79.feats), channel_id=1, source_target_pairs={{0,4},{4,8},{8,12},{12,16},{16,20},{20,24},{24,28},{28,32},{32,36}... | collective-permute-start | bytes 491528 | tf_op jit(solution)/shard_map/ppermute | solution.py:285
  33.6 3.0 %while.20 = (s32[]{:T(128)}, bf16[128,640]{1,0:T(8,128)(2,1)S(1)}, s32[]{:T(128)}, s32[]{:T(128)}) while((s32[]{:T(128)}, bf16[128,640]{1,0:T(8,128)(2,1)S(1)}, s32[]{:T(128)}, s32[]{:T(128)}) %tuple.62), condition=%wide.region_1.2_spmd, body=%wide.region_0.1_spmd.sunk | while | flops 327682 | bytes 4587733 | solution.py:296
  33.6 0.7 collective-permute-start
  34.3 0.0 collective-permute-done
  34.3 0.7 collective-permute-start.1
  35.0 0.0 collective-permute-done.1
  35.1 0.7 collective-permute-start.2
  35.7 0.0 collective-permute-done.2
  35.8 0.7 collective-permute-start.3
  36.5 0.0 collective-permute-done.3
  36.5 1.4 %collective-permute-done.13 = bf16[128,640]{1,0:T(8,128)(2,1)S(1)} collective-permute-done((bf16[128,640]{1,0:T(8,128)(2,1)S(1)}, bf16[128,640]{1,0:T(8,128)(2,1)S(1)}, u32[]{:S(2)}, u32[]{:S(2)}) %collective-permute-start.13) | collective-permute-done | bytes 163872 | tf_op jit(solution)/shard_map/ppermute | solution.py:285
  38.0 7.6 %collective-permute-done.14.w2 = bf16[160,1920]{1,0:T(8,128)(2,1)S(1)} collective-permute-done((bf16[160,1920]{1,0:T(8,128)(2,1)S(1)}, bf16[160,1920]{1,0:T(8,128)(2,1)S(1)}, u32[]{:S(2)}, u32[]{:S(2)}) %collective-permute-start.14) | collective-permute-done | bytes 614432 | tf_op jit(solution)/shard_map/ppermute | solution.py:33
  45.5 3.1 %collective-permute-start.15 = (bf16[160,1920]{1,0:T(8,128)(2,1)S(1)}, bf16[160,1920]{1,0:T(8,128)(2,1)S(1)}, u32[]{:S(2)}, u32[]{:S(2)}) collective-permute-start(bf16[160,1920]{1,0:T(8,128)(2,1)S(1)} %collective-permute-done.14.w2), channel_id=1, source_target_pairs={{0,1},{1,0},{2,3},{3,2},{4,5},{5,4},{6,7},{7,6},{8,9},{9,8},{10,11... | collective-permute-start | bytes 1843208 | tf_op jit(solution)/shard_map/ppermute | solution.py:33
  48.6 1.5 %while.21 = (s32[]{:T(128)}, bf16[128,640]{1,0:T(8,128)(2,1)S(1)}, s32[]{:T(128)}, s32[]{:T(128)}) while((s32[]{:T(128)}, bf16[128,640]{1,0:T(8,128)(2,1)S(1)}, s32[]{:T(128)}, s32[]{:T(128)}) %tuple.65), condition=%wide.region_3.4_spmd, body=%wide.region_2.3_spmd.sunk | while | flops 163842 | bytes 2293893 | solution.py:296
  48.7 0.7 collective-permute-start.4
  49.3 0.0 collective-permute-done.4
  49.4 0.7 collective-permute-start.5
  50.1 0.0 collective-permute-done.5
  50.1 0.1 collective-permute-done.15.w3
  50.3 1.3 %collective-permute-start.16 = (bf16[128,640]{1,0:T(8,128)(2,1)S(1)}, bf16[128,640]{1,0:T(8,128)(2,1)S(1)}, u32[]{:S(2)}, u32[]{:S(2)}) collective-permute-start(bf16[128,640]{1,0:T(8,128)(2,1)S(1)} %get-tuple-element.85), channel_id=1, source_target_pairs={{0,256},{8,264},{4,260},{12,268},{64,320},{72,328},{68,324},{76,33... | collective-permute-start | bytes 491528 | tf_op jit(solution)/shard_map/ppermute | solution.py:292
  51.6 2.3 %collective-permute-start.17 = (bf16[40,1920]{1,0:T(8,128)(2,1)S(1)}, bf16[40,1920]{1,0:T(8,128)(2,1)S(1)}, u32[]{:S(2)}, u32[]{:S(2)}) collective-permute-start(bf16[40,1920]{1,0:T(8,128)(2,1)S(1)} %get-tuple-element.86), channel_id=1, source_target_pairs={{0,1},{1,0},{2,3},{3,2},{4,5},{5,4},{6,7},{7,6},{8,9},{9,8},{10,11... | collective-permute-start | bytes 460808 | tf_op jit(solution)/shard_map/ppermute | solution.py:33
  53.9 25.1 %collective-permute-done.16 = bf16[128,640]{1,0:T(8,128)(2,1)S(1)} collective-permute-done((bf16[128,640]{1,0:T(8,128)(2,1)S(1)}, bf16[128,640]{1,0:T(8,128)(2,1)S(1)}, u32[]{:S(2)}, u32[]{:S(2)}) %collective-permute-start.16) | collective-permute-done | bytes 163872 | tf_op jit(solution)/shard_map/ppermute | solution.py:292
  79.0 0.0 collective-permute-done.17.c3
  79.1 2.5 %collective-permute-start.20 = (bf16[256,640]{1,0:T(8,128)(2,1)S(1)}, bf16[256,640]{1,0:T(8,128)(2,1)S(1)}, u32[]{:S(2)}, u32[]{:S(2)}) collective-permute-start(bf16[256,640]{1,0:T(8,128)(2,1)S(1)} %pad_maximum_fusion.a0), channel_id=1, source_target_pairs={{0,2},{1,3},{2,0},{3,1},{4,6},{5,7},{6,4},{7,5},{8,10},{9,11},{10,... | collective-permute-start | bytes 983048 | tf_op jit(solution)/shard_map/ppermute | solution.py:33
  81.6 3.9 %collective-permute-start.18 = (bf16[128,640]{1,0:T(8,128)(2,1)S(1)}, bf16[128,640]{1,0:T(8,128)(2,1)S(1)}, u32[]{:S(2)}, u32[]{:S(2)}) collective-permute-start(bf16[128,640]{1,0:T(8,128)(2,1)S(1)} %broadcast_select_fusion), channel_id=1, source_target_pairs={{0,1},{1,0},{2,3},{3,2},{4,5},{5,4},{6,7},{7,6},{8,9},{9,8},{10,11... | collective-permute-start | bytes 491528 | tf_op jit(solution)/shard_map/ppermute | solution.py:33
  85.5 1.9 %collective-permute-start.19 = (bf16[128,640]{1,0:T(8,128)(2,1)S(1)}, bf16[128,640]{1,0:T(8,128)(2,1)S(1)}, u32[]{:S(2)}, u32[]{:S(2)}) collective-permute-start(bf16[128,640]{1,0:T(8,128)(2,1)S(1)} %add.45), channel_id=1, source_target_pairs={{0,1},{1,0},{2,3},{3,2},{4,5},{5,4},{6,7},{7,6},{8,9},{9,8},{10,11... | collective-permute-start | bytes 491528 | tf_op jit(solution)/shard_map/ppermute | solution.py:33
  87.5 0.0 collective-permute-done.18.a1
  87.5 1.4 %collective-permute-done.19.a2 = bf16[128,640]{1,0:T(8,128)(2,1)S(1)} collective-permute-done((bf16[128,640]{1,0:T(8,128)(2,1)S(1)}, bf16[128,640]{1,0:T(8,128)(2,1)S(1)}, u32[]{:S(2)}, u32[]{:S(2)}) %collective-permute-start.19) | collective-permute-done | bytes 163872 | tf_op jit(solution)/shard_map/ppermute | solution.py:33
  88.8 3.6 %shard_map.69 = (bf16[128,640]{1,0:T(8,128)(2,1)S(1)}, f32[128,8]{1,0:T(8,128)S(1)}, f32[128,8]{1,0:T(8,128)S(1)}, f32[128,640]{1,0:T(8,128)S(1)}, bf16[640,1920]{1,0:T(8,128)(2,1)S(1)}) custom-call(s32[1]{0:T(128)} %bitcast.me_ref, bf16[128,640]{1,0:T(8,128)(2,1)S(1)} %get-tuple-element.79.feats, bf16[256,640]{1,0:T(8,128)(2,1)S(1)} %pad_maximum_fusion.a0, ...), custom_call_target="tpu_custom_call" | custom-call | flops 1006632960 | bytes 6234116 | tf_op jit(solution)/shard_map/pallas_call | solution.py:223
  92.4 0.0 collective-permute-done.20.a0
  92.5 2.2 %collective-permute-start.21 = (bf16[256,640]{1,0:T(8,128)(2,1)S(1)}, bf16[256,640]{1,0:T(8,128)(2,1)S(1)}, u32[]{:S(2)}, u32[]{:S(2)}) collective-permute-start(bf16[256,640]{1,0:T(8,128)(2,1)S(1)} %collective-permute-done.20.a0), channel_id=1, source_target_pairs={{0,1},{1,0},{2,3},{3,2},{4,5},{5,4},{6,7},{7,6},{8,9},{9,8},{10,11... | collective-permute-start | bytes 983048 | tf_op jit(solution)/shard_map/ppermute | solution.py:33
  94.7 2.9 %shard_map.70 = (f32[128,8]{1,0:T(8,128)S(1)}, f32[128,8]{1,0:T(8,128)S(1)}, f32[128,640]{1,0:T(8,128)S(1)}) custom-call(bf16[128,640]{1,0:T(8,128)(2,1)S(1)} %get-tuple-element.89.query, bf16[256,640]{1,0:T(8,128)(2,1)S(1)} %collective-permute-done.20.a0, bf16[640,1920]{1,0:T(8,128)(2,1)S(1)} %get-tuple-element.91.weight, ...), custom_call_target="tpu_custom_call" | custom-call | flops 503316480 | bytes 3620864 | tf_op jit(solution)/shard_map/pallas_call | solution.py:223
  97.6 0.0 collective-permute-done.21.a0
  97.6 3.8 %shard_map.71 = bf16[128,640]{1,0:T(8,128)(2,1)} custom-call(bf16[128,640]{1,0:T(8,128)(2,1)S(1)} %get-tuple-element.89.query, bf16[256,640]{1,0:T(8,128)(2,1)S(1)} %collective-permute-done.21.a0, bf16[640,1920]{1,0:T(8,128)(2,1)S(1)} %get-tuple-element.91.weight, f32[128,8]{1,0:T(8,128)S(1)} %get-tuple-element.95.top, f32[128,8]{1,0:T(8,128)S(1)} %get-tuple-element.96.den, ...), custom_call_target="tpu_custom_call" | custom-call | flops 503316480 | bytes 3612672 | tf_op jit(solution)/shard_map/pallas_call | solution.py:223
  (17 shorter events, 0.5 us)
Async XLA Ops:
  0.0 3.8 %collective-permute-start.6 = (bf16[128,640]{1,0:T(8,128)(2,1)}, bf16[128,640]{1,0:T(8,128)(2,1)S(1)}, u32[]{:S(2)}, u32[]{:S(2)}) collective-permute-start(bf16[128,640]{1,0:T(8,128)(2,1)} %bitcast.7), channel_id=1, source_target_pairs={{0,1},{1,0},{2,3},{3,2},{4,5},{5,4},{6,7},{7,6},{8,9},{9,8},{10,11... | collective-permute-start | bytes 491528 | tf_op jit(solution)/shard_map/ppermute | solution.py:33
  2.6 0.9 copy-start.2
  4.0 6.7 %collective-permute-start.7 = (bf16[2,128,160]{2,1,0:T(8,128)(2,1)S(1)}, bf16[2,128,160]{2,1,0:T(8,128)(2,1)S(1)}, u32[]{:S(2)}, u32[]{:S(2)}) collective-permute-start(bf16[2,128,160]{2,1,0:T(8,128)(2,1)S(1)} %get-tuple-element.70), channel_id=1, source_target_pairs={{0,2},{1,3},{2,0},{3,1},{4,6},{5,7},{6,4},{7,5},{8,10},{9,11},{10,... | collective-permute-start | bytes 245768 | tf_op jit(solution)/shard_map/ppermute | solution.py:33
  7.8 1.5 %copy-start = (bf16[9,160,640]{2,1,0:T(8,128)(2,1)S(1)}, bf16[9,160,640]{2,1,0:T(8,128)(2,1)}, u32[]{:S(2)}) copy-start(bf16[9,160,640]{2,1,0:T(8,128)(2,1)} %param.12) | copy-start | bytes 5529604
  10.7 9.6 %copy-start.1 = (bf16[160,1920]{1,0:T(8,128)(2,1)S(1)}, bf16[160,1920]{1,0:T(8,128)(2,1)}, u32[]{:S(2)}) copy-start(bf16[160,1920]{1,0:T(8,128)(2,1)} %w0.1) | copy-start | bytes 1843204
  10.7 16.6 %copy-start.3 = (f32[640]{0:T(1024)S(1)}, f32[640]{0:T(1024)}, u32[]{:S(2)}) copy-start(f32[640]{0:T(1024)} %param.13) | copy-start | bytes 7684
  10.7 16.6 %copy-start.4 = (f32[640]{0:T(1024)S(1)}, f32[640]{0:T(1024)}, u32[]{:S(2)}) copy-start(f32[640]{0:T(1024)} %param.14) | copy-start | bytes 7684
  13.1 4.3 %collective-permute-start.8 = (bf16[2,128,640]{2,1,0:T(8,128)(2,1)S(1)}, bf16[2,128,640]{2,1,0:T(8,128)(2,1)S(1)}, u32[]{:S(2)}, u32[]{:S(2)}) collective-permute-start(bf16[2,128,640]{2,1,0:T(8,128)(2,1)S(1)} %get-tuple-element.74), channel_id=1, source_target_pairs={{0,1},{1,0},{2,3},{3,2},{4,5},{5,4},{6,7},{7,6},{8,9},{9,8},{10,11... | collective-permute-start | bytes 983048 | tf_op jit(solution)/shard_map/ppermute | solution.py:33
  17.4 10.9 %collective-permute-start.9 = (bf16[128,640]{1,0:T(8,128)(2,1)S(1)}, bf16[128,640]{1,0:T(8,128)(2,1)S(1)}, u32[]{:S(2)}, u32[]{:S(2)}) collective-permute-start(bf16[128,640]{1,0:T(8,128)(2,1)S(1)} %fusion), channel_id=1, source_target_pairs={{0,2},{1,3},{2,0},{3,1},{4,6},{5,7},{6,4},{7,5},{8,10},{9,11},{10,... | collective-permute-start | bytes 491528 | tf_op jit(solution)/shard_map/ppermute | solution.py:33
  20.4 7.0 %collective-permute-start.10 = (bf16[40,1920]{1,0:T(8,128)(2,1)S(1)}, bf16[40,1920]{1,0:T(8,128)(2,1)S(1)}, u32[]{:S(2)}, u32[]{:S(2)}) collective-permute-start(bf16[40,1920]{1,0:T(8,128)(2,1)S(1)} %get-tuple-element.75), channel_id=1, source_target_pairs={{0,1},{1,0},{2,3},{3,2},{4,5},{5,4},{6,7},{7,6},{8,9},{9,8},{10,11... | collective-permute-start | bytes 460808 | tf_op jit(solution)/shard_map/ppermute | solution.py:33
  23.0 4.4 %collective-permute-start.11 = (bf16[40,1920]{1,0:T(8,128)(2,1)S(1)}, bf16[40,1920]{1,0:T(8,128)(2,1)S(1)}, u32[]{:S(2)}, u32[]{:S(2)}) collective-permute-start(bf16[40,1920]{1,0:T(8,128)(2,1)S(1)} %get-tuple-element.76), channel_id=1, source_target_pairs={{0,1},{1,0},{2,3},{3,2},{4,5},{5,4},{6,7},{7,6},{8,9},{9,8},{10,11... | collective-permute-start | bytes 460808 | tf_op jit(solution)/shard_map/ppermute | solution.py:33
  24.9 3.4 %collective-permute-start.12 = (bf16[40,1920]{1,0:T(8,128)(2,1)S(1)}, bf16[40,1920]{1,0:T(8,128)(2,1)S(1)}, u32[]{:S(2)}, u32[]{:S(2)}) collective-permute-start(bf16[40,1920]{1,0:T(8,128)(2,1)S(1)} %get-tuple-element.77), channel_id=1, source_target_pairs={{0,1},{1,0},{2,3},{3,2},{4,5},{5,4},{6,7},{7,6},{8,9},{9,8},{10,11... | collective-permute-start | bytes 460808 | tf_op jit(solution)/shard_map/ppermute | solution.py:33
  28.6 17.0 %collective-permute-start.14 = (bf16[160,1920]{1,0:T(8,128)(2,1)S(1)}, bf16[160,1920]{1,0:T(8,128)(2,1)S(1)}, u32[]{:S(2)}, u32[]{:S(2)}) collective-permute-start(bf16[160,1920]{1,0:T(8,128)(2,1)S(1)} %copy-done.1), channel_id=1, source_target_pairs={{0,2},{1,3},{2,0},{3,1},{4,6},{5,7},{6,4},{7,5},{8,10},{9,11},{10,... | collective-permute-start | bytes 1843208 | tf_op jit(solution)/shard_map/ppermute | solution.py:33
  31.0 7.0 %collective-permute-start.13 = (bf16[128,640]{1,0:T(8,128)(2,1)S(1)}, bf16[128,640]{1,0:T(8,128)(2,1)S(1)}, u32[]{:S(2)}, u32[]{:S(2)}) collective-permute-start(bf16[128,640]{1,0:T(8,128)(2,1)S(1)} %get-tuple-element.79.feats), channel_id=1, source_target_pairs={{0,4},{4,8},{8,12},{12,16},{16,20},{20,24},{24,28},{28,32},{32,36}... | collective-permute-start | bytes 491528 | tf_op jit(solution)/shard_map/ppermute | solution.py:285
  33.6 0.7 collective-permute-start
  34.3 0.7 collective-permute-start.1
  35.1 0.7 collective-permute-start.2
  35.8 0.7 collective-permute-start.3
  45.5 4.7 %collective-permute-start.15 = (bf16[160,1920]{1,0:T(8,128)(2,1)S(1)}, bf16[160,1920]{1,0:T(8,128)(2,1)S(1)}, u32[]{:S(2)}, u32[]{:S(2)}) collective-permute-start(bf16[160,1920]{1,0:T(8,128)(2,1)S(1)} %collective-permute-done.14.w2), channel_id=1, source_target_pairs={{0,1},{1,0},{2,3},{3,2},{4,5},{5,4},{6,7},{7,6},{8,9},{9,8},{10,11... | collective-permute-start | bytes 1843208 | tf_op jit(solution)/shard_map/ppermute | solution.py:33
  48.7 0.7 collective-permute-start.4
  49.4 0.7 collective-permute-start.5
  50.3 28.6 %collective-permute-start.16 = (bf16[128,640]{1,0:T(8,128)(2,1)S(1)}, bf16[128,640]{1,0:T(8,128)(2,1)S(1)}, u32[]{:S(2)}, u32[]{:S(2)}) collective-permute-start(bf16[128,640]{1,0:T(8,128)(2,1)S(1)} %get-tuple-element.85), channel_id=1, source_target_pairs={{0,256},{8,264},{4,260},{12,268},{64,320},{72,328},{68,324},{76,33... | collective-permute-start | bytes 491528 | tf_op jit(solution)/shard_map/ppermute | solution.py:292
  51.6 27.4 %collective-permute-start.17 = (bf16[40,1920]{1,0:T(8,128)(2,1)S(1)}, bf16[40,1920]{1,0:T(8,128)(2,1)S(1)}, u32[]{:S(2)}, u32[]{:S(2)}) collective-permute-start(bf16[40,1920]{1,0:T(8,128)(2,1)S(1)} %get-tuple-element.86), channel_id=1, source_target_pairs={{0,1},{1,0},{2,3},{3,2},{4,5},{5,4},{6,7},{7,6},{8,9},{9,8},{10,11... | collective-permute-start | bytes 460808 | tf_op jit(solution)/shard_map/ppermute | solution.py:33
  79.1 13.4 %collective-permute-start.20 = (bf16[256,640]{1,0:T(8,128)(2,1)S(1)}, bf16[256,640]{1,0:T(8,128)(2,1)S(1)}, u32[]{:S(2)}, u32[]{:S(2)}) collective-permute-start(bf16[256,640]{1,0:T(8,128)(2,1)S(1)} %pad_maximum_fusion.a0), channel_id=1, source_target_pairs={{0,2},{1,3},{2,0},{3,1},{4,6},{5,7},{6,4},{7,5},{8,10},{9,11},{10,... | collective-permute-start | bytes 983048 | tf_op jit(solution)/shard_map/ppermute | solution.py:33
  81.6 5.9 %collective-permute-start.18 = (bf16[128,640]{1,0:T(8,128)(2,1)S(1)}, bf16[128,640]{1,0:T(8,128)(2,1)S(1)}, u32[]{:S(2)}, u32[]{:S(2)}) collective-permute-start(bf16[128,640]{1,0:T(8,128)(2,1)S(1)} %broadcast_select_fusion), channel_id=1, source_target_pairs={{0,1},{1,0},{2,3},{3,2},{4,5},{5,4},{6,7},{7,6},{8,9},{9,8},{10,11... | collective-permute-start | bytes 491528 | tf_op jit(solution)/shard_map/ppermute | solution.py:33
  85.5 3.3 %collective-permute-start.19 = (bf16[128,640]{1,0:T(8,128)(2,1)S(1)}, bf16[128,640]{1,0:T(8,128)(2,1)S(1)}, u32[]{:S(2)}, u32[]{:S(2)}) collective-permute-start(bf16[128,640]{1,0:T(8,128)(2,1)S(1)} %add.45), channel_id=1, source_target_pairs={{0,1},{1,0},{2,3},{3,2},{4,5},{5,4},{6,7},{7,6},{8,9},{9,8},{10,11... | collective-permute-start | bytes 491528 | tf_op jit(solution)/shard_map/ppermute | solution.py:33
  92.5 5.2 %collective-permute-start.21 = (bf16[256,640]{1,0:T(8,128)(2,1)S(1)}, bf16[256,640]{1,0:T(8,128)(2,1)S(1)}, u32[]{:S(2)}, u32[]{:S(2)}) collective-permute-start(bf16[256,640]{1,0:T(8,128)(2,1)S(1)} %collective-permute-done.20.a0), channel_id=1, source_target_pairs={{0,1},{1,0},{2,3},{3,2},{4,5},{5,4},{6,7},{7,6},{8,9},{9,8},{10,11... | collective-permute-start | bytes 983048 | tf_op jit(solution)/shard_map/ppermute | solution.py:33
